TPU v7x, 32 devices: a whole 2x2x4 slice. The times are simulated.
32 devices in a mesh: seq: 8 (over z, x), blk: 4 (over y, core).
Axes of the slice: x: 2, y: 2, z: 4, core: 2. Of those that a mesh axis runs over, the one named last changes fastest.
Arguments:
- tokens: bfloat16 [16, 256, 768], P('seq', 'blk'), may hold values from -6 to 6
- ln1_gain: bfloat16 [768], replicated, may hold values from 0.099609375 to 1.8984375
- ln1_bias: bfloat16 [768], replicated, may hold values from -1.75 to 1.75
- query_key_value_weight: bfloat16 [768, 2304], replicated, may hold values from -0.21875 to 0.21875
- bias_qv: bfloat16 [1536], replicated, may hold values from -3 to 3
- output_weight: bfloat16 [768, 768], replicated, may hold values from -0.875 to 0.875
- output_bias: bfloat16 [768], replicated, may hold values from -1.75 to 1.75
- ln2_gain: bfloat16 [768], replicated, may hold values from 0.099609375 to 1.8984375
- ln2_bias: bfloat16 [768], replicated, may hold values from -1.75 to 1.75
- up_weight: bfloat16 [768, 3072], replicated, may hold values from -0.21875 to 0.21875
- up_bias: bfloat16 [3072], replicated, may hold values from -3 to 3
- down_weight: bfloat16 [3072, 768], replicated, may hold values from -0.109375 to 0.109375
- down_bias: bfloat16 [768], replicated, may hold values from -1.75 to 1.75
- segment_ids: int32 [16, 256], P('seq'), may hold values from 0 to 7, as said below
- block_output_gradient: bfloat16 [16, 256, 768], P('seq', 'blk'), may hold values from -6 to 6
Outputs:
- block_out: bfloat16 [16, 256, 768], P('seq', 'blk')
- in_grad: bfloat16 [16, 256, 768], P('seq', 'blk')
- grad_ln1_gain: float32 [768], P('seq')
- grad_ln1_bias: float32 [768], P('seq')
- grad_w_qkv: float32 [768, 2304], P('seq')
- grad_bias_qv: float32 [1536], P('seq')
- grad_w_out: float32 [768, 768], P('seq')
- grad_bias_out: float32 [768], P('seq')
- grad_ln2_gain: float32 [768], P('seq')
- grad_ln2_bias: float32 [768], P('seq')
- grad_w_up: float32 [768, 3072], P('seq')
- grad_bias_up: float32 [3072], P('seq')
- grad_w_down: float32 [3072, 768], P('seq')
- grad_bias_down: float32 [768], P('seq')
Inputs may be any that keep to these rules, and one draw needn't show every extreme that they name: `segment_ids`: each sequence's crop numbers start at 0 at its first patch and never fall; a patch attends to the patches of its own crop in its own sequence. Among each index of seq's 2 sequences, one has a crop that runs from patch 3 * (8) to patch 256 - 256 // 8 - 1.
All inputs are finite; a program needn't handle non-finite values.
Results may differ from a plain program's by a relative error of at most 0.015.
Values may be sent and summed in bfloat16 or wider, within the bound.
No kernel may reach another device: no remote copies, remote signals or barrier semaphores. Data moves between devices by JAX's collectives and lax.ppermute only.
A program may use at most 128 MiB of HBM per device.

v0:
```python
import math

import jax
import jax.numpy as jnp
from jax import lax
from jax.sharding import PartitionSpec as P

HEADS = 12


epsilon = 1e-06


def normalize(values, gain_vec, shift_vec):
    row_mean = jnp.mean(values, axis=-1, keepdims=True)
    centered = values - row_mean
    row_var = jnp.mean(centered * centered, axis=-1, keepdims=True)
    return centered * lax.rsqrt(row_var + epsilon) * gain_vec + shift_vec


def on_device(
    tokens,
    ln1_gain,
    ln1_bias,
    query_key_value_weight,
    bias_qv,
    output_weight,
    output_bias,
    ln2_gain,
    ln2_bias,
    up_weight,
    up_bias,
    down_weight,
    down_bias,
    segment_ids,
    block_output_gradient,
):
    seq_count, span_rows, model_width = tokens.shape
    seq_length = segment_ids.shape[1]
    head_count = HEADS
    head_size = model_width // head_count
    score_scale = 1.0 / math.sqrt(head_size)
    single_float = jnp.float32
    bf16 = jnp.bfloat16
    inputs = tokens.astype(single_float)
    first_float, norm1_pull = jax.vjp(
        normalize, inputs, ln1_gain.astype(single_float), ln1_bias.astype(single_float)
    )
    first_normed_input = first_float.astype(bf16)
    projected_output = jnp.einsum(
        "gft,tx->gfx",
        first_normed_input,
        query_key_value_weight,
        preferred_element_type=single_float,
    )
    bias_float = bias_qv.astype(single_float)
    queries = (projected_output[..., :model_width] + bias_float[:model_width]).astype(bf16)
    keys_local = projected_output[..., model_width : 2 * model_width].astype(bf16)
    values_local = (projected_output[..., 2 * model_width :] + bias_float[model_width:]).astype(
        bf16
    )
    key_all, value_all = (
        lax.all_gather(keys_local, "blk", axis=1, tiled=True),
        lax.all_gather(values_local, "blk", axis=1, tiled=True),
    )
    row_start = lax.axis_index("blk") * span_rows
    own_ids = lax.dynamic_slice_in_dim(segment_ids, row_start, span_rows, 1)
    same_crop = (own_ids[:, :, None] == segment_ids[:, None, :])[:, None]
    query_heads = queries.reshape(seq_count, span_rows, head_count, head_size)
    full_shape = (seq_count, seq_length, head_count, head_size)
    own_shape = (seq_count, span_rows, head_count, head_size)

    def scored(keys_all):
        raw_scores = jnp.einsum(
            "sqhe,skhe->shqk",
            query_heads,
            keys_all.reshape(full_shape),
            preferred_element_type=single_float,
        )
        return jnp.where(same_crop, raw_scores * score_scale, -1000000000.0)

    scores = scored(key_all)
    row_max = jnp.max(scores, axis=-1, keepdims=True)
    row_total = jnp.sum(jnp.exp(scores - row_max), axis=-1, keepdims=True)
    log_total = row_max + jnp.log(row_total)
    probs = jnp.exp(scores - log_total).astype(bf16)
    attended_values = jnp.einsum(
        "shqk,skhe->sqhe", probs, value_all.reshape(full_shape), preferred_element_type=single_float
    )
    attended_values = attended_values.reshape(seq_count, span_rows, model_width).astype(bf16)
    hidden_state = inputs + (
        jnp.einsum(
            "gft,tx->gfx", attended_values, output_weight, preferred_element_type=single_float
        )
        + output_bias.astype(single_float)
    )
    second_float, norm2_pull = jax.vjp(
        normalize, hidden_state, ln2_gain.astype(single_float), ln2_bias.astype(single_float)
    )
    second_normed_input = second_float.astype(bf16)
    up_projection = jnp.einsum(
        "bpm,mv->bpv", second_normed_input, up_weight, preferred_element_type=single_float
    ) + up_bias.astype(single_float)
    active_float, gelu_pull = jax.vjp(jax.nn.gelu, up_projection)
    active_mask = active_float.astype(bf16)
    block_out = (
        hidden_state
        + (
            jnp.einsum("nuo,ow->nuw", active_mask, down_weight, preferred_element_type=single_float)
            + down_bias.astype(single_float)
        )
    ).astype(bf16)
    grad_float = block_output_gradient.astype(single_float)
    down_gradient = jnp.einsum(
        "mjw,mjr->wr", active_mask, block_output_gradient, preferred_element_type=single_float
    )
    grad_bias_down = jnp.sum(grad_float, axis=(0, 1))
    (grad_up_in,) = gelu_pull(
        jnp.einsum(
            "hec,nc->hen", block_output_gradient, down_weight, preferred_element_type=single_float
        )
    )
    up_reduced = grad_up_in.astype(bf16)
    up_gradient = jnp.einsum(
        "yxe,yxh->eh", second_normed_input, up_reduced, preferred_element_type=single_float
    )
    grad_bias_up = jnp.sum(up_reduced.astype(single_float), axis=(0, 1))
    second_gradient = jnp.einsum(
        "vhm,bm->vhb", up_reduced, up_weight, preferred_element_type=single_float
    )
    hidden_part, grad_gain2, grad_shift2 = norm2_pull(second_gradient)
    grad_hidden = grad_float + hidden_part
    hidden_reduced = grad_hidden.astype(bf16)
    output_gradient = jnp.einsum(
        "uiy,uig->yg", attended_values, hidden_reduced, preferred_element_type=single_float
    )
    grad_bias_out = jnp.sum(hidden_reduced.astype(single_float), axis=(0, 1))
    attention_gradient_flat = jnp.einsum(
        "qfb,mb->qfm", hidden_reduced, output_weight, preferred_element_type=single_float
    ).astype(bf16)
    grad_att = attention_gradient_flat.reshape(own_shape)
    key_back, value_back = (
        lax.all_gather(keys_local, "blk", axis=1, tiled=True),
        lax.all_gather(values_local, "blk", axis=1, tiled=True),
    )
    scores_back = scored(key_back)
    probs_float = jnp.exp(scores_back - log_total)
    value_heads = value_back.reshape(full_shape)
    key_heads = key_back.reshape(full_shape)
    grad_probs = jnp.einsum(
        "sqhe,skhe->shqk", grad_att, value_heads, preferred_element_type=single_float
    )
    row_delta = jnp.sum(probs_float * grad_probs, axis=-1, keepdims=True)
    grad_scores = (probs_float * (grad_probs - row_delta)).astype(bf16)
    grad_query = (
        jnp.einsum("shqk,skhe->sqhe", grad_scores, key_heads, preferred_element_type=single_float)
        * score_scale
    )
    grad_query = grad_query.reshape(seq_count, span_rows, model_width).astype(bf16)
    probs_low = probs_float.astype(bf16)
    value_part = jnp.einsum(
        "shqk,sqhe->skhe", probs_low, grad_att, preferred_element_type=single_float
    )
    key_part = (
        jnp.einsum("shqk,sqhe->skhe", grad_scores, query_heads, preferred_element_type=single_float)
        * score_scale
    )
    key_part = key_part.reshape(seq_count, seq_length, model_width)
    value_part = value_part.reshape(seq_count, seq_length, model_width)
    grad_key, grad_value = (
        lax.psum_scatter(
            key_part.astype(jnp.bfloat16), "blk", scatter_dimension=1, tiled=True
        ).astype(jnp.float32),
        lax.psum_scatter(
            value_part.astype(jnp.bfloat16), "blk", scatter_dimension=1, tiled=True
        ).astype(jnp.float32),
    )
    grad_key = grad_key.astype(bf16)
    grad_value = grad_value.astype(bf16)
    projected_gradient = jnp.concatenate([grad_query, grad_key, grad_value], axis=-1)
    query_key_value_gradient = jnp.einsum(
        "uiy,uig->yg", first_normed_input, projected_gradient, preferred_element_type=single_float
    )
    grad_bias_qv = jnp.concatenate(
        [
            jnp.sum(grad_query.astype(single_float), axis=(0, 1)),
            jnp.sum(grad_value.astype(single_float), axis=(0, 1)),
        ]
    )
    first_gradient = jnp.einsum(
        "qfb,mb->qfm",
        projected_gradient,
        query_key_value_weight,
        preferred_element_type=single_float,
    )
    input_part, grad_gain1, grad_shift1 = norm1_pull(first_gradient)
    in_grad = (grad_hidden + input_part).astype(bf16)
    row_sums = (
        lax.psum_scatter(grad_gain1, "seq", scatter_dimension=0, tiled=True),
        lax.psum_scatter(grad_shift1, "seq", scatter_dimension=0, tiled=True),
        lax.psum_scatter(query_key_value_gradient, "seq", scatter_dimension=0, tiled=True),
        lax.psum_scatter(grad_bias_qv, "seq", scatter_dimension=0, tiled=True),
        lax.psum_scatter(output_gradient, "seq", scatter_dimension=0, tiled=True),
        lax.psum_scatter(grad_bias_out, "seq", scatter_dimension=0, tiled=True),
        lax.psum_scatter(grad_gain2, "seq", scatter_dimension=0, tiled=True),
        lax.psum_scatter(grad_shift2, "seq", scatter_dimension=0, tiled=True),
        lax.psum_scatter(up_gradient, "seq", scatter_dimension=0, tiled=True),
        lax.psum_scatter(grad_bias_up, "seq", scatter_dimension=0, tiled=True),
        lax.psum_scatter(down_gradient, "seq", scatter_dimension=0, tiled=True),
        lax.psum_scatter(grad_bias_down, "seq", scatter_dimension=0, tiled=True),
    )
    (
        gain1_part,
        shift1_part,
        qkv_part,
        bias_qv_part,
        out_part,
        bias_out_part,
        gain2_part,
        shift2_part,
        up_part,
        bias_up_part,
        down_part,
        bias_down_part,
    ) = row_sums
    summed = (
        lax.psum(gain1_part.astype(jnp.bfloat16), "blk").astype(jnp.float32),
        lax.psum(shift1_part.astype(jnp.bfloat16), "blk").astype(jnp.float32),
        lax.psum(qkv_part.astype(jnp.bfloat16), "blk").astype(jnp.float32),
        lax.psum(bias_qv_part.astype(jnp.bfloat16), "blk").astype(jnp.float32),
        lax.psum(out_part.astype(jnp.bfloat16), "blk").astype(jnp.float32),
        lax.psum(bias_out_part.astype(jnp.bfloat16), "blk").astype(jnp.float32),
        lax.psum(gain2_part.astype(jnp.bfloat16), "blk").astype(jnp.float32),
        lax.psum(shift2_part.astype(jnp.bfloat16), "blk").astype(jnp.float32),
        lax.psum(up_part.astype(jnp.bfloat16), "blk").astype(jnp.float32),
        lax.psum(bias_up_part.astype(jnp.bfloat16), "blk").astype(jnp.float32),
        lax.psum(down_part.astype(jnp.bfloat16), "blk").astype(jnp.float32),
        lax.psum(bias_down_part.astype(jnp.bfloat16), "blk").astype(jnp.float32),
    )
    return (
        block_out,
        in_grad,
        summed[0],
        summed[1],
        summed[2],
        summed[3],
        summed[4],
        summed[5],
        summed[6],
        summed[7],
        summed[8],
        summed[9],
        summed[10],
        summed[11],
    )


def solution(mesh):
    return jax.shard_map(
        on_device,
        mesh=mesh,
        in_specs=(
            P("seq", "blk", None),
            P(),
            P(),
            P(),
            P(),
            P(),
            P(),
            P(),
            P(),
            P(),
            P(),
            P(),
            P(),
            P("seq", None),
            P("seq", "blk", None),
        ),
        out_specs=(
            P("seq", "blk", None),
            P("seq", "blk", None),
            P("seq"),
            P("seq"),
            P("seq", None),
            P("seq"),
            P("seq", None),
            P("seq"),
            P("seq"),
            P("seq"),
            P("seq", None),
            P("seq"),
            P("seq", None),
            P("seq"),
        ),
        check_vma=False,
    )
```

profile of v0, /device:TPU:0, one launch (start us, length us, event | category | flops | bytes accessed | tf_op | source)
XLA Modules:
  0.0 738.7 jit_solution(17316226688732611584)
XLA Ops:
  7.2 1.4 convert_element_type.207
  13.6 1.6 fusion.13
  16.6 10.5 %all_gather.8 = bf16[2,256,768]{2,1,0:T(8,128)(2,1)} all-gather(bf16[2,64,768]{2,1,0:T(8,128)(2,1)S(1)} %get-tuple-element.46), channel_id=1, replica_groups=mesh['seq'=8,'blk'=4] {'blk'}, dimensions={1}, use_global_device_ids=true | all-gather | bytes 983040 | tf_op jit(solution)/shard_map/all_gather | solution.py:64
  27.1 2.3 copy.52
  29.4 1.9 copy.65
  31.3 10.3 %all_gather.9 = bf16[2,256,768]{2,1,0:T(8,128)(2,1)} all-gather(bf16[2,64,768]{2,1,0:T(8,128)(2,1)} %slice.33), channel_id=1, replica_groups=mesh['seq'=8,'blk'=4] {'blk'}, dimensions={1}, use_global_device_ids=true | all-gather | bytes 983040 | tf_op jit(solution)/shard_map/all_gather | solution.py:63
  41.6 2.3 copy.53
  44.1 1.8 fusion.67
  48.6 3.7 fusion.8
  52.4 2.6 convert_reduce_fusion
  55.0 2.4 multiply_reduce_fusion.1
  61.1 1.9 copy.66
  62.9 2.6 multiply_reduce_fusion
  67.0 1.2 multiply_convert_fusion
  68.2 2.3 copy.59
  70.6 2.8 convolution_convert_fusion
  73.4 2.3 copy.61
  75.7 3.1 convolution_bitcast_fusion.3
  79.1 2.4 convert_reduce_fusion.1
  82.5 2.1 convert_element_type.222
  84.6 1.6 constant_dynamic-update-slice_fusion.2
  86.2 8.4 %reduce-scatter.7.cloned.1.call-done = bf16[2,64,768]{2,1,0:T(8,128)(2,1)} async-done(((bf16[2,256,768]{2,1,0:T(8,128)(2,1)}), bf16[2,64,768]{2,1,0:T(8,128)(2,1)}) %reduce-scatter.7.cloned.1.call-update) | async-done | bytes 196624 | tf_op jit(solution)/shard_map/reduce_scatter | solution.py:171
  94.6 1.6 constant_dynamic-update-slice_fusion.1
  96.2 24.4 %reduce-scatter.9.cloned.1.call-done = bf16[2,64,768]{2,1,0:T(8,128)(2,1)} async-done(((bf16[2,256,768]{2,1,0:T(8,128)(2,1)}), bf16[2,64,768]{2,1,0:T(8,128)(2,1)}) %reduce-scatter.9.cloned.1.call-update) | async-done | bytes 196624 | tf_op jit(solution)/shard_map/reduce_scatter | solution.py:174
  120.6 1.6 constant_dynamic-update-slice_fusion
  122.2 5.3 convolution_bitcast_fusion.2
  128.2 6.4 convolution_bitcast_fusion.1
  134.7 6.6 convolution_bitcast_fusion
  143.2 1.2 dynamic-slice
  146.5 4.8 fusion.39
  151.9 2.6 fusion.63
  154.5 39.0 %reduce-scatter.13.cloned.1.call-done = f32[96,768]{1,0:T(8,128)} async-done(((f32[768,768]{1,0:T(8,128)}), f32[96,768]{1,0:T(8,128)}) %reduce-scatter.13.cloned.1.call-update) | async-done | bytes 294928 | tf_op jit(solution)/shard_map/reduce_scatter | solution.py:203
  193.5 1.6 convert_element_type.240
  195.2 130.0 %reduce-scatter.11.cloned.1.call-done = f32[96,2304]{1,0:T(8,128)} async-done(((f32[768,2304]{1,0:T(8,128)}), f32[96,2304]{1,0:T(8,128)}) %reduce-scatter.11.cloned.1.call-update) | async-done | bytes 884752 | tf_op jit(solution)/shard_map/reduce_scatter | solution.py:201
  325.2 2.0 convert_element_type.234
  327.1 164.4 %reduce-scatter.15.cloned.1.call-done = f32[96,3072]{1,0:T(8,128)} async-done(((f32[768,3072]{1,0:T(8,128)}), f32[96,3072]{1,0:T(8,128)}) %reduce-scatter.15.cloned.1.call-update) | async-done | bytes 1179664 | tf_op jit(solution)/shard_map/reduce_scatter | solution.py:207
  491.6 2.2 convert_element_type.249
  493.7 164.1 %reduce-scatter.17.cloned.1.call-done = f32[384,768]{1,0:T(8,128)} async-done(((f32[3072,768]{1,0:T(8,128)}), f32[384,768]{1,0:T(8,128)}) %reduce-scatter.17.cloned.1.call-update) | async-done | bytes 1179664 | tf_op jit(solution)/shard_map/reduce_scatter | solution.py:209
  657.8 2.1 convert_element_type.254
  660.0 1.3 pad_maximum_fusion
  662.0 1.9 fusion.50
  663.9 2.8 convert_reduce_fusion.3
  666.7 36.8 %all-reduce.8 = (bf16[768]{0:T(1024)(128)(2,1)}, bf16[768]{0:T(1024)(128)(2,1)}, bf16[1536]{0:T(1024)(128)(2,1)S(1)}, bf16[768]{0:T(1024)(128)(2,1)}, bf16[768]{...) all-reduce(f32[768]{0:T(1024)} %get-tuple-element.16, ...), channel_id=4, replica_groups=mesh['seq'=8,'blk'=4] {'seq'}, use_global_device_ids=true, to_apply=%region_14.15.clone | all-reduce | flops 9216 | bytes 55296
  705.0 1.3 dynamic-slice.29
  707.5 1.3 dynamic-slice.27
  710.7 6.5 all-reduce.9
  725.9 2.1 convert_element_type.235
  728.0 1.6 convert_element_type.241
  (149 shorter events, 35.0 us)
Async XLA Ops:
  7.2 6.4 copy-start
  7.2 87.4 %reduce-scatter.7.cloned.1.call-start = ((), (), s32[]{:S(2)}) async-start(), calls=%async_computation.6 | async-start | bytes 983040 | tf_op jit(solution)/shard_map/reduce_scatter | solution.py:171
  11.1 4.1 copy-start.24
  12.8 2.4 copy-start.27
  29.4 14.5 %copy-start.35 = (s32[2,256]{1,0:T(2,128)S(1)}, s32[2,256]{1,0:T(2,128)}, u32[]{:S(2)}) copy-start(s32[2,256]{1,0:T(2,128)} %param.28) | copy-start | bytes 6148
  44.1 2.5 copy-start.34
  44.1 2.5 copy-start.36
  44.1 2.5 copy-start.37
  44.1 2.5 copy-start.7
  46.0 1.2 copy-start.1
  46.5 0.9 copy-start.4
  46.5 1.4 copy-start.9
  46.5 1.4 copy-start.30
  46.6 1.8 copy-start.20
  47.1 1.5 copy-start.12
  47.9 4.4 copy-start.39
  48.4 9.0 %copy-start.3 = (f32[2,64,768]{2,1,0:T(8,128)}, f32[2,64,768]{2,1,0:T(8,128)S(1)}, u32[]{:S(2)}) copy-start(f32[2,64,768]{2,1,0:T(8,128)S(1)} %get-tuple-element.54) | copy-start | bytes 1179652
  48.4 9.0 %copy-start.22 = (f32[2,64]{1,0:T(2,128)}, f32[2,64]{1,0:T(2,128)S(1)}, u32[]{:S(2)}) copy-start(f32[2,64]{1,0:T(2,128)S(1)} %broadcast_multiply_fusion) | copy-start | bytes 1540
  48.6 8.8 %copy-start.26 = (f32[2,64]{1,0:T(2,128)}, f32[2,64]{1,0:T(2,128)S(1)}, u32[]{:S(2)}) copy-start(f32[2,64]{1,0:T(2,128)S(1)} %fusion.62) | copy-start | bytes 1540
  48.6 3.7 copy-start.16
  48.6 6.4 slice-start
  52.4 2.6 copy-start.6
  52.4 2.6 slice-start.1
  55.0 2.4 copy-start.14
  57.7 0.8 copy-start.10
  57.7 1.5 copy-start.32
  59.2 0.7 copy-start.15
  62.9 2.6 copy-start.2
  62.9 2.7 copy-start.21
  65.6 1.4 copy-start.11
  66.1 0.9 copy-start.8
  70.5 50.1 %reduce-scatter.9.cloned.1.call-start = ((), (), s32[]{:S(2)}) async-start(), calls=%async_computation.7 | async-start | bytes 983040 | tf_op jit(solution)/shard_map/reduce_scatter | solution.py:174
  75.7 117.8 %reduce-scatter.13.cloned.1.call-start = ((), (), s32[]{:S(2)}) async-start(), calls=%async_computation.9 | async-start | bytes 2654208 | tf_op jit(solution)/shard_map/reduce_scatter | solution.py:203
  78.8 246.3 %reduce-scatter.11.cloned.1.call-start = ((), (), s32[]{:S(2)}) async-start(), calls=%async_computation.8 | async-start | bytes 7962624 | tf_op jit(solution)/shard_map/reduce_scatter | solution.py:201
  127.5 0.7 copy-start.23
  127.6 364.0 %reduce-scatter.15.cloned.1.call-start = ((), (), s32[]{:S(2)}) async-start(), calls=%async_computation.10 | async-start | bytes 10616832 | tf_op jit(solution)/shard_map/reduce_scatter | solution.py:207
  134.6 523.2 %reduce-scatter.17.cloned.1.call-start = ((), (), s32[]{:S(2)}) async-start(), calls=%async_computation.11 | async-start | bytes 10616832 | tf_op jit(solution)/shard_map/reduce_scatter | solution.py:209
  141.3 0.7 copy-start.38
  141.3 1.3 copy-start.29
  141.3 584.6 %all-reduce.13.cloned.1.call-start = ((), (), s32[]{:S(2)}) async-start(), calls=%async_computation.12 | async-start | bytes 3538944 | tf_op jit(solution)/shard_map/psum | solution.py:229
  146.4 4.8 copy-start.17
  146.4 5.4 copy-start.5
  146.4 5.4 copy-start.13
  146.4 5.4 copy-start.25
  493.7 168.3 %copy-start.28 = (f32[2,64]{1,0:T(2,128)S(1)}, f32[2,64]{1,0:T(2,128)}, u32[]{:S(2)}) copy-start(f32[2,64]{1,0:T(2,128)} %copy-done.27) | copy-start | bytes 1540
  660.0 6.7 copy-start.31
  725.9 3.7 copy-start.19
  725.9 4.8 copy-start.18
  (1 other events, 0.6 us)
Sparse Core Ops, SparseCore 0:
  70.6 23.9 reduce-scatter.6
  97.3 23.2 reduce-scatter.8
  124.1 69.3 reduce-scatter.12
  197.1 128.0 reduce-scatter.10
  329.0 162.4 reduce-scatter.14
  495.4 162.3 reduce-scatter.16
  661.8 45.7 all-reduce.12
where the time goes:
time: 740 us; the launch traced here: 739 us
  waiting for transfers between devices  531 us (72%)
  blocking collectives  64.1 us (9%)
  matrix products  52.1 us (7%)
  other arithmetic  38.5 us (5%)
  local copies, waits for them, and re-layouts  36.4 us (5%)
  between operations  16.6 us (2%)
    reduce_scatter x1, waiting for transfers between devices, on_device(): lax.psum_scatter(up_gradient, 'seq', scatter_dimension=0, tiled=True)  164 us
    reduce_scatter x1, waiting for transfers between devices, on_device(): lax.psum_scatter(down_gradient, 'seq', scatter_dimension=0, tiled=True)  164 us
    reduce_scatter x1, waiting for transfers between devices, on_device(): lax.psum_scatter(query_key_value_gradient, 'seq', scatter_dimension=0, ti...  130 us
    reduce_scatter x1, waiting for transfers between devices, on_device(): lax.psum_scatter(output_gradient, 'seq', scatter_dimension=0, tiled=True)  39 us
    unnamed x1, blocking collectives  36.8 us
    reduce_scatter x1, waiting for transfers between devices, on_device(): lax.psum_scatter(value_part.astype(jnp.bfloat16), 'blk', scatter_dimensio...  24.4 us
    unnamed x95, local copies, waits for them, and re-layouts  16.6 us
  transfers between devices with their start and end apart: 7, of which 6 were waited for; matrix products, arithmetic and copies ran while one was open for 10% of the time, Pallas kernels for 0%

commit v1 on v0

v1 whole, which is shorter than its diff:
```python
import jax
import jax.numpy as jnp
from jax import lax
from jax.experimental import pallas as pl
from jax.experimental.pallas import tpu as pltpu
from jax.sharding import PartitionSpec as P

HEADS = 12
EPS = 1e-06
SLOTS = 8
F32 = jnp.float32
BF16 = jnp.bfloat16
GELU_C = 0.7978845608028654
GELU_A = 0.044715
PARAMS = pltpu.CompilerParams(vmem_limit_bytes=56 * 1024 * 1024)
GRID_PARAMS = pltpu.CompilerParams(
    vmem_limit_bytes=56 * 1024 * 1024, dimension_semantics=("arbitrary",)
)


def nn(a, b):
    return lax.dot_general(a, b, (((1,), (0,)), ((), ())), preferred_element_type=F32)


def nt(a, b):
    return lax.dot_general(a, b, (((1,), (1,)), ((), ())), preferred_element_type=F32)


def tn(a, b):
    return lax.dot_general(a, b, (((0,), (0,)), ((), ())), preferred_element_type=F32)


def standardize(x):
    centered = x - jnp.mean(x, axis=-1, keepdims=True)
    rstd = lax.rsqrt(jnp.mean(centered * centered, axis=-1, keepdims=True) + EPS)
    return centered * rstd, rstd


def norm_back(xhat, rstd, g):
    return rstd * (
        g
        - jnp.mean(g, axis=-1, keepdims=True)
        - xhat * jnp.mean(g * xhat, axis=-1, keepdims=True)
    )


def half_masks():
    lane = lax.broadcasted_iota(jnp.int32, (1, 128), 1)
    low = jnp.where(lane < 64, 1.0, 0.0)
    return low.astype(BF16), (1.0 - low).astype(BF16)


def crop_mask(seg_row):
    wide = jnp.broadcast_to(seg_row, (256, 256))
    return jnp.where(wide == wide.T, 1.0, 0.0)


def softmax_rows(scores, same):
    scores = jnp.where(same > 0.0, scores, -1e9)
    e = jnp.exp(scores - jnp.max(scores, axis=-1, keepdims=True))
    return e * (1.0 / jnp.sum(e, axis=-1, keepdims=True))


def forward_kernel(
    seg, t0, t1, t2, t3, pv, wqkv_hbm, wout_hbm,
    first_o, q_o, k_o, v_o, att_o, hid_o, sec_o,
    wqkv, wout, same, sem,
):
    load_qkv = pltpu.make_async_copy(wqkv_hbm, wqkv, sem.at[0])
    load_out = pltpu.make_async_copy(wout_hbm, wout, sem.at[1])
    load_qkv.start()
    load_out.start()
    for s in range(2):
        for p, t in enumerate((t0, t1, t2, t3)):
            xhat, _ = standardize(t[s].astype(F32))
            first_o[pl.ds(s * 256 + p * 64, 64), :] = (xhat * pv[0:1, :] + pv[1:2, :]).astype(BF16)
        same[s] = crop_mask(seg[s : s + 1, :])
    load_qkv.wait()
    for half in range(2):
        cols = pl.ds(half * 384, 384)
        q_o[:, cols] = (
            nn(first_o[...], wqkv[:, half * 384 : half * 384 + 384]) + pv[2:3, cols]
        ).astype(BF16) * BF16(0.125)
        k_o[:, cols] = nn(
            first_o[...], wqkv[:, 768 + half * 384 : 768 + half * 384 + 384]
        ).astype(BF16)
        v_o[:, cols] = (
            nn(first_o[...], wqkv[:, 1536 + half * 384 : 1536 + half * 384 + 384]) + pv[3:4, cols]
        ).astype(BF16)
    low, high = half_masks()

    def one_sequence(s, _):
        rows = pl.ds(pl.multiple_of(s * 256, 256), 256)
        for j in range(HEADS // 2):
            cols = pl.ds(j * 128, 128)
            q, k, v = q_o[rows, cols], k_o[rows, cols], v_o[rows, cols]
            out = None
            for keep in (low, high):
                probs = softmax_rows(nt(q * keep, k), same[s]).astype(BF16)
                part = nn(probs, v * keep)
                out = part if out is None else out + part
            att_o[rows, cols] = out.astype(BF16)
        return 0

    lax.fori_loop(0, 2, one_sequence, 0)
    load_out.wait()
    for s in range(2):
        for p, t in enumerate((t0, t1, t2, t3)):
            rows = pl.ds(s * 256 + p * 64, 64)
            hid = t[s].astype(F32) + (nn(att_o[rows, :], wout[...]) + pv[4:5, :])
            hid_o[rows, :] = hid
            xhat, _ = standardize(hid)
            sec_o[rows, :] = (xhat * pv[5:6, :] + pv[6:7, :]).astype(BF16)


def forward(seg, pieces, pv, wqkv, wout):
    bf = jax.ShapeDtypeStruct((512, 768), BF16)
    vmem = pl.BlockSpec(memory_space=pltpu.VMEM)
    hbm = pl.BlockSpec(memory_space=pl.ANY)
    return pl.pallas_call(
        forward_kernel,
        out_shape=(bf, bf, bf, bf, bf, jax.ShapeDtypeStruct((512, 768), F32), bf),
        in_specs=[vmem] * 6 + [hbm] * 2,
        out_specs=[vmem] * 7,
        scratch_shapes=[
            pltpu.VMEM((768, 2304), BF16),
            pltpu.VMEM((768, 768), BF16),
            pltpu.VMEM((2, 256, 256), F32),
            pltpu.SemaphoreType.DMA((2,)),
        ],
        compiler_params=PARAMS,
        name="forward",
    )(seg, *pieces, pv, wqkv, wout)


def own_rows(ref):
    return jnp.concatenate([ref[0:64, :], ref[256:320, :]], axis=0)


def gather_dy(pieces, dy):
    for s in range(2):
        for p, t in enumerate(pieces):
            dy[pl.ds(s * 256 + p * 64, 64), :] = t[s]


def pick_rows(transposed, chosen, core):
    for s in range(SLOTS):
        chosen[pl.ds(s * 48, 48), :] = transposed[pl.ds(pl.multiple_of(s * 96 + core * 48, 16), 48), :]


def put_slots(x_bit, product, keep, send, offset):
    tiles = product.shape[1] // 128
    for s in range(SLOTS):
        for t in range(tiles):
            value = product[s * 48 : s * 48 + 48, t * 128 : t * 128 + 128]
            rows = pl.ds(offset + t * 48, 48)

            @pl.when(x_bit == s % 2)
            def _():
                keep[s // 2, rows, :] = value

            @pl.when(x_bit != s % 2)
            def _():
                send[s // 2, rows, :] = value


def feed_step(ids, i, sec, dy, wup, bup, wdown, act_t, down_keep, down_send, act_own):
    y_bit, core, x_bit = ids[0], ids[1], ids[2]
    up = nn(sec[...], wup[...]) + bup[...]
    da = nt(dy[...], wdown[...])
    square = up * up
    tanh = jnp.tanh(GELU_C * up * (1.0 + GELU_A * square))
    cdf = 0.5 * (1.0 + tanh)
    act = (up * cdf).astype(BF16)
    slope = cdf + (0.5 * GELU_C) * up * (1.0 - tanh * tanh) * (1.0 + (3.0 * GELU_A) * square)
    dup = (da * slope).astype(BF16)
    act_t[...] = act.T
    dy_half = dy[:, pl.ds(pl.multiple_of(y_bit * 384, 128), 384)]
    mine = act_t[pl.ds(pl.multiple_of(core * 192, 64), 192), :]
    product = nn(mine, dy_half).astype(BF16)

    @pl.when(x_bit == lax.rem(i, 2))
    def _():
        for t in range(3):
            down_keep[0, pl.ds(t * 192, 192), :] = product[:, t * 128 : t * 128 + 128]

    @pl.when(x_bit != lax.rem(i, 2))
    def _():
        for t in range(3):
            down_send[0, pl.ds(t * 192, 192), :] = product[:, t * 128 : t * 128 + 128]

    act_own[0:64, :] = act[0:64, :]
    act_own[64:128, :] = act[256:320, :]
    bias = jnp.sum(dup[0:64, :].astype(F32), axis=0, keepdims=True) + jnp.sum(
        dup[256:320, :].astype(F32), axis=0, keepdims=True
    )
    return dup, bias


def feed_a_kernel(
    ids, sec, d0, d1, d2, d3, wup, bup, wdown,
    up_keep, up_send, down_keep, down_send, dsec, out_own, bias_o,
    dy, act_t, act_own, sec_t, chosen,
):
    i = pl.program_id(0)

    @pl.when(i == 0)
    def _():
        gather_dy((d0, d1, d2, d3), dy)
        sec_t[...] = sec[...].T
        pick_rows(sec_t, chosen, ids[1])
        dsec[...] = jnp.zeros_like(dsec)
        out_own[...] = jnp.zeros_like(out_own)

    dup, bias = feed_step(ids, i, sec, dy, wup, bup, wdown, act_t, down_keep, down_send, act_own)
    bias_o[...] = bias
    product = nn(chosen[...], dup).astype(BF16)
    put_slots(ids[2], product, up_keep, up_send, 0)
    dsec[...] += nt(dup, wup[...])
    out_own[...] += nn(act_own[...], wdown[...])


def feed_b_kernel(
    ids, sec, d0, d1, d2, d3, wup, bup, wdown, keep_in, send_in, dsec_in, own_in, hid, pv,
    down_keep, down_send, bias_o, dh_o, dhid_own, block_o, sums_o,
    dy, act_t, act_own, dsec, out_own,
):
    i = pl.program_id(0)

    @pl.when(i == 0)
    def _():
        gather_dy((d0, d1, d2, d3), dy)
        dsec[...] = dsec_in[...]
        out_own[...] = own_in[...]

    dup, bias = feed_step(ids, i, sec, dy, wup, bup, wdown, act_t, down_keep, down_send, act_own)
    bias_o[...] = bias
    dsec[...] += nt(dup, wup[...])
    out_own[...] += nn(act_own[...], wdown[...])

    @pl.when(i == 3)
    def _():
        for s in range(2):
            block_o[s] = (
                hid[pl.ds(s * 256, 64), :] + (out_own[pl.ds(s * 64, 64), :] + pv[7:8, :])
            ).astype(BF16)
        sums = [jnp.zeros((1, 768), F32)] * 4
        for s in range(2):
            for p in range(4):
                rows = pl.ds(s * 256 + p * 64, 64)
                xhat, rstd = standardize(hid[rows, :])
                dy_rows = dy[rows, :].astype(F32)
                grad = dsec[rows, :]
                dhid = dy_rows + norm_back(xhat, rstd, grad * pv[5:6, :])
                low = dhid.astype(BF16)
                dh_o[rows, :] = low
                if p == 0:
                    dhid_own[pl.ds(s * 64, 64), :] = dhid
                    parts = (grad * xhat, grad, low.astype(F32), dy_rows)
                    sums = [a + jnp.sum(b, axis=0, keepdims=True) for a, b in zip(sums, parts)]
        for r in range(4):
            sums_o[r : r + 1, :] = sums[r]
        sums_o[4:8, :] = jnp.zeros((4, 768), F32)


def whole_spec(shape):
    return pl.BlockSpec(shape, lambda i, ids: (0,) * len(shape))


def weight_specs(flip):
    def chunk(i, ids):
        y_bit = 1 - ids[0] if flip else ids[0]
        return y_bit * 4 + i

    return [
        pl.BlockSpec((768, 384), lambda i, ids: (0, chunk(i, ids))),
        pl.BlockSpec((1, 384), lambda i, ids: (0, chunk(i, ids))),
        pl.BlockSpec((384, 768), lambda i, ids: (chunk(i, ids), 0)),
    ]


def down_spec(flip):
    def place(i, ids):
        y_bit = 1 - ids[0] if flip else ids[0]
        return (y_bit * 2 + i // 2, 0, 0)

    return pl.BlockSpec((1, 576, 128), place)


def feed_a(ids, sec, dys, wup, bup, wdown):
    part = jax.ShapeDtypeStruct((4, 576, 128), BF16)
    slot_spec = pl.BlockSpec((4, 144, 128), lambda i, ids: (0, i, 0))
    return pl.pallas_call(
        feed_a_kernel,
        grid_spec=pltpu.PrefetchScalarGridSpec(
            num_scalar_prefetch=1,
            grid=(4,),
            in_specs=[whole_spec((512, 768))] + [whole_spec((2, 64, 768))] * 4 + weight_specs(False),
            out_specs=[
                slot_spec, slot_spec, down_spec(False), down_spec(False),
                whole_spec((512, 768)), whole_spec((128, 768)),
                pl.BlockSpec((1, 384), lambda i, ids: (0, i)),
            ],
            scratch_shapes=[
                pltpu.VMEM((512, 768), BF16),
                pltpu.VMEM((384, 512), BF16),
                pltpu.VMEM((128, 384), BF16),
                pltpu.VMEM((768, 512), BF16),
                pltpu.VMEM((384, 512), BF16),
            ],
        ),
        out_shape=(
            part, part, part, part,
            jax.ShapeDtypeStruct((512, 768), F32),
            jax.ShapeDtypeStruct((128, 768), F32),
            jax.ShapeDtypeStruct((1, 1536), F32),
        ),
        compiler_params=GRID_PARAMS,
        name="feed_a",
    )(ids, sec, *dys, wup, bup, wdown)


def feed_b(ids, sec, dys, wup, bup, wdown, keep_in, send_in, dsec_in, own_in, hid, pv):
    part = jax.ShapeDtypeStruct((4, 576, 128), BF16)
    anywhere = pl.BlockSpec(memory_space=pl.ANY)
    return pl.pallas_call(
        feed_b_kernel,
        grid_spec=pltpu.PrefetchScalarGridSpec(
            num_scalar_prefetch=1,
            grid=(4,),
            in_specs=[whole_spec((512, 768))]
            + [whole_spec((2, 64, 768))] * 4
            + weight_specs(True)
            + [
                anywhere, anywhere,
                whole_spec((512, 768)), whole_spec((128, 768)), whole_spec((512, 768)), whole_spec((8, 768)),
            ],
            out_specs=[
                down_spec(True), down_spec(True),
                pl.BlockSpec((1, 384), lambda i, ids: (0, i)),
                whole_spec((512, 768)), whole_spec((128, 768)), whole_spec((2, 64, 768)), whole_spec((8, 768)),
            ],
            scratch_shapes=[
                pltpu.VMEM((512, 768), BF16),
                pltpu.VMEM((384, 512), BF16),
                pltpu.VMEM((128, 384), BF16),
                pltpu.VMEM((512, 768), F32),
                pltpu.VMEM((128, 768), F32),
            ],
        ),
        out_shape=(
            part, part,
            jax.ShapeDtypeStruct((1, 1536), F32),
            jax.ShapeDtypeStruct((512, 768), BF16),
            jax.ShapeDtypeStruct((128, 768), F32),
            jax.ShapeDtypeStruct((2, 64, 768), BF16),
            jax.ShapeDtypeStruct((8, 768), F32),
        ),
        input_output_aliases={9: 0, 10: 1},
        compiler_params=GRID_PARAMS,
        name="feed_b",
    )(ids, sec, *dys, wup, bup, wdown, keep_in, send_in, dsec_in, own_in, hid, pv)


def attention_back_kernel(ids, seg, dh, wout, q_r, k_r, v_r, dproj_o, sums_o, same, datt):
    same[...] = crop_mask(seg[pl.ds(ids[1], 1), :])
    datt[...] = nt(dh[...], wout[...]).astype(BF16)
    low, high = half_masks()
    for j in range(HEADS // 4):
        cols = pl.ds(j * 128, 128)
        q, k, v, da = q_r[:, cols], k_r[:, cols], v_r[:, cols], datt[:, cols]
        dq = dk = dv = None
        for keep in (low, high):
            qh, kh, dah = q * keep, k * keep, da * keep
            probs = softmax_rows(nt(qh, k), same[...])
            dprobs = nt(dah, v)
            delta = jnp.sum(probs * dprobs, axis=-1, keepdims=True)
            ds = (probs * (dprobs - delta)).astype(BF16)
            parts = nn(ds, kh), tn(ds, qh), tn(probs.astype(BF16), dah)
            if dq is None:
                dq, dk, dv = parts
            else:
                dq, dk, dv = dq + parts[0], dk + parts[1], dv + parts[2]
        dq = (dq * 0.125).astype(BF16)
        dv = dv.astype(BF16)
        dproj_o[:, cols] = dq
        dproj_o[:, pl.ds(384 + j * 128, 128)] = dk.astype(BF16)
        dproj_o[:, pl.ds(768 + j * 128, 128)] = dv
        sums_o[0:1, cols] = jnp.sum(dq.astype(F32), axis=0, keepdims=True)
        sums_o[1:2, cols] = jnp.sum(dv.astype(F32), axis=0, keepdims=True)
    sums_o[2:8, :] = jnp.zeros((6, 384), F32)


def attention_back(ids, seg, dh, wout, q, k, v):
    mine = pl.BlockSpec((256, 384), lambda i, ids: (ids[1], ids[0]))
    return pl.pallas_call(
        attention_back_kernel,
        grid_spec=pltpu.PrefetchScalarGridSpec(
            num_scalar_prefetch=1,
            grid=(1,),
            in_specs=[
                whole_spec((2, 256)),
                pl.BlockSpec((256, 768), lambda i, ids: (ids[1], 0)),
                pl.BlockSpec((384, 768), lambda i, ids: (ids[0], 0)),
                mine, mine, mine,
            ],
            out_specs=[whole_spec((256, 1152)), whole_spec((8, 384))],
            scratch_shapes=[pltpu.VMEM((256, 256), F32), pltpu.VMEM((256, 384), BF16)],
        ),
        out_shape=(jax.ShapeDtypeStruct((256, 1152), BF16), jax.ShapeDtypeStruct((8, 384), F32)),
        compiler_params=GRID_PARAMS,
        name="attention_back",
    )(ids, seg, dh, wout, q, k, v)


def attention_weights_kernel(
    ids, own, other, first, att, dh, wq, wk, wv, t0, t2, vec,
    keep, send, dfirst_own, dfirst_send,
    dproj, turned, chosen, picked,
):
    core, x_bit = ids[1], ids[2]
    dproj[core] = own[...]
    for p in range(4):
        dproj[1 - core, pl.ds(p * 64, 64), :] = other[pl.ds((p ^ 1) * 64, 64), :]
    gain = jnp.zeros((1, 768), F32)
    shift = jnp.zeros((1, 768), F32)
    for s in range(2):
        for p, t in ((0, t0), (2, t2)):
            rows = dproj[s, pl.ds(p * 64, 64), :]
            part = nt(rows[:, 0:384], wq[...]) + nt(rows[:, 384:768], wk[...]) + nt(rows[:, 768:1152], wv[...])
            if p == 0:
                dfirst_own[s] = part
            else:
                dfirst_send[s] = part.astype(BF16)
            xhat, _ = standardize(t[s].astype(F32))
            gain += jnp.sum(part * xhat, axis=0, keepdims=True)
            shift += jnp.sum(part, axis=0, keepdims=True)
    turned[...] = first[...].T
    pick_rows(turned, chosen, core)
    product = nn(chosen[:, 0:256], dproj[0]) + nn(chosen[:, 256:512], dproj[1])
    put_slots(x_bit, product.astype(BF16), keep, send, 0)
    turned[...] = att[...].T
    pick_rows(turned, chosen, core)
    put_slots(x_bit, nn(chosen[...], dh[...]).astype(BF16), keep, send, 432)
    picked[...] = vec[...]
    for s in range(SLOTS):
        picked[s, 0:1, 0:96] = gain[:, s * 96 : s * 96 + 96]
        picked[s, 1:2, 0:96] = shift[:, s * 96 : s * 96 + 96]
    for s in range(SLOTS):
        value = picked[s].astype(BF16)

        @pl.when(x_bit == s % 2)
        def _():
            keep[s // 2, pl.ds(576, 16), :] = value

        @pl.when(x_bit != s % 2)
        def _():
            send[s // 2, pl.ds(576, 16), :] = value


def attention_weights(ids, own, other, first, att, dh, wqkv, t0, t2, vec):
    part = jax.ShapeDtypeStruct((4, 592, 128), BF16)
    heads = [pl.BlockSpec((768, 384), lambda i, ids, n=n: (0, 2 * n + ids[0])) for n in range(3)]
    return pl.pallas_call(
        attention_weights_kernel,
        grid_spec=pltpu.PrefetchScalarGridSpec(
            num_scalar_prefetch=1,
            grid=(1,),
            in_specs=[
                whole_spec((256, 1152)), whole_spec((256, 1152)),
                whole_spec((512, 768)), whole_spec((512, 768)),
                pl.BlockSpec((512, 384), lambda i, ids: (0, ids[0])),
                *heads,
                whole_spec((2, 64, 768)), whole_spec((2, 64, 768)),
                whole_spec((8, 16, 128)),
            ],
            out_specs=[
                whole_spec((4, 592, 128)), whole_spec((4, 592, 128)),
                whole_spec((2, 64, 768)), whole_spec((2, 64, 768)),
            ],
            scratch_shapes=[
                pltpu.VMEM((2, 256, 1152), BF16),
                pltpu.VMEM((768, 512), BF16),
                pltpu.VMEM((384, 512), BF16),
                pltpu.VMEM((8, 16, 128), F32),
            ],
        ),
        out_shape=(
            part, part,
            jax.ShapeDtypeStruct((2, 64, 768), F32),
            jax.ShapeDtypeStruct((2, 64, 768), BF16),
        ),
        compiler_params=GRID_PARAMS,
        name="attention_weights",
    )(ids, own, other, first, att, dh, wqkv, wqkv, wqkv, t0, t2, vec)


def input_grad_kernel(tokens, dfirst, received, dhid, pv, out):
    for s in range(2):
        xhat, rstd = standardize(tokens[s].astype(F32))
        grad = dfirst[s] + received[s].astype(F32)
        out[s] = (dhid[pl.ds(s * 64, 64), :] + norm_back(xhat, rstd, grad * pv[0:1, :])).astype(BF16)


def assemble_kernel(ids, *refs):
    ups, downs, atts = refs[0:4], refs[4:8], refs[8:12]
    up_o, down_o, out_o, qkv_o, vec_o = refs[12:]
    b = ids[3]
    total = jnp.zeros((16, 128), F32)
    for k in range(4):
        source = b ^ k
        y_bit, core = source // 2, lax.rem(source, 2)
        r48 = pl.ds(pl.multiple_of(core * 48, 16), 48)
        r192 = pl.ds(pl.multiple_of(core * 192, 64), 192)

        def cols(start, t):
            return pl.ds(pl.multiple_of(start + t * 128, 128), 128)

        for t in range(12):
            up_o[r48, cols(y_bit * 1536, t)] = ups[k][pl.ds(t * 48, 48), :].astype(F32)
        for t in range(3):
            down_o[r192, cols(y_bit * 384, t)] = downs[k][pl.ds(t * 192, 192), :].astype(F32)
            out_o[r48, cols(y_bit * 384, t)] = atts[k][pl.ds(432 + t * 48, 48), :].astype(F32)
        for t in range(9):
            qkv_o[r48, cols(y_bit * 384 + 768 * (t // 3), t % 3)] = atts[k][pl.ds(t * 48, 48), :].astype(F32)
        total += atts[k][pl.ds(576, 16), :].astype(F32)
    vec_o[...] = total


def assemble(ids, ups, downs, atts):
    vmem = pl.BlockSpec(memory_space=pltpu.VMEM)
    return pl.pallas_call(
        assemble_kernel,
        in_specs=[pl.BlockSpec(memory_space=pltpu.SMEM)] + [vmem] * 12,
        out_specs=[vmem] * 5,
        out_shape=(
            jax.ShapeDtypeStruct((96, 3072), F32),
            jax.ShapeDtypeStruct((384, 768), F32),
            jax.ShapeDtypeStruct((96, 768), F32),
            jax.ShapeDtypeStruct((96, 2304), F32),
            jax.ShapeDtypeStruct((16, 128), F32),
        ),
        compiler_params=PARAMS,
        name="assemble",
    )(ids, *ups, *downs, *atts)


def build(seq_size, blk_size):
    inner = seq_size // SLOTS

    def swap(x, axis, size, step):
        return lax.ppermute(x, axis, [(i, i ^ step) for i in range(size)])

    def core_swap(x):
        return swap(x, "blk", blk_size, 1)

    def y_swap(x):
        return swap(x, "blk", blk_size, 2)

    def seq_swap(x, step):
        return swap(x, "seq", seq_size, step * inner)

    def gather(x):
        across = y_swap(x)
        return x, core_swap(x), across, core_swap(across)

    def summed(keep, send, bits):
        got = seq_swap(send, 1)
        shape = keep.shape
        split = (2, 2) + shape[1:]
        both = keep.astype(F32).reshape(split), got.astype(F32).reshape(split)

        def take(a, i, axis):
            return lax.dynamic_index_in_dim(a, i, axis, keepdims=False)

        stay = sum(take(a, bits[1], 1) for a in both)
        leave = sum(take(a, 1 - bits[1], 1) for a in both).astype(BF16)
        got = seq_swap(leave, 2).astype(F32)
        leave = (take(stay, 1 - bits[2], 0) + take(got, 1 - bits[2], 0)).astype(BF16)
        stay = take(stay, bits[2], 0) + take(got, bits[2], 0)
        return (stay + seq_swap(leave, 4).astype(F32)).astype(BF16)

    def on_device(
        tokens, ln1_gain, ln1_bias, wqkv, bias_qv, wout, output_bias, ln2_gain, ln2_bias,
        wup, up_bias, wdown, down_bias, segment_ids, dy,
    ):
        b = lax.axis_index("blk")
        slot = lax.axis_index("seq") // inner
        bits = [(slot >> n) & 1 for n in range(3)]
        ids = jnp.stack([b // 2, b % 2, bits[0], b]).astype(jnp.int32)
        t_pieces = gather(tokens)
        d_pieces = gather(dy)
        pv = jnp.stack(
            [ln1_gain, ln1_bias, bias_qv[:768], bias_qv[768:], output_bias, ln2_gain, ln2_bias, down_bias]
        ).astype(F32)
        bup = up_bias.astype(F32).reshape(1, -1)
        seg = jnp.concatenate(
            [lax.dynamic_slice_in_dim(segment_ids, (b ^ p) * 64, 64, 1) for p in range(4)], axis=1
        )
        first, q, k, v, att, hid, sec = forward(seg, t_pieces, pv, wqkv, wout)
        up_keep, up_send, down_keep, down_send, dsec, own, bias_a = feed_a(
            ids, sec, d_pieces, wup, bup, wdown
        )
        up_sum = summed(up_keep, up_send, bits)
        down_keep, down_send, bias_b, dh, dhid_own, block_out, sums = feed_b(
            ids, sec, d_pieces, wup, bup, wdown, down_keep, down_send, dsec, own, hid, pv
        )
        down_sum = summed(down_keep, down_send, bits)
        dproj, head_sums = attention_back(ids, seg, dh, wout, q, k, v)
        dproj_other = core_swap(dproj)

        def rows(vector, per_slot):
            return vector.reshape(SLOTS, per_slot, 96)

        def placed(part, y_bit, size):
            return lax.dynamic_update_slice(jnp.zeros((2 * size,), F32), part, (y_bit * size,))

        qv = jnp.concatenate([placed(head_sums[0], b // 2, 384), placed(head_sums[1], b // 2, 384)])
        gelu_bias = jnp.where(
            b // 2 == 0,
            jnp.concatenate([bias_a[0], bias_b[0]]),
            jnp.concatenate([bias_b[0], bias_a[0]]),
        )
        vec = jnp.concatenate(
            [
                jnp.zeros((SLOTS, 2, 96), F32),
                rows(qv, 2), rows(sums[2], 1), rows(sums[0], 1), rows(sums[1], 1),
                rows(gelu_bias, 4), rows(sums[3], 1),
            ],
            axis=1,
        )
        vec = jnp.pad(vec, ((0, 0), (0, 4), (0, 32)))
        att_keep, att_send, dfirst_own, dfirst_send = attention_weights(
            ids, dproj, dproj_other, first, att, dh, wqkv, tokens, t_pieces[2], vec
        )
        att_sum = summed(att_keep, att_send, bits)
        dfirst_got = y_swap(dfirst_send)
        in_grad = pl.pallas_call(
            input_grad_kernel,
            out_shape=jax.ShapeDtypeStruct((2, 64, 768), BF16),
            compiler_params=PARAMS,
            name="input_grad",
        )(tokens, dfirst_own, dfirst_got, dhid_own, pv)
        up_o, down_o, out_o, qkv_o, vec_o = assemble(
            ids, gather(up_sum), gather(down_sum), gather(att_sum)
        )

        def flat(start, count):
            return vec_o[start : start + count, :96].reshape(-1)

        outs = [
            flat(0, 1), flat(1, 1), qkv_o, flat(2, 2), out_o, flat(4, 1), flat(5, 1), flat(6, 1),
            up_o, flat(7, 4), down_o, flat(11, 1),
        ]
        if inner > 1:
            groups = [list(range(g * inner, g * inner + inner)) for g in range(SLOTS)]
            outs = [
                lax.psum_scatter(o, "seq", scatter_dimension=0, axis_index_groups=groups, tiled=True)
                for o in outs
            ]
        return (block_out, in_grad, *outs)

    return on_device


def solution(mesh):
    data, vector, matrix = P("seq", "blk", None), P("seq"), P("seq", None)
    return jax.shard_map(
        build(mesh.shape["seq"], mesh.shape["blk"]),
        mesh=mesh,
        in_specs=(data,) + (P(),) * 12 + (matrix, data),
        out_specs=(
            data, data, vector, vector, matrix, vector, matrix, vector, vector, vector,
            matrix, vector, matrix, vector,
        ),
        check_vma=False,
    )
```

time: 740 us -> 152 us (0.21)
  waiting for transfers between devices: 531 us -> 39.9 us
  Pallas kernels: 0 us -> 64.1 us
  blocking collectives: 64.1 us -> 0 us
  matrix products: 52.1 us -> 0 us
  other arithmetic: 38.5 us -> 4.48 us
  starting transfers between devices: 0.47 us -> 24.1 us
  local copies, waits for them, and re-layouts: 36.4 us -> 17.8 us
  between operations: 16.6 us -> 1.15 us
    reduce_scatter x6 -> x0, waiting for transfers between devices: 530 us -> none  [the longest x1 164 us: on_device(): lax.psum_scatter(up_gradient, 'seq', scatter_dimension=0, tiled=True)]
    pallas_call x0 -> x7, Pallas kernels: none -> 64.1 us  [the longest x1 14.7 us: feed_a(): pl.pallas_call(feed_a_kernel, grid_spec=pltpu.PrefetchScalarGridSpec(num_...]
    dot_general x18 -> x0, matrix products: 52.1 us -> none  [the longest x1 6.62 us: on_device(): jnp.einsum('mjw,mjr->wr', active_mask, block_output_gradient, preferred_e...]
    ppermute x0 -> x26, waiting for transfers between devices: none -> 39.9 us  [swap(): return lax.ppermute(x, axis, [(i, i ^ step) for i in range(size)])]
    unnamed x1 -> x0, blocking collectives: 36.8 us -> none
    convert_element_type x25 -> x13, other arithmetic: 27.2 us -> 1.23 us  [the longest x1 0.6 us: on_device(): pv = jnp.stack([ln1_gain, ln1_bias, bias_qv[:768], bias_qv[768:], output_...]
    ppermute x0 -> x26, starting transfers between devices: none -> 24.1 us  [swap(): return lax.ppermute(x, axis, [(i, i ^ step) for i in range(size)])]
    all_gather x2 -> x0, blocking collectives: 20.8 us -> none  [the longest x1 10.5 us: on_device(): lax.all_gather(values_local, 'blk', axis=1, tiled=True)]
  transfers between devices with their start and end apart: 7 -> 26, of which waited for: 6 -> 7; matrix products, arithmetic and copies ran while one was open for 10% -> 9% of each run, Pallas kernels for 0% -> 17%
where the time goes in v1:
time: 152 us; the launch traced here: 151 us
  Pallas kernels  64.1 us (42%)
  waiting for transfers between devices  39.9 us (26%)
  starting transfers between devices  24.1 us (16%)
  local copies, waits for them, and re-layouts  17.8 us (12%)
  other arithmetic  4.48 us (3%)
    ppermute x26, waiting for transfers between devices, swap(): return lax.ppermute(x, axis, [(i, i ^ step) for i in range(size)])  39.9 us
    ppermute x26, starting transfers between devices, swap(): return lax.ppermute(x, axis, [(i, i ^ step) for i in range(size)])  24.1 us
    pallas_call x1, Pallas kernels, feed_a(): pl.pallas_call(feed_a_kernel, grid_spec=pltpu.PrefetchScalarGridSpec(num_...  14.7 us
    pallas_call x1, Pallas kernels, forward(): pl.pallas_call(forward_kernel, out_shape=(bf, bf, bf, bf, bf, jax.ShapeDt...  14.4 us
    pallas_call x1, Pallas kernels, feed_b(): pl.pallas_call(feed_b_kernel, grid_spec=pltpu.PrefetchScalarGridSpec(num_...  14.2 us
    pallas_call x1, Pallas kernels, attention_weights(): pl.pallas_call(attention_weights_kernel, grid_spec=pltpu.PrefetchScalarGr...  9.18 us
    pallas_call x1, Pallas kernels, attention_back(): pl.pallas_call(attention_back_kernel, grid_spec=pltpu.PrefetchScalarGridS...  5.61 us
    unnamed x56, local copies, waits for them, and re-layouts  5.26 us
  transfers between devices with their start and end apart: 26, of which 7 were waited for; matrix products, arithmetic and copies ran while one was open for 9% of the time, Pallas kernels for 17%

profile of v1, /device:TPU:0, one launch (start us, length us, event | category | flops | bytes accessed | tf_op | source)
XLA Modules:
  0.0 151.5 jit_solution(17641159245361382384)
XLA Ops:
  0.6 3.0 %collective-permute-start.1 = (bf16[2,64,768]{2,1,0:T(8,128)(2,1)}, bf16[2,64,768]{2,1,0:T(8,128)(2,1)S(1)}, u32[]{:S(2)}, u32[]{:S(2)}) collective-permute-start(bf16[2,64,768]{2,1,0:T(8,128)(2,1)} %tokens.1), channel_id=1, source_target_pairs={{0,2},{1,3},{2,0},{3,1},{4,6},{5,7},{6,4},{7,5},{8,10},{9,11},{10,... | collective-permute-start | bytes 589832 | tf_op jit(solution)/shard_map/ppermute | solution.py:552
  4.2 0.8 fusion.15
  5.0 0.7 stack.47
  5.7 0.7 stack.48
  6.3 0.7 stack.51
  7.0 0.7 stack.52
  7.7 0.7 stack.53
  8.4 0.7 stack.54
  9.7 1.3 reshape.151
  11.0 0.8 constant_dynamic-slice_fusion.3
  12.1 0.9 collective-permute-done.4.d2
  13.6 0.7 pad_add_fusion.seg
  14.3 0.7 copy-done.12
  14.9 0.7 copy-done.13
  15.6 14.4 %forward.1 = (bf16[512,768]{1,0:T(8,128)(2,1)}, bf16[512,768]{1,0:T(8,128)(2,1)}, bf16[512,768]{1,0:T(8,128)(2,1)}, bf16[512,768]{1,0:T(8,128)(2,1)}, bf16[512,7...) custom-call(s32[2,256]{1,0:T(2,128)} %pad_add_fusion.seg, bf16[2,64,768]{2,1,0:T(8,128)(2,1)} %tokens.1, ...), custom_call_target="tpu_custom_call" | custom-call | tf_op jit(solution)/shard_map/forward/pallas_call | solution.py:120
  30.1 0.6 copy-done.3
  30.8 14.7 %feed_a.1 = (bf16[4,576,128]{2,1,0:T(8,128)(2,1)}, bf16[4,576,128]{2,1,0:T(8,128)(2,1)}, bf16[4,576,128]{2,1,0:T(8,128)(2,1)}, bf16[4,576,128]{2,1,0:T(8,128)(2,...) custom-call(s32[4]{0:T(128)} %pad_add_fusion.1.ids, bf16[512,768]{1,0:T(8,128)(2,1)} %get-tuple-element.46.sec, ...), custom_call_target="tpu_custom_call" | custom-call | tf_op jit(solution)/shard_map/feed_a/pallas_call | solution.py:293
  45.6 14.2 %feed_b.1 = (bf16[4,576,128]{2,1,0:T(8,128)(2,1)}, bf16[4,576,128]{2,1,0:T(8,128)(2,1)}, f32[1,1536]{1,0:T(1,128)}, bf16[512,768]{1,0:T(8,128)(2,1)}, f32[128,76...) custom-call(s32[4]{0:T(128)} %pad_add_fusion.1.ids, ...), custom_call_target="tpu_custom_call", output_to_operand_aliasing={{0}: (9, {}), {1}: (10, {})} | custom-call | tf_op jit(solution)/shard_map/feed_b/pallas_call | solution.py:326
  59.8 5.6 %attention_back.1 = (bf16[256,1152]{1,0:T(8,128)(2,1)}, f32[8,384]{1,0:T(8,128)}) custom-call(s32[4]{0:T(128)} %pad_add_fusion.1.ids, s32[2,256]{1,0:T(2,128)} %pad_add_fusion.seg, bf16[512,768]{1,0:T(8,128)(2,1)} %get-tuple-element.53.dh, bf16[768,768]{1,0:T(8,128)(2,1)} %wout.1, bf16[512,768]{1,0:T(8,128)(2,1)} %get-tuple-element.54.q_r, ...), custom_call_target="tpu_custom_call" | custom-call | tf_op jit(solution)/shard_map/attention_back/pallas_call | solution.py:396
  65.9 1.7 %collective-permute-start.14 = (bf16[4,576,128]{2,1,0:T(8,128)(2,1)S(1)}, bf16[4,576,128]{2,1,0:T(8,128)(2,1)S(1)}, u32[]{:S(2)}, u32[]{:S(2)}) collective-permute-start(bf16[4,576,128]{2,1,0:T(8,128)(2,1)S(1)} %copy-done.11), channel_id=1, source_target_pairs={{0,4},{4,0},{8,12},{12,8},{16,20},{20,16},{24,28},{28,24},{1,5},{5... | collective-permute-start | bytes 1769480 | tf_op jit(solution)/shard_map/ppermute | solution.py:552
  67.9 0.8 slice_reduce_fusion.5
  70.1 0.6 pad.4.vec
  70.8 0.8 copy-done.7
  71.6 9.2 %attention_weights.1 = (bf16[4,592,128]{2,1,0:T(8,128)(2,1)}, bf16[4,592,128]{2,1,0:T(8,128)(2,1)}, f32[2,64,768]{2,1,0:T(8,128)}, bf16[2,64,768]{2,1,0:T(8,128)(2,1)}) custom-call(s32[4]{0:T(128)} %pad_add_fusion.1.ids, bf16[256,1152]{1,0:T(8,128)(2,1)} %get-tuple-element.57.own, bf16[256,1152]{1,0:T(8,128)(2,1)} %copy-done.7, ...), custom_call_target="tpu_custom_call" | custom-call | tf_op jit(solution)/shard_map/attention_weights/pallas_call | solution.py:464
  80.8 1.7 %collective-permute-start.20 = (bf16[4,592,128]{2,1,0:T(8,128)(2,1)}, bf16[4,592,128]{2,1,0:T(8,128)(2,1)S(1)}, u32[]{:S(2)}, u32[]{:S(2)}) collective-permute-start(bf16[4,592,128]{2,1,0:T(8,128)(2,1)} %get-tuple-element.72), channel_id=1, source_target_pairs={{0,4},{4,0},{8,12},{12,8},{16,20},{20,16},{24,28},{28,24},{1,5},{5... | collective-permute-start | bytes 1818632 | tf_op jit(solution)/shard_map/ppermute | solution.py:552
  82.8 1.6 %collective-permute-start.15 = (bf16[2,576,128]{2,1,0:T(8,128)(2,1)S(1)}, bf16[2,576,128]{2,1,0:T(8,128)(2,1)S(1)}, u32[]{:S(2)}, u32[]{:S(2)}) collective-permute-start(bf16[2,576,128]{2,1,0:T(8,128)(2,1)S(1)} %fusion.7), channel_id=1, source_target_pairs={{0,8},{4,12},{8,0},{12,4},{16,24},{20,28},{24,16},{28,20},{1,9},{5... | collective-permute-start | bytes 884744 | tf_op jit(solution)/shard_map/ppermute | solution.py:552
  84.5 10.3 %collective-permute-done.8 = bf16[4,576,128]{2,1,0:T(8,128)(2,1)S(1)} collective-permute-done((bf16[4,576,128]{2,1,0:T(8,128)(2,1)}, bf16[4,576,128]{2,1,0:T(8,128)(2,1)S(1)}, u32[]{:S(2)}, u32[]{:S(2)}) %collective-permute-start.8) | collective-permute-done | bytes 589856 | tf_op jit(solution)/shard_map/ppermute | solution.py:552
  94.9 1.9 %collective-permute-start.9 = (bf16[2,576,128]{2,1,0:T(8,128)(2,1)S(1)}, bf16[2,576,128]{2,1,0:T(8,128)(2,1)S(1)}, u32[]{:S(2)}, u32[]{:S(2)}) collective-permute-start(bf16[2,576,128]{2,1,0:T(8,128)(2,1)S(1)} %fusion.6), channel_id=1, source_target_pairs={{0,8},{4,12},{8,0},{12,4},{16,24},{20,28},{24,16},{28,20},{1,9},{5... | collective-permute-start | bytes 884744 | tf_op jit(solution)/shard_map/ppermute | solution.py:552
  96.9 1.0 copy-done.5
  98.0 1.9 %collective-permute-start.7 = (bf16[2,64,768]{2,1,0:T(8,128)(2,1)S(1)}, bf16[2,64,768]{2,1,0:T(8,128)(2,1)S(1)}, u32[]{:S(2)}, u32[]{:S(2)}) collective-permute-start(bf16[2,64,768]{2,1,0:T(8,128)(2,1)S(1)} %copy-done.27), channel_id=1, source_target_pairs={{0,2},{1,3},{2,0},{3,1},{4,6},{5,7},{6,4},{7,5},{8,10},{9,11},{10,... | collective-permute-start | bytes 589832 | tf_op jit(solution)/shard_map/ppermute | solution.py:552
  99.9 6.9 %collective-permute-done.20 = bf16[4,592,128]{2,1,0:T(8,128)(2,1)S(1)} collective-permute-done((bf16[4,592,128]{2,1,0:T(8,128)(2,1)}, bf16[4,592,128]{2,1,0:T(8,128)(2,1)S(1)}, u32[]{:S(2)}, u32[]{:S(2)}) %collective-permute-start.20) | collective-permute-done | bytes 606240 | tf_op jit(solution)/shard_map/ppermute | solution.py:552
  107.0 1.9 %collective-permute-start.21 = (bf16[2,592,128]{2,1,0:T(8,128)(2,1)S(1)}, bf16[2,592,128]{2,1,0:T(8,128)(2,1)S(1)}, u32[]{:S(2)}, u32[]{:S(2)}) collective-permute-start(bf16[2,592,128]{2,1,0:T(8,128)(2,1)S(1)} %fusion.3), channel_id=1, source_target_pairs={{0,8},{4,12},{8,0},{12,4},{16,24},{20,28},{24,16},{28,20},{1,9},{5... | collective-permute-start | bytes 909320 | tf_op jit(solution)/shard_map/ppermute | solution.py:552
  108.9 2.7 %collective-permute-start.16 = (bf16[576,128]{1,0:T(8,128)(2,1)S(1)}, bf16[576,128]{1,0:T(8,128)(2,1)S(1)}, u32[]{:S(2)}, u32[]{:S(2)}) collective-permute-start(bf16[576,128]{1,0:T(8,128)(2,1)S(1)} %fusion.14), channel_id=1, source_target_pairs={{0,16},{4,20},{8,24},{12,28},{16,0},{20,4},{24,8},{28,12},{1,17},{... | collective-permute-start | bytes 442376 | tf_op jit(solution)/shard_map/ppermute | solution.py:552
  112.1 9.2 %collective-permute-done.21 = bf16[2,592,128]{2,1,0:T(8,128)(2,1)S(1)} collective-permute-done((bf16[2,592,128]{2,1,0:T(8,128)(2,1)S(1)}, bf16[2,592,128]{2,1,0:T(8,128)(2,1)S(1)}, u32[]{:S(2)}, u32[]{:S(2)}) %collective-permute-start.21) | collective-permute-done | bytes 303136 | tf_op jit(solution)/shard_map/ppermute | solution.py:552
  121.4 1.2 collective-permute-start.22
  122.7 1.9 %collective-permute-start.18 = (bf16[576,128]{1,0:T(8,128)(2,1)S(1)}, bf16[576,128]{1,0:T(8,128)(2,1)S(1)}, u32[]{:S(2)}, u32[]{:S(2)}) collective-permute-start(bf16[576,128]{1,0:T(8,128)(2,1)S(1)} %fusion.9.refs_4_), channel_id=1, source_target_pairs={{0,2},{1,3},{2,0},{3,1},{4,6},{5,7},{6,4},{7,5},{8,10},{9,11},{10,... | collective-permute-start | bytes 442376 | tf_op jit(solution)/shard_map/ppermute | solution.py:552
  124.6 6.4 %collective-permute-done.22 = bf16[592,128]{1,0:T(8,128)(2,1)S(1)} collective-permute-done((bf16[592,128]{1,0:T(8,128)(2,1)S(1)}, bf16[592,128]{1,0:T(8,128)(2,1)S(1)}, u32[]{:S(2)}, u32[]{:S(2)}) %collective-permute-start.22) | collective-permute-done | bytes 151584 | tf_op jit(solution)/shard_map/ppermute | solution.py:552
  131.1 1.9 %collective-permute-start.24 = (bf16[592,128]{1,0:T(8,128)(2,1)S(1)}, bf16[592,128]{1,0:T(8,128)(2,1)S(1)}, u32[]{:S(2)}, u32[]{:S(2)}) collective-permute-start(bf16[592,128]{1,0:T(8,128)(2,1)S(1)} %fusion.5.refs_8_), channel_id=1, source_target_pairs={{0,2},{1,3},{2,0},{3,1},{4,6},{5,7},{6,4},{7,5},{8,10},{9,11},{10,... | collective-permute-start | bytes 454664 | tf_op jit(solution)/shard_map/ppermute | solution.py:552
  133.3 4.7 %collective-permute-done.24.refs_10_ = bf16[592,128]{1,0:T(8,128)(2,1)S(1)} collective-permute-done((bf16[592,128]{1,0:T(8,128)(2,1)S(1)}, bf16[592,128]{1,0:T(8,128)(2,1)S(1)}, u32[]{:S(2)}, u32[]{:S(2)}) %collective-permute-start.24) | collective-permute-done | bytes 151584 | tf_op jit(solution)/shard_map/ppermute | solution.py:552
  138.6 1.4 collective-permute-done.12.refs_2_
  140.0 2.3 %input_grad.1 = bf16[2,64,768]{2,1,0:T(8,128)(2,1)} custom-call(bf16[2,64,768]{2,1,0:T(8,128)(2,1)} %tokens.1, f32[2,64,768]{2,1,0:T(8,128)} %get-tuple-element.64.dfirst, bf16[2,64,768]{2,1,0:T(8,128)(2,1)} %copy-done.14, f32[128,768]{1,0:T(8,128)} %get-tuple-element.66.dhid, f32[8,768]{1,0:T(8,128)} %convert_element_type.75.pv), custom_call_target="tpu_custom_call" | custom-call | tf_op jit(solution)/shard_map/input_grad/pallas_call | solution.py:638
  143.1 0.7 copy-done.17
  143.7 3.7 %assemble.1 = (f32[96,3072]{1,0:T(8,128)}, f32[384,768]{1,0:T(8,128)}, f32[96,768]{1,0:T(8,128)}, f32[96,2304]{1,0:T(8,128)}, f32[16,128]{1,0:T(8,128)}) custom-call(s32[4]{0:T(128)} %pad_add_fusion.1.ids, bf16[576,128]{1,0:T(8,128)(2,1)} %copy-done.10, bf16[576,128]{1,0:T(8,128)(2,1)} %copy-done.21, bf16[576,128]{1,0:T(8,128)(2,1)} %copy-done.20, ...), custom_call_target="tpu_custom_call" | custom-call | tf_op jit(solution)/shard_map/assemble/pallas_call | solution.py:532
  147.4 0.7 slice.62
  148.1 1.4 slice_bitcast_fusion
  149.5 0.7 slice.58
  150.2 0.7 reshape.149
  150.9 0.6 reshape.145
  (129 shorter events, 7.5 us)
Async XLA Ops:
  0.6 11.2 %collective-permute-start.1 = (bf16[2,64,768]{2,1,0:T(8,128)(2,1)}, bf16[2,64,768]{2,1,0:T(8,128)(2,1)S(1)}, u32[]{:S(2)}, u32[]{:S(2)}) collective-permute-start(bf16[2,64,768]{2,1,0:T(8,128)(2,1)} %tokens.1), channel_id=1, source_target_pairs={{0,2},{1,3},{2,0},{3,1},{4,6},{5,7},{6,4},{7,5},{8,10},{9,11},{10,... | collective-permute-start | bytes 589832 | tf_op jit(solution)/shard_map/ppermute | solution.py:552
  3.7 10.6 %collective-permute-start = (bf16[2,64,768]{2,1,0:T(8,128)(2,1)}, bf16[2,64,768]{2,1,0:T(8,128)(2,1)S(1)}, u32[]{:S(2)}, u32[]{:S(2)}) collective-permute-start(bf16[2,64,768]{2,1,0:T(8,128)(2,1)} %tokens.1), channel_id=1, source_target_pairs={{0,1},{1,0},{2,3},{3,2},{4,5},{5,4},{6,7},{7,6},{8,9},{9,8},{10,11... | collective-permute-start | bytes 589832 | tf_op jit(solution)/shard_map/ppermute | solution.py:552
  3.7 9.3 %collective-permute-start.4 = (bf16[2,64,768]{2,1,0:T(8,128)(2,1)}, bf16[2,64,768]{2,1,0:T(8,128)(2,1)S(1)}, u32[]{:S(2)}, u32[]{:S(2)}) collective-permute-start(bf16[2,64,768]{2,1,0:T(8,128)(2,1)} %d0.3), channel_id=1, source_target_pairs={{0,2},{1,3},{2,0},{3,1},{4,6},{5,7},{6,4},{7,5},{8,10},{9,11},{10,... | collective-permute-start | bytes 589832 | tf_op jit(solution)/shard_map/ppermute | solution.py:552
  3.8 26.2 %collective-permute-start.3 = (bf16[2,64,768]{2,1,0:T(8,128)(2,1)}, bf16[2,64,768]{2,1,0:T(8,128)(2,1)S(1)}, u32[]{:S(2)}, u32[]{:S(2)}) collective-permute-start(bf16[2,64,768]{2,1,0:T(8,128)(2,1)} %d0.3), channel_id=1, source_target_pairs={{0,1},{1,0},{2,3},{3,2},{4,5},{5,4},{6,7},{7,6},{8,9},{9,8},{10,11... | collective-permute-start | bytes 589832 | tf_op jit(solution)/shard_map/ppermute | solution.py:552
  11.9 2.4 %copy-start.1 = (bf16[2,64,768]{2,1,0:T(8,128)(2,1)}, bf16[2,64,768]{2,1,0:T(8,128)(2,1)S(1)}, u32[]{:S(2)}) copy-start(bf16[2,64,768]{2,1,0:T(8,128)(2,1)S(1)} %collective-permute-done.1.t2) | copy-start | bytes 589828
  11.9 2.4 %collective-permute-start.2 = (bf16[2,64,768]{2,1,0:T(8,128)(2,1)S(1)}, bf16[2,64,768]{2,1,0:T(8,128)(2,1)S(1)}, u32[]{:S(2)}, u32[]{:S(2)}) collective-permute-start(bf16[2,64,768]{2,1,0:T(8,128)(2,1)S(1)} %collective-permute-done.1.t2), channel_id=1, source_target_pairs={{0,1},{1,0},{2,3},{3,2},{4,5},{5,4},{6,7},{7,6},{8,9},{9,8},{10,11... | collective-permute-start | bytes 589832 | tf_op jit(solution)/shard_map/ppermute | solution.py:552
  13.0 17.1 %copy-start.2 = (bf16[2,64,768]{2,1,0:T(8,128)(2,1)}, bf16[2,64,768]{2,1,0:T(8,128)(2,1)S(1)}, u32[]{:S(2)}) copy-start(bf16[2,64,768]{2,1,0:T(8,128)(2,1)S(1)} %collective-permute-done.4.d2) | copy-start | bytes 589828
  13.0 17.1 %collective-permute-start.5 = (bf16[2,64,768]{2,1,0:T(8,128)(2,1)S(1)}, bf16[2,64,768]{2,1,0:T(8,128)(2,1)S(1)}, u32[]{:S(2)}, u32[]{:S(2)}) collective-permute-start(bf16[2,64,768]{2,1,0:T(8,128)(2,1)S(1)} %collective-permute-done.4.d2), channel_id=1, source_target_pairs={{0,1},{1,0},{2,3},{3,2},{4,5},{5,4},{6,7},{7,6},{8,9},{9,8},{10,11... | collective-permute-start | bytes 589832 | tf_op jit(solution)/shard_map/ppermute | solution.py:552
  30.1 0.7 copy-start.4
  59.8 6.2 %copy-start.11 = (bf16[4,576,128]{2,1,0:T(8,128)(2,1)S(1)}, bf16[4,576,128]{2,1,0:T(8,128)(2,1)}, u32[]{:S(2)}) copy-start(bf16[4,576,128]{2,1,0:T(8,128)(2,1)} %get-tuple-element.70) | copy-start | bytes 1769476
  59.8 9.0 %copy-start.26 = (f32[1,1536]{1,0:T(1,128)S(1)}, f32[1,1536]{1,0:T(1,128)}, u32[]{:S(2)}) copy-start(f32[1,1536]{1,0:T(1,128)} %get-tuple-element.63) | copy-start | bytes 18436
  59.8 9.1 %copy-start.25 = (f32[1,1536]{1,0:T(1,128)S(1)}, f32[1,1536]{1,0:T(1,128)}, u32[]{:S(2)}) copy-start(f32[1,1536]{1,0:T(1,128)} %get-tuple-element.62) | copy-start | bytes 18436
  59.8 9.8 %copy-start.24 = (f32[8,768]{1,0:T(8,128)S(1)}, f32[8,768]{1,0:T(8,128)}, u32[]{:S(2)}) copy-start(f32[8,768]{1,0:T(8,128)} %get-tuple-element.61) | copy-start | bytes 73732
  65.4 5.3 %collective-permute-start.6 = (bf16[256,1152]{1,0:T(8,128)(2,1)}, bf16[256,1152]{1,0:T(8,128)(2,1)S(1)}, u32[]{:S(2)}, u32[]{:S(2)}) collective-permute-start(bf16[256,1152]{1,0:T(8,128)(2,1)} %get-tuple-element.57.own), channel_id=1, source_target_pairs={{0,1},{1,0},{2,3},{3,2},{4,5},{5,4},{6,7},{7,6},{8,9},{9,8},{10,11... | collective-permute-start | bytes 1769480 | tf_op jit(solution)/shard_map/ppermute | solution.py:552
  65.9 16.7 %collective-permute-start.14 = (bf16[4,576,128]{2,1,0:T(8,128)(2,1)S(1)}, bf16[4,576,128]{2,1,0:T(8,128)(2,1)S(1)}, u32[]{:S(2)}, u32[]{:S(2)}) collective-permute-start(bf16[4,576,128]{2,1,0:T(8,128)(2,1)S(1)} %copy-done.11), channel_id=1, source_target_pairs={{0,4},{4,0},{8,12},{12,8},{16,20},{20,16},{24,28},{28,24},{1,5},{5... | collective-permute-start | bytes 1769480 | tf_op jit(solution)/shard_map/ppermute | solution.py:552
  67.6 27.1 %collective-permute-start.8 = (bf16[4,576,128]{2,1,0:T(8,128)(2,1)}, bf16[4,576,128]{2,1,0:T(8,128)(2,1)S(1)}, u32[]{:S(2)}, u32[]{:S(2)}) collective-permute-start(bf16[4,576,128]{2,1,0:T(8,128)(2,1)} %get-tuple-element.68), channel_id=1, source_target_pairs={{0,4},{4,0},{8,12},{12,8},{16,20},{20,16},{24,28},{28,24},{1,5},{5... | collective-permute-start | bytes 1769480 | tf_op jit(solution)/shard_map/ppermute | solution.py:552
  70.8 0.8 copy-start.7
  71.6 10.9 %copy-start = (bf16[4,576,128]{2,1,0:T(8,128)(2,1)S(1)}, bf16[4,576,128]{2,1,0:T(8,128)(2,1)}, u32[]{:S(2)}) copy-start(bf16[4,576,128]{2,1,0:T(8,128)(2,1)} %get-tuple-element.69) | copy-start | bytes 1769476
  80.8 1.8 %copy-start.8 = (bf16[4,576,128]{2,1,0:T(8,128)(2,1)S(1)}, bf16[4,576,128]{2,1,0:T(8,128)(2,1)}, u32[]{:S(2)}) copy-start(bf16[4,576,128]{2,1,0:T(8,128)(2,1)} %get-tuple-element.67) | copy-start | bytes 1769476
  80.8 26.1 %collective-permute-start.20 = (bf16[4,592,128]{2,1,0:T(8,128)(2,1)}, bf16[4,592,128]{2,1,0:T(8,128)(2,1)S(1)}, u32[]{:S(2)}, u32[]{:S(2)}) collective-permute-start(bf16[4,592,128]{2,1,0:T(8,128)(2,1)} %get-tuple-element.72), channel_id=1, source_target_pairs={{0,4},{4,0},{8,12},{12,8},{16,20},{20,16},{24,28},{28,24},{1,5},{5... | collective-permute-start | bytes 1818632 | tf_op jit(solution)/shard_map/ppermute | solution.py:552
  82.8 17.0 %collective-permute-start.15 = (bf16[2,576,128]{2,1,0:T(8,128)(2,1)S(1)}, bf16[2,576,128]{2,1,0:T(8,128)(2,1)S(1)}, u32[]{:S(2)}, u32[]{:S(2)}) collective-permute-start(bf16[2,576,128]{2,1,0:T(8,128)(2,1)S(1)} %fusion.7), channel_id=1, source_target_pairs={{0,8},{4,12},{8,0},{12,4},{16,24},{20,28},{24,16},{28,20},{1,9},{5... | collective-permute-start | bytes 884744 | tf_op jit(solution)/shard_map/ppermute | solution.py:552
  94.9 16.7 %collective-permute-start.9 = (bf16[2,576,128]{2,1,0:T(8,128)(2,1)S(1)}, bf16[2,576,128]{2,1,0:T(8,128)(2,1)S(1)}, u32[]{:S(2)}, u32[]{:S(2)}) collective-permute-start(bf16[2,576,128]{2,1,0:T(8,128)(2,1)S(1)} %fusion.6), channel_id=1, source_target_pairs={{0,8},{4,12},{8,0},{12,4},{16,24},{20,28},{24,16},{28,20},{1,9},{5... | collective-permute-start | bytes 884744 | tf_op jit(solution)/shard_map/ppermute | solution.py:552
  96.8 1.1 copy-start.5
  96.9 1.1 copy-start.27
  98.0 35.3 %collective-permute-start.7 = (bf16[2,64,768]{2,1,0:T(8,128)(2,1)S(1)}, bf16[2,64,768]{2,1,0:T(8,128)(2,1)S(1)}, u32[]{:S(2)}, u32[]{:S(2)}) collective-permute-start(bf16[2,64,768]{2,1,0:T(8,128)(2,1)S(1)} %copy-done.27), channel_id=1, source_target_pairs={{0,2},{1,3},{2,0},{3,1},{4,6},{5,7},{6,4},{7,5},{8,10},{9,11},{10,... | collective-permute-start | bytes 589832 | tf_op jit(solution)/shard_map/ppermute | solution.py:552
  107.0 14.3 %collective-permute-start.21 = (bf16[2,592,128]{2,1,0:T(8,128)(2,1)S(1)}, bf16[2,592,128]{2,1,0:T(8,128)(2,1)S(1)}, u32[]{:S(2)}, u32[]{:S(2)}) collective-permute-start(bf16[2,592,128]{2,1,0:T(8,128)(2,1)S(1)} %fusion.3), channel_id=1, source_target_pairs={{0,8},{4,12},{8,0},{12,4},{16,24},{20,28},{24,16},{28,20},{1,9},{5... | collective-permute-start | bytes 909320 | tf_op jit(solution)/shard_map/ppermute | solution.py:552
  108.9 13.7 %collective-permute-start.16 = (bf16[576,128]{1,0:T(8,128)(2,1)S(1)}, bf16[576,128]{1,0:T(8,128)(2,1)S(1)}, u32[]{:S(2)}, u32[]{:S(2)}) collective-permute-start(bf16[576,128]{1,0:T(8,128)(2,1)S(1)} %fusion.14), channel_id=1, source_target_pairs={{0,16},{4,20},{8,24},{12,28},{16,0},{20,4},{24,8},{28,12},{1,17},{... | collective-permute-start | bytes 442376 | tf_op jit(solution)/shard_map/ppermute | solution.py:552
  111.7 21.3 %collective-permute-start.10 = (bf16[576,128]{1,0:T(8,128)(2,1)S(1)}, bf16[576,128]{1,0:T(8,128)(2,1)S(1)}, u32[]{:S(2)}, u32[]{:S(2)}) collective-permute-start(bf16[576,128]{1,0:T(8,128)(2,1)S(1)} %fusion.13), channel_id=1, source_target_pairs={{0,16},{4,20},{8,24},{12,28},{16,0},{20,4},{24,8},{28,12},{1,17},{... | collective-permute-start | bytes 442376 | tf_op jit(solution)/shard_map/ppermute | solution.py:552
  121.4 9.5 %collective-permute-start.22 = (bf16[592,128]{1,0:T(8,128)(2,1)S(1)}, bf16[592,128]{1,0:T(8,128)(2,1)S(1)}, u32[]{:S(2)}, u32[]{:S(2)}) collective-permute-start(bf16[592,128]{1,0:T(8,128)(2,1)S(1)} %fusion.12), channel_id=1, source_target_pairs={{0,16},{4,20},{8,24},{12,28},{16,0},{20,4},{24,8},{28,12},{1,17},{... | collective-permute-start | bytes 454664 | tf_op jit(solution)/shard_map/ppermute | solution.py:552
  122.7 19.6 %copy-start.9 = (bf16[576,128]{1,0:T(8,128)(2,1)}, bf16[576,128]{1,0:T(8,128)(2,1)S(1)}, u32[]{:S(2)}) copy-start(bf16[576,128]{1,0:T(8,128)(2,1)S(1)} %fusion.9.refs_4_) | copy-start | bytes 442372
  122.7 15.3 %collective-permute-start.18 = (bf16[576,128]{1,0:T(8,128)(2,1)S(1)}, bf16[576,128]{1,0:T(8,128)(2,1)S(1)}, u32[]{:S(2)}, u32[]{:S(2)}) collective-permute-start(bf16[576,128]{1,0:T(8,128)(2,1)S(1)} %fusion.9.refs_4_), channel_id=1, source_target_pairs={{0,2},{1,3},{2,0},{3,1},{4,6},{5,7},{6,4},{7,5},{8,10},{9,11},{10,... | collective-permute-start | bytes 442376 | tf_op jit(solution)/shard_map/ppermute | solution.py:552
  124.6 13.9 %collective-permute-start.17 = (bf16[576,128]{1,0:T(8,128)(2,1)S(1)}, bf16[576,128]{1,0:T(8,128)(2,1)S(1)}, u32[]{:S(2)}, u32[]{:S(2)}) collective-permute-start(bf16[576,128]{1,0:T(8,128)(2,1)S(1)} %fusion.9.refs_4_), channel_id=1, source_target_pairs={{0,1},{1,0},{2,3},{3,2},{4,5},{5,4},{6,7},{7,6},{8,9},{9,8},{10,11... | collective-permute-start | bytes 442376 | tf_op jit(solution)/shard_map/ppermute | solution.py:552
  131.1 11.3 %copy-start.6 = (bf16[592,128]{1,0:T(8,128)(2,1)}, bf16[592,128]{1,0:T(8,128)(2,1)S(1)}, u32[]{:S(2)}) copy-start(bf16[592,128]{1,0:T(8,128)(2,1)S(1)} %fusion.5.refs_8_) | copy-start | bytes 454660
  131.1 6.9 %collective-permute-start.24 = (bf16[592,128]{1,0:T(8,128)(2,1)S(1)}, bf16[592,128]{1,0:T(8,128)(2,1)S(1)}, u32[]{:S(2)}, u32[]{:S(2)}) collective-permute-start(bf16[592,128]{1,0:T(8,128)(2,1)S(1)} %fusion.5.refs_8_), channel_id=1, source_target_pairs={{0,2},{1,3},{2,0},{3,1},{4,6},{5,7},{6,4},{7,5},{8,10},{9,11},{10,... | collective-permute-start | bytes 454664 | tf_op jit(solution)/shard_map/ppermute | solution.py:552
  133.0 9.3 %copy-start.10 = (bf16[576,128]{1,0:T(8,128)(2,1)}, bf16[576,128]{1,0:T(8,128)(2,1)S(1)}, u32[]{:S(2)}) copy-start(bf16[576,128]{1,0:T(8,128)(2,1)S(1)} %fusion.11.refs_0_) | copy-start | bytes 442372
  133.0 6.9 %collective-permute-start.12 = (bf16[576,128]{1,0:T(8,128)(2,1)S(1)}, bf16[576,128]{1,0:T(8,128)(2,1)S(1)}, u32[]{:S(2)}, u32[]{:S(2)}) collective-permute-start(bf16[576,128]{1,0:T(8,128)(2,1)S(1)} %fusion.11.refs_0_), channel_id=1, source_target_pairs={{0,2},{1,3},{2,0},{3,1},{4,6},{5,7},{6,4},{7,5},{8,10},{9,11},{10,... | collective-permute-start | bytes 442376 | tf_op jit(solution)/shard_map/ppermute | solution.py:552
  133.3 6.7 %copy-start.14 = (bf16[2,64,768]{2,1,0:T(8,128)(2,1)}, bf16[2,64,768]{2,1,0:T(8,128)(2,1)S(1)}, u32[]{:S(2)}) copy-start(bf16[2,64,768]{2,1,0:T(8,128)(2,1)S(1)} %collective-permute-done.7.received) | copy-start | bytes 589828
  133.3 9.0 %collective-permute-start.23 = (bf16[592,128]{1,0:T(8,128)(2,1)S(1)}, bf16[592,128]{1,0:T(8,128)(2,1)S(1)}, u32[]{:S(2)}, u32[]{:S(2)}) collective-permute-start(bf16[592,128]{1,0:T(8,128)(2,1)S(1)} %fusion.5.refs_8_), channel_id=1, source_target_pairs={{0,1},{1,0},{2,3},{3,2},{4,5},{5,4},{6,7},{7,6},{8,9},{9,8},{10,11... | collective-permute-start | bytes 454664 | tf_op jit(solution)/shard_map/ppermute | solution.py:552
  138.0 4.4 %copy-start.15 = (bf16[592,128]{1,0:T(8,128)(2,1)}, bf16[592,128]{1,0:T(8,128)(2,1)S(1)}, u32[]{:S(2)}) copy-start(bf16[592,128]{1,0:T(8,128)(2,1)S(1)} %collective-permute-done.24.refs_10_) | copy-start | bytes 454660
  138.0 4.4 %collective-permute-start.25 = (bf16[592,128]{1,0:T(8,128)(2,1)S(1)}, bf16[592,128]{1,0:T(8,128)(2,1)S(1)}, u32[]{:S(2)}, u32[]{:S(2)}) collective-permute-start(bf16[592,128]{1,0:T(8,128)(2,1)S(1)} %collective-permute-done.24.refs_10_), channel_id=1, source_target_pairs={{0,1},{1,0},{2,3},{3,2},{4,5},{5,4},{6,7},{7,6},{8,9},{9,8},{10,11... | collective-permute-start | bytes 454664 | tf_op jit(solution)/shard_map/ppermute | solution.py:552
  138.0 4.4 %copy-start.18 = (bf16[576,128]{1,0:T(8,128)(2,1)}, bf16[576,128]{1,0:T(8,128)(2,1)S(1)}, u32[]{:S(2)}) copy-start(bf16[576,128]{1,0:T(8,128)(2,1)S(1)} %collective-permute-done.18.refs_6_) | copy-start | bytes 442372
  138.0 4.3 %collective-permute-start.11 = (bf16[576,128]{1,0:T(8,128)(2,1)S(1)}, bf16[576,128]{1,0:T(8,128)(2,1)S(1)}, u32[]{:S(2)}, u32[]{:S(2)}) collective-permute-start(bf16[576,128]{1,0:T(8,128)(2,1)S(1)} %fusion.11.refs_0_), channel_id=1, source_target_pairs={{0,1},{1,0},{2,3},{3,2},{4,5},{5,4},{6,7},{7,6},{8,9},{9,8},{10,11... | collective-permute-start | bytes 442376 | tf_op jit(solution)/shard_map/ppermute | solution.py:552
  138.5 3.9 %copy-start.19 = (bf16[576,128]{1,0:T(8,128)(2,1)}, bf16[576,128]{1,0:T(8,128)(2,1)S(1)}, u32[]{:S(2)}) copy-start(bf16[576,128]{1,0:T(8,128)(2,1)S(1)} %collective-permute-done.17.refs_5_) | copy-start | bytes 442372
  138.5 3.8 %collective-permute-start.19 = (bf16[576,128]{1,0:T(8,128)(2,1)S(1)}, bf16[576,128]{1,0:T(8,128)(2,1)S(1)}, u32[]{:S(2)}, u32[]{:S(2)}) collective-permute-start(bf16[576,128]{1,0:T(8,128)(2,1)S(1)} %collective-permute-done.18.refs_6_), channel_id=1, source_target_pairs={{0,1},{1,0},{2,3},{3,2},{4,5},{5,4},{6,7},{7,6},{8,9},{9,8},{10,11... | collective-permute-start | bytes 442376 | tf_op jit(solution)/shard_map/ppermute | solution.py:552
  139.9 2.4 %copy-start.20 = (bf16[576,128]{1,0:T(8,128)(2,1)}, bf16[576,128]{1,0:T(8,128)(2,1)S(1)}, u32[]{:S(2)}) copy-start(bf16[576,128]{1,0:T(8,128)(2,1)S(1)} %collective-permute-done.12.refs_2_) | copy-start | bytes 442372
  140.0 2.3 %collective-permute-start.13 = (bf16[576,128]{1,0:T(8,128)(2,1)S(1)}, bf16[576,128]{1,0:T(8,128)(2,1)S(1)}, u32[]{:S(2)}, u32[]{:S(2)}) collective-permute-start(bf16[576,128]{1,0:T(8,128)(2,1)S(1)} %collective-permute-done.12.refs_2_), channel_id=1, source_target_pairs={{0,1},{1,0},{2,3},{3,2},{4,5},{5,4},{6,7},{7,6},{8,9},{9,8},{10,11... | collective-permute-start | bytes 442376 | tf_op jit(solution)/shard_map/ppermute | solution.py:552
  142.3 0.7 copy-start.23
  142.3 0.8 copy-start.16
  (6 other events, 4.1 us)

commit v2 on v0

v2 whole, which is shorter than its diff:
```python
import jax
import jax.numpy as jnp
from jax import lax
from jax.experimental import pallas as pl
from jax.experimental.pallas import tpu as pltpu
from jax.sharding import PartitionSpec as P

HEADS = 12
EPS = 1e-06
SLOTS = 8
F32 = jnp.float32
BF16 = jnp.bfloat16
GELU_C = 0.7978845608028654
GELU_A = 0.044715
VMEM = pl.BlockSpec(memory_space=pltpu.VMEM)
HBM = pl.BlockSpec(memory_space=pltpu.HBM)


def nn(a, b):
    return lax.dot_general(a, b, (((1,), (0,)), ((), ())), preferred_element_type=F32)


def nt(a, b):
    return lax.dot_general(a, b, (((1,), (1,)), ((), ())), preferred_element_type=F32)


def tn(a, b):
    return lax.dot_general(a, b, (((0,), (0,)), ((), ())), preferred_element_type=F32)


def standardize(x):
    centered = x - jnp.mean(x, axis=-1, keepdims=True)
    rstd = lax.rsqrt(jnp.mean(centered * centered, axis=-1, keepdims=True) + EPS)
    return centered * rstd, rstd


def norm_back(xhat, rstd, g):
    return rstd * (
        g
        - jnp.mean(g, axis=-1, keepdims=True)
        - xhat * jnp.mean(g * xhat, axis=-1, keepdims=True)
    )


def row(ref):
    return ref[...].astype(F32).reshape(1, -1)


def half_masks():
    lane = lax.broadcasted_iota(jnp.int32, (1, 128), 1)
    low = jnp.where(lane < 64, 1.0, 0.0)
    return low.astype(BF16), (1.0 - low).astype(BF16)


def flip(bit, k):
    return lax.rem(bit + k, 2)


def softmax_rows(scores, same):
    scores = jnp.where(same > 0.0, scores, -1e9)
    e = jnp.exp(scores - jnp.max(scores, axis=-1, keepdims=True))
    return e * (1.0 / jnp.sum(e, axis=-1, keepdims=True))


def column_sum(x):
    return jnp.sum(x.astype(F32), axis=0, keepdims=True)


def call(kernel, outs, ins, args, scratch=(), limit=24, us=2.0):
    return pl.pallas_call(
        kernel,
        out_shape=tuple(jax.ShapeDtypeStruct(s, d) for s, d in outs),
        in_specs=ins,
        out_specs=tuple(VMEM for _ in outs),
        scratch_shapes=list(scratch),
        compiler_params=pltpu.CompilerParams(vmem_limit_bytes=limit * 1024 * 1024),
        cost_estimate=pl.CostEstimate(
            flops=int(us * 1e9), bytes_accessed=int(us * 1e5), transcendentals=0
        ),
        name=kernel.__name__,
    )(*args)


class Place:
    def __init__(self, inner):
        b = lax.axis_index("blk")
        slot = lax.axis_index("seq") // inner
        self.y, self.core = b // 2, lax.rem(b, 2)
        self.x, self.z_low, self.z_high = lax.rem(slot, 2), lax.rem(slot // 2, 2), slot // 4


def crop_mask(place, seg):
    ids = jnp.broadcast_to(seg[pl.ds(place.core, 1), :], (256, 256))
    first, second = ids[:, 0:128], ids[:, 128:256]
    tiles = jnp.where(place.y == 1, second, first), jnp.where(place.y == 1, first, second)
    tiles = [jnp.where(place.core == 1, pltpu.roll(t, 64, 1), t) for t in tiles]
    wide = jnp.concatenate(tiles, axis=1)
    return jnp.where(wide == wide.T, 1.0, 0.0)


def pick_rows(transposed, chosen, part, x_bit):
    for k in range(2):
        for z in range(4):
            start = pl.multiple_of((2 * z + flip(x_bit, k)) * 96 + part * 48, 16)
            chosen[pl.ds((4 * k + z) * 48, 48), :] = transposed[pl.ds(start, 48), :]


def put_slots(product, keep, send, offset):
    for t in range(product.shape[1] // 128):
        for z in range(4):
            tile = product[:, t * 128 : t * 128 + 128]
            keep[z, pl.ds(offset + t * 48, 48), :] = tile[z * 48 : z * 48 + 48]
            send[z, pl.ds(offset + t * 48, 48), :] = tile[192 + z * 48 : 240 + z * 48]


def gather_rows(pieces, out):
    for s in range(2):
        for p, piece in enumerate(pieces):
            out[pl.ds(s * 256 + p * 64, 64), :] = piece[s]


def both_cores(core, own, other, out):
    for p in range(4):
        out[core, pl.ds(p * 64, 64), :] = own[pl.ds(p * 64, 64), :]
        out[1 - core, pl.ds(p * 64, 64), :] = other[pl.ds((p ^ 1) * 64, 64), :]


def build_kernels(inner):
    def attention(seg, t0, t1, t2, t3, gain, shift, bias, wqkv_hbm, att_o, mine_o, first, q_s, k_s, v_s, wqkv, same, sem):
        place = Place(inner)
        loads = [
            pltpu.make_async_copy(wqkv_hbm.at[:, pl.ds(n * 768, 768)], wqkv.at[n], sem.at[n])
            for n in range(3)
        ]
        for load in loads:
            load.start()
        g, b = row(gain), row(shift)
        for p, t in enumerate((t0, t1, t2, t3)):
            xhat, _ = standardize(t[place.core].astype(F32))
            first[pl.ds(p * 64, 64), :] = (xhat * g + b).astype(BF16)
        same[...] = crop_mask(place, seg)
        biases = row(bias)
        loads[0].wait()
        q_s[...] = (nn(first[...], wqkv[0]) + biases[:, 0:768]).astype(BF16) * BF16(0.125)
        loads[1].wait()
        k_s[...] = nn(first[...], wqkv[1]).astype(BF16)
        loads[2].wait()
        v_s[...] = (nn(first[...], wqkv[2]) + biases[:, 768:1536]).astype(BF16)
        low, high = half_masks()
        for j in range(HEADS // 2):
            cols = pl.ds(j * 128, 128)
            q, k, v = q_s[:, cols], k_s[:, cols], v_s[:, cols]
            out = None
            for keep in (low, high):
                probs = softmax_rows(nt(q * keep, k), same[...]).astype(BF16)
                part = nn(probs, v * keep)
                out = part if out is None else out + part
            att_o[:, cols] = out.astype(BF16)
        half = pl.ds(pl.multiple_of(place.y * 384, 128), 384)
        for n, source in enumerate((q_s, k_s, v_s)):
            mine_o[:, pl.ds(n * 384, 384)] = source[:, half]

    def feed(
        att_own, att_other, t0, t1, t2, t3, out_bias, gain, shift, up_bias, d0, d1, d2, d3,
        wout_hbm, wup_hbm, wdown_hbm,
        sec_o, dup_o, act_o, send_o, dsec_o, part_o, hid_core_o, hid_own_o, dy_o,
        att, hid, wout, wup, wdown, sem,
    ):
        place = Place(inner)
        load_out = pltpu.make_async_copy(wout_hbm, wout, sem.at[0])
        load_out.start()
        loads = []
        for j in range(4):
            units = pl.ds(pl.multiple_of((2 * j + place.core) * 384, 128), 384)
            loads.append(
                (
                    pltpu.make_async_copy(wup_hbm.at[:, units], wup.at[:, pl.ds(j * 384, 384)], sem.at[1 + j]),
                    pltpu.make_async_copy(wdown_hbm.at[units, :], wdown.at[pl.ds(j * 384, 384), :], sem.at[5 + j]),
                )
            )
        for pair in loads:
            for load in pair:
                load.start()
        both_cores(place.core, att_own, att_other, att)
        gather_rows((d0, d1, d2, d3), dy_o)
        g, b, ob = row(gain), row(shift), row(out_bias)
        load_out.wait()
        for s in range(2):
            added = nn(att[s], wout[...]) + ob
            for p, t in enumerate((t0, t1, t2, t3)):
                h = t[s].astype(F32) + added[p * 64 : p * 64 + 64]
                hid[s, pl.ds(p * 64, 64), :] = h
                xhat, _ = standardize(h)
                sec_o[pl.ds(s * 256 + p * 64, 64), :] = (xhat * g + b).astype(BF16)
            hid_own_o[pl.ds(s * 64, 64), :] = hid[s, 0:64, :]
        hid_core_o[...] = hid[place.core]
        for j in range(4):
            for load in loads[j]:
                load.wait()
            cols = pl.ds(j * 384, 384)
            units = pl.ds(pl.multiple_of((2 * j + place.core) * 384, 128), 384)
            ub = up_bias[:, units].astype(F32)
            for s in range(2):
                rows = pl.ds(s * 256, 256)
                up = nn(sec_o[rows, :], wup[:, cols]) + ub
                da = nt(dy_o[rows, :], wdown[cols, :])
                square = up * up
                tanh = jnp.tanh(GELU_C * up * (1.0 + GELU_A * square))
                cdf = 0.5 * (1.0 + tanh)
                act_o[rows, cols] = (up * cdf).astype(BF16)
                slope = cdf + (0.5 * GELU_C) * up * (1.0 - tanh * tanh) * (1.0 + (3.0 * GELU_A) * square)
                dup_o[rows, cols] = (da * slope).astype(BF16)
        dsec_o[...] = nt(dup_o[pl.ds(pl.multiple_of(place.core * 256, 256), 256), :], wup[...])
        away = nt(dup_o[pl.ds(pl.multiple_of((1 - place.core) * 256, 256), 256), :], wup[...])
        for p in range(4):
            send_o[pl.ds(p * 64, 64), :] = away[(p ^ 1) * 64 : (p ^ 1) * 64 + 64].astype(BF16)
        for s in range(2):
            part = nn(act_o[pl.ds(s * 256, 128), :], wdown[...])
            part_o[pl.ds(s * 64, 64), :] = part[0:64]
            send_o[pl.ds(256 + s * 64, 64), :] = part[64:128].astype(BF16)

    def feed_weights(sec, dup, act, dy, up_keep, up_send, down_keep, down_send, bias_o, turned, chosen):
        place = Place(inner)
        turned[...] = sec[...].T
        pick_rows(turned, chosen, place.y, place.x)
        dy_half = dy[:, pl.ds(pl.multiple_of(place.y * 384, 128), 384)]
        for j in range(4):
            cols = pl.ds(j * 384, 384)
            put_slots(nn(chosen[...], dup[:, cols]).astype(BF16), up_keep, up_send, j * 144)
            bias_o[:, cols] = column_sum(dup[0:128, cols]) + column_sum(dup[256:384, cols])
        for k, out in enumerate((down_keep, down_send)):
            for z in range(2):
                j = 2 * z + flip(place.z_low, k)
                units = pl.ds(pl.multiple_of(j * 384, 128), 384)
                product = tn(act[:, units], dy_half).astype(BF16)
                for t in range(3):
                    out[z, pl.ds(t * 384, 384), :] = product[:, t * 128 : t * 128 + 128]

    def attention_back(
        dsec_in, got, part, hid_core, hid_own, d0, d1, d2, d3, gain, down_bias, seg, mine, wout_hbm,
        block_o, ex_o, dhid_o, sums_o, heads_o,
        wout, dh, datt, same, sem,
    ):
        place = Place(inner)
        load = pltpu.make_async_copy(
            wout_hbm.at[pl.ds(pl.multiple_of(place.y * 384, 128), 384), :], wout, sem.at[0]
        )
        load.start()
        same[...] = crop_mask(place, seg)
        g = row(gain)
        sums = [jnp.zeros((1, 768), F32)] * 3
        for p, d in enumerate((d0, d1, d2, d3)):
            rows = pl.ds(p * 64, 64)
            xhat, rstd = standardize(hid_core[rows, :])
            grad = dsec_in[rows, :] + got[rows, :].astype(F32)
            dhid = d[place.core].astype(F32) + norm_back(xhat, rstd, grad * g)
            low = dhid.astype(BF16)
            dh[rows, :] = low
            if p < 2:
                sums = [a + column_sum(v) for a, v in zip(sums, (low, grad * xhat, grad))]
            if p == 0:
                dhid_o[...] = dhid
            if p == 1:
                ex_o[pl.ds(256, 32), 0:768] = low[0:32]
                ex_o[pl.ds(256, 32), 768:1536] = low[32:64]
        for r in range(3):
            sums_o[r : r + 1, :] = sums[r]
        sums_o[3:4, :] = column_sum(d0[0]) + column_sum(d0[1])
        sums_o[4:8, :] = jnp.zeros((4, 768), F32)
        ex_o[0:256, 1152:1536] = dh[:, pl.ds(pl.multiple_of(place.y * 384, 128), 384)]
        load.wait()
        datt[...] = nt(dh[...], wout[...]).astype(BF16)
        low, high = half_masks()
        for j in range(HEADS // 4):
            cols = pl.ds(j * 128, 128)
            q, k, v = (mine[:, pl.ds(n * 384 + j * 128, 128)] for n in range(3))
            da = datt[:, cols]
            dq = dk = dv = None
            for keep in (low, high):
                qh, kh, dah = q * keep, k * keep, da * keep
                probs = softmax_rows(nt(qh, k), same[...])
                dprobs = nt(dah, v)
                delta = jnp.sum(probs * dprobs, axis=-1, keepdims=True)
                ds = (probs * (dprobs - delta)).astype(BF16)
                parts = nn(ds, kh), tn(ds, qh), tn(probs.astype(BF16), dah)
                if dq is None:
                    dq, dk, dv = parts
                else:
                    dq, dk, dv = dq + parts[0], dk + parts[1], dv + parts[2]
            dq = (dq * 0.125).astype(BF16)
            dv = dv.astype(BF16)
            ex_o[0:256, pl.ds(j * 128, 128)] = dq
            ex_o[0:256, pl.ds(384 + j * 128, 128)] = dk.astype(BF16)
            ex_o[0:256, pl.ds(768 + j * 128, 128)] = dv
            heads_o[0:1, cols] = column_sum(dq)
            heads_o[1:2, cols] = column_sum(dv)
        heads_o[2:8, :] = jnp.zeros((6, 384), F32)
        bias = row(down_bias)
        for s in range(2):
            rows = pl.ds(s * 64, 64)
            arrived = got[pl.ds(256 + s * 64, 64), :].astype(F32)
            block_o[s] = (hid_own[rows, :] + (part[rows, :] + arrived + bias)).astype(BF16)

    def attention_weights(
        own, other, att_own, att_other, t0, t1, t2, t3, gain, shift, sums, heads, up_sums, wqkv_hbm,
        keep, send, dfirst_own, dfirst_send,
        ex, first, att, turned, chosen, vec, wqkv, sem,
    ):
        place = Place(inner)
        loads = []
        for n in range(3):
            cols = pl.ds(pl.multiple_of(n * 768 + place.y * 384, 128), 384)
            loads.append(pltpu.make_async_copy(wqkv_hbm.at[:, cols], wqkv.at[n], sem.at[n]))
        for load in loads:
            load.start()
        both_cores(place.core, own.at[pl.ds(0, 256)], other.at[pl.ds(0, 256)], ex)
        both_cores(place.core, att_own, att_other, att)
        for load in loads:
            load.wait()
        g, b = row(gain), row(shift)
        dgain = jnp.zeros((1, 768), F32)
        dshift = jnp.zeros((1, 768), F32)
        for s in range(2):
            for p, t in enumerate((t0, t1, t2, t3)):
                rows = pl.ds(p * 64, 64)
                xhat, _ = standardize(t[s].astype(F32))
                first[s, rows, :] = (xhat * g + b).astype(BF16)
                if p % 2 == 0:
                    part = nt(ex[s, rows, 0:384], wqkv[0])
                    part += nt(ex[s, rows, 384:768], wqkv[1])
                    part += nt(ex[s, rows, 768:1152], wqkv[2])
                    dgain += column_sum(part * xhat)
                    dshift += column_sum(part)
                    if p == 0:
                        dfirst_own[s] = part
                    else:
                        dfirst_send[s] = part.astype(BF16)
        for s in range(2):
            turned[:, pl.ds(s * 256, 256)] = first[s].T
        pick_rows(turned, chosen, place.core, place.x)
        product = nn(chosen[:, 0:256], ex[0, :, 0:1152]) + nn(chosen[:, 256:512], ex[1, :, 0:1152])
        put_slots(product.astype(BF16), keep, send, 0)
        for s in range(2):
            turned[:, pl.ds(s * 256, 256)] = att[s].T
        pick_rows(turned, chosen, place.core, place.x)
        product = nn(chosen[:, 0:256], ex[0, :, 1152:1536]) + nn(chosen[:, 256:512], ex[1, :, 1152:1536])
        put_slots(product.astype(BF16), keep, send, 432)
        vec[...] = jnp.zeros_like(vec)
        for s in range(SLOTS):
            k, z = flip(place.x, s % 2), s // 2
            lanes = slice(s * 96, s * 96 + 96)
            vec[k, z, 0:1, 0:96] = dgain[:, lanes]
            vec[k, z, 1:2, 0:96] = dshift[:, lanes]
            vec[k, z, 4:5, 0:96] = sums[0:1, lanes]
            vec[k, z, 5:6, 0:96] = sums[1:2, lanes]
            vec[k, z, 6:7, 0:96] = sums[2:3, lanes]
            vec[k, z, 11:12, 0:96] = sums[3:4, lanes]
        for h in range(2):
            for n in range(2):
                for r in range(2):
                    start = h * 192 + r * 96
                    vec[flip(place.x, h), 2 * n + place.y, 2 + r : 3 + r, 0:96] = heads[
                        n : n + 1, start : start + 96
                    ]
        for z in range(4):
            for r in range(4):
                start = z * 384 + r * 96
                vec[flip(place.x, place.core), z, 7 + r : 8 + r, 0:96] = up_sums[:, start : start + 96]
        for z in range(4):
            keep[z, pl.ds(576, 16), :] = vec[0, z].astype(BF16)
            send[z, pl.ds(576, 16), :] = vec[1, z].astype(BF16)

    def input_grad(tokens, dfirst, received, dhid, other, gain, out):
        place = Place(inner)
        g = row(gain)

        def write(s, residual):
            xhat, rstd = standardize(tokens[s].astype(F32))
            grad = dfirst[s] + received[s].astype(F32)
            out[s] = (residual + norm_back(xhat, rstd, grad * g)).astype(BF16)

        write(place.core, dhid[...])
        away = jnp.concatenate([other[256:288, 0:768], other[256:288, 768:1536]], axis=0)
        write(1 - place.core, away.astype(F32))

    def halve_z_low(keep, got, stay, leave):
        halve(Place(inner).z_low, keep, got, stay, leave)

    def halve_z_high(keep, got, stay, leave):
        halve(Place(inner).z_high, keep, got, stay, leave)

    def halve(bit, keep, got, stay, leave):
        for i in range(stay.shape[0]):
            for out, k in ((leave, 1), (stay, 0)):
                at = 2 * i + flip(bit, k)
                out[i] = (keep[at].astype(F32) + got[at].astype(F32)).astype(BF16)

    def add(a, b, out):
        out[...] = (a[...].astype(F32) + b[...].astype(F32)).astype(BF16)

    def assemble_up(p0, p1, p2, p3, out):
        place = Place(inner)
        for k, piece in enumerate((p0, p1, p2, p3)):
            y, core = flip(place.y, k // 2), flip(place.core, k % 2)
            rows = pl.ds(pl.multiple_of(y * 48, 16), 48)
            for j in range(4):
                for t in range(3):
                    cols = pl.ds(pl.multiple_of((2 * j + core) * 384 + t * 128, 128), 128)
                    out[rows, cols] = piece[0, pl.ds((3 * j + t) * 48, 48), :].astype(F32)

    def assemble_down(mine, across, partner, partner_across, out):
        place = Place(inner)

        def write(own, other):
            for k, piece in enumerate((own, other)):
                for t in range(3):
                    cols = pl.ds(pl.multiple_of(flip(place.y, k) * 384 + t * 128, 128), 128)
                    out[:, cols] = piece[0, pl.ds(t * 384, 384), :].astype(F32)

        @pl.when(place.core == place.x)
        def _():
            write(mine, across)

        @pl.when(place.core != place.x)
        def _():
            write(partner, partner_across)

    def assemble_rest(p0, p1, p2, p3, out_o, qkv_o, gain1, shift1, qv, out_b, gain2, shift2, up_b, down_b):
        place = Place(inner)
        total = jnp.zeros((16, 128), F32)
        for k, piece in enumerate((p0, p1, p2, p3)):
            y, core = flip(place.y, k // 2), flip(place.core, k % 2)
            rows = pl.ds(pl.multiple_of(core * 48, 16), 48)
            for t in range(3):
                cols = pl.ds(pl.multiple_of(y * 384 + t * 128, 128), 128)
                out_o[rows, cols] = piece[0, pl.ds(432 + t * 48, 48), :].astype(F32)
                for n in range(3):
                    cols = pl.ds(pl.multiple_of(n * 768 + y * 384 + t * 128, 128), 128)
                    qkv_o[rows, cols] = piece[0, pl.ds((3 * n + t) * 48, 48), :].astype(F32)
            total += piece[0, pl.ds(576, 16), :].astype(F32)

        def lay(out, start, count):
            parts = [total[start + r : start + r + 1, 0:96] for r in range(count)]
            out[...] = jnp.concatenate(parts, axis=1).reshape(count * 96)

        for out, start, count in (
            (gain1, 0, 1), (shift1, 1, 1), (qv, 2, 2), (out_b, 4, 1), (gain2, 5, 1), (shift2, 6, 1),
            (up_b, 7, 4), (down_b, 11, 1),
        ):
            lay(out, start, count)

    return locals()


def build(seq_size, blk_size):
    inner = seq_size // SLOTS
    kernels = build_kernels(inner)

    def swap(x, axis, size, step):
        return lax.ppermute(x, axis, [(i, i ^ step) for i in range(size)])

    def core_swap(x):
        return swap(x, "blk", blk_size, 1)

    def y_swap(x):
        return swap(x, "blk", blk_size, 2)

    def seq_swap(x, step):
        return swap(x, "seq", seq_size, step * inner)

    def some(x, moved):
        pairs = []
        for s in range(seq_size):
            for b in range(blk_size):
                to = moved(s, b)
                if to is not None:
                    pairs.append((s * blk_size + b, to[0] * blk_size + to[1]))
        return lax.ppermute(x, ("seq", "blk"), pairs)

    def aligned(s, b):
        return (s // inner) % 2 == b % 2

    def gather(x):
        across = y_swap(x)
        return x, core_swap(x), across, core_swap(across)

    def halve(name, keep, got, us):
        n, rows, lanes = keep.shape
        shape = ((n // 2, rows, lanes), BF16)
        return call(kernels[name], (shape, shape), [VMEM] * 2, (keep, got), us=us)

    def add(a, b):
        return call(kernels["add"], ((a.shape, BF16),), [VMEM] * 2, (a, b), us=1.0)[0]

    def on_device(
        tokens, ln1_gain, ln1_bias, wqkv, bias_qv, wout, output_bias, ln2_gain, ln2_bias,
        wup, up_bias, wdown, down_bias, segment_ids, dy,
    ):
        t_pieces = gather(tokens)
        d_pieces = gather(dy)
        up_row = up_bias.reshape(1, -1)
        att, mine = call(
            kernels["attention"],
            (((256, 768), BF16), ((256, 1152), BF16)),
            [VMEM] * 8 + [HBM],
            (segment_ids, *t_pieces, ln1_gain, ln1_bias, bias_qv, wqkv),
            [pltpu.VMEM((256, 768), BF16)] * 4
            + [pltpu.VMEM((3, 768, 768), BF16), pltpu.VMEM((256, 256), F32), pltpu.SemaphoreType.DMA((3,))],
            us=6.0,
        )
        att_other = core_swap(att)
        sec, dup, act, partial, dsec, part, hid_core, hid_own, dy_rows = call(
            kernels["feed"],
            (
                ((512, 768), BF16), ((512, 1536), BF16), ((512, 1536), BF16), ((384, 768), BF16),
                ((256, 768), F32), ((128, 768), F32), ((256, 768), F32), ((128, 768), F32), ((512, 768), BF16),
            ),
            [VMEM] * 14 + [HBM] * 3,
            (
                att, att_other, *t_pieces, output_bias, ln2_gain, ln2_bias, up_row, *d_pieces,
                wout, wup, wdown,
            ),
            [
                pltpu.VMEM((2, 256, 768), BF16), pltpu.VMEM((2, 256, 768), F32),
                pltpu.VMEM((768, 768), BF16), pltpu.VMEM((768, 1536), BF16), pltpu.VMEM((1536, 768), BF16),
                pltpu.SemaphoreType.DMA((9,)),
            ],
            us=9.0,
        )
        arrived = core_swap(partial)
        chunk, half = ((4, 576, 128), BF16), ((2, 1152, 128), BF16)
        up_keep, up_send, down_keep, down_send, up_sums = call(
            kernels["feed_weights"],
            (chunk, chunk, half, half, ((1, 1536), F32)),
            [VMEM] * 4,
            (sec, dup, act, dy_rows),
            [pltpu.VMEM((768, 512), BF16), pltpu.VMEM((384, 512), BF16)],
            us=3.0,
        )
        stay, leave = halve("halve_z_low", up_keep, seq_swap(up_send, 1), 1.0)
        stay, leave = halve("halve_z_high", stay, seq_swap(leave, 2), 1.0)
        up_sum = add(stay, seq_swap(leave, 4))
        stay, leave = halve("halve_z_high", down_keep, seq_swap(down_send, 2), 1.0)
        down_part = add(stay, seq_swap(leave, 4))
        down_sum = add(
            down_part,
            some(down_part, lambda s, b: None if aligned(s, b) else (s ^ inner, b)),
        )
        block_out, ex, dhid, sums, heads = call(
            kernels["attention_back"],
            (
                ((2, 64, 768), BF16), ((288, 1536), BF16), ((64, 768), F32), ((8, 768), F32), ((8, 384), F32),
            ),
            [VMEM] * 13 + [HBM],
            (
                dsec, arrived, part, hid_core, hid_own, *d_pieces, ln2_gain, down_bias, segment_ids, mine, wout,
            ),
            [
                pltpu.VMEM((384, 768), BF16), pltpu.VMEM((256, 768), BF16), pltpu.VMEM((256, 384), BF16),
                pltpu.VMEM((256, 256), F32), pltpu.SemaphoreType.DMA((1,)),
            ],
            us=4.0,
        )
        ex_other = core_swap(ex)
        rest = ((4, 592, 128), BF16)
        rest_keep, rest_send, dfirst_own, dfirst_send = call(
            kernels["attention_weights"],
            (rest, rest, ((2, 64, 768), F32), ((2, 64, 768), BF16)),
            [VMEM] * 13 + [HBM],
            (ex, ex_other, att, att_other, *t_pieces, ln1_gain, ln1_bias, sums, heads, up_sums, wqkv),
            [
                pltpu.VMEM((2, 256, 1536), BF16), pltpu.VMEM((2, 256, 768), BF16), pltpu.VMEM((2, 256, 768), BF16),
                pltpu.VMEM((768, 512), BF16), pltpu.VMEM((384, 512), BF16), pltpu.VMEM((2, 4, 16, 128), F32),
                pltpu.VMEM((3, 768, 384), BF16), pltpu.SemaphoreType.DMA((3,)),
            ],
            us=4.0,
        )
        stay, leave = halve("halve_z_low", rest_keep, seq_swap(rest_send, 1), 1.0)
        stay, leave = halve("halve_z_high", stay, seq_swap(leave, 2), 1.0)
        rest_sum = add(stay, seq_swap(leave, 4))
        (in_grad,) = call(
            kernels["input_grad"],
            (((2, 64, 768), BF16),),
            [VMEM] * 6,
            (tokens, dfirst_own, y_swap(dfirst_send), dhid, ex_other, ln1_gain),
            us=1.0,
        )
        (up_o,) = call(kernels["assemble_up"], (((96, 3072), F32),), [VMEM] * 4, gather(up_sum), us=1.0)
        across = some(down_sum, lambda s, b: (s, b ^ 2) if aligned(s, b) else None)
        to_core = lambda s, b: (s, b ^ 1) if aligned(s, b) else None
        (down_o,) = call(
            kernels["assemble_down"],
            (((384, 768), F32),),
            [VMEM] * 4,
            (down_sum, across, some(down_sum, to_core), some(across, to_core)),
            us=1.0,
        )
        small = [96, 96, 192, 96, 96, 96, 384, 96]
        out_o, qkv_o, *vectors = call(
            kernels["assemble_rest"],
            (((96, 768), F32), ((96, 2304), F32)) + tuple(((n,), F32) for n in small),
            [VMEM] * 4,
            gather(rest_sum),
            us=1.0,
        )
        gain1, shift1, qv, out_b, gain2, shift2, up_b, down_b = vectors
        outs = [gain1, shift1, qkv_o, qv, out_o, out_b, gain2, shift2, up_o, up_b, down_o, down_b]
        if inner > 1:
            groups = [list(range(g * inner, g * inner + inner)) for g in range(SLOTS)]
            outs = [
                lax.psum_scatter(o, "seq", scatter_dimension=0, axis_index_groups=groups, tiled=True)
                for o in outs
            ]
        return (block_out, in_grad, *outs)

    return on_device


def solution(mesh):
    data, vector, matrix = P("seq", "blk", None), P("seq"), P("seq", None)
    return jax.shard_map(
        build(mesh.shape["seq"], mesh.shape["blk"]),
        mesh=mesh,
        in_specs=(data,) + (P(),) * 12 + (matrix, data),
        out_specs=(
            data, data, vector, vector, matrix, vector, matrix, vector, vector, vector,
            matrix, vector, matrix, vector,
        ),
        check_vma=False,
    )
```

time: 740 us -> 110 us (0.15)
  waiting for transfers between devices: 531 us -> 41.9 us
  blocking collectives: 64.1 us -> 0 us
  matrix products: 52.1 us -> 0 us
  other arithmetic: 38.5 us -> 0 us
  starting transfers between devices: 0.47 us -> 32.5 us
  local copies, waits for them, and re-layouts: 36.4 us -> 5.72 us
  Pallas kernels: 0 us -> 28.9 us
  between operations: 16.6 us -> 0.92 us
    reduce_scatter x6 -> x0, waiting for transfers between devices: 530 us -> none  [the longest x1 164 us: on_device(): lax.psum_scatter(up_gradient, 'seq', scatter_dimension=0, tiled=True)]
    dot_general x18 -> x0, matrix products: 52.1 us -> none  [the longest x1 6.62 us: on_device(): jnp.einsum('mjw,mjr->wr', active_mask, block_output_gradient, preferred_e...]
    ppermute x0 -> x28, waiting for transfers between devices: none -> 41.9 us  [the longest x24 38.9 us: swap(): return lax.ppermute(x, axis, [(i, i ^ step) for i in range(size)])]
    unnamed x1 -> x0, blocking collectives: 36.8 us -> none
    ppermute x0 -> x28, starting transfers between devices: none -> 32.5 us  [the longest x24 23.4 us: swap(): return lax.ppermute(x, axis, [(i, i ^ step) for i in range(size)])]
    pallas_call x0 -> x18, Pallas kernels: none -> 28.9 us  [call(): pl.pallas_call(kernel, out_shape=tuple((jax.ShapeDtypeStruct(s, d) for s,...]
    convert_element_type x25 -> x0, other arithmetic: 27.2 us -> none  [the longest x1 2.15 us: on_device(): up_part.astype(jnp.bfloat16)]
    all_gather x2 -> x0, blocking collectives: 20.8 us -> none  [the longest x1 10.5 us: on_device(): lax.all_gather(values_local, 'blk', axis=1, tiled=True)]
  transfers between devices with their start and end apart: 7 -> 28, of which waited for: 6 -> 10; matrix products, arithmetic and copies ran while one was open for 10% -> 0% of each run, Pallas kernels for 0% -> 13%
where the time goes in v2:
time: 110 us
  waiting for transfers between devices  41.9 us (38%)
  starting transfers between devices  32.5 us (30%)
  Pallas kernels  28.9 us (26%)
  local copies, waits for them, and re-layouts  5.72 us (5%)
    ppermute x24, waiting for transfers between devices, swap(): return lax.ppermute(x, axis, [(i, i ^ step) for i in range(size)])  38.9 us
    pallas_call x18, Pallas kernels, call(): pl.pallas_call(kernel, out_shape=tuple((jax.ShapeDtypeStruct(s, d) for s,...  28.9 us
    ppermute x24, starting transfers between devices, swap(): return lax.ppermute(x, axis, [(i, i ^ step) for i in range(size)])  23.4 us
    ppermute x4, starting transfers between devices, some(): return lax.ppermute(x, ('seq', 'blk'), pairs)  9.12 us
    unnamed x38, local copies, waits for them, and re-layouts  5.71 us
    ppermute x4, waiting for transfers between devices, some(): return lax.ppermute(x, ('seq', 'blk'), pairs)  2.99 us
  transfers between devices with their start and end apart: 28, of which 10 were waited for; matrix products, arithmetic and copies ran while one was open for 0% of the time, Pallas kernels for 13%

profile of v2, /device:TPU:0, one launch (start us, length us, event | category | flops | bytes accessed | tf_op | source)
XLA Modules:
  0.0 109.9 jit_solution(17461689887340369291)
XLA Ops:
  0.7 3.0 %collective-permute-start.1 = (bf16[2,64,768]{2,1,0:T(8,128)(2,1)}, bf16[2,64,768]{2,1,0:T(8,128)(2,1)S(1)}, u32[]{:S(2)}, u32[]{:S(2)}) collective-permute-start(bf16[2,64,768]{2,1,0:T(8,128)(2,1)} %tokens.1), channel_id=1, source_target_pairs={{0,2},{1,3},{2,0},{3,1},{4,6},{5,7},{6,4},{7,5},{8,10},{9,11},{10,... | collective-permute-start | bytes 589832 | tf_op jit(solution)/shard_map/ppermute | solution.py:460
  3.7 5.1 %collective-permute-done.1.t2 = bf16[2,64,768]{2,1,0:T(8,128)(2,1)S(1)} collective-permute-done((bf16[2,64,768]{2,1,0:T(8,128)(2,1)}, bf16[2,64,768]{2,1,0:T(8,128)(2,1)S(1)}, u32[]{:S(2)}, u32[]{:S(2)}) %collective-permute-start.1) | collective-permute-done | bytes 196640 | tf_op jit(solution)/shard_map/ppermute | solution.py:460
  8.8 1.7 %collective-permute-start.5 = (bf16[2,64,768]{2,1,0:T(8,128)(2,1)}, bf16[2,64,768]{2,1,0:T(8,128)(2,1)S(1)}, u32[]{:S(2)}, u32[]{:S(2)}) collective-permute-start(bf16[2,64,768]{2,1,0:T(8,128)(2,1)} %d0.3), channel_id=1, source_target_pairs={{0,2},{1,3},{2,0},{3,1},{4,6},{5,7},{6,4},{7,5},{8,10},{9,11},{10,... | collective-permute-start | bytes 589832 | tf_op jit(solution)/shard_map/ppermute | solution.py:460
  10.6 2.0 %copy-done.2 = bf16[768,2304]{1,0:T(8,128)(2,1)S(1)} copy-done((bf16[768,2304]{1,0:T(8,128)(2,1)S(1)}, bf16[768,2304]{1,0:T(8,128)(2,1)}, u32[]{:S(2)}) %copy-start.2) | copy-done | bytes 3538968
  12.6 0.9 copy-done.6
  13.5 0.7 copy-done.8
  14.2 0.7 copy-done.11
  14.9 0.7 copy-done.14
  15.5 0.7 copy-done.16
  16.3 4.9 %attention.1 = (bf16[256,768]{1,0:T(8,128)(2,1)S(1)}, bf16[256,1152]{1,0:T(8,128)(2,1)S(1)}) custom-call(s32[2,256]{1,0:T(2,128)S(1)} %copy-done.11, bf16[2,64,768]{2,1,0:T(8,128)(2,1)S(1)} %copy-done.6, bf16[2,64,768]{2,1,0:T(8,128)(2,1)S(1)} %collective-permute-done.t1, bf16[2,64,768]{2,1,0:T(8,128)(2,1)S(1)} %collective-permute-done.1.t2, ...), custom_call_target="tpu_custom_call" | custom-call | flops 6000000000 | bytes 600000 | tf_op jit(solution)/shard_map/attention/pallas_call | solution.py:70
  21.1 0.3 collective-permute-start.3
  21.4 0.3 collective-permute-start.4
  21.7 0.2 collective-permute-start.6
  22.0 1.2 %collective-permute-done.4.d1 = bf16[2,64,768]{2,1,0:T(8,128)(2,1)S(1)} collective-permute-done((bf16[2,64,768]{2,1,0:T(8,128)(2,1)S(1)}, bf16[2,64,768]{2,1,0:T(8,128)(2,1)S(1)}, u32[]{:S(2)}, u32[]{:S(2)}) %collective-permute-start.4) | collective-permute-done | bytes 196640 | tf_op jit(solution)/shard_map/ppermute | solution.py:460
  23.2 0.3 collective-permute-done.6.d3
  23.6 8.7 %feed.1 = (bf16[512,768]{1,0:T(8,128)(2,1)S(1)}, bf16[512,1536]{1,0:T(8,128)(2,1)S(1)}, bf16[512,1536]{1,0:T(8,128)(2,1)S(1)}, bf16[384,768]{1,0:T(8,128)(2,1)S(...) custom-call(bf16[256,768]{1,0:T(8,128)(2,1)S(1)} %get-tuple-element., ...), custom_call_target="tpu_custom_call" | custom-call | flops 8999999488 | bytes 900000 | tf_op jit(solution)/shard_map/feed/pallas_call | solution.py:70
  32.2 0.3 collective-permute-start.7
  32.5 1.8 %collective-permute-done.7.got = bf16[384,768]{1,0:T(8,128)(2,1)S(1)} collective-permute-done((bf16[384,768]{1,0:T(8,128)(2,1)S(1)}, bf16[384,768]{1,0:T(8,128)(2,1)S(1)}, u32[]{:S(2)}, u32[]{:S(2)}) %collective-permute-start.7) | collective-permute-done | bytes 589856 | tf_op jit(solution)/shard_map/ppermute | solution.py:460
  34.3 4.4 %attention_back.1 = (bf16[2,64,768]{2,1,0:T(8,128)(2,1)}, bf16[288,1536]{1,0:T(8,128)(2,1)S(1)}, f32[64,768]{1,0:T(8,128)S(1)}, f32[8,768]{1,0:T(8,128)S(1)}, f32[8,384]{1,0:T(8,128)S(1)}) custom-call(f32[256,768]{1,0:T(8,128)S(1)} %get-tuple-element.60.dsec_in, bf16[384,768]{1,0:T(8,128)(2,1)S(1)} %collective-permute-done.7.got, ...), custom_call_target="tpu_custom_call" | custom-call | flops 4000000000 | bytes 400000 | tf_op jit(solution)/shard_map/attention_back/pallas_call | solution.py:70
  38.7 0.3 collective-permute-start.8
  39.0 2.0 %feed_weights.1 = (bf16[4,576,128]{2,1,0:T(8,128)(2,1)S(1)}, bf16[4,576,128]{2,1,0:T(8,128)(2,1)S(1)}, bf16[2,1152,128]{2,1,0:T(8,128)(2,1)S(1)}, bf16[2,1152,128]{2,1,0:T(8,128)(2,1)S(1)}, f32[1,1536]{1,0:T(1,128)S(1)}) custom-call(bf16[512,768]{1,0:T(8,128)(2,1)S(1)} %get-tuple-element.70.sec, bf16[512,1536]{1,0:T(8,128)(2,1)S(1)} %get-tuple-element.71.dup, ...), custom_call_target="tpu_custom_call" | custom-call | flops 3000000000 | bytes 300000 | tf_op jit(solution)/shard_map/feed_weights/pallas_call | solution.py:70
  41.0 1.6 %collective-permute-start.22 = (bf16[2,1152,128]{2,1,0:T(8,128)(2,1)S(1)}, bf16[2,1152,128]{2,1,0:T(8,128)(2,1)S(1)}, u32[]{:S(2)}, u32[]{:S(2)}) collective-permute-start(bf16[2,1152,128]{2,1,0:T(8,128)(2,1)S(1)} %get-tuple-element.100), channel_id=1, source_target_pairs={{0,8},{4,12},{8,0},{12,4},{16,24},{20,28},{24,16},{28,20},{1,9},{5... | collective-permute-start | bytes 1769480 | tf_op jit(solution)/shard_map/ppermute | solution.py:460
  42.7 1.5 %collective-permute-start.16 = (bf16[4,576,128]{2,1,0:T(8,128)(2,1)S(1)}, bf16[4,576,128]{2,1,0:T(8,128)(2,1)S(1)}, u32[]{:S(2)}, u32[]{:S(2)}) collective-permute-start(bf16[4,576,128]{2,1,0:T(8,128)(2,1)S(1)} %get-tuple-element.93), channel_id=1, source_target_pairs={{0,4},{4,0},{8,12},{12,8},{16,20},{20,16},{24,28},{28,24},{1,5},{5... | collective-permute-start | bytes 1769480 | tf_op jit(solution)/shard_map/ppermute | solution.py:460
  44.2 3.7 %attention_weights.1 = (bf16[4,592,128]{2,1,0:T(8,128)(2,1)S(1)}, bf16[4,592,128]{2,1,0:T(8,128)(2,1)S(1)}, f32[2,64,768]{2,1,0:T(8,128)S(1)}, bf16[2,64,768]{2,1,0:T(8,128)(2,1)S(1)}) custom-call(bf16[288,1536]{1,0:T(8,128)(2,1)S(1)} %get-tuple-element.67.own, bf16[288,1536]{1,0:T(8,128)(2,1)S(1)} %collective-permute-done.8.other, ...), custom_call_target="tpu_custom_call" | custom-call | flops 4000000000 | bytes 400000 | tf_op jit(solution)/shard_map/attention_weights/pallas_call | solution.py:70
  47.9 0.6 collective-permute-start.10
  48.5 8.1 %collective-permute-done.22.got = bf16[2,1152,128]{2,1,0:T(8,128)(2,1)S(1)} collective-permute-done((bf16[2,1152,128]{2,1,0:T(8,128)(2,1)S(1)}, bf16[2,1152,128]{2,1,0:T(8,128)(2,1)S(1)}, u32[]{:S(2)}, u32[]{:S(2)}) %collective-permute-start.22) | collective-permute-done | bytes 589856 | tf_op jit(solution)/shard_map/ppermute | solution.py:460
  56.7 2.7 %collective-permute-start.23 = (bf16[1,1152,128]{2,1,0:T(8,128)(2,1)S(1)}, bf16[1,1152,128]{2,1,0:T(8,128)(2,1)S(1)}, u32[]{:S(2)}, u32[]{:S(2)}) collective-permute-start(bf16[1,1152,128]{2,1,0:T(8,128)(2,1)S(1)} %get-tuple-element.102), channel_id=1, source_target_pairs={{0,16},{4,20},{8,24},{12,28},{16,0},{20,4},{24,8},{28,12},{1,17},{... | collective-permute-start | bytes 884744 | tf_op jit(solution)/shard_map/ppermute | solution.py:460
  59.6 1.6 %collective-permute-start.17 = (bf16[2,576,128]{2,1,0:T(8,128)(2,1)S(1)}, bf16[2,576,128]{2,1,0:T(8,128)(2,1)S(1)}, u32[]{:S(2)}, u32[]{:S(2)}) collective-permute-start(bf16[2,576,128]{2,1,0:T(8,128)(2,1)S(1)} %get-tuple-element.95), channel_id=1, source_target_pairs={{0,8},{4,12},{8,0},{12,4},{16,24},{20,28},{24,16},{28,20},{1,9},{5... | collective-permute-start | bytes 884744 | tf_op jit(solution)/shard_map/ppermute | solution.py:460
  61.2 11.3 %collective-permute-done.23.b = bf16[1,1152,128]{2,1,0:T(8,128)(2,1)S(1)} collective-permute-done((bf16[1,1152,128]{2,1,0:T(8,128)(2,1)S(1)}, bf16[1,1152,128]{2,1,0:T(8,128)(2,1)S(1)}, u32[]{:S(2)}, u32[]{:S(2)}) %collective-permute-start.23) | collective-permute-done | bytes 294944 | tf_op jit(solution)/shard_map/ppermute | solution.py:460
  72.6 1.3 %collective-permute-start.24 = (bf16[1,1152,128]{2,1,0:T(8,128)(2,1)S(1)}, bf16[1,1152,128]{2,1,0:T(8,128)(2,1)S(1)}, u32[]{:S(2)}, u32[]{:S(2)}) collective-permute-start(bf16[1,1152,128]{2,1,0:T(8,128)(2,1)S(1)} %add.6.a), channel_id=1, source_target_pairs={{1,5},{3,7},{4,0},{6,2},{9,13},{11,15},{12,8},{14,10},{17,21},{19,... | collective-permute-start | bytes 884744 | tf_op jit(solution)/shard_map/ppermute | solution.py:478
  74.1 0.6 collective-permute-start.11
  74.8 3.4 %collective-permute-start.18 = (bf16[1,576,128]{2,1,0:T(8,128)(2,1)S(1)}, bf16[1,576,128]{2,1,0:T(8,128)(2,1)S(1)}, u32[]{:S(2)}, u32[]{:S(2)}) collective-permute-start(bf16[1,576,128]{2,1,0:T(8,128)(2,1)S(1)} %get-tuple-element.97), channel_id=1, source_target_pairs={{0,16},{4,20},{8,24},{12,28},{16,0},{20,4},{24,8},{28,12},{1,17},{... | collective-permute-start | bytes 442376 | tf_op jit(solution)/shard_map/ppermute | solution.py:460
  78.2 3.0 %collective-permute-done.24.b = bf16[1,1152,128]{2,1,0:T(8,128)(2,1)S(1)} collective-permute-done((bf16[1,1152,128]{2,1,0:T(8,128)(2,1)S(1)}, bf16[1,1152,128]{2,1,0:T(8,128)(2,1)S(1)}, u32[]{:S(2)}, u32[]{:S(2)}) %collective-permute-start.24) | collective-permute-done | bytes 294944 | tf_op jit(solution)/shard_map/ppermute | solution.py:478
  81.3 3.4 %collective-permute-start.25 = (bf16[1,1152,128]{2,1,0:T(8,128)(2,1)S(1)}, bf16[1,1152,128]{2,1,0:T(8,128)(2,1)S(1)}, u32[]{:S(2)}, u32[]{:S(2)}) collective-permute-start(bf16[1,1152,128]{2,1,0:T(8,128)(2,1)S(1)} %add.7.mine), channel_id=1, source_target_pairs={{0,2},{2,0},{5,7},{7,5},{8,10},{10,8},{13,15},{15,13},{16,18},{18,... | collective-permute-start | bytes 884744 | tf_op jit(solution)/shard_map/ppermute | solution.py:478
  84.7 2.4 %collective-permute-done.11.got = bf16[2,592,128]{2,1,0:T(8,128)(2,1)S(1)} collective-permute-done((bf16[2,592,128]{2,1,0:T(8,128)(2,1)S(1)}, bf16[2,592,128]{2,1,0:T(8,128)(2,1)S(1)}, u32[]{:S(2)}, u32[]{:S(2)}) %collective-permute-start.11) | collective-permute-done | bytes 303136 | tf_op jit(solution)/shard_map/ppermute | solution.py:460
  87.2 0.9 collective-permute-start.12
  88.1 1.6 %collective-permute-start.20 = (bf16[1,576,128]{2,1,0:T(8,128)(2,1)S(1)}, bf16[1,576,128]{2,1,0:T(8,128)(2,1)S(1)}, u32[]{:S(2)}, u32[]{:S(2)}) collective-permute-start(bf16[1,576,128]{2,1,0:T(8,128)(2,1)S(1)} %add.5.p0), channel_id=1, source_target_pairs={{0,2},{1,3},{2,0},{3,1},{4,6},{5,7},{6,4},{7,5},{8,10},{9,11},{10,... | collective-permute-start | bytes 442376 | tf_op jit(solution)/shard_map/ppermute | solution.py:460
  89.7 0.4 collective-permute-start.19
  90.1 2.0 %collective-permute-start.26 = (bf16[1,1152,128]{2,1,0:T(8,128)(2,1)S(1)}, bf16[1,1152,128]{2,1,0:T(8,128)(2,1)S(1)}, u32[]{:S(2)}, u32[]{:S(2)}) collective-permute-start(bf16[1,1152,128]{2,1,0:T(8,128)(2,1)S(1)} %add.7.mine), channel_id=1, source_target_pairs={{0,1},{2,3},{5,4},{7,6},{8,9},{10,11},{13,12},{15,14},{16,17},{18,... | collective-permute-start | bytes 884744 | tf_op jit(solution)/shard_map/ppermute | solution.py:478
  92.1 2.5 %collective-permute-done.20.p2 = bf16[1,576,128]{2,1,0:T(8,128)(2,1)S(1)} collective-permute-done((bf16[1,576,128]{2,1,0:T(8,128)(2,1)S(1)}, bf16[1,576,128]{2,1,0:T(8,128)(2,1)S(1)}, u32[]{:S(2)}, u32[]{:S(2)}) %collective-permute-start.20) | collective-permute-done | bytes 147488 | tf_op jit(solution)/shard_map/ppermute | solution.py:460
  94.7 2.4 %collective-permute-start.27 = (bf16[1,1152,128]{2,1,0:T(8,128)(2,1)S(1)}, bf16[1,1152,128]{2,1,0:T(8,128)(2,1)S(1)}, u32[]{:S(2)}, u32[]{:S(2)}) collective-permute-start(bf16[1,1152,128]{2,1,0:T(8,128)(2,1)S(1)} %collective-permute-done.25.across), channel_id=1, source_target_pairs={{0,1},{2,3},{5,4},{7,6},{8,9},{10,11},{13,12},{15,14},{16,17},{18,... | collective-permute-start | bytes 884744 | tf_op jit(solution)/shard_map/ppermute | solution.py:478
  97.1 1.6 %collective-permute-start.9 = (bf16[2,64,768]{2,1,0:T(8,128)(2,1)S(1)}, bf16[2,64,768]{2,1,0:T(8,128)(2,1)S(1)}, u32[]{:S(2)}, u32[]{:S(2)}) collective-permute-start(bf16[2,64,768]{2,1,0:T(8,128)(2,1)S(1)} %get-tuple-element.76), channel_id=1, source_target_pairs={{0,2},{1,3},{2,0},{3,1},{4,6},{5,7},{6,4},{7,5},{8,10},{9,11},{10,... | collective-permute-start | bytes 589832 | tf_op jit(solution)/shard_map/ppermute | solution.py:460
  98.7 0.6 collective-permute-start.14
  99.3 1.1 %assemble_up.1 = f32[96,3072]{1,0:T(8,128)} custom-call(bf16[1,576,128]{2,1,0:T(8,128)(2,1)S(1)} %add.5.p0, bf16[1,576,128]{2,1,0:T(8,128)(2,1)S(1)} %collective-permute-done.19.p1, bf16[1,576,128]{2,1,0:T(8,128)(2,1)S(1)} %collective-permute-done.20.p2, bf16[1,576,128]{2,1,0:T(8,128)(2,1)S(1)} %collective-permute-done.21.p3), custom_call_target="tpu_custom_call" | custom-call | flops 1000000000 | bytes 100000 | tf_op jit(solution)/shard_map/assemble_up/pallas_call | solution.py:70
  100.5 6.1 %collective-permute-done.14.p2 = bf16[1,592,128]{2,1,0:T(8,128)(2,1)S(1)} collective-permute-done((bf16[1,592,128]{2,1,0:T(8,128)(2,1)S(1)}, bf16[1,592,128]{2,1,0:T(8,128)(2,1)S(1)}, u32[]{:S(2)}, u32[]{:S(2)}) %collective-permute-start.14) | collective-permute-done | bytes 151584 | tf_op jit(solution)/shard_map/ppermute | solution.py:460
  106.6 1.0 input_grad.1
  107.6 1.2 %assemble_down.1 = f32[384,768]{1,0:T(8,128)} custom-call(bf16[1,1152,128]{2,1,0:T(8,128)(2,1)S(1)} %add.7.mine, bf16[1,1152,128]{2,1,0:T(8,128)(2,1)S(1)} %collective-permute-done.25.across, bf16[1,1152,128]{2,1,0:T(8,128)(2,1)S(1)} %collective-permute-done.26.partner, bf16[1,1152,128]{2,1,0:T(8,128)(2,1)S(1)} %collective-permute-done.27.partner_across), custom_call_target="tpu_custom_call" | custom-call | flops 1000000000 | bytes 100000 | tf_op jit(solution)/shard_map/assemble_down/pallas_call | solution.py:70
  108.8 1.1 %assemble_rest.1 = (f32[96,768]{1,0:T(8,128)}, f32[96,2304]{1,0:T(8,128)}, f32[96]{0:T(128)}, f32[96]{0:T(128)}, f32[192]{0:T(256)}, /*index=5*/f32[96]{0:T(128)...) custom-call(bf16[1,592,128]{2,1,0:T(8,128)(2,1)S(1)} %add.4.p0, bf16[1,592,128]{2,1,0:T(8,128)(2,1)S(1)} %collective-permute-done.13.p1, ...), custom_call_target="tpu_custom_call" | custom-call | flops 1000000000 | bytes 100000 | tf_op jit(solution)/shard_map/assemble_rest/pallas_call | solution.py:70
  (65 shorter events, 1.0 us)
Async XLA Ops:
  0.6 22.9 %copy-start.1 = (bf16[3072,768]{1,0:T(8,128)(2,1)S(1)}, bf16[3072,768]{1,0:T(8,128)(2,1)}, u32[]{:S(2)}) copy-start(bf16[3072,768]{1,0:T(8,128)(2,1)} %wdown_hbm.1) | copy-start | bytes 14155780
  0.7 22.8 %copy-start = (bf16[768,3072]{1,0:T(8,128)(2,1)S(1)}, bf16[768,3072]{1,0:T(8,128)(2,1)}, u32[]{:S(2)}) copy-start(bf16[768,3072]{1,0:T(8,128)(2,1)} %wup_hbm.1) | copy-start | bytes 14155780
  0.7 8.1 %collective-permute-start.1 = (bf16[2,64,768]{2,1,0:T(8,128)(2,1)}, bf16[2,64,768]{2,1,0:T(8,128)(2,1)S(1)}, u32[]{:S(2)}, u32[]{:S(2)}) collective-permute-start(bf16[2,64,768]{2,1,0:T(8,128)(2,1)} %tokens.1), channel_id=1, source_target_pairs={{0,2},{1,3},{2,0},{3,1},{4,6},{5,7},{6,4},{7,5},{8,10},{9,11},{10,... | collective-permute-start | bytes 589832 | tf_op jit(solution)/shard_map/ppermute | solution.py:460
  3.7 6.9 %collective-permute-start = (bf16[2,64,768]{2,1,0:T(8,128)(2,1)}, bf16[2,64,768]{2,1,0:T(8,128)(2,1)S(1)}, u32[]{:S(2)}, u32[]{:S(2)}) collective-permute-start(bf16[2,64,768]{2,1,0:T(8,128)(2,1)} %tokens.1), channel_id=1, source_target_pairs={{0,1},{1,0},{2,3},{3,2},{4,5},{5,4},{6,7},{7,6},{8,9},{9,8},{10,11... | collective-permute-start | bytes 589832 | tf_op jit(solution)/shard_map/ppermute | solution.py:460
  8.8 1.8 %collective-permute-start.2 = (bf16[2,64,768]{2,1,0:T(8,128)(2,1)S(1)}, bf16[2,64,768]{2,1,0:T(8,128)(2,1)S(1)}, u32[]{:S(2)}, u32[]{:S(2)}) collective-permute-start(bf16[2,64,768]{2,1,0:T(8,128)(2,1)S(1)} %collective-permute-done.1.t2), channel_id=1, source_target_pairs={{0,1},{1,0},{2,3},{3,2},{4,5},{5,4},{6,7},{7,6},{8,9},{9,8},{10,11... | collective-permute-start | bytes 589832 | tf_op jit(solution)/shard_map/ppermute | solution.py:460
  8.8 12.9 %collective-permute-start.5 = (bf16[2,64,768]{2,1,0:T(8,128)(2,1)}, bf16[2,64,768]{2,1,0:T(8,128)(2,1)S(1)}, u32[]{:S(2)}, u32[]{:S(2)}) collective-permute-start(bf16[2,64,768]{2,1,0:T(8,128)(2,1)} %d0.3), channel_id=1, source_target_pairs={{0,2},{1,3},{2,0},{3,1},{4,6},{5,7},{6,4},{7,5},{8,10},{9,11},{10,... | collective-permute-start | bytes 589832 | tf_op jit(solution)/shard_map/ppermute | solution.py:460
  10.6 2.0 %copy-start.2 = (bf16[768,2304]{1,0:T(8,128)(2,1)S(1)}, bf16[768,2304]{1,0:T(8,128)(2,1)}, u32[]{:S(2)}) copy-start(bf16[768,2304]{1,0:T(8,128)(2,1)} %wqkv_hbm.3) | copy-start | bytes 10616836
  12.6 0.9 copy-start.6
  13.5 0.7 copy-start.8
  14.2 0.7 copy-start.11
  14.9 0.7 copy-start.14
  15.5 0.7 copy-start.16
  16.2 5.2 %copy-start.5 = (bf16[2,64,768]{2,1,0:T(8,128)(2,1)S(1)}, bf16[2,64,768]{2,1,0:T(8,128)(2,1)}, u32[]{:S(2)}) copy-start(bf16[2,64,768]{2,1,0:T(8,128)(2,1)} %d0.3) | copy-start | bytes 589828
  16.2 5.7 %copy-start.18 = (bf16[3072]{0:T(1024)(128)(2,1)S(1)}, bf16[3072]{0:T(1024)(128)(2,1)}, u32[]{:S(2)}) copy-start(bf16[3072]{0:T(1024)(128)(2,1)} %param.25) | copy-start | bytes 18436
  16.2 7.3 %copy-start.4 = (bf16[768,768]{1,0:T(8,128)(2,1)S(1)}, bf16[768,768]{1,0:T(8,128)(2,1)}, u32[]{:S(2)}) copy-start(bf16[768,768]{1,0:T(8,128)(2,1)} %wout_hbm.3) | copy-start | bytes 3538948
  16.2 7.3 %copy-start.7 = (bf16[2,64,768]{2,1,0:T(8,128)(2,1)S(1)}, bf16[2,64,768]{2,1,0:T(8,128)(2,1)}, u32[]{:S(2)}) copy-start(bf16[2,64,768]{2,1,0:T(8,128)(2,1)} %tokens.1) | copy-start | bytes 589828
  16.2 7.3 %copy-start.9 = (bf16[768]{0:T(1024)(128)(2,1)S(1)}, bf16[768]{0:T(1024)(128)(2,1)}, u32[]{:S(2)}) copy-start(bf16[768]{0:T(1024)(128)(2,1)} %out_bias.1) | copy-start | bytes 4612
  16.2 7.3 %copy-start.10 = (bf16[768]{0:T(1024)(128)(2,1)S(1)}, bf16[768]{0:T(1024)(128)(2,1)}, u32[]{:S(2)}) copy-start(bf16[768]{0:T(1024)(128)(2,1)} %shift.4) | copy-start | bytes 4612
  16.3 7.3 %copy-start.12 = (bf16[768]{0:T(1024)(128)(2,1)S(1)}, bf16[768]{0:T(1024)(128)(2,1)}, u32[]{:S(2)}) copy-start(bf16[768]{0:T(1024)(128)(2,1)} %gain.7) | copy-start | bytes 4612
  21.1 2.4 %collective-permute-start.3 = (bf16[256,768]{1,0:T(8,128)(2,1)S(1)}, bf16[256,768]{1,0:T(8,128)(2,1)S(1)}, u32[]{:S(2)}, u32[]{:S(2)}) collective-permute-start(bf16[256,768]{1,0:T(8,128)(2,1)S(1)} %get-tuple-element.59.att_own), channel_id=1, source_target_pairs={{0,1},{1,0},{2,3},{3,2},{4,5},{5,4},{6,7},{7,6},{8,9},{9,8},{10,11... | collective-permute-start | bytes 1179656 | tf_op jit(solution)/shard_map/ppermute | solution.py:460
  21.4 1.8 %collective-permute-start.4 = (bf16[2,64,768]{2,1,0:T(8,128)(2,1)S(1)}, bf16[2,64,768]{2,1,0:T(8,128)(2,1)S(1)}, u32[]{:S(2)}, u32[]{:S(2)}) collective-permute-start(bf16[2,64,768]{2,1,0:T(8,128)(2,1)S(1)} %copy-done.5), channel_id=1, source_target_pairs={{0,1},{1,0},{2,3},{3,2},{4,5},{5,4},{6,7},{7,6},{8,9},{9,8},{10,11... | collective-permute-start | bytes 589832 | tf_op jit(solution)/shard_map/ppermute | solution.py:460
  21.7 1.8 %collective-permute-start.6 = (bf16[2,64,768]{2,1,0:T(8,128)(2,1)S(1)}, bf16[2,64,768]{2,1,0:T(8,128)(2,1)S(1)}, u32[]{:S(2)}, u32[]{:S(2)}) collective-permute-start(bf16[2,64,768]{2,1,0:T(8,128)(2,1)S(1)} %collective-permute-done.5.d2), channel_id=1, source_target_pairs={{0,1},{1,0},{2,3},{3,2},{4,5},{5,4},{6,7},{7,6},{8,9},{9,8},{10,11... | collective-permute-start | bytes 589832 | tf_op jit(solution)/shard_map/ppermute | solution.py:460
  22.0 12.3 %copy-start.13 = (bf16[768]{0:T(1024)(128)(2,1)S(1)}, bf16[768]{0:T(1024)(128)(2,1)}, u32[]{:S(2)}) copy-start(bf16[768]{0:T(1024)(128)(2,1)} %down_bias.1) | copy-start | bytes 4612
  32.2 2.1 %collective-permute-start.7 = (bf16[384,768]{1,0:T(8,128)(2,1)S(1)}, bf16[384,768]{1,0:T(8,128)(2,1)S(1)}, u32[]{:S(2)}, u32[]{:S(2)}) collective-permute-start(bf16[384,768]{1,0:T(8,128)(2,1)S(1)} %get-tuple-element.61), channel_id=1, source_target_pairs={{0,1},{1,0},{2,3},{3,2},{4,5},{5,4},{6,7},{7,6},{8,9},{9,8},{10,11... | collective-permute-start | bytes 1769480 | tf_op jit(solution)/shard_map/ppermute | solution.py:460
  38.7 5.5 %collective-permute-start.8 = (bf16[288,1536]{1,0:T(8,128)(2,1)S(1)}, bf16[288,1536]{1,0:T(8,128)(2,1)S(1)}, u32[]{:S(2)}, u32[]{:S(2)}) collective-permute-start(bf16[288,1536]{1,0:T(8,128)(2,1)S(1)} %get-tuple-element.67.own), channel_id=1, source_target_pairs={{0,1},{1,0},{2,3},{3,2},{4,5},{5,4},{6,7},{7,6},{8,9},{9,8},{10,11... | collective-permute-start | bytes 2654216 | tf_op jit(solution)/shard_map/ppermute | solution.py:460
  39.0 5.2 %copy-start.3 = (bf16[768,2304]{1,0:T(8,128)(2,1)S(1)}, bf16[768,2304]{1,0:T(8,128)(2,1)}, u32[]{:S(2)}) copy-start(bf16[768,2304]{1,0:T(8,128)(2,1)} %wqkv_hbm.3) | copy-start | bytes 10616836
  39.0 5.2 %copy-start.15 = (bf16[768]{0:T(1024)(128)(2,1)S(1)}, bf16[768]{0:T(1024)(128)(2,1)}, u32[]{:S(2)}) copy-start(bf16[768]{0:T(1024)(128)(2,1)} %shift.5) | copy-start | bytes 4612
  39.0 5.2 %copy-start.17 = (bf16[768]{0:T(1024)(128)(2,1)S(1)}, bf16[768]{0:T(1024)(128)(2,1)}, u32[]{:S(2)}) copy-start(bf16[768]{0:T(1024)(128)(2,1)} %gain.9) | copy-start | bytes 4612
  41.0 15.6 %collective-permute-start.22 = (bf16[2,1152,128]{2,1,0:T(8,128)(2,1)S(1)}, bf16[2,1152,128]{2,1,0:T(8,128)(2,1)S(1)}, u32[]{:S(2)}, u32[]{:S(2)}) collective-permute-start(bf16[2,1152,128]{2,1,0:T(8,128)(2,1)S(1)} %get-tuple-element.100), channel_id=1, source_target_pairs={{0,8},{4,12},{8,0},{12,4},{16,24},{20,28},{24,16},{28,20},{1,9},{5... | collective-permute-start | bytes 1769480 | tf_op jit(solution)/shard_map/ppermute | solution.py:460
  42.7 16.7 %collective-permute-start.16 = (bf16[4,576,128]{2,1,0:T(8,128)(2,1)S(1)}, bf16[4,576,128]{2,1,0:T(8,128)(2,1)S(1)}, u32[]{:S(2)}, u32[]{:S(2)}) collective-permute-start(bf16[4,576,128]{2,1,0:T(8,128)(2,1)S(1)} %get-tuple-element.93), channel_id=1, source_target_pairs={{0,4},{4,0},{8,12},{12,8},{16,20},{20,16},{24,28},{28,24},{1,5},{5... | collective-permute-start | bytes 1769480 | tf_op jit(solution)/shard_map/ppermute | solution.py:460
  47.9 26.0 %collective-permute-start.10 = (bf16[4,592,128]{2,1,0:T(8,128)(2,1)S(1)}, bf16[4,592,128]{2,1,0:T(8,128)(2,1)S(1)}, u32[]{:S(2)}, u32[]{:S(2)}) collective-permute-start(bf16[4,592,128]{2,1,0:T(8,128)(2,1)S(1)} %get-tuple-element.79), channel_id=1, source_target_pairs={{0,4},{4,0},{8,12},{12,8},{16,20},{20,16},{24,28},{28,24},{1,5},{5... | collective-permute-start | bytes 1818632 | tf_op jit(solution)/shard_map/ppermute | solution.py:460
  56.7 15.8 %collective-permute-start.23 = (bf16[1,1152,128]{2,1,0:T(8,128)(2,1)S(1)}, bf16[1,1152,128]{2,1,0:T(8,128)(2,1)S(1)}, u32[]{:S(2)}, u32[]{:S(2)}) collective-permute-start(bf16[1,1152,128]{2,1,0:T(8,128)(2,1)S(1)} %get-tuple-element.102), channel_id=1, source_target_pairs={{0,16},{4,20},{8,24},{12,28},{16,0},{20,4},{24,8},{28,12},{1,17},{... | collective-permute-start | bytes 884744 | tf_op jit(solution)/shard_map/ppermute | solution.py:460
  59.6 15.1 %collective-permute-start.17 = (bf16[2,576,128]{2,1,0:T(8,128)(2,1)S(1)}, bf16[2,576,128]{2,1,0:T(8,128)(2,1)S(1)}, u32[]{:S(2)}, u32[]{:S(2)}) collective-permute-start(bf16[2,576,128]{2,1,0:T(8,128)(2,1)S(1)} %get-tuple-element.95), channel_id=1, source_target_pairs={{0,8},{4,12},{8,0},{12,4},{16,24},{20,28},{24,16},{28,20},{1,9},{5... | collective-permute-start | bytes 884744 | tf_op jit(solution)/shard_map/ppermute | solution.py:460
  72.6 8.6 %collective-permute-start.24 = (bf16[1,1152,128]{2,1,0:T(8,128)(2,1)S(1)}, bf16[1,1152,128]{2,1,0:T(8,128)(2,1)S(1)}, u32[]{:S(2)}, u32[]{:S(2)}) collective-permute-start(bf16[1,1152,128]{2,1,0:T(8,128)(2,1)S(1)} %add.6.a), channel_id=1, source_target_pairs={{1,5},{3,7},{4,0},{6,2},{9,13},{11,15},{12,8},{14,10},{17,21},{19,... | collective-permute-start | bytes 884744 | tf_op jit(solution)/shard_map/ppermute | solution.py:478
  74.1 13.0 %collective-permute-start.11 = (bf16[2,592,128]{2,1,0:T(8,128)(2,1)S(1)}, bf16[2,592,128]{2,1,0:T(8,128)(2,1)S(1)}, u32[]{:S(2)}, u32[]{:S(2)}) collective-permute-start(bf16[2,592,128]{2,1,0:T(8,128)(2,1)S(1)} %get-tuple-element.81), channel_id=1, source_target_pairs={{0,8},{4,12},{8,0},{12,4},{16,24},{20,28},{24,16},{28,20},{1,9},{5... | collective-permute-start | bytes 909320 | tf_op jit(solution)/shard_map/ppermute | solution.py:460
  74.8 13.3 %collective-permute-start.18 = (bf16[1,576,128]{2,1,0:T(8,128)(2,1)S(1)}, bf16[1,576,128]{2,1,0:T(8,128)(2,1)S(1)}, u32[]{:S(2)}, u32[]{:S(2)}) collective-permute-start(bf16[1,576,128]{2,1,0:T(8,128)(2,1)S(1)} %get-tuple-element.97), channel_id=1, source_target_pairs={{0,16},{4,20},{8,24},{12,28},{16,0},{20,4},{24,8},{28,12},{1,17},{... | collective-permute-start | bytes 442376 | tf_op jit(solution)/shard_map/ppermute | solution.py:460
  81.3 13.4 %collective-permute-start.25 = (bf16[1,1152,128]{2,1,0:T(8,128)(2,1)S(1)}, bf16[1,1152,128]{2,1,0:T(8,128)(2,1)S(1)}, u32[]{:S(2)}, u32[]{:S(2)}) collective-permute-start(bf16[1,1152,128]{2,1,0:T(8,128)(2,1)S(1)} %add.7.mine), channel_id=1, source_target_pairs={{0,2},{2,0},{5,7},{7,5},{8,10},{10,8},{13,15},{15,13},{16,18},{18,... | collective-permute-start | bytes 884744 | tf_op jit(solution)/shard_map/ppermute | solution.py:478
  87.2 9.9 %collective-permute-start.12 = (bf16[1,592,128]{2,1,0:T(8,128)(2,1)S(1)}, bf16[1,592,128]{2,1,0:T(8,128)(2,1)S(1)}, u32[]{:S(2)}, u32[]{:S(2)}) collective-permute-start(bf16[1,592,128]{2,1,0:T(8,128)(2,1)S(1)} %get-tuple-element.83), channel_id=1, source_target_pairs={{0,16},{4,20},{8,24},{12,28},{16,0},{20,4},{24,8},{28,12},{1,17},{... | collective-permute-start | bytes 454664 | tf_op jit(solution)/shard_map/ppermute | solution.py:460
  88.1 6.5 %collective-permute-start.20 = (bf16[1,576,128]{2,1,0:T(8,128)(2,1)S(1)}, bf16[1,576,128]{2,1,0:T(8,128)(2,1)S(1)}, u32[]{:S(2)}, u32[]{:S(2)}) collective-permute-start(bf16[1,576,128]{2,1,0:T(8,128)(2,1)S(1)} %add.5.p0), channel_id=1, source_target_pairs={{0,2},{1,3},{2,0},{3,1},{4,6},{5,7},{6,4},{7,5},{8,10},{9,11},{10,... | collective-permute-start | bytes 442376 | tf_op jit(solution)/shard_map/ppermute | solution.py:460
  89.7 9.0 %collective-permute-start.19 = (bf16[1,576,128]{2,1,0:T(8,128)(2,1)S(1)}, bf16[1,576,128]{2,1,0:T(8,128)(2,1)S(1)}, u32[]{:S(2)}, u32[]{:S(2)}) collective-permute-start(bf16[1,576,128]{2,1,0:T(8,128)(2,1)S(1)} %add.5.p0), channel_id=1, source_target_pairs={{0,1},{1,0},{2,3},{3,2},{4,5},{5,4},{6,7},{7,6},{8,9},{9,8},{10,11... | collective-permute-start | bytes 442376 | tf_op jit(solution)/shard_map/ppermute | solution.py:460
  90.1 17.5 %collective-permute-start.26 = (bf16[1,1152,128]{2,1,0:T(8,128)(2,1)S(1)}, bf16[1,1152,128]{2,1,0:T(8,128)(2,1)S(1)}, u32[]{:S(2)}, u32[]{:S(2)}) collective-permute-start(bf16[1,1152,128]{2,1,0:T(8,128)(2,1)S(1)} %add.7.mine), channel_id=1, source_target_pairs={{0,1},{2,3},{5,4},{7,6},{8,9},{10,11},{13,12},{15,14},{16,17},{18,... | collective-permute-start | bytes 884744 | tf_op jit(solution)/shard_map/ppermute | solution.py:478
  94.7 4.7 %collective-permute-start.21 = (bf16[1,576,128]{2,1,0:T(8,128)(2,1)S(1)}, bf16[1,576,128]{2,1,0:T(8,128)(2,1)S(1)}, u32[]{:S(2)}, u32[]{:S(2)}) collective-permute-start(bf16[1,576,128]{2,1,0:T(8,128)(2,1)S(1)} %collective-permute-done.20.p2), channel_id=1, source_target_pairs={{0,1},{1,0},{2,3},{3,2},{4,5},{5,4},{6,7},{7,6},{8,9},{9,8},{10,11... | collective-permute-start | bytes 442376 | tf_op jit(solution)/shard_map/ppermute | solution.py:460
  94.7 13.0 %collective-permute-start.27 = (bf16[1,1152,128]{2,1,0:T(8,128)(2,1)S(1)}, bf16[1,1152,128]{2,1,0:T(8,128)(2,1)S(1)}, u32[]{:S(2)}, u32[]{:S(2)}) collective-permute-start(bf16[1,1152,128]{2,1,0:T(8,128)(2,1)S(1)} %collective-permute-done.25.across), channel_id=1, source_target_pairs={{0,1},{2,3},{5,4},{7,6},{8,9},{10,11},{13,12},{15,14},{16,17},{18,... | collective-permute-start | bytes 884744 | tf_op jit(solution)/shard_map/ppermute | solution.py:478
  97.1 9.5 %collective-permute-start.9 = (bf16[2,64,768]{2,1,0:T(8,128)(2,1)S(1)}, bf16[2,64,768]{2,1,0:T(8,128)(2,1)S(1)}, u32[]{:S(2)}, u32[]{:S(2)}) collective-permute-start(bf16[2,64,768]{2,1,0:T(8,128)(2,1)S(1)} %get-tuple-element.76), channel_id=1, source_target_pairs={{0,2},{1,3},{2,0},{3,1},{4,6},{5,7},{6,4},{7,5},{8,10},{9,11},{10,... | collective-permute-start | bytes 589832 | tf_op jit(solution)/shard_map/ppermute | solution.py:460
  98.7 7.9 %collective-permute-start.14 = (bf16[1,592,128]{2,1,0:T(8,128)(2,1)S(1)}, bf16[1,592,128]{2,1,0:T(8,128)(2,1)S(1)}, u32[]{:S(2)}, u32[]{:S(2)}) collective-permute-start(bf16[1,592,128]{2,1,0:T(8,128)(2,1)S(1)} %add.4.p0), channel_id=1, source_target_pairs={{0,2},{1,3},{2,0},{3,1},{4,6},{5,7},{6,4},{7,5},{8,10},{9,11},{10,... | collective-permute-start | bytes 454664 | tf_op jit(solution)/shard_map/ppermute | solution.py:460
  100.5 8.4 %collective-permute-start.13 = (bf16[1,592,128]{2,1,0:T(8,128)(2,1)S(1)}, bf16[1,592,128]{2,1,0:T(8,128)(2,1)S(1)}, u32[]{:S(2)}, u32[]{:S(2)}) collective-permute-start(bf16[1,592,128]{2,1,0:T(8,128)(2,1)S(1)} %add.4.p0), channel_id=1, source_target_pairs={{0,1},{1,0},{2,3},{3,2},{4,5},{5,4},{6,7},{7,6},{8,9},{9,8},{10,11... | collective-permute-start | bytes 454664 | tf_op jit(solution)/shard_map/ppermute | solution.py:460
  106.6 2.2 %collective-permute-start.15 = (bf16[1,592,128]{2,1,0:T(8,128)(2,1)S(1)}, bf16[1,592,128]{2,1,0:T(8,128)(2,1)S(1)}, u32[]{:S(2)}, u32[]{:S(2)}) collective-permute-start(bf16[1,592,128]{2,1,0:T(8,128)(2,1)S(1)} %collective-permute-done.14.p2), channel_id=1, source_target_pairs={{0,1},{1,0},{2,3},{3,2},{4,5},{5,4},{6,7},{7,6},{8,9},{9,8},{10,11... | collective-permute-start | bytes 454664 | tf_op jit(solution)/shard_map/ppermute | solution.py:460

commit v3 on v2

v3 whole, which is shorter than its diff:
```python
import jax
import jax.numpy as jnp
from jax import lax
from jax.experimental import pallas as pl
from jax.experimental.pallas import tpu as pltpu
from jax.sharding import PartitionSpec as P

HEADS = 12
EPS = 1e-06
SLOTS = 8
F32 = jnp.float32
BF16 = jnp.bfloat16
GELU_C = 0.7978845608028654
GELU_A = 0.044715
US = 0.01
FILL = 20.0
VMEM = pl.BlockSpec(memory_space=pltpu.VMEM)
HBM = pl.BlockSpec(memory_space=pltpu.HBM)
ANY = pl.BlockSpec(memory_space=pl.ANY)


def nn(a, b):
    return lax.dot_general(a, b, (((1,), (0,)), ((), ())), preferred_element_type=F32)


def nt(a, b):
    return lax.dot_general(a, b, (((1,), (1,)), ((), ())), preferred_element_type=F32)


def tn(a, b):
    return lax.dot_general(a, b, (((0,), (0,)), ((), ())), preferred_element_type=F32)


def standardize(x):
    centered = x - jnp.mean(x, axis=-1, keepdims=True)
    rstd = lax.rsqrt(jnp.mean(centered * centered, axis=-1, keepdims=True) + EPS)
    return centered * rstd, rstd


def norm_back(xhat, rstd, g):
    return rstd * (
        g
        - jnp.mean(g, axis=-1, keepdims=True)
        - xhat * jnp.mean(g * xhat, axis=-1, keepdims=True)
    )


def row(ref):
    return ref[...].astype(F32).reshape(1, -1)


def half_masks():
    lane = lax.broadcasted_iota(jnp.int32, (1, 128), 1)
    low = jnp.where(lane < 64, 1.0, 0.0)
    return low.astype(BF16), (1.0 - low).astype(BF16)


def flip(bit, k):
    return lax.rem(bit + k, 2)


def softmax_rows(scores, same):
    scores = jnp.where(same > 0.0, scores, -1e9)
    e = jnp.exp(scores - jnp.max(scores, axis=-1, keepdims=True))
    return e * (1.0 / jnp.sum(e, axis=-1, keepdims=True))


def column_sum(x):
    return jnp.sum(x.astype(F32), axis=0, keepdims=True)


def call(kernel, outs, ins, args, scratch=(), limit=24, us=2.0):
    return pl.pallas_call(
        kernel,
        out_shape=tuple(jax.ShapeDtypeStruct(s, d) for s, d in outs),
        in_specs=ins,
        out_specs=tuple(VMEM for _ in outs),
        scratch_shapes=list(scratch),
        compiler_params=pltpu.CompilerParams(vmem_limit_bytes=limit * 1024 * 1024),
        cost_estimate=pl.CostEstimate(
            flops=int(us * 1e9), bytes_accessed=int(us * 1e5), transcendentals=0
        ),
        name=kernel.__name__,
    )(*args)


def in_hbm(*arrays):
    return tuple(pltpu.with_memory_space_constraint(a, pltpu.HBM) for a in arrays)


class Place:
    def __init__(self, inner):
        b = lax.axis_index("blk")
        slot = lax.axis_index("seq") // inner
        self.y, self.core = b // 2, lax.rem(b, 2)
        self.x, self.z_low, self.z_high = lax.rem(slot, 2), lax.rem(slot // 2, 2), slot // 4


def crop_mask(place, seg):
    ids = jnp.broadcast_to(seg[pl.ds(place.core, 1), :], (256, 256))
    first, second = ids[:, 0:128], ids[:, 128:256]
    tiles = jnp.where(place.y == 1, second, first), jnp.where(place.y == 1, first, second)
    tiles = [jnp.where(place.core == 1, pltpu.roll(t, 64, 1), t) for t in tiles]
    wide = jnp.concatenate(tiles, axis=1)
    return jnp.where(wide == wide.T, 1.0, 0.0)


def pick_rows(transposed, chosen, part, x_bit):
    for k in range(2):
        for z in range(4):
            start = pl.multiple_of((2 * z + flip(x_bit, k)) * 96 + part * 48, 16)
            chosen[pl.ds((4 * k + z) * 48, 48), :] = transposed[pl.ds(start, 48), :]


def put_slots(product, keep, send, offset):
    for t in range(product.shape[1] // 128):
        for z in range(4):
            tile = product[:, t * 128 : t * 128 + 128]
            keep[z, pl.ds(offset + t * 48, 48), :] = tile[z * 48 : z * 48 + 48]
            send[z, pl.ds(offset + t * 48, 48), :] = tile[192 + z * 48 : 240 + z * 48]


def gather_rows(pieces, out):
    for s in range(2):
        for p, piece in enumerate(pieces):
            out[pl.ds(s * 256 + p * 64, 64), :] = piece[s]


def both_cores(core, own, other, out):
    for p in range(4):
        out[core, pl.ds(p * 64, 64), :] = own[pl.ds(p * 64, 64), :]
        out[1 - core, pl.ds(p * 64, 64), :] = other[pl.ds((p ^ 1) * 64, 64), :]


def build_kernels(inner):
    def near(
        t1, tokens_hbm, seg_hbm, g1_hbm, s1_hbm, qv_hbm, ob_hbm, g2_hbm, s2_hbm, db_hbm, ub_hbm,
        wqkv_hbm, wout_hbm, wup_hbm, wdown_hbm,
        near_o, same_o, vec_o, up_bias_o, t0, wqkv, wout, wup, wdown,
        first, seg, g1, s1, qv, ob, g2, s2, db, ub, sem,
    ):
        place = Place(inner)
        pairs = [
            (g1_hbm, g1), (s1_hbm, s1), (qv_hbm, qv), (ob_hbm, ob), (g2_hbm, g2), (s2_hbm, s2),
            (db_hbm, db), (ub_hbm, ub), (seg_hbm, seg), (tokens_hbm, t0),
        ]
        small = len(pairs)
        pairs += [(wqkv_hbm.at[:, pl.ds(n * 768, 768)], wqkv.at[:, pl.ds(n * 768, 768)]) for n in range(3)]
        pairs.append((wout_hbm, wout))
        for j in range(4):
            units = pl.ds(pl.multiple_of((2 * j + place.core) * 384, 128), 384)
            mine = pl.ds(j * 384, 384)
            pairs += [(wup_hbm.at[:, units], wup.at[:, mine]), (wdown_hbm.at[units, :], wdown.at[mine, :])]
        loads = [pltpu.make_async_copy(a, b, sem.at[i]) for i, (a, b) in enumerate(pairs)]
        for load in loads:
            load.start()
        for load in loads[:small]:
            load.wait()
        both = row(qv)
        for r, value in enumerate(
            (row(g1), row(s1), both[:, 0:768], both[:, 768:1536], row(ob), row(g2), row(s2), row(db))
        ):
            vec_o[r : r + 1, :] = value
        flat = row(ub)
        for j in range(4):
            start = 2 * j * 384
            up_bias_o[:, pl.ds(j * 384, 384)] = jnp.where(
                place.core == 1, flat[:, start + 384 : start + 768], flat[:, start : start + 384]
            )
        same_o[...] = crop_mask(place, seg)
        for p, t in enumerate((t0, t1)):
            xhat, _ = standardize(t[place.core].astype(F32))
            first[pl.ds(p * 64, 64), :] = (xhat * vec_o[0:1, :] + vec_o[1:2, :]).astype(BF16)
        for n in range(3):
            loads[small + n].wait()
            project(n, first[...], wqkv, vec_o, near_o)
        for load in loads[small + 3 :]:
            load.wait()

    def project(n, first, wqkv, vec, out):
        cols = pl.ds(n * 768, 768)
        value = nn(first, wqkv[:, cols])
        if n != 1:
            value = value + vec[2 + n // 2 : 3 + n // 2, :]
        value = value.astype(BF16)
        out[:, cols] = value * BF16(0.125) if n == 0 else value

    def attention(near_in, same, vec, t2, t3, wqkv, att_o, mine_o, first, far, qkv):
        place = Place(inner)
        for p, t in enumerate((t2, t3)):
            xhat, _ = standardize(t[place.core].astype(F32))
            first[pl.ds(p * 64, 64), :] = (xhat * vec[0:1, :] + vec[1:2, :]).astype(BF16)
        for n in range(3):
            project(n, first[...], wqkv, vec, far)
        qkv[0:128, :] = near_in[...]
        qkv[128:256, :] = far[...]
        low, high = half_masks()
        for j in range(HEADS // 2):
            q, k, v = (qkv[:, pl.ds(n * 768 + j * 128, 128)] for n in range(3))
            out = None
            for keep in (low, high):
                probs = softmax_rows(nt(q * keep, k), same[...]).astype(BF16)
                part = nn(probs, v * keep)
                out = part if out is None else out + part
            att_o[:, pl.ds(j * 128, 128)] = out.astype(BF16)
        for n in range(3):
            half = pl.ds(pl.multiple_of(n * 768 + place.y * 384, 128), 384)
            mine_o[:, pl.ds(n * 384, 384)] = qkv[:, half]

    def feed(
        att_own, att_other, t0, t1, t2, t3, vec, up_bias, d0, d1, d2, d3, wout, wup, wdown,
        sec_o, dup_o, act_o, send_o, dsec_o, hid_core_o, hid_own_o, dy_o,
        att, hid,
    ):
        place = Place(inner)
        both_cores(place.core, att_own, att_other, att)
        gather_rows((d0, d1, d2, d3), dy_o)
        g, b, ob = vec[5:6, :], vec[6:7, :], vec[4:5, :]
        for s in range(2):
            added = nn(att[s], wout[...]) + ob
            for p, t in enumerate((t0, t1, t2, t3)):
                h = t[s].astype(F32) + added[p * 64 : p * 64 + 64]
                hid[s, pl.ds(p * 64, 64), :] = h
                xhat, _ = standardize(h)
                sec_o[pl.ds(s * 256 + p * 64, 64), :] = (xhat * g + b).astype(BF16)
            hid_own_o[pl.ds(s * 64, 64), :] = hid[s, 0:64, :]
        hid_core_o[...] = hid[place.core]
        for j in range(4):
            cols = pl.ds(j * 384, 384)
            for s in range(2):
                rows = pl.ds(s * 256, 256)
                up = nn(sec_o[rows, :], wup[:, cols]) + up_bias[:, cols]
                da = nt(dy_o[rows, :], wdown[cols, :])
                square = up * up
                tanh = jnp.tanh(up * (GELU_C + (GELU_C * GELU_A) * square))
                cdf = 0.5 + 0.5 * tanh
                act_o[rows, cols] = (up * cdf).astype(BF16)
                slope = cdf + (1.0 - tanh * tanh) * (
                    up * ((0.5 * GELU_C) + (1.5 * GELU_C * GELU_A) * square)
                )
                dup_o[rows, cols] = (da * slope).astype(BF16)
        away = nt(dup_o[pl.ds(pl.multiple_of((1 - place.core) * 256, 256), 256), :], wup[...])
        for p in range(4):
            send_o[pl.ds(p * 64, 64), :] = away[(p ^ 1) * 64 : (p ^ 1) * 64 + 64].astype(BF16)
        dsec_o[...] = nt(dup_o[pl.ds(pl.multiple_of(place.core * 256, 256), 256), :], wup[...])

    def feed_weights(sec, dup, act, dy, up_keep, up_send, down_keep, down_send, bias_o, turned, chosen):
        place = Place(inner)
        turned[...] = sec[...].T
        pick_rows(turned, chosen, place.y, place.x)
        for j in range(4):
            cols = pl.ds(j * 384, 384)
            put_slots(nn(chosen[...], dup[:, cols]).astype(BF16), up_keep, up_send, j * 144)
            bias_o[:, cols] = column_sum(dup[0:128, cols]) + column_sum(dup[256:384, cols])
        dy_half = dy[:, pl.ds(pl.multiple_of(place.y * 384, 128), 384)]
        for k, out in enumerate((down_keep, down_send)):
            for z in range(2):
                j = 2 * z + flip(place.z_low, k)
                units = pl.ds(pl.multiple_of(j * 384, 128), 384)
                product = tn(act[:, units], dy_half).astype(BF16)
                for t in range(3):
                    out[z, pl.ds(t * 384, 384), :] = product[:, t * 128 : t * 128 + 128]

    def attention_back(
        dsec_in, got, hid_core, d0, d1, d2, d3, vec, same, mine, wout, up_sums,
        exa_o, exb_o, dhid_o, sums_o, heads_o,
        dh, datt,
    ):
        place = Place(inner)
        g = vec[5:6, :]
        sums = [jnp.zeros((1, 768), F32)] * 3
        for p, d in enumerate((d0, d1, d2, d3)):
            rows = pl.ds(p * 64, 64)
            xhat, rstd = standardize(hid_core[rows, :])
            grad = dsec_in[rows, :] + got[rows, :].astype(F32)
            dhid = d[place.core].astype(F32) + norm_back(xhat, rstd, grad * g)
            low = dhid.astype(BF16)
            dh[rows, :] = low
            if p < 2:
                sums = [a + column_sum(v) for a, v in zip(sums, (low, grad * xhat, grad))]
            if p == 0:
                dhid_o[...] = dhid
            if p == 1:
                exb_o[pl.ds(256, 64), :] = low
        for r in range(3):
            sums_o[r : r + 1, :] = sums[r]
        sums_o[3:4, :] = column_sum(d0[0]) + column_sum(d0[1])
        sums_o[4:8, :] = jnp.zeros((4, 768), F32)
        exb_o[0:256, 384:768] = dh[:, pl.ds(pl.multiple_of(place.y * 384, 128), 384)]
        datt[...] = nt(dh[...], wout[pl.ds(pl.multiple_of(place.y * 384, 128), 384), :]).astype(BF16)
        low, high = half_masks()
        for j in range(HEADS // 4):
            cols = pl.ds(j * 128, 128)
            q, k, v = (mine[:, pl.ds(n * 384 + j * 128, 128)] for n in range(3))
            da = datt[:, cols]
            dq = dk = dv = None
            for keep in (low, high):
                qh, kh, dah = q * keep, k * keep, da * keep
                probs = softmax_rows(nt(qh, k), same[...])
                dprobs = nt(dah, v)
                delta = jnp.sum(probs * dprobs, axis=-1, keepdims=True)
                ds = (probs * (dprobs - delta)).astype(BF16)
                parts = nn(ds, kh), tn(ds, qh), tn(probs.astype(BF16), dah)
                if dq is None:
                    dq, dk, dv = parts
                else:
                    dq, dk, dv = dq + parts[0], dk + parts[1], dv + parts[2]
            dq = (dq * 0.125).astype(BF16)
            dv = dv.astype(BF16)
            exa_o[:, cols] = dq
            exa_o[:, pl.ds(384 + j * 128, 128)] = dk.astype(BF16)
            exb_o[0:256, cols] = dv
            heads_o[0:1, cols] = column_sum(dq)
            heads_o[1:2, cols] = column_sum(dv)
        heads_o[2:8, :] = jnp.zeros((6, 384), F32)

    def turn(
        att_own, att_other, t0, t1, t2, t3, params, act, wdown, before,
        first_o, att_o, part_o, part_send,
        first, att, turned,
    ):
        place = Place(inner)
        both_cores(place.core, att_own, att_other, att)
        for s in range(2):
            for p, t in enumerate((t0, t1, t2, t3)):
                xhat, _ = standardize(t[s].astype(F32))
                first[s, pl.ds(p * 64, 64), :] = (xhat * params[0:1, :] + params[1:2, :]).astype(BF16)
        for source, chosen in ((first, first_o), (att, att_o)):
            for s in range(2):
                turned[:, pl.ds(s * 256, 256)] = source[s].T
            pick_rows(turned, chosen, place.core, place.x)
        for s in range(2):
            part = nn(act[pl.ds(s * 256, 128), :], wdown[...])
            part_o[s] = part[0:64]
            part_send[s] = part[64:128].astype(BF16)

    def attention_weights(
        owna, ownb, othera, otherb, first, att, t0, t2, params, sums, heads, up_sums, wqkv,
        keep, send, dfirst_own, dfirst_send,
        exa, exb, vec,
    ):
        place = Place(inner)
        weights = [wqkv[:, pl.ds(pl.multiple_of(n * 768 + place.y * 384, 128), 384)] for n in range(3)]
        both_cores(place.core, owna, othera, exa)
        both_cores(place.core, ownb, otherb, exb)
        for chosen, source, lanes, offset in (
            (first, exa, slice(0, 768), 0),
            (first, exb, slice(0, 384), 288),
            (att, exb, slice(384, 768), 432),
        ):
            product = nn(chosen[:, 0:256], source[0, :, lanes]) + nn(chosen[:, 256:512], source[1, :, lanes])
            put_slots(product.astype(BF16), keep, send, offset)
        dgain = jnp.zeros((1, 768), F32)
        dshift = jnp.zeros((1, 768), F32)
        for s in range(2):
            for p, t in ((0, t0), (2, t2)):
                rows = pl.ds(p * 64, 64)
                xhat, _ = standardize(t[s].astype(F32))
                part = nt(exa[s, rows, 0:384], weights[0])
                part += nt(exa[s, rows, 384:768], weights[1])
                part += nt(exb[s, rows, 0:384], weights[2])
                dgain += column_sum(part * xhat)
                dshift += column_sum(part)
                if p == 0:
                    dfirst_own[s] = part
                else:
                    dfirst_send[s] = part.astype(BF16)
        vec[...] = jnp.zeros_like(vec)
        for s in range(SLOTS):
            k, z = flip(place.x, s % 2), s // 2
            lanes = slice(s * 96, s * 96 + 96)
            vec[k, z, 0:1, 0:96] = dgain[:, lanes]
            vec[k, z, 1:2, 0:96] = dshift[:, lanes]
            vec[k, z, 4:5, 0:96] = sums[0:1, lanes]
            vec[k, z, 5:6, 0:96] = sums[1:2, lanes]
            vec[k, z, 6:7, 0:96] = sums[2:3, lanes]
            vec[k, z, 11:12, 0:96] = sums[3:4, lanes]
        for h in range(2):
            for n in range(2):
                for r in range(2):
                    start = h * 192 + r * 96
                    vec[flip(place.x, h), 2 * n + place.y, 2 + r : 3 + r, 0:96] = heads[
                        n : n + 1, start : start + 96
                    ]
        for z in range(4):
            for r in range(4):
                start = z * 384 + r * 96
                vec[flip(place.x, place.core), z, 7 + r : 8 + r, 0:96] = up_sums[:, start : start + 96]
        for z in range(4):
            keep[z, pl.ds(576, 16), :] = vec[0, z].astype(BF16)
            send[z, pl.ds(576, 16), :] = vec[1, z].astype(BF16)

    def input_grad(tokens, dfirst, received, dhid, other, vec, hid_own, part, part_got, out, block_o):
        place = Place(inner)

        def write(s, residual):
            xhat, rstd = standardize(tokens[s].astype(F32))
            grad = dfirst[s] + received[s].astype(F32)
            out[s] = (residual + norm_back(xhat, rstd, grad * vec[0:1, :])).astype(BF16)

        write(place.core, dhid[...])
        write(1 - place.core, other[256:320, :].astype(F32))
        for s in range(2):
            added = part[s] + part_got[s].astype(F32) + vec[7:8, :]
            block_o[s] = (hid_own[pl.ds(s * 64, 64), :] + added).astype(BF16)

    def halve_z_low(keep, got, before, stay, leave):
        halve(Place(inner).z_low, keep, got, stay, leave)

    def halve_z_high(keep, got, before, stay, leave):
        halve(Place(inner).z_high, keep, got, stay, leave)

    def halve(bit, keep, got, stay, leave):
        for i in range(stay.shape[0]):
            for out, k in ((leave, 1), (stay, 0)):
                at = 2 * i + flip(bit, k)
                out[i] = (keep[at].astype(F32) + got[at].astype(F32)).astype(BF16)

    def add(a, b, before, out):
        out[...] = (a[...].astype(F32) + b[...].astype(F32)).astype(BF16)

    def assemble_up(p0, p1, p2, p3, out):
        place = Place(inner)
        for k, piece in enumerate((p0, p1, p2, p3)):
            y, core = flip(place.y, k // 2), flip(place.core, k % 2)
            rows = pl.ds(pl.multiple_of(y * 48, 16), 48)
            for j in range(4):
                for t in range(3):
                    cols = pl.ds(pl.multiple_of((2 * j + core) * 384 + t * 128, 128), 128)
                    out[rows, cols] = piece[0, pl.ds((3 * j + t) * 48, 48), :].astype(F32)

    def assemble_down(mine, across, partner, partner_across, out):
        place = Place(inner)

        def write(own, other):
            for k, piece in enumerate((own, other)):
                for t in range(3):
                    cols = pl.ds(pl.multiple_of(flip(place.y, k) * 384 + t * 128, 128), 128)
                    out[:, cols] = piece[0, pl.ds(t * 384, 384), :].astype(F32)

        @pl.when(place.core == place.x)
        def _():
            write(mine, across)

        @pl.when(place.core != place.x)
        def _():
            write(partner, partner_across)

    def assemble_rest(p0, p1, p2, p3, out_o, qkv_o, gain1, shift1, qv, out_b, gain2, shift2, up_b, down_b):
        place = Place(inner)
        total = jnp.zeros((16, 128), F32)
        for k, piece in enumerate((p0, p1, p2, p3)):
            y, core = flip(place.y, k // 2), flip(place.core, k % 2)
            rows = pl.ds(pl.multiple_of(core * 48, 16), 48)
            for t in range(3):
                cols = pl.ds(pl.multiple_of(y * 384 + t * 128, 128), 128)
                out_o[rows, cols] = piece[0, pl.ds(432 + t * 48, 48), :].astype(F32)
                for n in range(3):
                    cols = pl.ds(pl.multiple_of(n * 768 + y * 384 + t * 128, 128), 128)
                    qkv_o[rows, cols] = piece[0, pl.ds((3 * n + t) * 48, 48), :].astype(F32)
            total += piece[0, pl.ds(576, 16), :].astype(F32)

        def lay(out, start, count):
            parts = [total[start + r : start + r + 1, 0:96] for r in range(count)]
            out[...] = jnp.concatenate(parts, axis=1).reshape(count * 96)

        for out, start, count in (
            (gain1, 0, 1), (shift1, 1, 1), (qv, 2, 2), (out_b, 4, 1), (gain2, 5, 1), (shift2, 6, 1),
            (up_b, 7, 4), (down_b, 11, 1),
        ):
            lay(out, start, count)

    return locals()


def build(seq_size, blk_size):
    inner = seq_size // SLOTS
    kernels = build_kernels(inner)

    def swap(x, axis, size, step):
        return lax.ppermute(x, axis, [(i, i ^ step) for i in range(size)])

    def core_swap(x):
        return swap(x, "blk", blk_size, 1)

    def y_swap(x):
        return swap(x, "blk", blk_size, 2)

    def seq_swap(x, step):
        return swap(x, "seq", seq_size, step * inner)

    def some(x, moved):
        pairs = []
        for s in range(seq_size):
            for b in range(blk_size):
                to = moved(s, b)
                if to is not None:
                    pairs.append((s * blk_size + b, to[0] * blk_size + to[1]))
        return lax.ppermute(x, ("seq", "blk"), pairs)

    def aligned(s, b):
        return (s // inner) % 2 == b % 2

    def gather(x):
        across = y_swap(x)
        return x, core_swap(x), across, core_swap(across)

    def halve(name, keep, got, before):
        n, rows, lanes = keep.shape
        shape = ((n // 2, rows, lanes), BF16)
        return call(kernels[name], (shape, shape), [VMEM, VMEM, ANY], (keep, got, before), us=US)

    def add(a, b, before):
        return call(kernels["add"], ((a.shape, BF16),), [VMEM, VMEM, ANY], (a, b, before), us=US)[0]

    def on_device(
        tokens, ln1_gain, ln1_bias, wqkv, bias_qv, wout, output_bias, ln2_gain, ln2_bias,
        wup, up_bias, wdown, down_bias, segment_ids, dy,
    ):
        t1 = core_swap(tokens)
        t2 = y_swap(tokens)
        hbm = in_hbm(
            tokens, segment_ids, ln1_gain, ln1_bias, bias_qv, output_bias, ln2_gain, ln2_bias, down_bias,
            up_bias, wqkv, wout, wup, wdown,
        )
        near_qkv, same, vec, up_row, t0, wqkv, wout, wup, wdown = call(
            kernels["near"],
            (
                ((128, 2304), BF16), ((256, 256), F32), ((8, 768), F32), ((1, 1536), F32), ((2, 64, 768), BF16),
                ((768, 2304), BF16), ((768, 768), BF16), ((768, 1536), BF16), ((1536, 768), BF16),
            ),
            [VMEM] + [HBM] * 14,
            (t1, *hbm),
            [pltpu.VMEM((128, 768), BF16), pltpu.VMEM((2, 256), jnp.int32)]
            + [pltpu.VMEM((n,), BF16) for n in (768, 768, 1536, 768, 768, 768, 768, 3072)]
            + [pltpu.SemaphoreType.DMA((22,))],
            us=3.0,
        )
        near_qkv, t2 = lax.optimization_barrier((near_qkv, t2))
        t3 = core_swap(t2)
        t_pieces = t0, t1, t2, t3
        d_pieces = gather(dy)
        att, mine = call(
            kernels["attention"],
            (((256, 768), BF16), ((256, 1152), BF16)),
            [VMEM] * 6,
            (near_qkv, same, vec, t2, t3, wqkv),
            [pltpu.VMEM((128, 768), BF16), pltpu.VMEM((128, 2304), BF16), pltpu.VMEM((256, 2304), BF16)],
            us=US,
        )
        att_other = core_swap(att)
        chunk, half = ((4, 576, 128), BF16), ((2, 1152, 128), BF16)
        own = (2, 64, 768)
        sec, dup, act, partial, dsec, hid_core, hid_own, dy_rows = call(
            kernels["feed"],
            (
                ((512, 768), BF16), ((512, 1536), BF16), ((512, 1536), BF16), ((256, 768), BF16),
                ((256, 768), F32), ((256, 768), F32), ((128, 768), F32), ((512, 768), BF16),
            ),
            [VMEM] * 15,
            (att, att_other, *t_pieces, vec, up_row, *d_pieces, wout, wup, wdown),
            [pltpu.VMEM((2, 256, 768), BF16), pltpu.VMEM((2, 256, 768), F32)],
            us=US,
        )
        arrived = core_swap(partial)
        up_keep, up_send, down_keep, down_send, up_sums = call(
            kernels["feed_weights"],
            (chunk, chunk, half, half, ((1, 1536), F32)),
            [VMEM] * 4,
            (sec, dup, act, dy_rows),
            [pltpu.VMEM((768, 512), BF16), pltpu.VMEM((384, 512), BF16)],
            us=FILL,
        )
        exa, exb, dhid, sums, heads = call(
            kernels["attention_back"],
            (((256, 768), BF16), ((320, 768), BF16), ((64, 768), F32), ((8, 768), F32), ((8, 384), F32)),
            [VMEM] * 12,
            (dsec, arrived, hid_core, *d_pieces, vec, same, mine, wout, up_sums),
            [pltpu.VMEM((256, 768), BF16), pltpu.VMEM((256, 384), BF16)],
            us=US,
        )
        exa_other, exb_other = core_swap(exa), core_swap(exb)
        rest = ((4, 592, 128), BF16)
        first_t, att_t, part, part_send = call(
            kernels["turn"],
            (((384, 512), BF16), ((384, 512), BF16), (own, F32), (own, BF16)),
            [VMEM] * 9 + [ANY],
            (att, att_other, *t_pieces, vec, act, wdown, sums),
            [pltpu.VMEM((2, 256, 768), BF16), pltpu.VMEM((2, 256, 768), BF16), pltpu.VMEM((768, 512), BF16)],
            us=FILL,
        )
        rest_keep, rest_send, dfirst_own, dfirst_send = call(
            kernels["attention_weights"],
            (rest, rest, (own, F32), (own, BF16)),
            [VMEM] * 13,
            (exa, exb, exa_other, exb_other, first_t, att_t, t0, t2, vec, sums, heads, up_sums, wqkv),
            [
                pltpu.VMEM((2, 256, 768), BF16), pltpu.VMEM((2, 256, 768), BF16),
                pltpu.VMEM((2, 4, 16, 128), F32),
            ],
            us=US,
        )
        down_stay, down_leave = halve("halve_z_high", down_keep, seq_swap(down_send, 2), rest_keep)
        up_stay, up_leave = halve("halve_z_low", up_keep, seq_swap(up_send, 1), down_stay)
        down_part = add(down_stay, seq_swap(down_leave, 4), up_stay)
        up_stay, up_leave = halve("halve_z_high", up_stay, seq_swap(up_leave, 2), down_part)
        rest_stay, rest_leave = halve("halve_z_low", rest_keep, seq_swap(rest_send, 1), up_stay)
        over_x = some(down_part, lambda s, b: None if aligned(s, b) else (s ^ inner, b))
        down_sum = add(down_part, over_x, rest_stay)
        up_sum = add(up_stay, seq_swap(up_leave, 4), down_sum)
        rest_stay, rest_leave = halve("halve_z_high", rest_stay, seq_swap(rest_leave, 2), up_sum)
        rest_sum = add(rest_stay, seq_swap(rest_leave, 4), up_sum)
        up_pieces = gather(up_sum)
        across = some(down_sum, lambda s, b: (s, b ^ 2) if aligned(s, b) else None)
        to_core = lambda s, b: (s, b ^ 1) if aligned(s, b) else None
        down_pieces = down_sum, across, some(down_sum, to_core), some(across, to_core)
        in_grad, block_out = call(
            kernels["input_grad"],
            ((own, BF16), (own, BF16)),
            [VMEM] * 9,
            (
                t0, dfirst_own, y_swap(dfirst_send), dhid, exb_other, vec, hid_own, part,
                core_swap(part_send),
            ),
            us=US,
        )
        (up_o,) = call(kernels["assemble_up"], (((96, 3072), F32),), [VMEM] * 4, up_pieces, us=US)
        (down_o,) = call(kernels["assemble_down"], (((384, 768), F32),), [VMEM] * 4, down_pieces, us=US)
        small = [96, 96, 192, 96, 96, 96, 384, 96]
        across = y_swap(rest_sum)
        hop, in_grad, up_o, down_o = lax.optimization_barrier((across, in_grad, up_o, down_o))
        out_o, qkv_o, *vectors = call(
            kernels["assemble_rest"],
            (((96, 768), F32), ((96, 2304), F32)) + tuple(((n,), F32) for n in small),
            [VMEM] * 4,
            (rest_sum, core_swap(rest_sum), hop, core_swap(hop)),
            us=US,
        )
        gain1, shift1, qv, out_b, gain2, shift2, up_b, down_b = vectors
        outs = [gain1, shift1, qkv_o, qv, out_o, out_b, gain2, shift2, up_o, up_b, down_o, down_b]
        if inner > 1:
            groups = [list(range(g * inner, g * inner + inner)) for g in range(SLOTS)]
            outs = [
                lax.psum_scatter(o, "seq", scatter_dimension=0, axis_index_groups=groups, tiled=True)
                for o in outs
            ]
        return (block_out, in_grad, *outs)

    return on_device


def solution(mesh):
    data, vector, matrix = P("seq", "blk", None), P("seq"), P("seq", None)
    return jax.shard_map(
        build(mesh.shape["seq"], mesh.shape["blk"]),
        mesh=mesh,
        in_specs=(data,) + (P(),) * 12 + (matrix, data),
        out_specs=(
            data, data, vector, vector, matrix, vector, matrix, vector, vector, vector,
            matrix, vector, matrix, vector,
        ),
        check_vma=False,
    )
```

time: 110 us -> 93.5 us (0.85)
  waiting for transfers between devices: 41.9 us -> 29.8 us
  local copies, waits for them, and re-layouts: 5.72 us -> 0.01 us
    ppermute x24 -> x26, waiting for transfers between devices: 38.9 us -> 26.8 us  [swap(): return lax.ppermute(x, axis, [(i, i ^ step) for i in range(size)])]
    unnamed x38 -> x2, local copies, waits for them, and re-layouts: 5.71 us -> 0.01 us
    ppermute x24 -> x26, starting transfers between devices: 23.4 us -> 25.5 us  [swap(): return lax.ppermute(x, axis, [(i, i ^ step) for i in range(size)])]
    ppermute x4, starting transfers between devices: 9.12 us -> 7.9 us  [some(): return lax.ppermute(x, ('seq', 'blk'), pairs)]
    pallas_call x18 -> x20, Pallas kernels: 28.9 us -> 29.2 us  [call(): pl.pallas_call(kernel, out_shape=tuple((jax.ShapeDtypeStruct(s, d) for s,...]
  transfers between devices with their start and end apart: 28 -> 30, of which waited for: 10 -> 14; matrix products, arithmetic and copies ran while one was open for 0% -> 0% of each run, Pallas kernels for 13% -> 24%
where the time goes in v3:
time: 93.5 us; the launch traced here: 93.3 us
  starting transfers between devices  33.4 us (36%)
  waiting for transfers between devices  29.8 us (32%)
  Pallas kernels  29.2 us (31%)
    pallas_call x20, Pallas kernels, call(): pl.pallas_call(kernel, out_shape=tuple((jax.ShapeDtypeStruct(s, d) for s,...  29.2 us
    ppermute x26, waiting for transfers between devices, swap(): return lax.ppermute(x, axis, [(i, i ^ step) for i in range(size)])  26.8 us
    ppermute x26, starting transfers between devices, swap(): return lax.ppermute(x, axis, [(i, i ^ step) for i in range(size)])  25.5 us
    ppermute x4, starting transfers between devices, some(): return lax.ppermute(x, ('seq', 'blk'), pairs)  7.9 us
    ppermute x4, waiting for transfers between devices, some(): return lax.ppermute(x, ('seq', 'blk'), pairs)  2.97 us
  transfers between devices with their start and end apart: 30, of which 14 were waited for; matrix products, arithmetic and copies ran while one was open for 0% of the time, Pallas kernels for 24%

profile of v3, /device:TPU:0, one launch (start us, length us, event | category | flops | bytes accessed | tf_op | source)
XLA Modules:
  0.0 93.3 jit_solution(17401038491968178516)
XLA Ops:
  0.7 0.5 collective-permute-start
  1.2 2.6 %collective-permute-start.1 = (bf16[2,64,768]{2,1,0:T(8,128)(2,1)}, bf16[2,64,768]{2,1,0:T(8,128)(2,1)S(1)}, u32[]{:S(2)}, u32[]{:S(2)}) collective-permute-start(bf16[2,64,768]{2,1,0:T(8,128)(2,1)} %tokens_hbm.1), channel_id=1, source_target_pairs={{0,2},{1,3},{2,0},{3,1},{4,6},{5,7},{6,4},{7,5},{8,10},{9,11},{10,... | collective-permute-start | bytes 589832 | tf_op jit(solution)/shard_map/ppermute | solution.py:481
  3.8 4.1 %near.1 = (bf16[128,2304]{1,0:T(8,128)(2,1)S(1)}, f32[256,256]{1,0:T(8,128)S(1)}, f32[8,768]{1,0:T(8,128)S(1)}, f32[1,1536]{1,0:T(1,128)S(1)}, bf16[2,64,768]{2,...) custom-call(bf16[2,64,768]{2,1,0:T(8,128)(2,1)S(1)} %collective-perm, ...), custom_call_target="tpu_custom_call" | custom-call | flops 3000000000 | bytes 300000 | tf_op jit(solution)/shard_map/near/pallas_call | solution.py:73
  7.9 1.6 %collective-permute-done.1.t2 = bf16[2,64,768]{2,1,0:T(8,128)(2,1)S(1)} collective-permute-done((bf16[2,64,768]{2,1,0:T(8,128)(2,1)}, bf16[2,64,768]{2,1,0:T(8,128)(2,1)S(1)}, u32[]{:S(2)}, u32[]{:S(2)}) %collective-permute-start.1) | collective-permute-done | bytes 196640 | tf_op jit(solution)/shard_map/ppermute | solution.py:481
  9.5 1.8 %collective-permute-start.5 = (bf16[2,64,768]{2,1,0:T(8,128)(2,1)S(1)}, bf16[2,64,768]{2,1,0:T(8,128)(2,1)S(1)}, u32[]{:S(2)}, u32[]{:S(2)}) collective-permute-start(bf16[2,64,768]{2,1,0:T(8,128)(2,1)S(1)} %copy-done), channel_id=1, source_target_pairs={{0,2},{1,3},{2,0},{3,1},{4,6},{5,7},{6,4},{7,5},{8,10},{9,11},{10,... | collective-permute-start | bytes 589832 | tf_op jit(solution)/shard_map/ppermute | solution.py:481
  11.2 3.6 %attention.1 = (bf16[256,768]{1,0:T(8,128)(2,1)S(1)}, bf16[256,1152]{1,0:T(8,128)(2,1)S(1)}) custom-call(bf16[128,2304]{1,0:T(8,128)(2,1)S(1)} %get-tuple-element.81.near_in, f32[256,256]{1,0:T(8,128)S(1)} %get-tuple-element.82.same, f32[8,768]{1,0:T(8,128)S(1)} %get-tuple-element.83.vec.params, bf16[2,64,768]{2,1,0:T(8,128)(2,1)S(1)} %collective-permute-done.1.t2, ...), custom_call_target="tpu_custom_call" | custom-call | flops 10000000 | bytes 1000 | tf_op jit(solution)/shard_map/attention/pallas_call | solution.py:73
  14.8 0.3 collective-permute-start.3
  15.1 0.3 collective-permute-start.4
  15.4 1.4 %collective-permute-done.5.d2 = bf16[2,64,768]{2,1,0:T(8,128)(2,1)S(1)} collective-permute-done((bf16[2,64,768]{2,1,0:T(8,128)(2,1)S(1)}, bf16[2,64,768]{2,1,0:T(8,128)(2,1)S(1)}, u32[]{:S(2)}, u32[]{:S(2)}) %collective-permute-start.5) | collective-permute-done | bytes 196640 | tf_op jit(solution)/shard_map/ppermute | solution.py:481
  16.9 1.3 %collective-permute-done.6.d3 = bf16[2,64,768]{2,1,0:T(8,128)(2,1)S(1)} collective-permute-done((bf16[2,64,768]{2,1,0:T(8,128)(2,1)S(1)}, bf16[2,64,768]{2,1,0:T(8,128)(2,1)S(1)}, u32[]{:S(2)}, u32[]{:S(2)}) %collective-permute-start.6) | collective-permute-done | bytes 196640 | tf_op jit(solution)/shard_map/ppermute | solution.py:481
  18.3 6.1 %feed.1 = (bf16[512,768]{1,0:T(8,128)(2,1)S(1)}, bf16[512,1536]{1,0:T(8,128)(2,1)S(1)}, bf16[512,1536]{1,0:T(8,128)(2,1)S(1)}, bf16[256,768]{1,0:T(8,128)(2,1)S(...) custom-call(bf16[256,768]{1,0:T(8,128)(2,1)S(1)} %get-tuple-element., ...), custom_call_target="tpu_custom_call" | custom-call | flops 10000000 | bytes 1000 | tf_op jit(solution)/shard_map/feed/pallas_call | solution.py:73
  24.4 0.2 collective-permute-start.7
  24.6 2.0 %feed_weights.1 = (bf16[4,576,128]{2,1,0:T(8,128)(2,1)S(1)}, bf16[4,576,128]{2,1,0:T(8,128)(2,1)S(1)}, bf16[2,1152,128]{2,1,0:T(8,128)(2,1)S(1)}, bf16[2,1152,128]{2,1,0:T(8,128)(2,1)S(1)}, f32[1,1536]{1,0:T(1,128)S(1)}) custom-call(bf16[512,768]{1,0:T(8,128)(2,1)S(1)} %get-tuple-element.95.sec, bf16[512,1536]{1,0:T(8,128)(2,1)S(1)} %get-tuple-element.96.dup, ...), custom_call_target="tpu_custom_call" | custom-call | flops 20000000000 | bytes 2000000 | tf_op jit(solution)/shard_map/feed_weights/pallas_call | solution.py:73
  26.7 1.8 %collective-permute-start.13 = (bf16[4,576,128]{2,1,0:T(8,128)(2,1)S(1)}, bf16[4,576,128]{2,1,0:T(8,128)(2,1)S(1)}, u32[]{:S(2)}, u32[]{:S(2)}) collective-permute-start(bf16[4,576,128]{2,1,0:T(8,128)(2,1)S(1)} %get-tuple-element.116), channel_id=1, source_target_pairs={{0,4},{4,0},{8,12},{12,8},{16,20},{20,16},{24,28},{28,24},{1,5},{5... | collective-permute-start | bytes 1769480 | tf_op jit(solution)/shard_map/ppermute | solution.py:481
  28.5 1.6 %collective-permute-start.14 = (bf16[2,1152,128]{2,1,0:T(8,128)(2,1)S(1)}, bf16[2,1152,128]{2,1,0:T(8,128)(2,1)S(1)}, u32[]{:S(2)}, u32[]{:S(2)}) collective-permute-start(bf16[2,1152,128]{2,1,0:T(8,128)(2,1)S(1)} %get-tuple-element.118), channel_id=1, source_target_pairs={{0,8},{4,12},{8,0},{12,4},{16,24},{20,28},{24,16},{28,20},{1,9},{5... | collective-permute-start | bytes 1769480 | tf_op jit(solution)/shard_map/ppermute | solution.py:481
  30.1 3.4 %attention_back.1 = (bf16[256,768]{1,0:T(8,128)(2,1)S(1)}, bf16[320,768]{1,0:T(8,128)(2,1)S(1)}, f32[64,768]{1,0:T(8,128)S(1)}, f32[8,768]{1,0:T(8,128)S(1)}, f32[8,384]{1,0:T(8,128)S(1)}) custom-call(f32[256,768]{1,0:T(8,128)S(1)} %get-tuple-element.91.dsec_in, bf16[256,768]{1,0:T(8,128)(2,1)S(1)} %collective-permute-done.7.got, ...), custom_call_target="tpu_custom_call" | custom-call | flops 10000000 | bytes 1000 | tf_op jit(solution)/shard_map/attention_back/pallas_call | solution.py:73
  33.5 0.5 collective-permute-start.9
  34.0 1.3 %turn.1 = (bf16[384,512]{1,0:T(8,128)(2,1)S(1)}, bf16[384,512]{1,0:T(8,128)(2,1)S(1)}, f32[2,64,768]{2,1,0:T(8,128)S(1)}, bf16[2,64,768]{2,1,0:T(8,128)(2,1)S(1)}) custom-call(bf16[256,768]{1,0:T(8,128)(2,1)S(1)} %get-tuple-element.86.att_own, bf16[256,768]{1,0:T(8,128)(2,1)S(1)} %collective-permute-done.3.att_other, ...), custom_call_target="tpu_custom_call" | custom-call | flops 20000000000 | bytes 2000000 | tf_op jit(solution)/shard_map/turn/pallas_call | solution.py:73
  35.3 0.6 collective-permute-done.9.otherb.other
  35.9 3.3 %attention_weights.1 = (bf16[4,592,128]{2,1,0:T(8,128)(2,1)S(1)}, bf16[4,592,128]{2,1,0:T(8,128)(2,1)S(1)}, f32[2,64,768]{2,1,0:T(8,128)S(1)}, bf16[2,64,768]{2,1,0:T(8,128)(2,1)S(1)}) custom-call(bf16[256,768]{1,0:T(8,128)(2,1)S(1)} %get-tuple-element.100.owna, bf16[320,768]{1,0:T(8,128)(2,1)S(1)} %get-tuple-element.101.ownb, ...), custom_call_target="tpu_custom_call" | custom-call | flops 10000000 | bytes 1000 | tf_op jit(solution)/shard_map/attention_weights/pallas_call | solution.py:73
  39.2 0.6 collective-permute-start.12
  39.8 4.0 %collective-permute-done.14.got = bf16[2,1152,128]{2,1,0:T(8,128)(2,1)S(1)} collective-permute-done((bf16[2,1152,128]{2,1,0:T(8,128)(2,1)S(1)}, bf16[2,1152,128]{2,1,0:T(8,128)(2,1)S(1)}, u32[]{:S(2)}, u32[]{:S(2)}) %collective-permute-start.14) | collective-permute-done | bytes 589856 | tf_op jit(solution)/shard_map/ppermute | solution.py:481
  43.9 2.7 %collective-permute-start.16 = (bf16[1,1152,128]{2,1,0:T(8,128)(2,1)S(1)}, bf16[1,1152,128]{2,1,0:T(8,128)(2,1)S(1)}, u32[]{:S(2)}, u32[]{:S(2)}) collective-permute-start(bf16[1,1152,128]{2,1,0:T(8,128)(2,1)S(1)} %get-tuple-element.122), channel_id=1, source_target_pairs={{0,16},{4,20},{8,24},{12,28},{16,0},{20,4},{24,8},{28,12},{1,17},{... | collective-permute-start | bytes 884744 | tf_op jit(solution)/shard_map/ppermute | solution.py:481
  46.7 1.6 %collective-permute-start.15 = (bf16[2,576,128]{2,1,0:T(8,128)(2,1)S(1)}, bf16[2,576,128]{2,1,0:T(8,128)(2,1)S(1)}, u32[]{:S(2)}, u32[]{:S(2)}) collective-permute-start(bf16[2,576,128]{2,1,0:T(8,128)(2,1)S(1)} %get-tuple-element.121), channel_id=1, source_target_pairs={{0,8},{4,12},{8,0},{12,4},{16,24},{20,28},{24,16},{28,20},{1,9},{5... | collective-permute-start | bytes 884744 | tf_op jit(solution)/shard_map/ppermute | solution.py:481
  48.3 11.1 %collective-permute-done.16.b = bf16[1,1152,128]{2,1,0:T(8,128)(2,1)S(1)} collective-permute-done((bf16[1,1152,128]{2,1,0:T(8,128)(2,1)S(1)}, bf16[1,1152,128]{2,1,0:T(8,128)(2,1)S(1)}, u32[]{:S(2)}, u32[]{:S(2)}) %collective-permute-start.16) | collective-permute-done | bytes 294944 | tf_op jit(solution)/shard_map/ppermute | solution.py:481
  59.5 1.3 %collective-permute-start.19 = (bf16[1,1152,128]{2,1,0:T(8,128)(2,1)S(1)}, bf16[1,1152,128]{2,1,0:T(8,128)(2,1)S(1)}, u32[]{:S(2)}, u32[]{:S(2)}) collective-permute-start(bf16[1,1152,128]{2,1,0:T(8,128)(2,1)S(1)} %add.4.before.a), channel_id=1, source_target_pairs={{1,5},{3,7},{4,0},{6,2},{9,13},{11,15},{12,8},{14,10},{17,21},{19,... | collective-permute-start | bytes 884744 | tf_op jit(solution)/shard_map/ppermute | solution.py:499
  61.1 0.7 collective-permute-start.17
  61.8 3.4 %collective-permute-start.18 = (bf16[1,576,128]{2,1,0:T(8,128)(2,1)S(1)}, bf16[1,576,128]{2,1,0:T(8,128)(2,1)S(1)}, u32[]{:S(2)}, u32[]{:S(2)}) collective-permute-start(bf16[1,576,128]{2,1,0:T(8,128)(2,1)S(1)} %get-tuple-element.126), channel_id=1, source_target_pairs={{0,16},{4,20},{8,24},{12,28},{16,0},{20,4},{24,8},{28,12},{1,17},{... | collective-permute-start | bytes 442376 | tf_op jit(solution)/shard_map/ppermute | solution.py:481
  65.1 3.0 %collective-permute-done.19.b = bf16[1,1152,128]{2,1,0:T(8,128)(2,1)S(1)} collective-permute-done((bf16[1,1152,128]{2,1,0:T(8,128)(2,1)S(1)}, bf16[1,1152,128]{2,1,0:T(8,128)(2,1)S(1)}, u32[]{:S(2)}, u32[]{:S(2)}) %collective-permute-start.19) | collective-permute-done | bytes 294944 | tf_op jit(solution)/shard_map/ppermute | solution.py:499
  68.2 3.5 %collective-permute-start.25 = (bf16[1,1152,128]{2,1,0:T(8,128)(2,1)S(1)}, bf16[1,1152,128]{2,1,0:T(8,128)(2,1)S(1)}, u32[]{:S(2)}, u32[]{:S(2)}) collective-permute-start(bf16[1,1152,128]{2,1,0:T(8,128)(2,1)S(1)} %add.5.before.mine), channel_id=1, source_target_pairs={{0,2},{2,0},{5,7},{7,5},{8,10},{10,8},{13,15},{15,13},{16,18},{18,... | collective-permute-start | bytes 884744 | tf_op jit(solution)/shard_map/ppermute | solution.py:499
  71.6 0.7 collective-permute-done.18.b
  72.4 0.7 collective-permute-done.17.got
  73.2 2.8 %collective-permute-start.20 = (bf16[1,592,128]{2,1,0:T(8,128)(2,1)S(1)}, bf16[1,592,128]{2,1,0:T(8,128)(2,1)S(1)}, u32[]{:S(2)}, u32[]{:S(2)}) collective-permute-start(bf16[1,592,128]{2,1,0:T(8,128)(2,1)S(1)} %get-tuple-element.128), channel_id=1, source_target_pairs={{0,16},{4,20},{8,24},{12,28},{16,0},{20,4},{24,8},{28,12},{1,17},{... | collective-permute-start | bytes 454664 | tf_op jit(solution)/shard_map/ppermute | solution.py:481
  76.0 1.5 %collective-permute-start.10 = (bf16[2,64,768]{2,1,0:T(8,128)(2,1)S(1)}, bf16[2,64,768]{2,1,0:T(8,128)(2,1)S(1)}, u32[]{:S(2)}, u32[]{:S(2)}) collective-permute-start(bf16[2,64,768]{2,1,0:T(8,128)(2,1)S(1)} %get-tuple-element.107), channel_id=1, source_target_pairs={{0,2},{1,3},{2,0},{3,1},{4,6},{5,7},{6,4},{7,5},{8,10},{9,11},{10,... | collective-permute-start | bytes 589832 | tf_op jit(solution)/shard_map/ppermute | solution.py:481
  77.5 0.5 collective-permute-start.23
  78.0 1.9 %collective-permute-start.26 = (bf16[1,1152,128]{2,1,0:T(8,128)(2,1)S(1)}, bf16[1,1152,128]{2,1,0:T(8,128)(2,1)S(1)}, u32[]{:S(2)}, u32[]{:S(2)}) collective-permute-start(bf16[1,1152,128]{2,1,0:T(8,128)(2,1)S(1)} %add.5.before.mine), channel_id=1, source_target_pairs={{0,1},{2,3},{5,4},{7,6},{8,9},{10,11},{13,12},{15,14},{16,17},{18,... | collective-permute-start | bytes 884744 | tf_op jit(solution)/shard_map/ppermute | solution.py:499
  79.9 3.4 %collective-permute-done.20.b = bf16[1,592,128]{2,1,0:T(8,128)(2,1)S(1)} collective-permute-done((bf16[1,592,128]{2,1,0:T(8,128)(2,1)S(1)}, bf16[1,592,128]{2,1,0:T(8,128)(2,1)S(1)}, u32[]{:S(2)}, u32[]{:S(2)}) %collective-permute-start.20) | collective-permute-done | bytes 151584 | tf_op jit(solution)/shard_map/ppermute | solution.py:481
  83.3 1.3 %collective-permute-start.27 = (bf16[1,1152,128]{2,1,0:T(8,128)(2,1)S(1)}, bf16[1,1152,128]{2,1,0:T(8,128)(2,1)S(1)}, u32[]{:S(2)}, u32[]{:S(2)}) collective-permute-start(bf16[1,1152,128]{2,1,0:T(8,128)(2,1)S(1)} %collective-permute-done.25.across), channel_id=1, source_target_pairs={{0,1},{2,3},{5,4},{7,6},{8,9},{10,11},{13,12},{15,14},{16,17},{18,... | collective-permute-start | bytes 884744 | tf_op jit(solution)/shard_map/ppermute | solution.py:499
  84.6 1.7 %collective-permute-start.21 = (bf16[1,592,128]{2,1,0:T(8,128)(2,1)S(1)}, bf16[1,592,128]{2,1,0:T(8,128)(2,1)S(1)}, u32[]{:S(2)}, u32[]{:S(2)}) collective-permute-start(bf16[1,592,128]{2,1,0:T(8,128)(2,1)S(1)} %add.7.p0), channel_id=1, source_target_pairs={{0,2},{1,3},{2,0},{3,1},{4,6},{5,7},{6,4},{7,5},{8,10},{9,11},{10,... | collective-permute-start | bytes 454664 | tf_op jit(solution)/shard_map/ppermute | solution.py:481
  86.3 0.5 collective-permute-done.23.p2
  86.8 1.1 %input_grad.1 = (bf16[2,64,768]{2,1,0:T(8,128)(2,1)}, bf16[2,64,768]{2,1,0:T(8,128)(2,1)}) custom-call(bf16[2,64,768]{2,1,0:T(8,128)(2,1)S(1)} %get-tuple-element.79.t0.tokens, f32[2,64,768]{2,1,0:T(8,128)S(1)} %get-tuple-element.106.dfirst, bf16[2,64,768]{2,1,0:T(8,128)(2,1)S(1)} %collective-permute-done.10.received, ...), custom_call_target="tpu_custom_call" | custom-call | flops 10000000 | bytes 1000 | tf_op jit(solution)/shard_map/input_grad/pallas_call | solution.py:73
  87.9 0.3 collective-permute-done.24.p3
  88.2 1.1 %assemble_up.1 = f32[96,3072]{1,0:T(8,128)} custom-call(bf16[1,576,128]{2,1,0:T(8,128)(2,1)S(1)} %add.6.before.p0, bf16[1,576,128]{2,1,0:T(8,128)(2,1)S(1)} %collective-permute-done.22.p1, bf16[1,576,128]{2,1,0:T(8,128)(2,1)S(1)} %collective-permute-done.23.p2, bf16[1,576,128]{2,1,0:T(8,128)(2,1)S(1)} %collective-permute-done.24.p3), custom_call_target="tpu_custom_call" | custom-call | flops 10000000 | bytes 1000 | tf_op jit(solution)/shard_map/assemble_up/pallas_call | solution.py:73
  89.3 0.3 collective-permute-start.28
  89.6 1.2 %assemble_down.1 = f32[384,768]{1,0:T(8,128)} custom-call(bf16[1,1152,128]{2,1,0:T(8,128)(2,1)S(1)} %add.5.before.mine, bf16[1,1152,128]{2,1,0:T(8,128)(2,1)S(1)} %collective-permute-done.25.across, bf16[1,1152,128]{2,1,0:T(8,128)(2,1)S(1)} %collective-permute-done.26.partner, bf16[1,1152,128]{2,1,0:T(8,128)(2,1)S(1)} %collective-permute-done.27.partner_across), custom_call_target="tpu_custom_call" | custom-call | flops 10000000 | bytes 1000 | tf_op jit(solution)/shard_map/assemble_down/pallas_call | solution.py:73
  90.8 0.2 collective-permute-start.29
  91.0 1.1 %collective-permute-done.29.p3 = bf16[1,592,128]{2,1,0:T(8,128)(2,1)S(1)} collective-permute-done((bf16[1,592,128]{2,1,0:T(8,128)(2,1)S(1)}, bf16[1,592,128]{2,1,0:T(8,128)(2,1)S(1)}, u32[]{:S(2)}, u32[]{:S(2)}) %collective-permute-start.29) | collective-permute-done | bytes 151584 | tf_op jit(solution)/shard_map/ppermute | solution.py:481
  92.2 1.1 %assemble_rest.1 = (f32[96,768]{1,0:T(8,128)}, f32[96,2304]{1,0:T(8,128)}, f32[96]{0:T(128)}, f32[96]{0:T(128)}, f32[192]{0:T(256)}, /*index=5*/f32[96]{0:T(128)...) custom-call(bf16[1,592,128]{2,1,0:T(8,128)(2,1)S(1)} %add.7.p0, bf16[1,592,128]{2,1,0:T(8,128)(2,1)S(1)} %collective-permute-done.28.p1, ...), custom_call_target="tpu_custom_call" | custom-call | flops 10000000 | bytes 1000 | tf_op jit(solution)/shard_map/assemble_rest/pallas_call | solution.py:73
  (34 shorter events, 1.0 us)
Async XLA Ops:
  0.6 8.8 %copy-start = (bf16[2,64,768]{2,1,0:T(8,128)(2,1)S(1)}, bf16[2,64,768]{2,1,0:T(8,128)(2,1)}, u32[]{:S(2)}) copy-start(bf16[2,64,768]{2,1,0:T(8,128)(2,1)} %d0.3) | copy-start | bytes 589828
  0.7 3.1 %collective-permute-start = (bf16[2,64,768]{2,1,0:T(8,128)(2,1)}, bf16[2,64,768]{2,1,0:T(8,128)(2,1)S(1)}, u32[]{:S(2)}, u32[]{:S(2)}) collective-permute-start(bf16[2,64,768]{2,1,0:T(8,128)(2,1)} %tokens_hbm.1), channel_id=1, source_target_pairs={{0,1},{1,0},{2,3},{3,2},{4,5},{5,4},{6,7},{7,6},{8,9},{9,8},{10,11... | collective-permute-start | bytes 589832 | tf_op jit(solution)/shard_map/ppermute | solution.py:481
  1.2 8.3 %collective-permute-start.1 = (bf16[2,64,768]{2,1,0:T(8,128)(2,1)}, bf16[2,64,768]{2,1,0:T(8,128)(2,1)S(1)}, u32[]{:S(2)}, u32[]{:S(2)}) collective-permute-start(bf16[2,64,768]{2,1,0:T(8,128)(2,1)} %tokens_hbm.1), channel_id=1, source_target_pairs={{0,2},{1,3},{2,0},{3,1},{4,6},{5,7},{6,4},{7,5},{8,10},{9,11},{10,... | collective-permute-start | bytes 589832 | tf_op jit(solution)/shard_map/ppermute | solution.py:481
  9.5 1.8 %collective-permute-start.2 = (bf16[2,64,768]{2,1,0:T(8,128)(2,1)S(1)}, bf16[2,64,768]{2,1,0:T(8,128)(2,1)S(1)}, u32[]{:S(2)}, u32[]{:S(2)}) collective-permute-start(bf16[2,64,768]{2,1,0:T(8,128)(2,1)S(1)} %collective-permute-done.1.t2), channel_id=1, source_target_pairs={{0,1},{1,0},{2,3},{3,2},{4,5},{5,4},{6,7},{7,6},{8,9},{9,8},{10,11... | collective-permute-start | bytes 589832 | tf_op jit(solution)/shard_map/ppermute | solution.py:481
  9.5 7.3 %collective-permute-start.5 = (bf16[2,64,768]{2,1,0:T(8,128)(2,1)S(1)}, bf16[2,64,768]{2,1,0:T(8,128)(2,1)S(1)}, u32[]{:S(2)}, u32[]{:S(2)}) collective-permute-start(bf16[2,64,768]{2,1,0:T(8,128)(2,1)S(1)} %copy-done), channel_id=1, source_target_pairs={{0,2},{1,3},{2,0},{3,1},{4,6},{5,7},{6,4},{7,5},{8,10},{9,11},{10,... | collective-permute-start | bytes 589832 | tf_op jit(solution)/shard_map/ppermute | solution.py:481
  14.8 3.4 %collective-permute-start.3 = (bf16[256,768]{1,0:T(8,128)(2,1)S(1)}, bf16[256,768]{1,0:T(8,128)(2,1)S(1)}, u32[]{:S(2)}, u32[]{:S(2)}) collective-permute-start(bf16[256,768]{1,0:T(8,128)(2,1)S(1)} %get-tuple-element.86.att_own), channel_id=1, source_target_pairs={{0,1},{1,0},{2,3},{3,2},{4,5},{5,4},{6,7},{7,6},{8,9},{9,8},{10,11... | collective-permute-start | bytes 1179656 | tf_op jit(solution)/shard_map/ppermute | solution.py:481
  15.1 1.8 %collective-permute-start.4 = (bf16[2,64,768]{2,1,0:T(8,128)(2,1)S(1)}, bf16[2,64,768]{2,1,0:T(8,128)(2,1)S(1)}, u32[]{:S(2)}, u32[]{:S(2)}) collective-permute-start(bf16[2,64,768]{2,1,0:T(8,128)(2,1)S(1)} %copy-done), channel_id=1, source_target_pairs={{0,1},{1,0},{2,3},{3,2},{4,5},{5,4},{6,7},{7,6},{8,9},{9,8},{10,11... | collective-permute-start | bytes 589832 | tf_op jit(solution)/shard_map/ppermute | solution.py:481
  16.8 1.4 %collective-permute-start.6 = (bf16[2,64,768]{2,1,0:T(8,128)(2,1)S(1)}, bf16[2,64,768]{2,1,0:T(8,128)(2,1)S(1)}, u32[]{:S(2)}, u32[]{:S(2)}) collective-permute-start(bf16[2,64,768]{2,1,0:T(8,128)(2,1)S(1)} %collective-permute-done.5.d2), channel_id=1, source_target_pairs={{0,1},{1,0},{2,3},{3,2},{4,5},{5,4},{6,7},{7,6},{8,9},{9,8},{10,11... | collective-permute-start | bytes 589832 | tf_op jit(solution)/shard_map/ppermute | solution.py:481
  24.4 5.7 %collective-permute-start.7 = (bf16[256,768]{1,0:T(8,128)(2,1)S(1)}, bf16[256,768]{1,0:T(8,128)(2,1)S(1)}, u32[]{:S(2)}, u32[]{:S(2)}) collective-permute-start(bf16[256,768]{1,0:T(8,128)(2,1)S(1)} %get-tuple-element.92), channel_id=1, source_target_pairs={{0,1},{1,0},{2,3},{3,2},{4,5},{5,4},{6,7},{7,6},{8,9},{9,8},{10,11... | collective-permute-start | bytes 1179656 | tf_op jit(solution)/shard_map/ppermute | solution.py:481
  26.7 19.9 %collective-permute-start.13 = (bf16[4,576,128]{2,1,0:T(8,128)(2,1)S(1)}, bf16[4,576,128]{2,1,0:T(8,128)(2,1)S(1)}, u32[]{:S(2)}, u32[]{:S(2)}) collective-permute-start(bf16[4,576,128]{2,1,0:T(8,128)(2,1)S(1)} %get-tuple-element.116), channel_id=1, source_target_pairs={{0,4},{4,0},{8,12},{12,8},{16,20},{20,16},{24,28},{28,24},{1,5},{5... | collective-permute-start | bytes 1769480 | tf_op jit(solution)/shard_map/ppermute | solution.py:481
  28.5 15.3 %collective-permute-start.14 = (bf16[2,1152,128]{2,1,0:T(8,128)(2,1)S(1)}, bf16[2,1152,128]{2,1,0:T(8,128)(2,1)S(1)}, u32[]{:S(2)}, u32[]{:S(2)}) collective-permute-start(bf16[2,1152,128]{2,1,0:T(8,128)(2,1)S(1)} %get-tuple-element.118), channel_id=1, source_target_pairs={{0,8},{4,12},{8,0},{12,4},{16,24},{20,28},{24,16},{28,20},{1,9},{5... | collective-permute-start | bytes 1769480 | tf_op jit(solution)/shard_map/ppermute | solution.py:481
  33.4 1.9 %collective-permute-start.8 = (bf16[256,768]{1,0:T(8,128)(2,1)S(1)}, bf16[256,768]{1,0:T(8,128)(2,1)S(1)}, u32[]{:S(2)}, u32[]{:S(2)}) collective-permute-start(bf16[256,768]{1,0:T(8,128)(2,1)S(1)} %get-tuple-element.100.owna), channel_id=1, source_target_pairs={{0,1},{1,0},{2,3},{3,2},{4,5},{5,4},{6,7},{7,6},{8,9},{9,8},{10,11... | collective-permute-start | bytes 1179656 | tf_op jit(solution)/shard_map/ppermute | solution.py:481
  33.5 2.4 %collective-permute-start.9 = (bf16[320,768]{1,0:T(8,128)(2,1)S(1)}, bf16[320,768]{1,0:T(8,128)(2,1)S(1)}, u32[]{:S(2)}, u32[]{:S(2)}) collective-permute-start(bf16[320,768]{1,0:T(8,128)(2,1)S(1)} %get-tuple-element.101.ownb), channel_id=1, source_target_pairs={{0,1},{1,0},{2,3},{3,2},{4,5},{5,4},{6,7},{7,6},{8,9},{9,8},{10,11... | collective-permute-start | bytes 1474568 | tf_op jit(solution)/shard_map/ppermute | solution.py:481
  39.2 21.7 %collective-permute-start.12 = (bf16[4,592,128]{2,1,0:T(8,128)(2,1)S(1)}, bf16[4,592,128]{2,1,0:T(8,128)(2,1)S(1)}, u32[]{:S(2)}, u32[]{:S(2)}) collective-permute-start(bf16[4,592,128]{2,1,0:T(8,128)(2,1)S(1)} %get-tuple-element.114), channel_id=1, source_target_pairs={{0,4},{4,0},{8,12},{12,8},{16,20},{20,16},{24,28},{28,24},{1,5},{5... | collective-permute-start | bytes 1818632 | tf_op jit(solution)/shard_map/ppermute | solution.py:481
  43.9 15.5 %collective-permute-start.16 = (bf16[1,1152,128]{2,1,0:T(8,128)(2,1)S(1)}, bf16[1,1152,128]{2,1,0:T(8,128)(2,1)S(1)}, u32[]{:S(2)}, u32[]{:S(2)}) collective-permute-start(bf16[1,1152,128]{2,1,0:T(8,128)(2,1)S(1)} %get-tuple-element.122), channel_id=1, source_target_pairs={{0,16},{4,20},{8,24},{12,28},{16,0},{20,4},{24,8},{28,12},{1,17},{... | collective-permute-start | bytes 884744 | tf_op jit(solution)/shard_map/ppermute | solution.py:481
  46.7 14.1 %collective-permute-start.15 = (bf16[2,576,128]{2,1,0:T(8,128)(2,1)S(1)}, bf16[2,576,128]{2,1,0:T(8,128)(2,1)S(1)}, u32[]{:S(2)}, u32[]{:S(2)}) collective-permute-start(bf16[2,576,128]{2,1,0:T(8,128)(2,1)S(1)} %get-tuple-element.121), channel_id=1, source_target_pairs={{0,8},{4,12},{8,0},{12,4},{16,24},{20,28},{24,16},{28,20},{1,9},{5... | collective-permute-start | bytes 884744 | tf_op jit(solution)/shard_map/ppermute | solution.py:481
  59.5 8.6 %collective-permute-start.19 = (bf16[1,1152,128]{2,1,0:T(8,128)(2,1)S(1)}, bf16[1,1152,128]{2,1,0:T(8,128)(2,1)S(1)}, u32[]{:S(2)}, u32[]{:S(2)}) collective-permute-start(bf16[1,1152,128]{2,1,0:T(8,128)(2,1)S(1)} %add.4.before.a), channel_id=1, source_target_pairs={{1,5},{3,7},{4,0},{6,2},{9,13},{11,15},{12,8},{14,10},{17,21},{19,... | collective-permute-start | bytes 884744 | tf_op jit(solution)/shard_map/ppermute | solution.py:499
  61.1 12.0 %collective-permute-start.17 = (bf16[2,592,128]{2,1,0:T(8,128)(2,1)S(1)}, bf16[2,592,128]{2,1,0:T(8,128)(2,1)S(1)}, u32[]{:S(2)}, u32[]{:S(2)}) collective-permute-start(bf16[2,592,128]{2,1,0:T(8,128)(2,1)S(1)} %get-tuple-element.125), channel_id=1, source_target_pairs={{0,8},{4,12},{8,0},{12,4},{16,24},{20,28},{24,16},{28,20},{1,9},{5... | collective-permute-start | bytes 909320 | tf_op jit(solution)/shard_map/ppermute | solution.py:481
  61.8 10.6 %collective-permute-start.18 = (bf16[1,576,128]{2,1,0:T(8,128)(2,1)S(1)}, bf16[1,576,128]{2,1,0:T(8,128)(2,1)S(1)}, u32[]{:S(2)}, u32[]{:S(2)}) collective-permute-start(bf16[1,576,128]{2,1,0:T(8,128)(2,1)S(1)} %get-tuple-element.126), channel_id=1, source_target_pairs={{0,16},{4,20},{8,24},{12,28},{16,0},{20,4},{24,8},{28,12},{1,17},{... | collective-permute-start | bytes 442376 | tf_op jit(solution)/shard_map/ppermute | solution.py:481
  68.2 9.8 %collective-permute-start.25 = (bf16[1,1152,128]{2,1,0:T(8,128)(2,1)S(1)}, bf16[1,1152,128]{2,1,0:T(8,128)(2,1)S(1)}, u32[]{:S(2)}, u32[]{:S(2)}) collective-permute-start(bf16[1,1152,128]{2,1,0:T(8,128)(2,1)S(1)} %add.5.before.mine), channel_id=1, source_target_pairs={{0,2},{2,0},{5,7},{7,5},{8,10},{10,8},{13,15},{15,13},{16,18},{18,... | collective-permute-start | bytes 884744 | tf_op jit(solution)/shard_map/ppermute | solution.py:499
  73.2 10.1 %collective-permute-start.20 = (bf16[1,592,128]{2,1,0:T(8,128)(2,1)S(1)}, bf16[1,592,128]{2,1,0:T(8,128)(2,1)S(1)}, u32[]{:S(2)}, u32[]{:S(2)}) collective-permute-start(bf16[1,592,128]{2,1,0:T(8,128)(2,1)S(1)} %get-tuple-element.128), channel_id=1, source_target_pairs={{0,16},{4,20},{8,24},{12,28},{16,0},{20,4},{24,8},{28,12},{1,17},{... | collective-permute-start | bytes 454664 | tf_op jit(solution)/shard_map/ppermute | solution.py:481
  76.0 8.7 %collective-permute-start.11 = (bf16[2,64,768]{2,1,0:T(8,128)(2,1)S(1)}, bf16[2,64,768]{2,1,0:T(8,128)(2,1)S(1)}, u32[]{:S(2)}, u32[]{:S(2)}) collective-permute-start(bf16[2,64,768]{2,1,0:T(8,128)(2,1)S(1)} %get-tuple-element.111), channel_id=1, source_target_pairs={{0,1},{1,0},{2,3},{3,2},{4,5},{5,4},{6,7},{7,6},{8,9},{9,8},{10,11... | collective-permute-start | bytes 589832 | tf_op jit(solution)/shard_map/ppermute | solution.py:481
  76.0 10.3 %collective-permute-start.10 = (bf16[2,64,768]{2,1,0:T(8,128)(2,1)S(1)}, bf16[2,64,768]{2,1,0:T(8,128)(2,1)S(1)}, u32[]{:S(2)}, u32[]{:S(2)}) collective-permute-start(bf16[2,64,768]{2,1,0:T(8,128)(2,1)S(1)} %get-tuple-element.107), channel_id=1, source_target_pairs={{0,2},{1,3},{2,0},{3,1},{4,6},{5,7},{6,4},{7,5},{8,10},{9,11},{10,... | collective-permute-start | bytes 589832 | tf_op jit(solution)/shard_map/ppermute | solution.py:481
  77.5 9.3 %collective-permute-start.23 = (bf16[1,576,128]{2,1,0:T(8,128)(2,1)S(1)}, bf16[1,576,128]{2,1,0:T(8,128)(2,1)S(1)}, u32[]{:S(2)}, u32[]{:S(2)}) collective-permute-start(bf16[1,576,128]{2,1,0:T(8,128)(2,1)S(1)} %add.6.before.p0), channel_id=1, source_target_pairs={{0,2},{1,3},{2,0},{3,1},{4,6},{5,7},{6,4},{7,5},{8,10},{9,11},{10,... | collective-permute-start | bytes 442376 | tf_op jit(solution)/shard_map/ppermute | solution.py:481
  78.0 11.6 %collective-permute-start.26 = (bf16[1,1152,128]{2,1,0:T(8,128)(2,1)S(1)}, bf16[1,1152,128]{2,1,0:T(8,128)(2,1)S(1)}, u32[]{:S(2)}, u32[]{:S(2)}) collective-permute-start(bf16[1,1152,128]{2,1,0:T(8,128)(2,1)S(1)} %add.5.before.mine), channel_id=1, source_target_pairs={{0,1},{2,3},{5,4},{7,6},{8,9},{10,11},{13,12},{15,14},{16,17},{18,... | collective-permute-start | bytes 884744 | tf_op jit(solution)/shard_map/ppermute | solution.py:499
  83.3 6.3 %collective-permute-start.27 = (bf16[1,1152,128]{2,1,0:T(8,128)(2,1)S(1)}, bf16[1,1152,128]{2,1,0:T(8,128)(2,1)S(1)}, u32[]{:S(2)}, u32[]{:S(2)}) collective-permute-start(bf16[1,1152,128]{2,1,0:T(8,128)(2,1)S(1)} %collective-permute-done.25.across), channel_id=1, source_target_pairs={{0,1},{2,3},{5,4},{7,6},{8,9},{10,11},{13,12},{15,14},{16,17},{18,... | collective-permute-start | bytes 884744 | tf_op jit(solution)/shard_map/ppermute | solution.py:499
  84.6 6.1 %collective-permute-start.21 = (bf16[1,592,128]{2,1,0:T(8,128)(2,1)S(1)}, bf16[1,592,128]{2,1,0:T(8,128)(2,1)S(1)}, u32[]{:S(2)}, u32[]{:S(2)}) collective-permute-start(bf16[1,592,128]{2,1,0:T(8,128)(2,1)S(1)} %add.7.p0), channel_id=1, source_target_pairs={{0,2},{1,3},{2,0},{3,1},{4,6},{5,7},{6,4},{7,5},{8,10},{9,11},{10,... | collective-permute-start | bytes 454664 | tf_op jit(solution)/shard_map/ppermute | solution.py:481
  86.3 1.6 %collective-permute-start.22 = (bf16[1,576,128]{2,1,0:T(8,128)(2,1)S(1)}, bf16[1,576,128]{2,1,0:T(8,128)(2,1)S(1)}, u32[]{:S(2)}, u32[]{:S(2)}) collective-permute-start(bf16[1,576,128]{2,1,0:T(8,128)(2,1)S(1)} %add.6.before.p0), channel_id=1, source_target_pairs={{0,1},{1,0},{2,3},{3,2},{4,5},{5,4},{6,7},{7,6},{8,9},{9,8},{10,11... | collective-permute-start | bytes 442376 | tf_op jit(solution)/shard_map/ppermute | solution.py:481
  86.8 1.4 %collective-permute-start.24 = (bf16[1,576,128]{2,1,0:T(8,128)(2,1)S(1)}, bf16[1,576,128]{2,1,0:T(8,128)(2,1)S(1)}, u32[]{:S(2)}, u32[]{:S(2)}) collective-permute-start(bf16[1,576,128]{2,1,0:T(8,128)(2,1)S(1)} %collective-permute-done.23.p2), channel_id=1, source_target_pairs={{0,1},{1,0},{2,3},{3,2},{4,5},{5,4},{6,7},{7,6},{8,9},{9,8},{10,11... | collective-permute-start | bytes 442376 | tf_op jit(solution)/shard_map/ppermute | solution.py:481
  89.3 1.7 %collective-permute-start.28 = (bf16[1,592,128]{2,1,0:T(8,128)(2,1)S(1)}, bf16[1,592,128]{2,1,0:T(8,128)(2,1)S(1)}, u32[]{:S(2)}, u32[]{:S(2)}) collective-permute-start(bf16[1,592,128]{2,1,0:T(8,128)(2,1)S(1)} %add.7.p0), channel_id=1, source_target_pairs={{0,1},{1,0},{2,3},{3,2},{4,5},{5,4},{6,7},{7,6},{8,9},{9,8},{10,11... | collective-permute-start | bytes 454664 | tf_op jit(solution)/shard_map/ppermute | solution.py:481
  90.8 1.4 %collective-permute-start.29 = (bf16[1,592,128]{2,1,0:T(8,128)(2,1)S(1)}, bf16[1,592,128]{2,1,0:T(8,128)(2,1)S(1)}, u32[]{:S(2)}, u32[]{:S(2)}) collective-permute-start(bf16[1,592,128]{2,1,0:T(8,128)(2,1)S(1)} %collective-permute-done.21.p2), channel_id=1, source_target_pairs={{0,1},{1,0},{2,3},{3,2},{4,5},{5,4},{6,7},{7,6},{8,9},{9,8},{10,11... | collective-permute-start | bytes 454664 | tf_op jit(solution)/shard_map/ppermute | solution.py:481

commit v4 on v3

--- a/solution.py
+++ b/solution.py
@@ -14,6 +14,7 @@
 GELU_A = 0.044715
 US = 0.01
 FILL = 20.0
+STEP = 0.2
 VMEM = pl.BlockSpec(memory_space=pltpu.VMEM)
 HBM = pl.BlockSpec(memory_space=pltpu.HBM)
 ANY = pl.BlockSpec(memory_space=pl.ANY)
@@ -59,10 +60,10 @@
     return lax.rem(bit + k, 2)
 
 
-def softmax_rows(scores, same):
-    scores = jnp.where(same > 0.0, scores, -1e9)
+def softmax_parts(scores, mask):
+    scores = scores + mask
     e = jnp.exp(scores - jnp.max(scores, axis=-1, keepdims=True))
-    return e * (1.0 / jnp.sum(e, axis=-1, keepdims=True))
+    return e, 1.0 / jnp.sum(e, axis=-1, keepdims=True)
 
 
 def column_sum(x):
@@ -102,7 +103,7 @@
     tiles = jnp.where(place.y == 1, second, first), jnp.where(place.y == 1, first, second)
     tiles = [jnp.where(place.core == 1, pltpu.roll(t, 64, 1), t) for t in tiles]
     wide = jnp.concatenate(tiles, axis=1)
-    return jnp.where(wide == wide.T, 1.0, 0.0)
+    return jnp.where(wide == wide.T, 0.0, -1e9)
 
 
 def pick_rows(transposed, chosen, part, x_bit):
@@ -134,15 +135,15 @@
 
 def build_kernels(inner):
     def near(
-        t1, tokens_hbm, seg_hbm, g1_hbm, s1_hbm, qv_hbm, ob_hbm, g2_hbm, s2_hbm, db_hbm, ub_hbm,
+        t1, dy_hbm, tokens_hbm, seg_hbm, g1_hbm, s1_hbm, qv_hbm, ob_hbm, g2_hbm, s2_hbm, db_hbm, ub_hbm,
         wqkv_hbm, wout_hbm, wup_hbm, wdown_hbm,
-        near_o, same_o, vec_o, up_bias_o, t0, wqkv, wout, wup, wdown,
+        near_o, same_o, vec_o, up_bias_o, t0, d0, wqkv, wout, wup, wdown,
         first, seg, g1, s1, qv, ob, g2, s2, db, ub, sem,
     ):
         place = Place(inner)
         pairs = [
             (g1_hbm, g1), (s1_hbm, s1), (qv_hbm, qv), (ob_hbm, ob), (g2_hbm, g2), (s2_hbm, s2),
-            (db_hbm, db), (ub_hbm, ub), (seg_hbm, seg), (tokens_hbm, t0),
+            (db_hbm, db), (ub_hbm, ub), (seg_hbm, seg), (tokens_hbm, t0), (dy_hbm, d0),
         ]
         small = len(pairs)
         pairs += [(wqkv_hbm.at[:, pl.ds(n * 768, 768)], wqkv.at[:, pl.ds(n * 768, 768)]) for n in range(3)]
@@ -185,46 +186,68 @@
         value = value.astype(BF16)
         out[:, cols] = value * BF16(0.125) if n == 0 else value
 
-    def attention(near_in, same, vec, t2, t3, wqkv, att_o, mine_o, first, far, qkv):
-        place = Place(inner)
-        for p, t in enumerate((t2, t3)):
-            xhat, _ = standardize(t[place.core].astype(F32))
+    def split_sequences(tokens, mine, away):
+        core = Place(inner).core
+        mine[...] = tokens[core]
+        away[...] = tokens[1 - core]
+
+    def attention(near_in, mask, vec, t2, t3, wqkv, before, atta_o, attb_o, mine_o, probs_o, first, far, qkv):
+        place = Place(inner)
+        for p, t in enumerate((t2[place.core], t3[...])):
+            xhat, _ = standardize(t.astype(F32))
             first[pl.ds(p * 64, 64), :] = (xhat * vec[0:1, :] + vec[1:2, :]).astype(BF16)
         for n in range(3):
             project(n, first[...], wqkv, vec, far)
         qkv[0:128, :] = near_in[...]
         qkv[128:256, :] = far[...]
         low, high = half_masks()
-        for j in range(HEADS // 2):
-            q, k, v = (qkv[:, pl.ds(n * 768 + j * 128, 128)] for n in range(3))
-            out = None
-            for keep in (low, high):
-                probs = softmax_rows(nt(q * keep, k), same[...]).astype(BF16)
-                part = nn(probs, v * keep)
-                out = part if out is None else out + part
-            att_o[:, pl.ds(j * 128, 128)] = out.astype(BF16)
-        for n in range(3):
-            half = pl.ds(pl.multiple_of(n * 768 + place.y * 384, 128), 384)
-            mine_o[:, pl.ds(n * 384, 384)] = qkv[:, half]
-
-    def feed(
-        att_own, att_other, t0, t1, t2, t3, vec, up_bias, d0, d1, d2, d3, wout, wup, wdown,
-        sec_o, dup_o, act_o, send_o, dsec_o, hid_core_o, hid_own_o, dy_o,
+        for half in range(2):
+            for j in range(HEADS // 4):
+                start = flip(place.y, half) * 384 + j * 128
+                cols = [pl.ds(pl.multiple_of(n * 768 + start, 128), 128) for n in range(3)]
+                q, k, v = (qkv[:, c] for c in cols)
+                out = None
+                for h, keep in enumerate((low, high)):
+                    e, scale = softmax_parts(nt(q * keep, k), mask[...])
+                    if half == 0:
+                        probs = e * scale
+                        probs_o[2 * j + h] = probs
+                        part = nn(probs.astype(BF16), v * keep)
+                    else:
+                        part = nn(e.astype(BF16), v * keep) * scale
+                    out = part if out is None else out + part
+                (atta_o, attb_o)[half][:, pl.ds(j * 128, 128)] = out.astype(BF16)
+                if half == 0:
+                    for n, value in enumerate((q, k, v)):
+                        mine_o[:, pl.ds(n * 384 + j * 128, 128)] = value
+
+    def residual(
+        atta, attb, othera, otherb, t0, t1, t2, t3_core, t3_away, vec, wout,
+        att_own_o, att_other_o, sec_o, hid_core_o, hid_own_o, t3_o,
         att, hid,
     ):
         place = Place(inner)
-        both_cores(place.core, att_own, att_other, att)
-        gather_rows((d0, d1, d2, d3), dy_o)
+        for out, halves in ((att_own_o, (atta, attb)), (att_other_o, (othera, otherb))):
+            for n, part in enumerate(halves):
+                cols = pl.ds(pl.multiple_of(flip(place.y, n) * 384, 128), 384)
+                out[:, cols] = part[...]
+        both_cores(place.core, att_own_o, att_other_o, att)
+        t3_o[place.core] = t3_core[...]
+        t3_o[1 - place.core] = t3_away[...]
         g, b, ob = vec[5:6, :], vec[6:7, :], vec[4:5, :]
         for s in range(2):
             added = nn(att[s], wout[...]) + ob
-            for p, t in enumerate((t0, t1, t2, t3)):
+            for p, t in enumerate((t0, t1, t2, t3_o)):
                 h = t[s].astype(F32) + added[p * 64 : p * 64 + 64]
                 hid[s, pl.ds(p * 64, 64), :] = h
                 xhat, _ = standardize(h)
                 sec_o[pl.ds(s * 256 + p * 64, 64), :] = (xhat * g + b).astype(BF16)
             hid_own_o[pl.ds(s * 64, 64), :] = hid[s, 0:64, :]
         hid_core_o[...] = hid[place.core]
+
+    def feed(sec_o, up_bias, d0, d1, d2, d3, wup, wdown, dup_o, act_o, send_o, dsec_o, dy_o):
+        place = Place(inner)
+        gather_rows((d0, d1, d2, d3), dy_o)
         for j in range(4):
             cols = pl.ds(j * 384, 384)
             for s in range(2):
@@ -258,11 +281,14 @@
                 j = 2 * z + flip(place.z_low, k)
                 units = pl.ds(pl.multiple_of(j * 384, 128), 384)
                 product = tn(act[:, units], dy_half).astype(BF16)
-                for t in range(3):
-                    out[z, pl.ds(t * 384, 384), :] = product[:, t * 128 : t * 128 + 128]
+                for h in range(2):
+                    for t in range(3):
+                        out[z, h, pl.ds(t * 192, 192), :] = product[
+                            h * 192 : h * 192 + 192, t * 128 : t * 128 + 128
+                        ]
 
     def attention_back(
-        dsec_in, got, hid_core, d0, d1, d2, d3, vec, same, mine, wout, up_sums,
+        dsec_in, got, hid_core, d0, d1, d2, d3, vec, probs_in, mine, wout, up_sums,
         exa_o, exb_o, dhid_o, sums_o, heads_o,
         dh, datt,
     ):
@@ -294,9 +320,9 @@
             q, k, v = (mine[:, pl.ds(n * 384 + j * 128, 128)] for n in range(3))
             da = datt[:, cols]
             dq = dk = dv = None
-            for keep in (low, high):
+            for h, keep in enumerate((low, high)):
                 qh, kh, dah = q * keep, k * keep, da * keep
-                probs = softmax_rows(nt(qh, k), same[...])
+                probs = probs_in[2 * j + h]
                 dprobs = nt(dah, v)
                 delta = jnp.sum(probs * dprobs, axis=-1, keepdims=True)
                 ds = (probs * (dprobs - delta)).astype(BF16)
@@ -337,7 +363,7 @@
     def attention_weights(
         owna, ownb, othera, otherb, first, att, t0, t2, params, sums, heads, up_sums, wqkv,
         keep, send, dfirst_own, dfirst_send,
-        exa, exb, vec,
+        exa, exb, rows, vec,
     ):
         place = Place(inner)
         weights = [wqkv[:, pl.ds(pl.multiple_of(n * 768 + place.y * 384, 128), 384)] for n in range(3)]
@@ -352,19 +378,20 @@
             put_slots(product.astype(BF16), keep, send, offset)
         dgain = jnp.zeros((1, 768), F32)
         dshift = jnp.zeros((1, 768), F32)
-        for s in range(2):
-            for p, t in ((0, t0), (2, t2)):
-                rows = pl.ds(p * 64, 64)
-                xhat, _ = standardize(t[s].astype(F32))
-                part = nt(exa[s, rows, 0:384], weights[0])
-                part += nt(exa[s, rows, 384:768], weights[1])
-                part += nt(exb[s, rows, 0:384], weights[2])
-                dgain += column_sum(part * xhat)
-                dshift += column_sum(part)
-                if p == 0:
-                    dfirst_own[s] = part
-                else:
-                    dfirst_send[s] = part.astype(BF16)
+        pieces = [(s, p, t) for s in range(2) for p, t in ((0, t0), (2, t2))]
+        for i, (s, p, t) in enumerate(pieces):
+            rows[pl.ds(i * 64, 64), 0:768] = exa[s, pl.ds(p * 64, 64), :]
+            rows[pl.ds(i * 64, 64), 768:1152] = exb[s, pl.ds(p * 64, 64), 0:384]
+        parts = sum(nt(rows[:, pl.ds(n * 384, 384)], weights[n]) for n in range(3))
+        for i, (s, p, t) in enumerate(pieces):
+            part = parts[i * 64 : i * 64 + 64]
+            xhat, _ = standardize(t[s].astype(F32))
+            dgain += column_sum(part * xhat)
+            dshift += column_sum(part)
+            if p == 0:
+                dfirst_own[s] = part
+            else:
+                dfirst_send[s] = part.astype(BF16)
         vec[...] = jnp.zeros_like(vec)
         for s in range(SLOTS):
             k, z = flip(place.x, s % 2), s // 2
@@ -390,7 +417,11 @@
             keep[z, pl.ds(576, 16), :] = vec[0, z].astype(BF16)
             send[z, pl.ds(576, 16), :] = vec[1, z].astype(BF16)
 
-    def input_grad(tokens, dfirst, received, dhid, other, vec, hid_own, part, part_got, out, block_o):
+    def input_grad(
+        tokens, dfirst, received, dhid, other, vec, hid_own, part, part_got, before,
+        out, block_o, mark,
+    ):
+        mark[...] = jnp.zeros_like(mark)
         place = Place(inner)
 
         def write(s, residual):
@@ -419,32 +450,40 @@
     def add(a, b, before, out):
         out[...] = (a[...].astype(F32) + b[...].astype(F32)).astype(BF16)
 
-    def assemble_up(p0, p1, p2, p3, out):
-        place = Place(inner)
-        for k, piece in enumerate((p0, p1, p2, p3)):
+    def add_split(a, b, before, kept, sent):
+        core = Place(inner).core
+        for out, k in ((sent, 1), (kept, 0)):
+            at = flip(core, k)
+            out[...] = (a[0, at].astype(F32) + b[0, at].astype(F32)).astype(BF16)
+
+    def pick(kept, got, before, own, other):
+        place = Place(inner)
+
+        def write(mine, others):
+            own[...] = mine[...]
+            other[...] = others[...]
+
+        @pl.when(place.core == place.x)
+        def _():
+            write(kept, got)
+
+        @pl.when(place.core != place.x)
+        def _():
+            write(got, kept)
+
+    def assemble_feed(a0, a1, a2, a3, b0, b1, b2, b3, up_o, down_o):
+        place = Place(inner)
+        for k, (up, down) in enumerate(((a0, b0), (a1, b1), (a2, b2), (a3, b3))):
             y, core = flip(place.y, k // 2), flip(place.core, k % 2)
             rows = pl.ds(pl.multiple_of(y * 48, 16), 48)
             for j in range(4):
                 for t in range(3):
                     cols = pl.ds(pl.multiple_of((2 * j + core) * 384 + t * 128, 128), 128)
-                    out[rows, cols] = piece[0, pl.ds((3 * j + t) * 48, 48), :].astype(F32)
-
-    def assemble_down(mine, across, partner, partner_across, out):
-        place = Place(inner)
-
-        def write(own, other):
-            for k, piece in enumerate((own, other)):
-                for t in range(3):
-                    cols = pl.ds(pl.multiple_of(flip(place.y, k) * 384 + t * 128, 128), 128)
-                    out[:, cols] = piece[0, pl.ds(t * 384, 384), :].astype(F32)
-
-        @pl.when(place.core == place.x)
-        def _():
-            write(mine, across)
-
-        @pl.when(place.core != place.x)
-        def _():
-            write(partner, partner_across)
+                    up_o[rows, cols] = up[0, pl.ds((3 * j + t) * 48, 48), :].astype(F32)
+            rows = pl.ds(pl.multiple_of(core * 192, 64), 192)
+            for t in range(3):
+                cols = pl.ds(pl.multiple_of(y * 384 + t * 128, 128), 128)
+                down_o[rows, cols] = down[pl.ds(t * 192, 192), :].astype(F32)
 
     def assemble_rest(p0, p1, p2, p3, out_o, qkv_o, gain1, shift1, qv, out_b, gain2, shift2, up_b, down_b):
         place = Place(inner)
@@ -489,29 +528,16 @@
     def seq_swap(x, step):
         return swap(x, "seq", seq_size, step * inner)
 
-    def some(x, moved):
-        pairs = []
-        for s in range(seq_size):
-            for b in range(blk_size):
-                to = moved(s, b)
-                if to is not None:
-                    pairs.append((s * blk_size + b, to[0] * blk_size + to[1]))
-        return lax.ppermute(x, ("seq", "blk"), pairs)
-
-    def aligned(s, b):
-        return (s // inner) % 2 == b % 2
-
     def gather(x):
         across = y_swap(x)
         return x, core_swap(x), across, core_swap(across)
 
     def halve(name, keep, got, before):
-        n, rows, lanes = keep.shape
-        shape = ((n // 2, rows, lanes), BF16)
-        return call(kernels[name], (shape, shape), [VMEM, VMEM, ANY], (keep, got, before), us=US)
-
-    def add(a, b, before):
-        return call(kernels["add"], ((a.shape, BF16),), [VMEM, VMEM, ANY], (a, b, before), us=US)[0]
+        shape = ((keep.shape[0] // 2, *keep.shape[1:]), BF16)
+        return call(kernels[name], (shape, shape), [VMEM, VMEM, ANY], (keep, got, before), us=STEP)
+
+    def add(a, b, before, us):
+        return call(kernels["add"], ((a.shape, BF16),), [VMEM, VMEM, ANY], (a, b, before), us=us)[0]
 
     def on_device(
         tokens, ln1_gain, ln1_bias, wqkv, bias_qv, wout, output_bias, ln2_gain, ln2_bias,
@@ -520,46 +546,57 @@
         t1 = core_swap(tokens)
         t2 = y_swap(tokens)
         hbm = in_hbm(
-            tokens, segment_ids, ln1_gain, ln1_bias, bias_qv, output_bias, ln2_gain, ln2_bias, down_bias,
+            dy, tokens, segment_ids, ln1_gain, ln1_bias, bias_qv, output_bias, ln2_gain, ln2_bias, down_bias,
             up_bias, wqkv, wout, wup, wdown,
         )
-        near_qkv, same, vec, up_row, t0, wqkv, wout, wup, wdown = call(
+        near_qkv, mask, vec, up_row, t0, d0, wqkv, wout, wup, wdown = call(
             kernels["near"],
             (
-                ((128, 2304), BF16), ((256, 256), F32), ((8, 768), F32), ((1, 1536), F32), ((2, 64, 768), BF16),
+                ((128, 2304), BF16), ((256, 256), F32), ((8, 768), F32), ((1, 1536), F32), ((2, 64, 768), BF16), ((2, 64, 768), BF16),
                 ((768, 2304), BF16), ((768, 768), BF16), ((768, 1536), BF16), ((1536, 768), BF16),
             ),
-            [VMEM] + [HBM] * 14,
+            [VMEM] + [HBM] * 15,
             (t1, *hbm),
             [pltpu.VMEM((128, 768), BF16), pltpu.VMEM((2, 256), jnp.int32)]
             + [pltpu.VMEM((n,), BF16) for n in (768, 768, 1536, 768, 768, 768, 768, 3072)]
-            + [pltpu.SemaphoreType.DMA((22,))],
+            + [pltpu.SemaphoreType.DMA((23,))],
             us=3.0,
         )
         near_qkv, t2 = lax.optimization_barrier((near_qkv, t2))
-        t3 = core_swap(t2)
-        t_pieces = t0, t1, t2, t3
-        d_pieces = gather(dy)
-        att, mine = call(
+        rows = ((64, 768), BF16)
+        t2_core, t2_away = call(kernels["split_sequences"], (rows, rows), [VMEM], (t2,), us=US)
+        t3_core, t3_away = core_swap(t2_away), core_swap(t2_core)
+        d_pieces = gather(d0)
+        atta, attb, mine, probs = call(
             kernels["attention"],
-            (((256, 768), BF16), ((256, 1152), BF16)),
-            [VMEM] * 6,
-            (near_qkv, same, vec, t2, t3, wqkv),
+            (((256, 384), BF16), ((256, 384), BF16), ((256, 1152), BF16), ((6, 256, 256), F32)),
+            [VMEM] * 6 + [ANY],
+            (near_qkv, mask, vec, t2, t3_core, wqkv, t3_away),
             [pltpu.VMEM((128, 768), BF16), pltpu.VMEM((128, 2304), BF16), pltpu.VMEM((256, 2304), BF16)],
             us=US,
         )
-        att_other = core_swap(att)
-        chunk, half = ((4, 576, 128), BF16), ((2, 1152, 128), BF16)
+        chunk, half = ((4, 576, 128), BF16), ((2, 2, 576, 128), BF16)
         own = (2, 64, 768)
-        sec, dup, act, partial, dsec, hid_core, hid_own, dy_rows = call(
+        att, att_other, sec, hid_core, hid_own, t3 = call(
+            kernels["residual"],
+            (
+                ((256, 768), BF16), ((256, 768), BF16), ((512, 768), BF16), ((256, 768), F32),
+                ((128, 768), F32), (own, BF16),
+            ),
+            [VMEM] * 11,
+            (atta, attb, core_swap(atta), core_swap(attb), t0, t1, t2, t3_core, t3_away, vec, wout),
+            [pltpu.VMEM((2, 256, 768), BF16), pltpu.VMEM((2, 256, 768), F32)],
+            us=US,
+        )
+        t_pieces = t0, t1, t2, t3
+        dup, act, partial, dsec, dy_rows = call(
             kernels["feed"],
             (
-                ((512, 768), BF16), ((512, 1536), BF16), ((512, 1536), BF16), ((256, 768), BF16),
-                ((256, 768), F32), ((256, 768), F32), ((128, 768), F32), ((512, 768), BF16),
+                ((512, 1536), BF16), ((512, 1536), BF16), ((256, 768), BF16), ((256, 768), F32),
+                ((512, 768), BF16),
             ),
-            [VMEM] * 15,
-            (att, att_other, *t_pieces, vec, up_row, *d_pieces, wout, wup, wdown),
-            [pltpu.VMEM((2, 256, 768), BF16), pltpu.VMEM((2, 256, 768), F32)],
+            [VMEM] * 8,
+            (sec, up_row, *d_pieces, wup, wdown),
             us=US,
         )
         arrived = core_swap(partial)
@@ -575,7 +612,7 @@
             kernels["attention_back"],
             (((256, 768), BF16), ((320, 768), BF16), ((64, 768), F32), ((8, 768), F32), ((8, 384), F32)),
             [VMEM] * 12,
-            (dsec, arrived, hid_core, *d_pieces, vec, same, mine, wout, up_sums),
+            (dsec, arrived, hid_core, *d_pieces, vec, probs, mine, wout, up_sums),
             [pltpu.VMEM((256, 768), BF16), pltpu.VMEM((256, 384), BF16)],
             us=US,
         )
@@ -596,44 +633,54 @@
             (exa, exb, exa_other, exb_other, first_t, att_t, t0, t2, vec, sums, heads, up_sums, wqkv),
             [
                 pltpu.VMEM((2, 256, 768), BF16), pltpu.VMEM((2, 256, 768), BF16),
-                pltpu.VMEM((2, 4, 16, 128), F32),
+                pltpu.VMEM((256, 1152), BF16), pltpu.VMEM((2, 4, 16, 128), F32),
             ],
             us=US,
         )
         down_stay, down_leave = halve("halve_z_high", down_keep, seq_swap(down_send, 2), rest_keep)
         up_stay, up_leave = halve("halve_z_low", up_keep, seq_swap(up_send, 1), down_stay)
-        down_part = add(down_stay, seq_swap(down_leave, 4), up_stay)
-        up_stay, up_leave = halve("halve_z_high", up_stay, seq_swap(up_leave, 2), down_part)
         rest_stay, rest_leave = halve("halve_z_low", rest_keep, seq_swap(rest_send, 1), up_stay)
-        over_x = some(down_part, lambda s, b: None if aligned(s, b) else (s ^ inner, b))
-        down_sum = add(down_part, over_x, rest_stay)
-        up_sum = add(up_stay, seq_swap(up_leave, 4), down_sum)
-        rest_stay, rest_leave = halve("halve_z_high", rest_stay, seq_swap(rest_leave, 2), up_sum)
-        rest_sum = add(rest_stay, seq_swap(rest_leave, 4), up_sum)
-        up_pieces = gather(up_sum)
-        across = some(down_sum, lambda s, b: (s, b ^ 2) if aligned(s, b) else None)
-        to_core = lambda s, b: (s, b ^ 1) if aligned(s, b) else None
-        down_pieces = down_sum, across, some(down_sum, to_core), some(across, to_core)
-        in_grad, block_out = call(
+        in_grad, block_out, mark = call(
             kernels["input_grad"],
-            ((own, BF16), (own, BF16)),
-            [VMEM] * 9,
+            ((own, BF16), (own, BF16), ((8, 128), F32)),
+            [VMEM] * 9 + [ANY],
             (
                 t0, dfirst_own, y_swap(dfirst_send), dhid, exb_other, vec, hid_own, part,
-                core_swap(part_send),
+                core_swap(part_send), rest_stay,
             ),
             us=US,
         )
-        (up_o,) = call(kernels["assemble_up"], (((96, 3072), F32),), [VMEM] * 4, up_pieces, us=US)
-        (down_o,) = call(kernels["assemble_down"], (((384, 768), F32),), [VMEM] * 4, down_pieces, us=US)
+        piece = ((576, 128), BF16)
+        down_kept, down_sent = call(
+            kernels["add_split"],
+            (piece, piece),
+            [VMEM, VMEM, ANY],
+            (down_stay, seq_swap(down_leave, 4), mark),
+            us=STEP,
+        )
+        up_stay, up_leave = halve("halve_z_high", up_stay, seq_swap(up_leave, 2), down_kept)
+        down_own, down_other = call(
+            kernels["pick"], (piece, piece), [VMEM, VMEM, ANY], (down_kept, core_swap(down_sent), up_stay), us=STEP
+        )
+        rest_stay, rest_leave = halve("halve_z_high", rest_stay, seq_swap(rest_leave, 2), down_own)
+        up_sum = add(up_stay, seq_swap(up_leave, 4), rest_stay, STEP)
+        down_sum = add(down_own, seq_swap(down_other, 1), up_sum, STEP)
+        rest_sum = add(rest_stay, seq_swap(rest_leave, 4), down_sum, FILL)
+        up_pieces, down_pieces, rest_across = gather(up_sum), gather(down_sum), y_swap(rest_sum)
+        up_o, down_o = call(
+            kernels["assemble_feed"],
+            (((96, 3072), F32), ((384, 768), F32)),
+            [VMEM] * 8,
+            (*up_pieces, *down_pieces),
+            us=US,
+        )
+        rest_across, up_o, down_o = lax.optimization_barrier((rest_across, up_o, down_o))
         small = [96, 96, 192, 96, 96, 96, 384, 96]
-        across = y_swap(rest_sum)
-        hop, in_grad, up_o, down_o = lax.optimization_barrier((across, in_grad, up_o, down_o))
         out_o, qkv_o, *vectors = call(
             kernels["assemble_rest"],
             (((96, 768), F32), ((96, 2304), F32)) + tuple(((n,), F32) for n in small),
             [VMEM] * 4,
-            (rest_sum, core_swap(rest_sum), hop, core_swap(hop)),
+            (rest_sum, core_swap(rest_sum), rest_across, core_swap(rest_across)),
             us=US,
         )
         gain1, shift1, qv, out_b, gain2, shift2, up_b, down_b = vectors

time: 93.5 us -> 85.7 us (0.917)
  starting transfers between devices: 33.4 us -> 25.1 us
  waiting for transfers between devices: 29.8 us -> 33.5 us
  Pallas kernels: 29.2 us -> 26.1 us
    ppermute x4 -> x0, starting transfers between devices: 7.9 us -> none  [some(): return lax.ppermute(x, ('seq', 'blk'), pairs)]
    ppermute x26 -> x33, waiting for transfers between devices: 26.8 us -> 33.5 us  [swap(): return lax.ppermute(x, axis, [(i, i ^ step) for i in range(size)])]
    pallas_call x20 -> x22, Pallas kernels: 29.2 us -> 26.1 us  [call(): pl.pallas_call(kernel, out_shape=tuple((jax.ShapeDtypeStruct(s, d) for s,...]
    ppermute x4 -> x0, waiting for transfers between devices: 2.97 us -> none  [some(): return lax.ppermute(x, ('seq', 'blk'), pairs)]
    ppermute x26 -> x33, starting transfers between devices: 25.5 us -> 25.1 us  [swap(): return lax.ppermute(x, axis, [(i, i ^ step) for i in range(size)])]
  transfers between devices with their start and end apart: 30 -> 33, of which waited for: 14 -> 17; matrix products, arithmetic and copies ran while one was open for 0% -> 0% of each run, Pallas kernels for 24% -> 23%
where the time goes in v4:
time: 85.7 us; the launch traced here: 85.6 us
  waiting for transfers between devices  33.5 us (39%)
  Pallas kernels  26.1 us (30%)
  starting transfers between devices  25.1 us (29%)
    ppermute x33, waiting for transfers between devices, swap(): return lax.ppermute(x, axis, [(i, i ^ step) for i in range(size)])  33.5 us
    pallas_call x22, Pallas kernels, call(): pl.pallas_call(kernel, out_shape=tuple((jax.ShapeDtypeStruct(s, d) for s,...  26.1 us
    ppermute x33, starting transfers between devices, swap(): return lax.ppermute(x, axis, [(i, i ^ step) for i in range(size)])  25.1 us
  transfers between devices with their start and end apart: 33, of which 17 were waited for; matrix products, arithmetic and copies ran while one was open for 0% of the time, Pallas kernels for 23%

profile of v4, /device:TPU:0, one launch (start us, length us, event | category | flops | bytes accessed | tf_op | source)
XLA Modules:
  0.0 85.6 jit_solution(6025861162967133504)
XLA Ops:
  0.6 0.5 collective-permute-start
  1.2 2.6 %collective-permute-start.1 = (bf16[2,64,768]{2,1,0:T(8,128)(2,1)}, bf16[2,64,768]{2,1,0:T(8,128)(2,1)S(1)}, u32[]{:S(2)}, u32[]{:S(2)}) collective-permute-start(bf16[2,64,768]{2,1,0:T(8,128)(2,1)} %tokens_hbm.1), channel_id=1, source_target_pairs={{0,2},{1,3},{2,0},{3,1},{4,6},{5,7},{6,4},{7,5},{8,10},{9,11},{10,... | collective-permute-start | bytes 589832 | tf_op jit(solution)/shard_map/ppermute | solution.py:520
  3.8 4.2 %near.1 = (bf16[128,2304]{1,0:T(8,128)(2,1)S(1)}, f32[256,256]{1,0:T(8,128)S(1)}, f32[8,768]{1,0:T(8,128)S(1)}, f32[1,1536]{1,0:T(1,128)S(1)}, bf16[2,64,768]{2,...) custom-call(bf16[2,64,768]{2,1,0:T(8,128)(2,1)S(1)} %collective-perm, ...), custom_call_target="tpu_custom_call" | custom-call | flops 3000000000 | bytes 300000 | tf_op jit(solution)/shard_map/near/pallas_call | solution.py:74
  8.0 1.6 %collective-permute-start.7 = (bf16[2,64,768]{2,1,0:T(8,128)(2,1)S(1)}, bf16[2,64,768]{2,1,0:T(8,128)(2,1)S(1)}, u32[]{:S(2)}, u32[]{:S(2)}) collective-permute-start(bf16[2,64,768]{2,1,0:T(8,128)(2,1)S(1)} %get-tuple-element.107.d0), channel_id=1, source_target_pairs={{0,2},{1,3},{2,0},{3,1},{4,6},{5,7},{6,4},{7,5},{8,10},{9,11},{10,... | collective-permute-start | bytes 589832 | tf_op jit(solution)/shard_map/ppermute | solution.py:520
  9.7 0.5 collective-permute-start.3
  10.2 0.8 collective-permute-done.2.t3.t3_core
  11.2 2.9 %attention.1 = (bf16[256,384]{1,0:T(8,128)(2,1)S(1)}, bf16[256,384]{1,0:T(8,128)(2,1)S(1)}, bf16[256,1152]{1,0:T(8,128)(2,1)S(1)}, f32[6,256,256]{2,1,0:T(8,128)S(1)}) custom-call(bf16[128,2304]{1,0:T(8,128)(2,1)S(1)} %get-tuple-element.95.near_in, f32[256,256]{1,0:T(8,128)S(1)} %get-tuple-element.96.mask, f32[8,768]{1,0:T(8,128)S(1)} %get-tuple-element.97.vec.params, ...), custom_call_target="tpu_custom_call" | custom-call | flops 10000000 | bytes 1000 | tf_op jit(solution)/shard_map/attention/pallas_call | solution.py:74
  14.1 0.4 collective-permute-start.4
  14.7 0.4 collective-permute-start.6
  15.2 0.4 collective-permute-done.4.othera
  15.6 0.4 collective-permute-done.5.otherb
  16.0 1.5 %residual.1 = (bf16[256,768]{1,0:T(8,128)(2,1)S(1)}, bf16[256,768]{1,0:T(8,128)(2,1)S(1)}, bf16[512,768]{1,0:T(8,128)(2,1)S(1)}, f32[256,768]{1,0:T(8,128)S(1)},...) custom-call(bf16[256,384]{1,0:T(8,128)(2,1)S(1)} %get-tuple-element.102.atta, ...), custom_call_target="tpu_custom_call" | custom-call | flops 10000000 | bytes 1000 | tf_op jit(solution)/shard_map/residual/pallas_call | solution.py:74
  17.5 5.0 %feed.1 = (bf16[512,1536]{1,0:T(8,128)(2,1)S(1)}, bf16[512,1536]{1,0:T(8,128)(2,1)S(1)}, bf16[256,768]{1,0:T(8,128)(2,1)S(1)}, f32[256,768]{1,0:T(8,128)S(1)}, bf16[512,768]{1,0:T(8,128)(2,1)S(1)}) custom-call(bf16[512,768]{1,0:T(8,128)(2,1)S(1)} %get-tuple-element.105.sec_o.sec, f32[1,1536]{1,0:T(1,128)S(1)} %get-tuple-element.106.up_bias, ...), custom_call_target="tpu_custom_call" | custom-call | flops 10000000 | bytes 1000 | tf_op jit(solution)/shard_map/feed/pallas_call | solution.py:74
  22.5 0.4 collective-permute-start.9
  22.9 2.0 %feed_weights.1 = (bf16[4,576,128]{2,1,0:T(8,128)(2,1)S(1)}, bf16[4,576,128]{2,1,0:T(8,128)(2,1)S(1)}, bf16[2,2,576,128]{3,2,1,0:T(8,128)(2,1)S(1)}, bf16[2,2,576,128]{3,2,1,0:T(8,128)(2,1)S(1)}, f32[1,1536]{1,0:T(1,128)S(1)}) custom-call(bf16[512,768]{1,0:T(8,128)(2,1)S(1)} %get-tuple-element.105.sec_o.sec, bf16[512,1536]{1,0:T(8,128)(2,1)S(1)} %get-tuple-element.115.dup, ...), custom_call_target="tpu_custom_call" | custom-call | flops 20000000000 | bytes 2000000 | tf_op jit(solution)/shard_map/feed_weights/pallas_call | solution.py:74
  24.9 1.6 %collective-permute-start.15 = (bf16[4,576,128]{2,1,0:T(8,128)(2,1)S(1)}, bf16[4,576,128]{2,1,0:T(8,128)(2,1)S(1)}, u32[]{:S(2)}, u32[]{:S(2)}) collective-permute-start(bf16[4,576,128]{2,1,0:T(8,128)(2,1)S(1)} %get-tuple-element.137), channel_id=1, source_target_pairs={{0,4},{4,0},{8,12},{12,8},{16,20},{20,16},{24,28},{28,24},{1,5},{5... | collective-permute-start | bytes 1769480 | tf_op jit(solution)/shard_map/ppermute | solution.py:520
  26.5 1.6 %collective-permute-start.16 = (bf16[2,2,576,128]{3,2,1,0:T(8,128)(2,1)S(1)}, bf16[2,2,576,128]{3,2,1,0:T(8,128)(2,1)S(1)}, u32[]{:S(2)}, u32[]{:S(2)}) collective-permute-start(bf16[2,2,576,128]{3,2,1,0:T(8,128)(2,1)S(1)} %get-tuple-element.139), channel_id=1, source_target_pairs={{0,8},{4,12},{8,0},{12,4},{16,24},{20,28},{24,16},{28,20},{1,9},{5... | collective-permute-start | bytes 1769480 | tf_op jit(solution)/shard_map/ppermute | solution.py:520
  28.1 2.7 %attention_back.1 = (bf16[256,768]{1,0:T(8,128)(2,1)S(1)}, bf16[320,768]{1,0:T(8,128)(2,1)S(1)}, f32[64,768]{1,0:T(8,128)S(1)}, f32[8,768]{1,0:T(8,128)S(1)}, f32[8,384]{1,0:T(8,128)S(1)}) custom-call(f32[256,768]{1,0:T(8,128)S(1)} %get-tuple-element.110.dsec_in, bf16[256,768]{1,0:T(8,128)(2,1)S(1)} %collective-permute-done.9.got, ...), custom_call_target="tpu_custom_call" | custom-call | flops 10000000 | bytes 1000 | tf_op jit(solution)/shard_map/attention_back/pallas_call | solution.py:74
  30.9 0.5 collective-permute-start.11
  31.4 1.4 %turn.1 = (bf16[384,512]{1,0:T(8,128)(2,1)S(1)}, bf16[384,512]{1,0:T(8,128)(2,1)S(1)}, f32[2,64,768]{2,1,0:T(8,128)S(1)}, bf16[2,64,768]{2,1,0:T(8,128)(2,1)S(1)}) custom-call(bf16[256,768]{1,0:T(8,128)(2,1)S(1)} %get-tuple-element.121.att_own, bf16[256,768]{1,0:T(8,128)(2,1)S(1)} %get-tuple-element.122.att_other, ...), custom_call_target="tpu_custom_call" | custom-call | flops 20000000000 | bytes 2000000 | tf_op jit(solution)/shard_map/turn/pallas_call | solution.py:74
  32.9 0.5 collective-permute-done.11.otherb.other
  33.3 1.8 %attention_weights.1 = (bf16[4,592,128]{2,1,0:T(8,128)(2,1)S(1)}, bf16[4,592,128]{2,1,0:T(8,128)(2,1)S(1)}, f32[2,64,768]{2,1,0:T(8,128)S(1)}, bf16[2,64,768]{2,1,0:T(8,128)(2,1)S(1)}) custom-call(bf16[256,768]{1,0:T(8,128)(2,1)S(1)} %get-tuple-element.119.owna, bf16[320,768]{1,0:T(8,128)(2,1)S(1)} %get-tuple-element.120.ownb, ...), custom_call_target="tpu_custom_call" | custom-call | flops 10000000 | bytes 1000 | tf_op jit(solution)/shard_map/attention_weights/pallas_call | solution.py:74
  35.1 0.6 collective-permute-start.14
  35.7 6.0 %collective-permute-done.16.got = bf16[2,2,576,128]{3,2,1,0:T(8,128)(2,1)S(1)} collective-permute-done((bf16[2,2,576,128]{3,2,1,0:T(8,128)(2,1)S(1)}, bf16[2,2,576,128]{3,2,1,0:T(8,128)(2,1)S(1)}, u32[]{:S(2)}, u32[]{:S(2)}) %collective-permute-start.16) | collective-permute-done | bytes 589856 | tf_op jit(solution)/shard_map/ppermute | solution.py:520
  41.8 2.6 %collective-permute-start.18 = (bf16[1,2,576,128]{3,2,1,0:T(8,128)(2,1)S(1)}, bf16[1,2,576,128]{3,2,1,0:T(8,128)(2,1)S(1)}, u32[]{:S(2)}, u32[]{:S(2)}) collective-permute-start(bf16[1,2,576,128]{3,2,1,0:T(8,128)(2,1)S(1)} %get-tuple-element.146), channel_id=1, source_target_pairs={{0,16},{4,20},{8,24},{12,28},{16,0},{20,4},{24,8},{28,12},{1,17},{... | collective-permute-start | bytes 884744 | tf_op jit(solution)/shard_map/ppermute | solution.py:520
  44.5 1.5 %collective-permute-start.12 = (bf16[2,64,768]{2,1,0:T(8,128)(2,1)S(1)}, bf16[2,64,768]{2,1,0:T(8,128)(2,1)S(1)}, u32[]{:S(2)}, u32[]{:S(2)}) collective-permute-start(bf16[2,64,768]{2,1,0:T(8,128)(2,1)S(1)} %get-tuple-element.129), channel_id=1, source_target_pairs={{0,2},{1,3},{2,0},{3,1},{4,6},{5,7},{6,4},{7,5},{8,10},{9,11},{10,... | collective-permute-start | bytes 589832 | tf_op jit(solution)/shard_map/ppermute | solution.py:520
  46.2 1.6 %collective-permute-start.20 = (bf16[2,576,128]{2,1,0:T(8,128)(2,1)S(1)}, bf16[2,576,128]{2,1,0:T(8,128)(2,1)S(1)}, u32[]{:S(2)}, u32[]{:S(2)}) collective-permute-start(bf16[2,576,128]{2,1,0:T(8,128)(2,1)S(1)} %get-tuple-element.150), channel_id=1, source_target_pairs={{0,8},{4,12},{8,0},{12,4},{16,24},{20,28},{24,16},{28,20},{1,9},{5... | collective-permute-start | bytes 884744 | tf_op jit(solution)/shard_map/ppermute | solution.py:520
  47.8 5.6 %collective-permute-done.14.got = bf16[4,592,128]{2,1,0:T(8,128)(2,1)S(1)} collective-permute-done((bf16[4,592,128]{2,1,0:T(8,128)(2,1)S(1)}, bf16[4,592,128]{2,1,0:T(8,128)(2,1)S(1)}, u32[]{:S(2)}, u32[]{:S(2)}) %collective-permute-start.14) | collective-permute-done | bytes 606240 | tf_op jit(solution)/shard_map/ppermute | solution.py:520
  53.5 1.7 %collective-permute-start.17 = (bf16[2,592,128]{2,1,0:T(8,128)(2,1)S(1)}, bf16[2,592,128]{2,1,0:T(8,128)(2,1)S(1)}, u32[]{:S(2)}, u32[]{:S(2)}) collective-permute-start(bf16[2,592,128]{2,1,0:T(8,128)(2,1)S(1)} %get-tuple-element.145), channel_id=1, source_target_pairs={{0,8},{4,12},{8,0},{12,4},{16,24},{20,28},{24,16},{28,20},{1,9},{5... | collective-permute-start | bytes 909320 | tf_op jit(solution)/shard_map/ppermute | solution.py:520
  55.3 1.1 %input_grad.1 = (bf16[2,64,768]{2,1,0:T(8,128)(2,1)}, bf16[2,64,768]{2,1,0:T(8,128)(2,1)}, f32[8,128]{1,0:T(8,128)S(1)}) custom-call(bf16[2,64,768]{2,1,0:T(8,128)(2,1)S(1)} %get-tuple-element.93.t0.tokens, f32[2,64,768]{2,1,0:T(8,128)S(1)} %get-tuple-element.128.dfirst, bf16[2,64,768]{2,1,0:T(8,128)(2,1)S(1)} %collective-permute-done.12.received, ...), custom_call_target="tpu_custom_call" | custom-call | flops 10000000 | bytes 1000 | tf_op jit(solution)/shard_map/input_grad/pallas_call | solution.py:74
  56.4 0.8 collective-permute-done.18.b
  57.4 3.9 %collective-permute-done.20.got = bf16[2,576,128]{2,1,0:T(8,128)(2,1)S(1)} collective-permute-done((bf16[2,576,128]{2,1,0:T(8,128)(2,1)S(1)}, bf16[2,576,128]{2,1,0:T(8,128)(2,1)S(1)}, u32[]{:S(2)}, u32[]{:S(2)}) %collective-permute-start.20) | collective-permute-done | bytes 294944 | tf_op jit(solution)/shard_map/ppermute | solution.py:520
  61.4 0.5 collective-permute-start.23
  61.9 0.6 collective-permute-start.22
  62.5 7.7 %collective-permute-done.17.got = bf16[2,592,128]{2,1,0:T(8,128)(2,1)S(1)} collective-permute-done((bf16[2,592,128]{2,1,0:T(8,128)(2,1)S(1)}, bf16[2,592,128]{2,1,0:T(8,128)(2,1)S(1)}, u32[]{:S(2)}, u32[]{:S(2)}) %collective-permute-start.17) | collective-permute-done | bytes 303136 | tf_op jit(solution)/shard_map/ppermute | solution.py:520
  70.3 0.5 collective-permute-start.21
  71.1 2.1 %collective-permute-start.30 = (bf16[576,128]{1,0:T(8,128)(2,1)S(1)}, bf16[576,128]{1,0:T(8,128)(2,1)S(1)}, u32[]{:S(2)}, u32[]{:S(2)}) collective-permute-start(bf16[576,128]{1,0:T(8,128)(2,1)S(1)} %add.4.before.b0), channel_id=1, source_target_pairs={{0,2},{1,3},{2,0},{3,1},{4,6},{5,7},{6,4},{7,5},{8,10},{9,11},{10,... | collective-permute-start | bytes 442376 | tf_op jit(solution)/shard_map/ppermute | solution.py:520
  73.1 4.7 %collective-permute-done.21.b = bf16[1,592,128]{2,1,0:T(8,128)(2,1)S(1)} collective-permute-done((bf16[1,592,128]{2,1,0:T(8,128)(2,1)S(1)}, bf16[1,592,128]{2,1,0:T(8,128)(2,1)S(1)}, u32[]{:S(2)}, u32[]{:S(2)}) %collective-permute-start.21) | collective-permute-done | bytes 151584 | tf_op jit(solution)/shard_map/ppermute | solution.py:520
  77.8 1.4 %collective-permute-start.25 = (bf16[1,592,128]{2,1,0:T(8,128)(2,1)S(1)}, bf16[1,592,128]{2,1,0:T(8,128)(2,1)S(1)}, u32[]{:S(2)}, u32[]{:S(2)}) collective-permute-start(bf16[1,592,128]{2,1,0:T(8,128)(2,1)S(1)} %add.5.p0), channel_id=1, source_target_pairs={{0,2},{1,3},{2,0},{3,1},{4,6},{5,7},{6,4},{7,5},{8,10},{9,11},{10,... | collective-permute-start | bytes 454664 | tf_op jit(solution)/shard_map/ppermute | solution.py:520
  79.2 0.5 collective-permute-start.26
  79.7 0.5 collective-permute-start.28
  80.2 0.3 collective-permute-done.29.b1
  80.8 0.3 collective-permute-done.31.b3
  81.1 0.2 collective-permute-done.28.a3
  81.3 1.6 %assemble_feed.1 = (f32[96,3072]{1,0:T(8,128)}, f32[384,768]{1,0:T(8,128)}) custom-call(bf16[1,576,128]{2,1,0:T(8,128)(2,1)S(1)} %add.3.before.a0, bf16[1,576,128]{2,1,0:T(8,128)(2,1)S(1)} %collective-permute-done.26.a1, bf16[1,576,128]{2,1,0:T(8,128)(2,1)S(1)} %collective-permute-done.27.a2, bf16[1,576,128]{2,1,0:T(8,128)(2,1)S(1)} %collective-permute-done.28.a3, ...), custom_call_target="tpu_custom_call" | custom-call | flops 10000000 | bytes 1000 | tf_op jit(solution)/shard_map/assemble_feed/pallas_call | solution.py:74
  82.8 0.2 collective-permute-done.25.p2
  83.1 1.3 %collective-permute-done.32.p3 = bf16[1,592,128]{2,1,0:T(8,128)(2,1)S(1)} collective-permute-done((bf16[1,592,128]{2,1,0:T(8,128)(2,1)S(1)}, bf16[1,592,128]{2,1,0:T(8,128)(2,1)S(1)}, u32[]{:S(2)}, u32[]{:S(2)}) %collective-permute-start.32) | collective-permute-done | bytes 151584 | tf_op jit(solution)/shard_map/ppermute | solution.py:520
  84.5 1.1 %assemble_rest.1 = (f32[96,768]{1,0:T(8,128)}, f32[96,2304]{1,0:T(8,128)}, f32[96]{0:T(128)}, f32[96]{0:T(128)}, f32[192]{0:T(256)}, /*index=5*/f32[96]{0:T(128)...) custom-call(bf16[1,592,128]{2,1,0:T(8,128)(2,1)S(1)} %add.5.p0, bf16[1,592,128]{2,1,0:T(8,128)(2,1)S(1)} %collective-permute-done.24.p1, ...), custom_call_target="tpu_custom_call" | custom-call | flops 10000000 | bytes 1000 | tf_op jit(solution)/shard_map/assemble_rest/pallas_call | solution.py:74
  (40 shorter events, 1.9 us)
Async XLA Ops:
  0.6 3.1 %collective-permute-start = (bf16[2,64,768]{2,1,0:T(8,128)(2,1)}, bf16[2,64,768]{2,1,0:T(8,128)(2,1)S(1)}, u32[]{:S(2)}, u32[]{:S(2)}) collective-permute-start(bf16[2,64,768]{2,1,0:T(8,128)(2,1)} %tokens_hbm.1), channel_id=1, source_target_pairs={{0,1},{1,0},{2,3},{3,2},{4,5},{5,4},{6,7},{7,6},{8,9},{9,8},{10,11... | collective-permute-start | bytes 589832 | tf_op jit(solution)/shard_map/ppermute | solution.py:520
  1.2 8.5 %collective-permute-start.1 = (bf16[2,64,768]{2,1,0:T(8,128)(2,1)}, bf16[2,64,768]{2,1,0:T(8,128)(2,1)S(1)}, u32[]{:S(2)}, u32[]{:S(2)}) collective-permute-start(bf16[2,64,768]{2,1,0:T(8,128)(2,1)} %tokens_hbm.1), channel_id=1, source_target_pairs={{0,2},{1,3},{2,0},{3,1},{4,6},{5,7},{6,4},{7,5},{8,10},{9,11},{10,... | collective-permute-start | bytes 589832 | tf_op jit(solution)/shard_map/ppermute | solution.py:520
  8.0 7.0 %collective-permute-start.7 = (bf16[2,64,768]{2,1,0:T(8,128)(2,1)S(1)}, bf16[2,64,768]{2,1,0:T(8,128)(2,1)S(1)}, u32[]{:S(2)}, u32[]{:S(2)}) collective-permute-start(bf16[2,64,768]{2,1,0:T(8,128)(2,1)S(1)} %get-tuple-element.107.d0), channel_id=1, source_target_pairs={{0,2},{1,3},{2,0},{3,1},{4,6},{5,7},{6,4},{7,5},{8,10},{9,11},{10,... | collective-permute-start | bytes 589832 | tf_op jit(solution)/shard_map/ppermute | solution.py:520
  9.7 1.4 %collective-permute-start.2 = (bf16[64,768]{1,0:T(8,128)(2,1)S(1)}, bf16[64,768]{1,0:T(8,128)(2,1)S(1)}, u32[]{:S(2)}, u32[]{:S(2)}) collective-permute-start(bf16[64,768]{1,0:T(8,128)(2,1)S(1)} %get-tuple-element.99), channel_id=1, source_target_pairs={{0,1},{1,0},{2,3},{3,2},{4,5},{5,4},{6,7},{7,6},{8,9},{9,8},{10,11... | collective-permute-start | bytes 294920 | tf_op jit(solution)/shard_map/ppermute | solution.py:520
  9.7 1.4 %collective-permute-start.3 = (bf16[64,768]{1,0:T(8,128)(2,1)S(1)}, bf16[64,768]{1,0:T(8,128)(2,1)S(1)}, u32[]{:S(2)}, u32[]{:S(2)}) collective-permute-start(bf16[64,768]{1,0:T(8,128)(2,1)S(1)} %get-tuple-element.101), channel_id=1, source_target_pairs={{0,1},{1,0},{2,3},{3,2},{4,5},{5,4},{6,7},{7,6},{8,9},{9,8},{10,11... | collective-permute-start | bytes 294920 | tf_op jit(solution)/shard_map/ppermute | solution.py:520
  14.1 1.5 %collective-permute-start.4 = (bf16[256,384]{1,0:T(8,128)(2,1)S(1)}, bf16[256,384]{1,0:T(8,128)(2,1)S(1)}, u32[]{:S(2)}, u32[]{:S(2)}) collective-permute-start(bf16[256,384]{1,0:T(8,128)(2,1)S(1)} %get-tuple-element.102.atta), channel_id=1, source_target_pairs={{0,1},{1,0},{2,3},{3,2},{4,5},{5,4},{6,7},{7,6},{8,9},{9,8},{10,11... | collective-permute-start | bytes 589832 | tf_op jit(solution)/shard_map/ppermute | solution.py:520
  14.5 1.4 %collective-permute-start.5 = (bf16[256,384]{1,0:T(8,128)(2,1)S(1)}, bf16[256,384]{1,0:T(8,128)(2,1)S(1)}, u32[]{:S(2)}, u32[]{:S(2)}) collective-permute-start(bf16[256,384]{1,0:T(8,128)(2,1)S(1)} %get-tuple-element.103.attb), channel_id=1, source_target_pairs={{0,1},{1,0},{2,3},{3,2},{4,5},{5,4},{6,7},{7,6},{8,9},{9,8},{10,11... | collective-permute-start | bytes 589832 | tf_op jit(solution)/shard_map/ppermute | solution.py:520
  14.7 2.8 %collective-permute-start.6 = (bf16[2,64,768]{2,1,0:T(8,128)(2,1)S(1)}, bf16[2,64,768]{2,1,0:T(8,128)(2,1)S(1)}, u32[]{:S(2)}, u32[]{:S(2)}) collective-permute-start(bf16[2,64,768]{2,1,0:T(8,128)(2,1)S(1)} %get-tuple-element.107.d0), channel_id=1, source_target_pairs={{0,1},{1,0},{2,3},{3,2},{4,5},{5,4},{6,7},{7,6},{8,9},{9,8},{10,11... | collective-permute-start | bytes 589832 | tf_op jit(solution)/shard_map/ppermute | solution.py:520
  15.0 2.4 %collective-permute-start.8 = (bf16[2,64,768]{2,1,0:T(8,128)(2,1)S(1)}, bf16[2,64,768]{2,1,0:T(8,128)(2,1)S(1)}, u32[]{:S(2)}, u32[]{:S(2)}) collective-permute-start(bf16[2,64,768]{2,1,0:T(8,128)(2,1)S(1)} %collective-permute-done.7.d2), channel_id=1, source_target_pairs={{0,1},{1,0},{2,3},{3,2},{4,5},{5,4},{6,7},{7,6},{8,9},{9,8},{10,11... | collective-permute-start | bytes 589832 | tf_op jit(solution)/shard_map/ppermute | solution.py:520
  22.5 5.6 %collective-permute-start.9 = (bf16[256,768]{1,0:T(8,128)(2,1)S(1)}, bf16[256,768]{1,0:T(8,128)(2,1)S(1)}, u32[]{:S(2)}, u32[]{:S(2)}) collective-permute-start(bf16[256,768]{1,0:T(8,128)(2,1)S(1)} %get-tuple-element.111), channel_id=1, source_target_pairs={{0,1},{1,0},{2,3},{3,2},{4,5},{5,4},{6,7},{7,6},{8,9},{9,8},{10,11... | collective-permute-start | bytes 1179656 | tf_op jit(solution)/shard_map/ppermute | solution.py:520
  24.9 21.1 %collective-permute-start.15 = (bf16[4,576,128]{2,1,0:T(8,128)(2,1)S(1)}, bf16[4,576,128]{2,1,0:T(8,128)(2,1)S(1)}, u32[]{:S(2)}, u32[]{:S(2)}) collective-permute-start(bf16[4,576,128]{2,1,0:T(8,128)(2,1)S(1)} %get-tuple-element.137), channel_id=1, source_target_pairs={{0,4},{4,0},{8,12},{12,8},{16,20},{20,16},{24,28},{28,24},{1,5},{5... | collective-permute-start | bytes 1769480 | tf_op jit(solution)/shard_map/ppermute | solution.py:520
  26.5 15.2 %collective-permute-start.16 = (bf16[2,2,576,128]{3,2,1,0:T(8,128)(2,1)S(1)}, bf16[2,2,576,128]{3,2,1,0:T(8,128)(2,1)S(1)}, u32[]{:S(2)}, u32[]{:S(2)}) collective-permute-start(bf16[2,2,576,128]{3,2,1,0:T(8,128)(2,1)S(1)} %get-tuple-element.139), channel_id=1, source_target_pairs={{0,8},{4,12},{8,0},{12,4},{16,24},{20,28},{24,16},{28,20},{1,9},{5... | collective-permute-start | bytes 1769480 | tf_op jit(solution)/shard_map/ppermute | solution.py:520
  30.8 2.0 %collective-permute-start.10 = (bf16[256,768]{1,0:T(8,128)(2,1)S(1)}, bf16[256,768]{1,0:T(8,128)(2,1)S(1)}, u32[]{:S(2)}, u32[]{:S(2)}) collective-permute-start(bf16[256,768]{1,0:T(8,128)(2,1)S(1)} %get-tuple-element.119.owna), channel_id=1, source_target_pairs={{0,1},{1,0},{2,3},{3,2},{4,5},{5,4},{6,7},{7,6},{8,9},{9,8},{10,11... | collective-permute-start | bytes 1179656 | tf_op jit(solution)/shard_map/ppermute | solution.py:520
  30.9 2.4 %collective-permute-start.11 = (bf16[320,768]{1,0:T(8,128)(2,1)S(1)}, bf16[320,768]{1,0:T(8,128)(2,1)S(1)}, u32[]{:S(2)}, u32[]{:S(2)}) collective-permute-start(bf16[320,768]{1,0:T(8,128)(2,1)S(1)} %get-tuple-element.120.ownb), channel_id=1, source_target_pairs={{0,1},{1,0},{2,3},{3,2},{4,5},{5,4},{6,7},{7,6},{8,9},{9,8},{10,11... | collective-permute-start | bytes 1474568 | tf_op jit(solution)/shard_map/ppermute | solution.py:520
  35.1 18.3 %collective-permute-start.14 = (bf16[4,592,128]{2,1,0:T(8,128)(2,1)S(1)}, bf16[4,592,128]{2,1,0:T(8,128)(2,1)S(1)}, u32[]{:S(2)}, u32[]{:S(2)}) collective-permute-start(bf16[4,592,128]{2,1,0:T(8,128)(2,1)S(1)} %get-tuple-element.135), channel_id=1, source_target_pairs={{0,4},{4,0},{8,12},{12,8},{16,20},{20,16},{24,28},{28,24},{1,5},{5... | collective-permute-start | bytes 1818632 | tf_op jit(solution)/shard_map/ppermute | solution.py:520
  41.8 15.4 %collective-permute-start.18 = (bf16[1,2,576,128]{3,2,1,0:T(8,128)(2,1)S(1)}, bf16[1,2,576,128]{3,2,1,0:T(8,128)(2,1)S(1)}, u32[]{:S(2)}, u32[]{:S(2)}) collective-permute-start(bf16[1,2,576,128]{3,2,1,0:T(8,128)(2,1)S(1)} %get-tuple-element.146), channel_id=1, source_target_pairs={{0,16},{4,20},{8,24},{12,28},{16,0},{20,4},{24,8},{28,12},{1,17},{... | collective-permute-start | bytes 884744 | tf_op jit(solution)/shard_map/ppermute | solution.py:520
  44.5 10.8 %collective-permute-start.13 = (bf16[2,64,768]{2,1,0:T(8,128)(2,1)S(1)}, bf16[2,64,768]{2,1,0:T(8,128)(2,1)S(1)}, u32[]{:S(2)}, u32[]{:S(2)}) collective-permute-start(bf16[2,64,768]{2,1,0:T(8,128)(2,1)S(1)} %get-tuple-element.133), channel_id=1, source_target_pairs={{0,1},{1,0},{2,3},{3,2},{4,5},{5,4},{6,7},{7,6},{8,9},{9,8},{10,11... | collective-permute-start | bytes 589832 | tf_op jit(solution)/shard_map/ppermute | solution.py:520
  44.5 10.8 %collective-permute-start.12 = (bf16[2,64,768]{2,1,0:T(8,128)(2,1)S(1)}, bf16[2,64,768]{2,1,0:T(8,128)(2,1)S(1)}, u32[]{:S(2)}, u32[]{:S(2)}) collective-permute-start(bf16[2,64,768]{2,1,0:T(8,128)(2,1)S(1)} %get-tuple-element.129), channel_id=1, source_target_pairs={{0,2},{1,3},{2,0},{3,1},{4,6},{5,7},{6,4},{7,5},{8,10},{9,11},{10,... | collective-permute-start | bytes 589832 | tf_op jit(solution)/shard_map/ppermute | solution.py:520
  46.2 15.1 %collective-permute-start.20 = (bf16[2,576,128]{2,1,0:T(8,128)(2,1)S(1)}, bf16[2,576,128]{2,1,0:T(8,128)(2,1)S(1)}, u32[]{:S(2)}, u32[]{:S(2)}) collective-permute-start(bf16[2,576,128]{2,1,0:T(8,128)(2,1)S(1)} %get-tuple-element.150), channel_id=1, source_target_pairs={{0,8},{4,12},{8,0},{12,4},{16,24},{20,28},{24,16},{28,20},{1,9},{5... | collective-permute-start | bytes 884744 | tf_op jit(solution)/shard_map/ppermute | solution.py:520
  53.5 16.7 %collective-permute-start.17 = (bf16[2,592,128]{2,1,0:T(8,128)(2,1)S(1)}, bf16[2,592,128]{2,1,0:T(8,128)(2,1)S(1)}, u32[]{:S(2)}, u32[]{:S(2)}) collective-permute-start(bf16[2,592,128]{2,1,0:T(8,128)(2,1)S(1)} %get-tuple-element.145), channel_id=1, source_target_pairs={{0,8},{4,12},{8,0},{12,4},{16,24},{20,28},{24,16},{28,20},{1,9},{5... | collective-permute-start | bytes 909320 | tf_op jit(solution)/shard_map/ppermute | solution.py:520
  57.3 4.6 %collective-permute-start.19 = (bf16[576,128]{1,0:T(8,128)(2,1)S(1)}, bf16[576,128]{1,0:T(8,128)(2,1)S(1)}, u32[]{:S(2)}, u32[]{:S(2)}) collective-permute-start(bf16[576,128]{1,0:T(8,128)(2,1)S(1)} %get-tuple-element.149), channel_id=1, source_target_pairs={{0,1},{1,0},{2,3},{3,2},{4,5},{5,4},{6,7},{7,6},{8,9},{9,8},{10,11... | collective-permute-start | bytes 442376 | tf_op jit(solution)/shard_map/ppermute | solution.py:520
  61.4 9.5 %collective-permute-start.23 = (bf16[1,576,128]{2,1,0:T(8,128)(2,1)S(1)}, bf16[1,576,128]{2,1,0:T(8,128)(2,1)S(1)}, u32[]{:S(2)}, u32[]{:S(2)}) collective-permute-start(bf16[1,576,128]{2,1,0:T(8,128)(2,1)S(1)} %get-tuple-element.156), channel_id=1, source_target_pairs={{0,16},{4,20},{8,24},{12,28},{16,0},{20,4},{24,8},{28,12},{1,17},{... | collective-permute-start | bytes 442376 | tf_op jit(solution)/shard_map/ppermute | solution.py:520
  61.9 9.1 %collective-permute-start.22 = (bf16[576,128]{1,0:T(8,128)(2,1)S(1)}, bf16[576,128]{1,0:T(8,128)(2,1)S(1)}, u32[]{:S(2)}, u32[]{:S(2)}) collective-permute-start(bf16[576,128]{1,0:T(8,128)(2,1)S(1)} %get-tuple-element.155), channel_id=1, source_target_pairs={{0,4},{4,0},{8,12},{12,8},{16,20},{20,16},{24,28},{28,24},{1,5},{5... | collective-permute-start | bytes 442376 | tf_op jit(solution)/shard_map/ppermute | solution.py:520
  70.3 7.4 %collective-permute-start.21 = (bf16[1,592,128]{2,1,0:T(8,128)(2,1)S(1)}, bf16[1,592,128]{2,1,0:T(8,128)(2,1)S(1)}, u32[]{:S(2)}, u32[]{:S(2)}) collective-permute-start(bf16[1,592,128]{2,1,0:T(8,128)(2,1)S(1)} %get-tuple-element.154), channel_id=1, source_target_pairs={{0,16},{4,20},{8,24},{12,28},{16,0},{20,4},{24,8},{28,12},{1,17},{... | collective-permute-start | bytes 454664 | tf_op jit(solution)/shard_map/ppermute | solution.py:520
  70.9 8.8 %collective-permute-start.27 = (bf16[1,576,128]{2,1,0:T(8,128)(2,1)S(1)}, bf16[1,576,128]{2,1,0:T(8,128)(2,1)S(1)}, u32[]{:S(2)}, u32[]{:S(2)}) collective-permute-start(bf16[1,576,128]{2,1,0:T(8,128)(2,1)S(1)} %add.3.before.a0), channel_id=1, source_target_pairs={{0,2},{1,3},{2,0},{3,1},{4,6},{5,7},{6,4},{7,5},{8,10},{9,11},{10,... | collective-permute-start | bytes 442376 | tf_op jit(solution)/shard_map/ppermute | solution.py:520
  71.1 8.6 %collective-permute-start.30 = (bf16[576,128]{1,0:T(8,128)(2,1)S(1)}, bf16[576,128]{1,0:T(8,128)(2,1)S(1)}, u32[]{:S(2)}, u32[]{:S(2)}) collective-permute-start(bf16[576,128]{1,0:T(8,128)(2,1)S(1)} %add.4.before.b0), channel_id=1, source_target_pairs={{0,2},{1,3},{2,0},{3,1},{4,6},{5,7},{6,4},{7,5},{8,10},{9,11},{10,... | collective-permute-start | bytes 442376 | tf_op jit(solution)/shard_map/ppermute | solution.py:520
  77.8 5.3 %collective-permute-start.25 = (bf16[1,592,128]{2,1,0:T(8,128)(2,1)S(1)}, bf16[1,592,128]{2,1,0:T(8,128)(2,1)S(1)}, u32[]{:S(2)}, u32[]{:S(2)}) collective-permute-start(bf16[1,592,128]{2,1,0:T(8,128)(2,1)S(1)} %add.5.p0), channel_id=1, source_target_pairs={{0,2},{1,3},{2,0},{3,1},{4,6},{5,7},{6,4},{7,5},{8,10},{9,11},{10,... | collective-permute-start | bytes 454664 | tf_op jit(solution)/shard_map/ppermute | solution.py:520
  79.2 1.4 %collective-permute-start.29 = (bf16[576,128]{1,0:T(8,128)(2,1)S(1)}, bf16[576,128]{1,0:T(8,128)(2,1)S(1)}, u32[]{:S(2)}, u32[]{:S(2)}) collective-permute-start(bf16[576,128]{1,0:T(8,128)(2,1)S(1)} %add.4.before.b0), channel_id=1, source_target_pairs={{0,1},{1,0},{2,3},{3,2},{4,5},{5,4},{6,7},{7,6},{8,9},{9,8},{10,11... | collective-permute-start | bytes 442376 | tf_op jit(solution)/shard_map/ppermute | solution.py:520
  79.2 1.6 %collective-permute-start.26 = (bf16[1,576,128]{2,1,0:T(8,128)(2,1)S(1)}, bf16[1,576,128]{2,1,0:T(8,128)(2,1)S(1)}, u32[]{:S(2)}, u32[]{:S(2)}) collective-permute-start(bf16[1,576,128]{2,1,0:T(8,128)(2,1)S(1)} %add.3.before.a0), channel_id=1, source_target_pairs={{0,1},{1,0},{2,3},{3,2},{4,5},{5,4},{6,7},{7,6},{8,9},{9,8},{10,11... | collective-permute-start | bytes 442376 | tf_op jit(solution)/shard_map/ppermute | solution.py:520
  79.7 1.4 %collective-permute-start.31 = (bf16[576,128]{1,0:T(8,128)(2,1)S(1)}, bf16[576,128]{1,0:T(8,128)(2,1)S(1)}, u32[]{:S(2)}, u32[]{:S(2)}) collective-permute-start(bf16[576,128]{1,0:T(8,128)(2,1)S(1)} %collective-permute-done.30.b2), channel_id=1, source_target_pairs={{0,1},{1,0},{2,3},{3,2},{4,5},{5,4},{6,7},{7,6},{8,9},{9,8},{10,11... | collective-permute-start | bytes 442376 | tf_op jit(solution)/shard_map/ppermute | solution.py:520
  79.7 1.6 %collective-permute-start.28 = (bf16[1,576,128]{2,1,0:T(8,128)(2,1)S(1)}, bf16[1,576,128]{2,1,0:T(8,128)(2,1)S(1)}, u32[]{:S(2)}, u32[]{:S(2)}) collective-permute-start(bf16[1,576,128]{2,1,0:T(8,128)(2,1)S(1)} %collective-permute-done.27.a2), channel_id=1, source_target_pairs={{0,1},{1,0},{2,3},{3,2},{4,5},{5,4},{6,7},{7,6},{8,9},{9,8},{10,11... | collective-permute-start | bytes 442376 | tf_op jit(solution)/shard_map/ppermute | solution.py:520
  80.6 2.6 %collective-permute-start.24 = (bf16[1,592,128]{2,1,0:T(8,128)(2,1)S(1)}, bf16[1,592,128]{2,1,0:T(8,128)(2,1)S(1)}, u32[]{:S(2)}, u32[]{:S(2)}) collective-permute-start(bf16[1,592,128]{2,1,0:T(8,128)(2,1)S(1)} %add.5.p0), channel_id=1, source_target_pairs={{0,1},{1,0},{2,3},{3,2},{4,5},{5,4},{6,7},{7,6},{8,9},{9,8},{10,11... | collective-permute-start | bytes 454664 | tf_op jit(solution)/shard_map/ppermute | solution.py:520
  83.1 1.4 %collective-permute-start.32 = (bf16[1,592,128]{2,1,0:T(8,128)(2,1)S(1)}, bf16[1,592,128]{2,1,0:T(8,128)(2,1)S(1)}, u32[]{:S(2)}, u32[]{:S(2)}) collective-permute-start(bf16[1,592,128]{2,1,0:T(8,128)(2,1)S(1)} %collective-permute-done.25.p2), channel_id=1, source_target_pairs={{0,1},{1,0},{2,3},{3,2},{4,5},{5,4},{6,7},{7,6},{8,9},{9,8},{10,11... | collective-permute-start | bytes 454664 | tf_op jit(solution)/shard_map/ppermute | solution.py:520

commit v5 on v4

--- a/solution.py
+++ b/solution.py
@@ -248,8 +248,8 @@
     def feed(sec_o, up_bias, d0, d1, d2, d3, wup, wdown, dup_o, act_o, send_o, dsec_o, dy_o):
         place = Place(inner)
         gather_rows((d0, d1, d2, d3), dy_o)
-        for j in range(4):
-            cols = pl.ds(j * 384, 384)
+        for j in range(6):
+            cols = pl.ds(j * 256, 256)
             for s in range(2):
                 rows = pl.ds(s * 256, 256)
                 up = nn(sec_o[rows, :], wup[:, cols]) + up_bias[:, cols]
@@ -271,9 +271,9 @@
         place = Place(inner)
         turned[...] = sec[...].T
         pick_rows(turned, chosen, place.y, place.x)
-        for j in range(4):
-            cols = pl.ds(j * 384, 384)
-            put_slots(nn(chosen[...], dup[:, cols]).astype(BF16), up_keep, up_send, j * 144)
+        for j in range(2):
+            cols = pl.ds(j * 768, 768)
+            put_slots(nn(chosen[...], dup[:, cols]).astype(BF16), up_keep, up_send, j * 288)
             bias_o[:, cols] = column_sum(dup[0:128, cols]) + column_sum(dup[256:384, cols])
         dy_half = dy[:, pl.ds(pl.multiple_of(place.y * 384, 128), 384)]
         for k, out in enumerate((down_keep, down_send)):
@@ -450,6 +450,11 @@
     def add(a, b, before, out):
         out[...] = (a[...].astype(F32) + b[...].astype(F32)).astype(BF16)
 
+    def add_wide(a, b, before, out):
+        rows = a.shape[1]
+        out[:, 0:rows, :] = (a[...].astype(F32) + b[...].astype(F32)).astype(BF16)
+        out[:, rows : out.shape[1], :] = jnp.zeros((1, out.shape[1] - rows, 128), BF16)
+
     def add_split(a, b, before, kept, sent):
         core = Place(inner).core
         for out, k in ((sent, 1), (kept, 0)):
@@ -471,22 +476,27 @@
         def _():
             write(got, kept)
 
-    def assemble_feed(a0, a1, a2, a3, b0, b1, b2, b3, up_o, down_o):
-        place = Place(inner)
-        for k, (up, down) in enumerate(((a0, b0), (a1, b1), (a2, b2), (a3, b3))):
+    def assemble_down(p0, p1, p2, p3, out):
+        place = Place(inner)
+        for k, piece in enumerate((p0, p1, p2, p3)):
+            y, core = flip(place.y, k // 2), flip(place.core, k % 2)
+            rows = pl.ds(pl.multiple_of(core * 192, 64), 192)
+            for t in range(3):
+                cols = pl.ds(pl.multiple_of(y * 384 + t * 128, 128), 128)
+                out[rows, cols] = piece[pl.ds(t * 192, 192), :].astype(F32)
+
+    def assemble_last(
+        a0, a1, a2, a3, p0, p1, p2, p3,
+        up_o, out_o, qkv_o, gain1, shift1, qv, out_b, gain2, shift2, up_b, down_b,
+    ):
+        place = Place(inner)
+        for k, piece in enumerate((a0, a1, a2, a3)):
             y, core = flip(place.y, k // 2), flip(place.core, k % 2)
             rows = pl.ds(pl.multiple_of(y * 48, 16), 48)
             for j in range(4):
                 for t in range(3):
                     cols = pl.ds(pl.multiple_of((2 * j + core) * 384 + t * 128, 128), 128)
-                    up_o[rows, cols] = up[0, pl.ds((3 * j + t) * 48, 48), :].astype(F32)
-            rows = pl.ds(pl.multiple_of(core * 192, 64), 192)
-            for t in range(3):
-                cols = pl.ds(pl.multiple_of(y * 384 + t * 128, 128), 128)
-                down_o[rows, cols] = down[pl.ds(t * 192, 192), :].astype(F32)
-
-    def assemble_rest(p0, p1, p2, p3, out_o, qkv_o, gain1, shift1, qv, out_b, gain2, shift2, up_b, down_b):
-        place = Place(inner)
+                    up_o[rows, cols] = piece[0, pl.ds((3 * j + t) * 48, 48), :].astype(F32)
         total = jnp.zeros((16, 128), F32)
         for k, piece in enumerate((p0, p1, p2, p3)):
             y, core = flip(place.y, k // 2), flip(place.core, k % 2)
@@ -532,9 +542,9 @@
         across = y_swap(x)
         return x, core_swap(x), across, core_swap(across)
 
-    def halve(name, keep, got, before):
+    def halve(name, keep, got, before, us=STEP):
         shape = ((keep.shape[0] // 2, *keep.shape[1:]), BF16)
-        return call(kernels[name], (shape, shape), [VMEM, VMEM, ANY], (keep, got, before), us=STEP)
+        return call(kernels[name], (shape, shape), [VMEM, VMEM, ANY], (keep, got, before), us=us)
 
     def add(a, b, before, us):
         return call(kernels["add"], ((a.shape, BF16),), [VMEM, VMEM, ANY], (a, b, before), us=us)[0]
@@ -639,14 +649,15 @@
         )
         down_stay, down_leave = halve("halve_z_high", down_keep, seq_swap(down_send, 2), rest_keep)
         up_stay, up_leave = halve("halve_z_low", up_keep, seq_swap(up_send, 1), down_stay)
-        rest_stay, rest_leave = halve("halve_z_low", rest_keep, seq_swap(rest_send, 1), up_stay)
+        rest_stay, rest_leave = halve("halve_z_low", rest_keep, seq_swap(rest_send, 1), up_stay, FILL)
+        up_stay, up_leave = halve("halve_z_high", up_stay, seq_swap(up_leave, 2), rest_stay)
         in_grad, block_out, mark = call(
             kernels["input_grad"],
             ((own, BF16), (own, BF16), ((8, 128), F32)),
             [VMEM] * 9 + [ANY],
             (
                 t0, dfirst_own, y_swap(dfirst_send), dhid, exb_other, vec, hid_own, part,
-                core_swap(part_send), rest_stay,
+                core_swap(part_send), up_stay,
             ),
             us=US,
         )
@@ -658,29 +669,31 @@
             (down_stay, seq_swap(down_leave, 4), mark),
             us=STEP,
         )
-        up_stay, up_leave = halve("halve_z_high", up_stay, seq_swap(up_leave, 2), down_kept)
         down_own, down_other = call(
-            kernels["pick"], (piece, piece), [VMEM, VMEM, ANY], (down_kept, core_swap(down_sent), up_stay), us=STEP
+            kernels["pick"], (piece, piece), [VMEM, VMEM, ANY], (down_kept, core_swap(down_sent), mark), us=STEP
         )
         rest_stay, rest_leave = halve("halve_z_high", rest_stay, seq_swap(rest_leave, 2), down_own)
-        up_sum = add(up_stay, seq_swap(up_leave, 4), rest_stay, STEP)
-        down_sum = add(down_own, seq_swap(down_other, 1), up_sum, STEP)
-        rest_sum = add(rest_stay, seq_swap(rest_leave, 4), down_sum, FILL)
-        up_pieces, down_pieces, rest_across = gather(up_sum), gather(down_sum), y_swap(rest_sum)
-        up_o, down_o = call(
-            kernels["assemble_feed"],
-            (((96, 3072), F32), ((384, 768), F32)),
+        down_sum = add(down_own, seq_swap(down_other, 1), rest_stay, 0.001)
+        (up_sum,) = call(
+            kernels["add_wide"],
+            (((1, 592, 128), BF16),),
+            [VMEM, VMEM, ANY],
+            (up_stay, seq_swap(up_leave, 4), down_sum),
+            us=STEP,
+        )
+        rest_sum = add(rest_stay, seq_swap(rest_leave, 4), up_sum, FILL)
+        up_across, down_pieces, rest_across = y_swap(up_sum), gather(down_sum), y_swap(rest_sum)
+        (down_o,) = call(kernels["assemble_down"], (((384, 768), F32),), [VMEM] * 4, down_pieces, us=US)
+        up_across, rest_across, down_o = lax.optimization_barrier((up_across, rest_across, down_o))
+        small = [96, 96, 192, 96, 96, 96, 384, 96]
+        up_o, out_o, qkv_o, *vectors = call(
+            kernels["assemble_last"],
+            (((96, 3072), F32), ((96, 768), F32), ((96, 2304), F32)) + tuple(((n,), F32) for n in small),
             [VMEM] * 8,
-            (*up_pieces, *down_pieces),
-            us=US,
-        )
-        rest_across, up_o, down_o = lax.optimization_barrier((rest_across, up_o, down_o))
-        small = [96, 96, 192, 96, 96, 96, 384, 96]
-        out_o, qkv_o, *vectors = call(
-            kernels["assemble_rest"],
-            (((96, 768), F32), ((96, 2304), F32)) + tuple(((n,), F32) for n in small),
-            [VMEM] * 4,
-            (rest_sum, core_swap(rest_sum), rest_across, core_swap(rest_across)),
+            (
+                up_sum, core_swap(up_sum), up_across, core_swap(up_across),
+                rest_sum, core_swap(rest_sum), rest_across, core_swap(rest_across),
+            ),
             us=US,
         )
         gain1, shift1, qv, out_b, gain2, shift2, up_b, down_b = vectors

time: 85.7 us -> 83.2 us (0.971)
  waiting for transfers between devices: 33.5 us -> 28.2 us
  starting transfers between devices: 25.1 us -> 28.7 us
    ppermute x33, waiting for transfers between devices: 33.5 us -> 28.2 us  [swap(): return lax.ppermute(x, axis, [(i, i ^ step) for i in range(size)])]
    ppermute x33, starting transfers between devices: 25.1 us -> 28.7 us  [swap(): return lax.ppermute(x, axis, [(i, i ^ step) for i in range(size)])]
  transfers between devices with their start and end apart: 33 -> 33, of which waited for: 17 -> 16; matrix products, arithmetic and copies ran while one was open for 0% -> 0% of each run, Pallas kernels for 23% -> 24%
where the time goes in v5:
time: 83.2 us; the launch traced here: 83.1 us
  starting transfers between devices  28.7 us (34%)
  waiting for transfers between devices  28.2 us (34%)
  Pallas kernels  25.3 us (30%)
  between operations  0.84 us (1%)
    ppermute x33, starting transfers between devices, swap(): return lax.ppermute(x, axis, [(i, i ^ step) for i in range(size)])  28.7 us
    ppermute x33, waiting for transfers between devices, swap(): return lax.ppermute(x, axis, [(i, i ^ step) for i in range(size)])  28.2 us
    pallas_call x22, Pallas kernels, call(): pl.pallas_call(kernel, out_shape=tuple((jax.ShapeDtypeStruct(s, d) for s,...  25.3 us
  transfers between devices with their start and end apart: 33, of which 16 were waited for; matrix products, arithmetic and copies ran while one was open for 0% of the time, Pallas kernels for 24%

profile of v5, /device:TPU:0, one launch (start us, length us, event | category | flops | bytes accessed | tf_op | source)
XLA Modules:
  0.0 83.1 jit_solution(4482627883820593882)
XLA Ops:
  0.6 0.5 collective-permute-start
  1.2 2.6 %collective-permute-start.1 = (bf16[2,64,768]{2,1,0:T(8,128)(2,1)}, bf16[2,64,768]{2,1,0:T(8,128)(2,1)S(1)}, u32[]{:S(2)}, u32[]{:S(2)}) collective-permute-start(bf16[2,64,768]{2,1,0:T(8,128)(2,1)} %tokens_hbm.1), channel_id=1, source_target_pairs={{0,2},{1,3},{2,0},{3,1},{4,6},{5,7},{6,4},{7,5},{8,10},{9,11},{10,... | collective-permute-start | bytes 589832 | tf_op jit(solution)/shard_map/ppermute | solution.py:530
  3.8 4.2 %near.1 = (bf16[128,2304]{1,0:T(8,128)(2,1)S(1)}, f32[256,256]{1,0:T(8,128)S(1)}, f32[8,768]{1,0:T(8,128)S(1)}, f32[1,1536]{1,0:T(1,128)S(1)}, bf16[2,64,768]{2,...) custom-call(bf16[2,64,768]{2,1,0:T(8,128)(2,1)S(1)} %collective-perm, ...), custom_call_target="tpu_custom_call" | custom-call | flops 3000000000 | bytes 300000 | tf_op jit(solution)/shard_map/near/pallas_call | solution.py:74
  8.0 1.6 %collective-permute-start.7 = (bf16[2,64,768]{2,1,0:T(8,128)(2,1)S(1)}, bf16[2,64,768]{2,1,0:T(8,128)(2,1)S(1)}, u32[]{:S(2)}, u32[]{:S(2)}) collective-permute-start(bf16[2,64,768]{2,1,0:T(8,128)(2,1)S(1)} %get-tuple-element.106.d0), channel_id=1, source_target_pairs={{0,2},{1,3},{2,0},{3,1},{4,6},{5,7},{6,4},{7,5},{8,10},{9,11},{10,... | collective-permute-start | bytes 589832 | tf_op jit(solution)/shard_map/ppermute | solution.py:530
  9.7 0.5 collective-permute-start.3
  10.2 0.8 collective-permute-done.2.t3.t3_core
  11.2 2.9 %attention.1 = (bf16[256,384]{1,0:T(8,128)(2,1)S(1)}, bf16[256,384]{1,0:T(8,128)(2,1)S(1)}, bf16[256,1152]{1,0:T(8,128)(2,1)S(1)}, f32[6,256,256]{2,1,0:T(8,128)S(1)}) custom-call(bf16[128,2304]{1,0:T(8,128)(2,1)S(1)} %get-tuple-element.94.near_in, f32[256,256]{1,0:T(8,128)S(1)} %get-tuple-element.95.mask, f32[8,768]{1,0:T(8,128)S(1)} %get-tuple-element.96.vec.params, ...), custom_call_target="tpu_custom_call" | custom-call | flops 10000000 | bytes 1000 | tf_op jit(solution)/shard_map/attention/pallas_call | solution.py:74
  14.1 0.4 collective-permute-start.4
  14.7 0.4 collective-permute-start.6
  15.2 0.4 collective-permute-done.4.othera
  15.6 0.4 collective-permute-done.5.otherb
  16.0 1.5 %residual.1 = (bf16[256,768]{1,0:T(8,128)(2,1)S(1)}, bf16[256,768]{1,0:T(8,128)(2,1)S(1)}, bf16[512,768]{1,0:T(8,128)(2,1)S(1)}, f32[256,768]{1,0:T(8,128)S(1)},...) custom-call(bf16[256,384]{1,0:T(8,128)(2,1)S(1)} %get-tuple-element.101.atta, ...), custom_call_target="tpu_custom_call" | custom-call | flops 10000000 | bytes 1000 | tf_op jit(solution)/shard_map/residual/pallas_call | solution.py:74
  17.5 4.3 %feed.1 = (bf16[512,1536]{1,0:T(8,128)(2,1)S(1)}, bf16[512,1536]{1,0:T(8,128)(2,1)S(1)}, bf16[256,768]{1,0:T(8,128)(2,1)S(1)}, f32[256,768]{1,0:T(8,128)S(1)}, bf16[512,768]{1,0:T(8,128)(2,1)S(1)}) custom-call(bf16[512,768]{1,0:T(8,128)(2,1)S(1)} %get-tuple-element.104.sec_o.sec, f32[1,1536]{1,0:T(1,128)S(1)} %get-tuple-element.105.up_bias, ...), custom_call_target="tpu_custom_call" | custom-call | flops 10000000 | bytes 1000 | tf_op jit(solution)/shard_map/feed/pallas_call | solution.py:74
  21.8 0.4 collective-permute-start.9
  22.1 1.9 %feed_weights.1 = (bf16[4,576,128]{2,1,0:T(8,128)(2,1)S(1)}, bf16[4,576,128]{2,1,0:T(8,128)(2,1)S(1)}, bf16[2,2,576,128]{3,2,1,0:T(8,128)(2,1)S(1)}, bf16[2,2,576,128]{3,2,1,0:T(8,128)(2,1)S(1)}, f32[1,1536]{1,0:T(1,128)S(1)}) custom-call(bf16[512,768]{1,0:T(8,128)(2,1)S(1)} %get-tuple-element.104.sec_o.sec, bf16[512,1536]{1,0:T(8,128)(2,1)S(1)} %get-tuple-element.114.dup, ...), custom_call_target="tpu_custom_call" | custom-call | flops 20000000000 | bytes 2000000 | tf_op jit(solution)/shard_map/feed_weights/pallas_call | solution.py:74
  24.0 1.6 %collective-permute-start.14 = (bf16[4,576,128]{2,1,0:T(8,128)(2,1)S(1)}, bf16[4,576,128]{2,1,0:T(8,128)(2,1)S(1)}, u32[]{:S(2)}, u32[]{:S(2)}) collective-permute-start(bf16[4,576,128]{2,1,0:T(8,128)(2,1)S(1)} %get-tuple-element.134), channel_id=1, source_target_pairs={{0,4},{4,0},{8,12},{12,8},{16,20},{20,16},{24,28},{28,24},{1,5},{5... | collective-permute-start | bytes 1769480 | tf_op jit(solution)/shard_map/ppermute | solution.py:530
  25.6 1.6 %collective-permute-start.15 = (bf16[2,2,576,128]{3,2,1,0:T(8,128)(2,1)S(1)}, bf16[2,2,576,128]{3,2,1,0:T(8,128)(2,1)S(1)}, u32[]{:S(2)}, u32[]{:S(2)}) collective-permute-start(bf16[2,2,576,128]{3,2,1,0:T(8,128)(2,1)S(1)} %get-tuple-element.136), channel_id=1, source_target_pairs={{0,8},{4,12},{8,0},{12,4},{16,24},{20,28},{24,16},{28,20},{1,9},{5... | collective-permute-start | bytes 1769480 | tf_op jit(solution)/shard_map/ppermute | solution.py:530
  27.2 2.9 %attention_back.1 = (bf16[256,768]{1,0:T(8,128)(2,1)S(1)}, bf16[320,768]{1,0:T(8,128)(2,1)S(1)}, f32[64,768]{1,0:T(8,128)S(1)}, f32[8,768]{1,0:T(8,128)S(1)}, f32[8,384]{1,0:T(8,128)S(1)}) custom-call(f32[256,768]{1,0:T(8,128)S(1)} %get-tuple-element.109.dsec_in, bf16[256,768]{1,0:T(8,128)(2,1)S(1)} %collective-permute-done.9.got, ...), custom_call_target="tpu_custom_call" | custom-call | flops 10000000 | bytes 1000 | tf_op jit(solution)/shard_map/attention_back/pallas_call | solution.py:74
  30.1 0.5 collective-permute-start.11
  30.6 1.4 %turn.1 = (bf16[384,512]{1,0:T(8,128)(2,1)S(1)}, bf16[384,512]{1,0:T(8,128)(2,1)S(1)}, f32[2,64,768]{2,1,0:T(8,128)S(1)}, bf16[2,64,768]{2,1,0:T(8,128)(2,1)S(1)}) custom-call(bf16[256,768]{1,0:T(8,128)(2,1)S(1)} %get-tuple-element.120.att_own, bf16[256,768]{1,0:T(8,128)(2,1)S(1)} %get-tuple-element.121.att_other, ...), custom_call_target="tpu_custom_call" | custom-call | flops 20000000000 | bytes 2000000 | tf_op jit(solution)/shard_map/turn/pallas_call | solution.py:74
  32.1 0.5 collective-permute-done.11.otherb.other
  32.6 1.8 %attention_weights.1 = (bf16[4,592,128]{2,1,0:T(8,128)(2,1)S(1)}, bf16[4,592,128]{2,1,0:T(8,128)(2,1)S(1)}, f32[2,64,768]{2,1,0:T(8,128)S(1)}, bf16[2,64,768]{2,1,0:T(8,128)(2,1)S(1)}) custom-call(bf16[256,768]{1,0:T(8,128)(2,1)S(1)} %get-tuple-element.118.owna, bf16[320,768]{1,0:T(8,128)(2,1)S(1)} %get-tuple-element.119.ownb, ...), custom_call_target="tpu_custom_call" | custom-call | flops 10000000 | bytes 1000 | tf_op jit(solution)/shard_map/attention_weights/pallas_call | solution.py:74
  34.3 0.6 collective-permute-start.17
  34.9 1.6 %collective-permute-start.12 = (bf16[2,64,768]{2,1,0:T(8,128)(2,1)S(1)}, bf16[2,64,768]{2,1,0:T(8,128)(2,1)S(1)}, u32[]{:S(2)}, u32[]{:S(2)}) collective-permute-start(bf16[2,64,768]{2,1,0:T(8,128)(2,1)S(1)} %get-tuple-element.128), channel_id=1, source_target_pairs={{0,2},{1,3},{2,0},{3,1},{4,6},{5,7},{6,4},{7,5},{8,10},{9,11},{10,... | collective-permute-start | bytes 589832 | tf_op jit(solution)/shard_map/ppermute | solution.py:530
  36.5 4.3 %collective-permute-done.15.got = bf16[2,2,576,128]{3,2,1,0:T(8,128)(2,1)S(1)} collective-permute-done((bf16[2,2,576,128]{3,2,1,0:T(8,128)(2,1)S(1)}, bf16[2,2,576,128]{3,2,1,0:T(8,128)(2,1)S(1)}, u32[]{:S(2)}, u32[]{:S(2)}) %collective-permute-start.15) | collective-permute-done | bytes 589856 | tf_op jit(solution)/shard_map/ppermute | solution.py:530
  41.1 1.6 %collective-permute-start.16 = (bf16[2,576,128]{2,1,0:T(8,128)(2,1)S(1)}, bf16[2,576,128]{2,1,0:T(8,128)(2,1)S(1)}, u32[]{:S(2)}, u32[]{:S(2)}) collective-permute-start(bf16[2,576,128]{2,1,0:T(8,128)(2,1)S(1)} %get-tuple-element.140), channel_id=1, source_target_pairs={{0,8},{4,12},{8,0},{12,4},{16,24},{20,28},{24,16},{28,20},{1,9},{5... | collective-permute-start | bytes 884744 | tf_op jit(solution)/shard_map/ppermute | solution.py:530
  42.7 2.6 %collective-permute-start.19 = (bf16[1,2,576,128]{3,2,1,0:T(8,128)(2,1)S(1)}, bf16[1,2,576,128]{3,2,1,0:T(8,128)(2,1)S(1)}, u32[]{:S(2)}, u32[]{:S(2)}) collective-permute-start(bf16[1,2,576,128]{3,2,1,0:T(8,128)(2,1)S(1)} %get-tuple-element.147), channel_id=1, source_target_pairs={{0,16},{4,20},{8,24},{12,28},{16,0},{20,4},{24,8},{28,12},{1,17},{... | collective-permute-start | bytes 884744 | tf_op jit(solution)/shard_map/ppermute | solution.py:530
  45.3 7.2 %collective-permute-done.17.got = bf16[4,592,128]{2,1,0:T(8,128)(2,1)S(1)} collective-permute-done((bf16[4,592,128]{2,1,0:T(8,128)(2,1)S(1)}, bf16[4,592,128]{2,1,0:T(8,128)(2,1)S(1)}, u32[]{:S(2)}, u32[]{:S(2)}) %collective-permute-start.17) | collective-permute-done | bytes 606240 | tf_op jit(solution)/shard_map/ppermute | solution.py:530
  52.6 1.7 %collective-permute-start.22 = (bf16[2,592,128]{2,1,0:T(8,128)(2,1)S(1)}, bf16[2,592,128]{2,1,0:T(8,128)(2,1)S(1)}, u32[]{:S(2)}, u32[]{:S(2)}) collective-permute-start(bf16[2,592,128]{2,1,0:T(8,128)(2,1)S(1)} %get-tuple-element.153), channel_id=1, source_target_pairs={{0,8},{4,12},{8,0},{12,4},{16,24},{20,28},{24,16},{28,20},{1,9},{5... | collective-permute-start | bytes 909320 | tf_op jit(solution)/shard_map/ppermute | solution.py:530
  54.4 1.6 %collective-permute-done.16.got = bf16[2,576,128]{2,1,0:T(8,128)(2,1)S(1)} collective-permute-done((bf16[2,576,128]{2,1,0:T(8,128)(2,1)S(1)}, bf16[2,576,128]{2,1,0:T(8,128)(2,1)S(1)}, u32[]{:S(2)}, u32[]{:S(2)}) %collective-permute-start.16) | collective-permute-done | bytes 294944 | tf_op jit(solution)/shard_map/ppermute | solution.py:530
  56.1 1.1 %input_grad.1 = (bf16[2,64,768]{2,1,0:T(8,128)(2,1)}, bf16[2,64,768]{2,1,0:T(8,128)(2,1)}, f32[8,128]{1,0:T(8,128)S(1)}) custom-call(bf16[2,64,768]{2,1,0:T(8,128)(2,1)S(1)} %get-tuple-element.92.t0.tokens, f32[2,64,768]{2,1,0:T(8,128)S(1)} %get-tuple-element.127.dfirst, bf16[2,64,768]{2,1,0:T(8,128)(2,1)S(1)} %collective-permute-done.12.received, ...), custom_call_target="tpu_custom_call" | custom-call | flops 10000000 | bytes 1000 | tf_op jit(solution)/shard_map/input_grad/pallas_call | solution.py:74
  57.3 1.5 %collective-permute-start.18 = (bf16[1,576,128]{2,1,0:T(8,128)(2,1)S(1)}, bf16[1,576,128]{2,1,0:T(8,128)(2,1)S(1)}, u32[]{:S(2)}, u32[]{:S(2)}) collective-permute-start(bf16[1,576,128]{2,1,0:T(8,128)(2,1)S(1)} %get-tuple-element.146), channel_id=1, source_target_pairs={{0,16},{4,20},{8,24},{12,28},{16,0},{20,4},{24,8},{28,12},{1,17},{... | collective-permute-start | bytes 442376 | tf_op jit(solution)/shard_map/ppermute | solution.py:530
  58.9 1.0 %collective-permute-start.21 = (bf16[576,128]{1,0:T(8,128)(2,1)S(1)}, bf16[576,128]{1,0:T(8,128)(2,1)S(1)}, u32[]{:S(2)}, u32[]{:S(2)}) collective-permute-start(bf16[576,128]{1,0:T(8,128)(2,1)S(1)} %get-tuple-element.152), channel_id=1, source_target_pairs={{0,4},{4,0},{8,12},{12,8},{16,20},{20,16},{24,28},{28,24},{1,5},{5... | collective-permute-start | bytes 442376 | tf_op jit(solution)/shard_map/ppermute | solution.py:530
  60.0 4.3 %collective-permute-done.22.got = bf16[2,592,128]{2,1,0:T(8,128)(2,1)S(1)} collective-permute-done((bf16[2,592,128]{2,1,0:T(8,128)(2,1)S(1)}, bf16[2,592,128]{2,1,0:T(8,128)(2,1)S(1)}, u32[]{:S(2)}, u32[]{:S(2)}) %collective-permute-start.22) | collective-permute-done | bytes 303136 | tf_op jit(solution)/shard_map/ppermute | solution.py:530
  64.4 1.3 %collective-permute-start.25 = (bf16[1,592,128]{2,1,0:T(8,128)(2,1)S(1)}, bf16[1,592,128]{2,1,0:T(8,128)(2,1)S(1)}, u32[]{:S(2)}, u32[]{:S(2)}) collective-permute-start(bf16[1,592,128]{2,1,0:T(8,128)(2,1)S(1)} %get-tuple-element.155), channel_id=1, source_target_pairs={{0,16},{4,20},{8,24},{12,28},{16,0},{20,4},{24,8},{28,12},{1,17},{... | collective-permute-start | bytes 454664 | tf_op jit(solution)/shard_map/ppermute | solution.py:530
  65.7 1.6 %collective-permute-start.28 = (bf16[576,128]{1,0:T(8,128)(2,1)S(1)}, bf16[576,128]{1,0:T(8,128)(2,1)S(1)}, u32[]{:S(2)}, u32[]{:S(2)}) collective-permute-start(bf16[576,128]{1,0:T(8,128)(2,1)S(1)} %add.2.before.p0), channel_id=1, source_target_pairs={{0,2},{1,3},{2,0},{3,1},{4,6},{5,7},{6,4},{7,5},{8,10},{9,11},{10,... | collective-permute-start | bytes 442376 | tf_op jit(solution)/shard_map/ppermute | solution.py:530
  67.3 4.1 %collective-permute-done.18.b = bf16[1,576,128]{2,1,0:T(8,128)(2,1)S(1)} collective-permute-done((bf16[1,576,128]{2,1,0:T(8,128)(2,1)S(1)}, bf16[1,576,128]{2,1,0:T(8,128)(2,1)S(1)}, u32[]{:S(2)}, u32[]{:S(2)}) %collective-permute-start.18) | collective-permute-done | bytes 147488 | tf_op jit(solution)/shard_map/ppermute | solution.py:530
  71.5 1.7 %collective-permute-start.24 = (bf16[1,592,128]{2,1,0:T(8,128)(2,1)S(1)}, bf16[1,592,128]{2,1,0:T(8,128)(2,1)S(1)}, u32[]{:S(2)}, u32[]{:S(2)}) collective-permute-start(bf16[1,592,128]{2,1,0:T(8,128)(2,1)S(1)} %add_wide.1.before.a0), channel_id=1, source_target_pairs={{0,2},{1,3},{2,0},{3,1},{4,6},{5,7},{6,4},{7,5},{8,10},{9,11},{10,... | collective-permute-start | bytes 454664 | tf_op jit(solution)/shard_map/ppermute | solution.py:530
  73.1 1.1 %collective-permute-done.25.b = bf16[1,592,128]{2,1,0:T(8,128)(2,1)S(1)} collective-permute-done((bf16[1,592,128]{2,1,0:T(8,128)(2,1)S(1)}, bf16[1,592,128]{2,1,0:T(8,128)(2,1)S(1)}, u32[]{:S(2)}, u32[]{:S(2)}) %collective-permute-start.25) | collective-permute-done | bytes 151584 | tf_op jit(solution)/shard_map/ppermute | solution.py:530
  74.3 1.7 %collective-permute-start.26 = (bf16[1,592,128]{2,1,0:T(8,128)(2,1)S(1)}, bf16[1,592,128]{2,1,0:T(8,128)(2,1)S(1)}, u32[]{:S(2)}, u32[]{:S(2)}) collective-permute-start(bf16[1,592,128]{2,1,0:T(8,128)(2,1)S(1)} %add.3.p0), channel_id=1, source_target_pairs={{0,2},{1,3},{2,0},{3,1},{4,6},{5,7},{6,4},{7,5},{8,10},{9,11},{10,... | collective-permute-start | bytes 454664 | tf_op jit(solution)/shard_map/ppermute | solution.py:530
  75.9 0.5 collective-permute-start.29
  76.4 0.9 %collective-permute-done.27.p1 = bf16[576,128]{1,0:T(8,128)(2,1)S(1)} collective-permute-done((bf16[576,128]{1,0:T(8,128)(2,1)S(1)}, bf16[576,128]{1,0:T(8,128)(2,1)S(1)}, u32[]{:S(2)}, u32[]{:S(2)}) %collective-permute-start.27) | collective-permute-done | bytes 147488 | tf_op jit(solution)/shard_map/ppermute | solution.py:530
  77.5 1.1 %assemble_down.1 = f32[384,768]{1,0:T(8,128)} custom-call(bf16[576,128]{1,0:T(8,128)(2,1)S(1)} %add.2.before.p0, bf16[576,128]{1,0:T(8,128)(2,1)S(1)} %collective-permute-done.27.p1, bf16[576,128]{1,0:T(8,128)(2,1)S(1)} %collective-permute-done.28.p2, bf16[576,128]{1,0:T(8,128)(2,1)S(1)} %collective-permute-done.29.p3), custom_call_target="tpu_custom_call" | custom-call | flops 10000000 | bytes 1000 | tf_op jit(solution)/shard_map/assemble_down/pallas_call | solution.py:74
  78.6 1.3 %collective-permute-done.26.p2 = bf16[1,592,128]{2,1,0:T(8,128)(2,1)S(1)} collective-permute-done((bf16[1,592,128]{2,1,0:T(8,128)(2,1)S(1)}, bf16[1,592,128]{2,1,0:T(8,128)(2,1)S(1)}, u32[]{:S(2)}, u32[]{:S(2)}) %collective-permute-start.26) | collective-permute-done | bytes 151584 | tf_op jit(solution)/shard_map/ppermute | solution.py:530
  80.0 0.5 collective-permute-start.32
  80.5 0.9 %collective-permute-done.30.a3 = bf16[1,592,128]{2,1,0:T(8,128)(2,1)S(1)} collective-permute-done((bf16[1,592,128]{2,1,0:T(8,128)(2,1)S(1)}, bf16[1,592,128]{2,1,0:T(8,128)(2,1)S(1)}, u32[]{:S(2)}, u32[]{:S(2)}) %collective-permute-start.30) | collective-permute-done | bytes 151584 | tf_op jit(solution)/shard_map/ppermute | solution.py:530
  81.3 0.2 collective-permute-done.32.p3
  81.6 1.5 %assemble_last.1 = (f32[96,3072]{1,0:T(8,128)}, f32[96,768]{1,0:T(8,128)}, f32[96,2304]{1,0:T(8,128)}, f32[96]{0:T(128)}, f32[96]{0:T(128)}, /*index=5*/f32[192]...) custom-call(bf16[1,592,128]{2,1,0:T(8,128)(2,1)S(1)} %add_wide.1.before.a0, ...), custom_call_target="tpu_custom_call" | custom-call | flops 10000000 | bytes 1000 | tf_op jit(solution)/shard_map/assemble_last/pallas_call | solution.py:74
  (40 shorter events, 1.7 us)
Async XLA Ops:
  0.6 3.1 %collective-permute-start = (bf16[2,64,768]{2,1,0:T(8,128)(2,1)}, bf16[2,64,768]{2,1,0:T(8,128)(2,1)S(1)}, u32[]{:S(2)}, u32[]{:S(2)}) collective-permute-start(bf16[2,64,768]{2,1,0:T(8,128)(2,1)} %tokens_hbm.1), channel_id=1, source_target_pairs={{0,1},{1,0},{2,3},{3,2},{4,5},{5,4},{6,7},{7,6},{8,9},{9,8},{10,11... | collective-permute-start | bytes 589832 | tf_op jit(solution)/shard_map/ppermute | solution.py:530
  1.2 8.5 %collective-permute-start.1 = (bf16[2,64,768]{2,1,0:T(8,128)(2,1)}, bf16[2,64,768]{2,1,0:T(8,128)(2,1)S(1)}, u32[]{:S(2)}, u32[]{:S(2)}) collective-permute-start(bf16[2,64,768]{2,1,0:T(8,128)(2,1)} %tokens_hbm.1), channel_id=1, source_target_pairs={{0,2},{1,3},{2,0},{3,1},{4,6},{5,7},{6,4},{7,5},{8,10},{9,11},{10,... | collective-permute-start | bytes 589832 | tf_op jit(solution)/shard_map/ppermute | solution.py:530
  8.0 7.0 %collective-permute-start.7 = (bf16[2,64,768]{2,1,0:T(8,128)(2,1)S(1)}, bf16[2,64,768]{2,1,0:T(8,128)(2,1)S(1)}, u32[]{:S(2)}, u32[]{:S(2)}) collective-permute-start(bf16[2,64,768]{2,1,0:T(8,128)(2,1)S(1)} %get-tuple-element.106.d0), channel_id=1, source_target_pairs={{0,2},{1,3},{2,0},{3,1},{4,6},{5,7},{6,4},{7,5},{8,10},{9,11},{10,... | collective-permute-start | bytes 589832 | tf_op jit(solution)/shard_map/ppermute | solution.py:530
  9.7 1.4 %collective-permute-start.2 = (bf16[64,768]{1,0:T(8,128)(2,1)S(1)}, bf16[64,768]{1,0:T(8,128)(2,1)S(1)}, u32[]{:S(2)}, u32[]{:S(2)}) collective-permute-start(bf16[64,768]{1,0:T(8,128)(2,1)S(1)} %get-tuple-element.98), channel_id=1, source_target_pairs={{0,1},{1,0},{2,3},{3,2},{4,5},{5,4},{6,7},{7,6},{8,9},{9,8},{10,11... | collective-permute-start | bytes 294920 | tf_op jit(solution)/shard_map/ppermute | solution.py:530
  9.7 1.4 %collective-permute-start.3 = (bf16[64,768]{1,0:T(8,128)(2,1)S(1)}, bf16[64,768]{1,0:T(8,128)(2,1)S(1)}, u32[]{:S(2)}, u32[]{:S(2)}) collective-permute-start(bf16[64,768]{1,0:T(8,128)(2,1)S(1)} %get-tuple-element.100), channel_id=1, source_target_pairs={{0,1},{1,0},{2,3},{3,2},{4,5},{5,4},{6,7},{7,6},{8,9},{9,8},{10,11... | collective-permute-start | bytes 294920 | tf_op jit(solution)/shard_map/ppermute | solution.py:530
  14.1 1.5 %collective-permute-start.4 = (bf16[256,384]{1,0:T(8,128)(2,1)S(1)}, bf16[256,384]{1,0:T(8,128)(2,1)S(1)}, u32[]{:S(2)}, u32[]{:S(2)}) collective-permute-start(bf16[256,384]{1,0:T(8,128)(2,1)S(1)} %get-tuple-element.101.atta), channel_id=1, source_target_pairs={{0,1},{1,0},{2,3},{3,2},{4,5},{5,4},{6,7},{7,6},{8,9},{9,8},{10,11... | collective-permute-start | bytes 589832 | tf_op jit(solution)/shard_map/ppermute | solution.py:530
  14.5 1.4 %collective-permute-start.5 = (bf16[256,384]{1,0:T(8,128)(2,1)S(1)}, bf16[256,384]{1,0:T(8,128)(2,1)S(1)}, u32[]{:S(2)}, u32[]{:S(2)}) collective-permute-start(bf16[256,384]{1,0:T(8,128)(2,1)S(1)} %get-tuple-element.102.attb), channel_id=1, source_target_pairs={{0,1},{1,0},{2,3},{3,2},{4,5},{5,4},{6,7},{7,6},{8,9},{9,8},{10,11... | collective-permute-start | bytes 589832 | tf_op jit(solution)/shard_map/ppermute | solution.py:530
  14.7 2.8 %collective-permute-start.6 = (bf16[2,64,768]{2,1,0:T(8,128)(2,1)S(1)}, bf16[2,64,768]{2,1,0:T(8,128)(2,1)S(1)}, u32[]{:S(2)}, u32[]{:S(2)}) collective-permute-start(bf16[2,64,768]{2,1,0:T(8,128)(2,1)S(1)} %get-tuple-element.106.d0), channel_id=1, source_target_pairs={{0,1},{1,0},{2,3},{3,2},{4,5},{5,4},{6,7},{7,6},{8,9},{9,8},{10,11... | collective-permute-start | bytes 589832 | tf_op jit(solution)/shard_map/ppermute | solution.py:530
  15.0 2.4 %collective-permute-start.8 = (bf16[2,64,768]{2,1,0:T(8,128)(2,1)S(1)}, bf16[2,64,768]{2,1,0:T(8,128)(2,1)S(1)}, u32[]{:S(2)}, u32[]{:S(2)}) collective-permute-start(bf16[2,64,768]{2,1,0:T(8,128)(2,1)S(1)} %collective-permute-done.7.d2), channel_id=1, source_target_pairs={{0,1},{1,0},{2,3},{3,2},{4,5},{5,4},{6,7},{7,6},{8,9},{9,8},{10,11... | collective-permute-start | bytes 589832 | tf_op jit(solution)/shard_map/ppermute | solution.py:530
  21.8 5.4 %collective-permute-start.9 = (bf16[256,768]{1,0:T(8,128)(2,1)S(1)}, bf16[256,768]{1,0:T(8,128)(2,1)S(1)}, u32[]{:S(2)}, u32[]{:S(2)}) collective-permute-start(bf16[256,768]{1,0:T(8,128)(2,1)S(1)} %get-tuple-element.110), channel_id=1, source_target_pairs={{0,1},{1,0},{2,3},{3,2},{4,5},{5,4},{6,7},{7,6},{8,9},{9,8},{10,11... | collective-permute-start | bytes 1179656 | tf_op jit(solution)/shard_map/ppermute | solution.py:530
  24.0 16.9 %collective-permute-start.14 = (bf16[4,576,128]{2,1,0:T(8,128)(2,1)S(1)}, bf16[4,576,128]{2,1,0:T(8,128)(2,1)S(1)}, u32[]{:S(2)}, u32[]{:S(2)}) collective-permute-start(bf16[4,576,128]{2,1,0:T(8,128)(2,1)S(1)} %get-tuple-element.134), channel_id=1, source_target_pairs={{0,4},{4,0},{8,12},{12,8},{16,20},{20,16},{24,28},{28,24},{1,5},{5... | collective-permute-start | bytes 1769480 | tf_op jit(solution)/shard_map/ppermute | solution.py:530
  25.6 15.2 %collective-permute-start.15 = (bf16[2,2,576,128]{3,2,1,0:T(8,128)(2,1)S(1)}, bf16[2,2,576,128]{3,2,1,0:T(8,128)(2,1)S(1)}, u32[]{:S(2)}, u32[]{:S(2)}) collective-permute-start(bf16[2,2,576,128]{3,2,1,0:T(8,128)(2,1)S(1)} %get-tuple-element.136), channel_id=1, source_target_pairs={{0,8},{4,12},{8,0},{12,4},{16,24},{20,28},{24,16},{28,20},{1,9},{5... | collective-permute-start | bytes 1769480 | tf_op jit(solution)/shard_map/ppermute | solution.py:530
  30.1 2.0 %collective-permute-start.10 = (bf16[256,768]{1,0:T(8,128)(2,1)S(1)}, bf16[256,768]{1,0:T(8,128)(2,1)S(1)}, u32[]{:S(2)}, u32[]{:S(2)}) collective-permute-start(bf16[256,768]{1,0:T(8,128)(2,1)S(1)} %get-tuple-element.118.owna), channel_id=1, source_target_pairs={{0,1},{1,0},{2,3},{3,2},{4,5},{5,4},{6,7},{7,6},{8,9},{9,8},{10,11... | collective-permute-start | bytes 1179656 | tf_op jit(solution)/shard_map/ppermute | solution.py:530
  30.1 2.4 %collective-permute-start.11 = (bf16[320,768]{1,0:T(8,128)(2,1)S(1)}, bf16[320,768]{1,0:T(8,128)(2,1)S(1)}, u32[]{:S(2)}, u32[]{:S(2)}) collective-permute-start(bf16[320,768]{1,0:T(8,128)(2,1)S(1)} %get-tuple-element.119.ownb), channel_id=1, source_target_pairs={{0,1},{1,0},{2,3},{3,2},{4,5},{5,4},{6,7},{7,6},{8,9},{9,8},{10,11... | collective-permute-start | bytes 1474568 | tf_op jit(solution)/shard_map/ppermute | solution.py:530
  34.3 18.2 %collective-permute-start.17 = (bf16[4,592,128]{2,1,0:T(8,128)(2,1)S(1)}, bf16[4,592,128]{2,1,0:T(8,128)(2,1)S(1)}, u32[]{:S(2)}, u32[]{:S(2)}) collective-permute-start(bf16[4,592,128]{2,1,0:T(8,128)(2,1)S(1)} %get-tuple-element.141), channel_id=1, source_target_pairs={{0,4},{4,0},{8,12},{12,8},{16,20},{20,16},{24,28},{28,24},{1,5},{5... | collective-permute-start | bytes 1818632 | tf_op jit(solution)/shard_map/ppermute | solution.py:530
  34.9 21.1 %collective-permute-start.13 = (bf16[2,64,768]{2,1,0:T(8,128)(2,1)S(1)}, bf16[2,64,768]{2,1,0:T(8,128)(2,1)S(1)}, u32[]{:S(2)}, u32[]{:S(2)}) collective-permute-start(bf16[2,64,768]{2,1,0:T(8,128)(2,1)S(1)} %get-tuple-element.132), channel_id=1, source_target_pairs={{0,1},{1,0},{2,3},{3,2},{4,5},{5,4},{6,7},{7,6},{8,9},{9,8},{10,11... | collective-permute-start | bytes 589832 | tf_op jit(solution)/shard_map/ppermute | solution.py:530
  34.9 21.1 %collective-permute-start.12 = (bf16[2,64,768]{2,1,0:T(8,128)(2,1)S(1)}, bf16[2,64,768]{2,1,0:T(8,128)(2,1)S(1)}, u32[]{:S(2)}, u32[]{:S(2)}) collective-permute-start(bf16[2,64,768]{2,1,0:T(8,128)(2,1)S(1)} %get-tuple-element.128), channel_id=1, source_target_pairs={{0,2},{1,3},{2,0},{3,1},{4,6},{5,7},{6,4},{7,5},{8,10},{9,11},{10,... | collective-permute-start | bytes 589832 | tf_op jit(solution)/shard_map/ppermute | solution.py:530
  41.1 14.9 %collective-permute-start.16 = (bf16[2,576,128]{2,1,0:T(8,128)(2,1)S(1)}, bf16[2,576,128]{2,1,0:T(8,128)(2,1)S(1)}, u32[]{:S(2)}, u32[]{:S(2)}) collective-permute-start(bf16[2,576,128]{2,1,0:T(8,128)(2,1)S(1)} %get-tuple-element.140), channel_id=1, source_target_pairs={{0,8},{4,12},{8,0},{12,4},{16,24},{20,28},{24,16},{28,20},{1,9},{5... | collective-permute-start | bytes 884744 | tf_op jit(solution)/shard_map/ppermute | solution.py:530
  42.7 14.4 %collective-permute-start.19 = (bf16[1,2,576,128]{3,2,1,0:T(8,128)(2,1)S(1)}, bf16[1,2,576,128]{3,2,1,0:T(8,128)(2,1)S(1)}, u32[]{:S(2)}, u32[]{:S(2)}) collective-permute-start(bf16[1,2,576,128]{3,2,1,0:T(8,128)(2,1)S(1)} %get-tuple-element.147), channel_id=1, source_target_pairs={{0,16},{4,20},{8,24},{12,28},{16,0},{20,4},{24,8},{28,12},{1,17},{... | collective-permute-start | bytes 884744 | tf_op jit(solution)/shard_map/ppermute | solution.py:530
  52.6 11.7 %collective-permute-start.22 = (bf16[2,592,128]{2,1,0:T(8,128)(2,1)S(1)}, bf16[2,592,128]{2,1,0:T(8,128)(2,1)S(1)}, u32[]{:S(2)}, u32[]{:S(2)}) collective-permute-start(bf16[2,592,128]{2,1,0:T(8,128)(2,1)S(1)} %get-tuple-element.153), channel_id=1, source_target_pairs={{0,8},{4,12},{8,0},{12,4},{16,24},{20,28},{24,16},{28,20},{1,9},{5... | collective-permute-start | bytes 909320 | tf_op jit(solution)/shard_map/ppermute | solution.py:530
  57.3 1.6 %collective-permute-start.20 = (bf16[576,128]{1,0:T(8,128)(2,1)S(1)}, bf16[576,128]{1,0:T(8,128)(2,1)S(1)}, u32[]{:S(2)}, u32[]{:S(2)}) collective-permute-start(bf16[576,128]{1,0:T(8,128)(2,1)S(1)} %get-tuple-element.150), channel_id=1, source_target_pairs={{0,1},{1,0},{2,3},{3,2},{4,5},{5,4},{6,7},{7,6},{8,9},{9,8},{10,11... | collective-permute-start | bytes 442376 | tf_op jit(solution)/shard_map/ppermute | solution.py:530
  57.3 14.1 %collective-permute-start.18 = (bf16[1,576,128]{2,1,0:T(8,128)(2,1)S(1)}, bf16[1,576,128]{2,1,0:T(8,128)(2,1)S(1)}, u32[]{:S(2)}, u32[]{:S(2)}) collective-permute-start(bf16[1,576,128]{2,1,0:T(8,128)(2,1)S(1)} %get-tuple-element.146), channel_id=1, source_target_pairs={{0,16},{4,20},{8,24},{12,28},{16,0},{20,4},{24,8},{28,12},{1,17},{... | collective-permute-start | bytes 442376 | tf_op jit(solution)/shard_map/ppermute | solution.py:530
  58.9 6.7 %collective-permute-start.21 = (bf16[576,128]{1,0:T(8,128)(2,1)S(1)}, bf16[576,128]{1,0:T(8,128)(2,1)S(1)}, u32[]{:S(2)}, u32[]{:S(2)}) collective-permute-start(bf16[576,128]{1,0:T(8,128)(2,1)S(1)} %get-tuple-element.152), channel_id=1, source_target_pairs={{0,4},{4,0},{8,12},{12,8},{16,20},{20,16},{24,28},{28,24},{1,5},{5... | collective-permute-start | bytes 442376 | tf_op jit(solution)/shard_map/ppermute | solution.py:530
  64.4 9.8 %collective-permute-start.25 = (bf16[1,592,128]{2,1,0:T(8,128)(2,1)S(1)}, bf16[1,592,128]{2,1,0:T(8,128)(2,1)S(1)}, u32[]{:S(2)}, u32[]{:S(2)}) collective-permute-start(bf16[1,592,128]{2,1,0:T(8,128)(2,1)S(1)} %get-tuple-element.155), channel_id=1, source_target_pairs={{0,16},{4,20},{8,24},{12,28},{16,0},{20,4},{24,8},{28,12},{1,17},{... | collective-permute-start | bytes 454664 | tf_op jit(solution)/shard_map/ppermute | solution.py:530
  65.7 10.2 %collective-permute-start.28 = (bf16[576,128]{1,0:T(8,128)(2,1)S(1)}, bf16[576,128]{1,0:T(8,128)(2,1)S(1)}, u32[]{:S(2)}, u32[]{:S(2)}) collective-permute-start(bf16[576,128]{1,0:T(8,128)(2,1)S(1)} %add.2.before.p0), channel_id=1, source_target_pairs={{0,2},{1,3},{2,0},{3,1},{4,6},{5,7},{6,4},{7,5},{8,10},{9,11},{10,... | collective-permute-start | bytes 442376 | tf_op jit(solution)/shard_map/ppermute | solution.py:530
  71.5 7.2 %collective-permute-start.24 = (bf16[1,592,128]{2,1,0:T(8,128)(2,1)S(1)}, bf16[1,592,128]{2,1,0:T(8,128)(2,1)S(1)}, u32[]{:S(2)}, u32[]{:S(2)}) collective-permute-start(bf16[1,592,128]{2,1,0:T(8,128)(2,1)S(1)} %add_wide.1.before.a0), channel_id=1, source_target_pairs={{0,2},{1,3},{2,0},{3,1},{4,6},{5,7},{6,4},{7,5},{8,10},{9,11},{10,... | collective-permute-start | bytes 454664 | tf_op jit(solution)/shard_map/ppermute | solution.py:530
  74.3 5.7 %collective-permute-start.26 = (bf16[1,592,128]{2,1,0:T(8,128)(2,1)S(1)}, bf16[1,592,128]{2,1,0:T(8,128)(2,1)S(1)}, u32[]{:S(2)}, u32[]{:S(2)}) collective-permute-start(bf16[1,592,128]{2,1,0:T(8,128)(2,1)S(1)} %add.3.p0), channel_id=1, source_target_pairs={{0,2},{1,3},{2,0},{3,1},{4,6},{5,7},{6,4},{7,5},{8,10},{9,11},{10,... | collective-permute-start | bytes 454664 | tf_op jit(solution)/shard_map/ppermute | solution.py:530
  75.9 1.4 %collective-permute-start.27 = (bf16[576,128]{1,0:T(8,128)(2,1)S(1)}, bf16[576,128]{1,0:T(8,128)(2,1)S(1)}, u32[]{:S(2)}, u32[]{:S(2)}) collective-permute-start(bf16[576,128]{1,0:T(8,128)(2,1)S(1)} %add.2.before.p0), channel_id=1, source_target_pairs={{0,1},{1,0},{2,3},{3,2},{4,5},{5,4},{6,7},{7,6},{8,9},{9,8},{10,11... | collective-permute-start | bytes 442376 | tf_op jit(solution)/shard_map/ppermute | solution.py:530
  75.9 1.6 %collective-permute-start.29 = (bf16[576,128]{1,0:T(8,128)(2,1)S(1)}, bf16[576,128]{1,0:T(8,128)(2,1)S(1)}, u32[]{:S(2)}, u32[]{:S(2)}) collective-permute-start(bf16[576,128]{1,0:T(8,128)(2,1)S(1)} %collective-permute-done.28.p2), channel_id=1, source_target_pairs={{0,1},{1,0},{2,3},{3,2},{4,5},{5,4},{6,7},{7,6},{8,9},{9,8},{10,11... | collective-permute-start | bytes 442376 | tf_op jit(solution)/shard_map/ppermute | solution.py:530
  76.4 4.0 %collective-permute-start.23 = (bf16[1,592,128]{2,1,0:T(8,128)(2,1)S(1)}, bf16[1,592,128]{2,1,0:T(8,128)(2,1)S(1)}, u32[]{:S(2)}, u32[]{:S(2)}) collective-permute-start(bf16[1,592,128]{2,1,0:T(8,128)(2,1)S(1)} %add_wide.1.before.a0), channel_id=1, source_target_pairs={{0,1},{1,0},{2,3},{3,2},{4,5},{5,4},{6,7},{7,6},{8,9},{9,8},{10,11... | collective-permute-start | bytes 454664 | tf_op jit(solution)/shard_map/ppermute | solution.py:530
  77.3 3.2 %collective-permute-start.31 = (bf16[1,592,128]{2,1,0:T(8,128)(2,1)S(1)}, bf16[1,592,128]{2,1,0:T(8,128)(2,1)S(1)}, u32[]{:S(2)}, u32[]{:S(2)}) collective-permute-start(bf16[1,592,128]{2,1,0:T(8,128)(2,1)S(1)} %add.3.p0), channel_id=1, source_target_pairs={{0,1},{1,0},{2,3},{3,2},{4,5},{5,4},{6,7},{7,6},{8,9},{9,8},{10,11... | collective-permute-start | bytes 454664 | tf_op jit(solution)/shard_map/ppermute | solution.py:530
  80.0 1.4 %collective-permute-start.30 = (bf16[1,592,128]{2,1,0:T(8,128)(2,1)S(1)}, bf16[1,592,128]{2,1,0:T(8,128)(2,1)S(1)}, u32[]{:S(2)}, u32[]{:S(2)}) collective-permute-start(bf16[1,592,128]{2,1,0:T(8,128)(2,1)S(1)} %collective-permute-done.24.a2), channel_id=1, source_target_pairs={{0,1},{1,0},{2,3},{3,2},{4,5},{5,4},{6,7},{7,6},{8,9},{9,8},{10,11... | collective-permute-start | bytes 454664 | tf_op jit(solution)/shard_map/ppermute | solution.py:530
  80.0 1.6 %collective-permute-start.32 = (bf16[1,592,128]{2,1,0:T(8,128)(2,1)S(1)}, bf16[1,592,128]{2,1,0:T(8,128)(2,1)S(1)}, u32[]{:S(2)}, u32[]{:S(2)}) collective-permute-start(bf16[1,592,128]{2,1,0:T(8,128)(2,1)S(1)} %collective-permute-done.26.p2), channel_id=1, source_target_pairs={{0,1},{1,0},{2,3},{3,2},{4,5},{5,4},{6,7},{7,6},{8,9},{9,8},{10,11... | collective-permute-start | bytes 454664 | tf_op jit(solution)/shard_map/ppermute | solution.py:530

commit v6 on v5

--- a/solution.py
+++ b/solution.py
@@ -223,15 +223,15 @@
 
     def residual(
         atta, attb, othera, otherb, t0, t1, t2, t3_core, t3_away, vec, wout,
-        att_own_o, att_other_o, sec_o, hid_core_o, hid_own_o, t3_o,
-        att, hid,
+        att, sec_o, hid, t3_o,
     ):
         place = Place(inner)
-        for out, halves in ((att_own_o, (atta, attb)), (att_other_o, (othera, otherb))):
-            for n, part in enumerate(halves):
-                cols = pl.ds(pl.multiple_of(flip(place.y, n) * 384, 128), 384)
-                out[:, cols] = part[...]
-        both_cores(place.core, att_own_o, att_other_o, att)
+        for n in range(2):
+            cols = pl.ds(pl.multiple_of(flip(place.y, n) * 384, 128), 384)
+            att[place.core, :, cols] = (atta, attb)[n][...]
+            for p in range(4):
+                rows = pl.ds((p ^ 1) * 64, 64)
+                att[1 - place.core, pl.ds(p * 64, 64), cols] = (othera, otherb)[n][rows, :]
         t3_o[place.core] = t3_core[...]
         t3_o[1 - place.core] = t3_away[...]
         g, b, ob = vec[5:6, :], vec[6:7, :], vec[4:5, :]
@@ -242,12 +242,12 @@
                 hid[s, pl.ds(p * 64, 64), :] = h
                 xhat, _ = standardize(h)
                 sec_o[pl.ds(s * 256 + p * 64, 64), :] = (xhat * g + b).astype(BF16)
-            hid_own_o[pl.ds(s * 64, 64), :] = hid[s, 0:64, :]
-        hid_core_o[...] = hid[place.core]
-
-    def feed(sec_o, up_bias, d0, d1, d2, d3, wup, wdown, dup_o, act_o, send_o, dsec_o, dy_o):
+
+    def feed(sec_o, up_bias, d0, d1, d2, d3, wup, wdown, dup_o, act_o, send_o, dsec_o, dy_o, chosen_o, turned):
         place = Place(inner)
         gather_rows((d0, d1, d2, d3), dy_o)
+        turned[...] = sec_o[...].T
+        pick_rows(turned, chosen_o, place.y, place.x)
         for j in range(6):
             cols = pl.ds(j * 256, 256)
             for s in range(2):
@@ -267,14 +267,11 @@
             send_o[pl.ds(p * 64, 64), :] = away[(p ^ 1) * 64 : (p ^ 1) * 64 + 64].astype(BF16)
         dsec_o[...] = nt(dup_o[pl.ds(pl.multiple_of(place.core * 256, 256), 256), :], wup[...])
 
-    def feed_weights(sec, dup, act, dy, up_keep, up_send, down_keep, down_send, bias_o, turned, chosen):
-        place = Place(inner)
-        turned[...] = sec[...].T
-        pick_rows(turned, chosen, place.y, place.x)
+    def feed_weights(chosen, dup, act, dy, up_keep, up_send, down_keep, down_send):
+        place = Place(inner)
         for j in range(2):
             cols = pl.ds(j * 768, 768)
             put_slots(nn(chosen[...], dup[:, cols]).astype(BF16), up_keep, up_send, j * 288)
-            bias_o[:, cols] = column_sum(dup[0:128, cols]) + column_sum(dup[256:384, cols])
         dy_half = dy[:, pl.ds(pl.multiple_of(place.y * 384, 128), 384)]
         for k, out in enumerate((down_keep, down_send)):
             for z in range(2):
@@ -288,7 +285,7 @@
                         ]
 
     def attention_back(
-        dsec_in, got, hid_core, d0, d1, d2, d3, vec, probs_in, mine, wout, up_sums,
+        dsec_in, got, hid_core, d0, d1, d2, d3, vec, probs_in, mine, wout, before,
         exa_o, exb_o, dhid_o, sums_o, heads_o,
         dh, datt,
     ):
@@ -297,7 +294,7 @@
         sums = [jnp.zeros((1, 768), F32)] * 3
         for p, d in enumerate((d0, d1, d2, d3)):
             rows = pl.ds(p * 64, 64)
-            xhat, rstd = standardize(hid_core[rows, :])
+            xhat, rstd = standardize(hid_core[place.core, rows, :])
             grad = dsec_in[rows, :] + got[rows, :].astype(F32)
             dhid = d[place.core].astype(F32) + norm_back(xhat, rstd, grad * g)
             low = dhid.astype(BF16)
@@ -341,12 +338,12 @@
         heads_o[2:8, :] = jnp.zeros((6, 384), F32)
 
     def turn(
-        att_own, att_other, t0, t1, t2, t3, params, act, wdown, before,
-        first_o, att_o, part_o, part_send,
-        first, att, turned,
+        att, t0, t1, t2, t3, params, act, wdown, dup, before,
+        first_o, att_o, part_o, part_send, bias_o,
+        first, turned,
     ):
         place = Place(inner)
-        both_cores(place.core, att_own, att_other, att)
+        bias_o[...] = column_sum(dup[0:128, :]) + column_sum(dup[256:384, :])
         for s in range(2):
             for p, t in enumerate((t0, t1, t2, t3)):
                 xhat, _ = standardize(t[s].astype(F32))
@@ -417,6 +414,9 @@
             keep[z, pl.ds(576, 16), :] = vec[0, z].astype(BF16)
             send[z, pl.ds(576, 16), :] = vec[1, z].astype(BF16)
 
+    def hold(received, part_got, before, mark):
+        mark[...] = jnp.zeros_like(mark)
+
     def input_grad(
         tokens, dfirst, received, dhid, other, vec, hid_own, part, part_got, before,
         out, block_o, mark,
@@ -433,7 +433,7 @@
         write(1 - place.core, other[256:320, :].astype(F32))
         for s in range(2):
             added = part[s] + part_got[s].astype(F32) + vec[7:8, :]
-            block_o[s] = (hid_own[pl.ds(s * 64, 64), :] + added).astype(BF16)
+            block_o[s] = (hid_own[s, 0:64, :] + added).astype(BF16)
 
     def halve_z_low(keep, got, before, stay, leave):
         halve(Place(inner).z_low, keep, got, stay, leave)
@@ -587,53 +587,49 @@
         )
         chunk, half = ((4, 576, 128), BF16), ((2, 2, 576, 128), BF16)
         own = (2, 64, 768)
-        att, att_other, sec, hid_core, hid_own, t3 = call(
+        att, sec, hid, t3 = call(
             kernels["residual"],
-            (
-                ((256, 768), BF16), ((256, 768), BF16), ((512, 768), BF16), ((256, 768), F32),
-                ((128, 768), F32), (own, BF16),
-            ),
+            (((2, 256, 768), BF16), ((512, 768), BF16), ((2, 256, 768), F32), (own, BF16)),
             [VMEM] * 11,
             (atta, attb, core_swap(atta), core_swap(attb), t0, t1, t2, t3_core, t3_away, vec, wout),
-            [pltpu.VMEM((2, 256, 768), BF16), pltpu.VMEM((2, 256, 768), F32)],
             us=US,
         )
         t_pieces = t0, t1, t2, t3
-        dup, act, partial, dsec, dy_rows = call(
+        dup, act, partial, dsec, dy_rows, second_t = call(
             kernels["feed"],
             (
                 ((512, 1536), BF16), ((512, 1536), BF16), ((256, 768), BF16), ((256, 768), F32),
-                ((512, 768), BF16),
+                ((512, 768), BF16), ((384, 512), BF16),
             ),
             [VMEM] * 8,
             (sec, up_row, *d_pieces, wup, wdown),
+            [pltpu.VMEM((768, 512), BF16)],
             us=US,
         )
         arrived = core_swap(partial)
-        up_keep, up_send, down_keep, down_send, up_sums = call(
+        up_keep, up_send, down_keep, down_send = call(
             kernels["feed_weights"],
-            (chunk, chunk, half, half, ((1, 1536), F32)),
+            (chunk, chunk, half, half),
             [VMEM] * 4,
-            (sec, dup, act, dy_rows),
-            [pltpu.VMEM((768, 512), BF16), pltpu.VMEM((384, 512), BF16)],
+            (second_t, dup, act, dy_rows),
             us=FILL,
         )
         exa, exb, dhid, sums, heads = call(
             kernels["attention_back"],
             (((256, 768), BF16), ((320, 768), BF16), ((64, 768), F32), ((8, 768), F32), ((8, 384), F32)),
-            [VMEM] * 12,
-            (dsec, arrived, hid_core, *d_pieces, vec, probs, mine, wout, up_sums),
+            [VMEM] * 11 + [ANY],
+            (dsec, arrived, hid, *d_pieces, vec, probs, mine, wout, down_keep),
             [pltpu.VMEM((256, 768), BF16), pltpu.VMEM((256, 384), BF16)],
             us=US,
         )
         exa_other, exb_other = core_swap(exa), core_swap(exb)
         rest = ((4, 592, 128), BF16)
-        first_t, att_t, part, part_send = call(
+        first_t, att_t, part, part_send, up_sums = call(
             kernels["turn"],
-            (((384, 512), BF16), ((384, 512), BF16), (own, F32), (own, BF16)),
+            (((384, 512), BF16), ((384, 512), BF16), (own, F32), (own, BF16), ((1, 1536), F32)),
             [VMEM] * 9 + [ANY],
-            (att, att_other, *t_pieces, vec, act, wdown, sums),
-            [pltpu.VMEM((2, 256, 768), BF16), pltpu.VMEM((2, 256, 768), BF16), pltpu.VMEM((768, 512), BF16)],
+            (att, *t_pieces, vec, act, wdown, dup, sums),
+            [pltpu.VMEM((2, 256, 768), BF16), pltpu.VMEM((768, 512), BF16)],
             us=FILL,
         )
         rest_keep, rest_send, dfirst_own, dfirst_send = call(
@@ -651,15 +647,9 @@
         up_stay, up_leave = halve("halve_z_low", up_keep, seq_swap(up_send, 1), down_stay)
         rest_stay, rest_leave = halve("halve_z_low", rest_keep, seq_swap(rest_send, 1), up_stay, FILL)
         up_stay, up_leave = halve("halve_z_high", up_stay, seq_swap(up_leave, 2), rest_stay)
-        in_grad, block_out, mark = call(
-            kernels["input_grad"],
-            ((own, BF16), (own, BF16), ((8, 128), F32)),
-            [VMEM] * 9 + [ANY],
-            (
-                t0, dfirst_own, y_swap(dfirst_send), dhid, exb_other, vec, hid_own, part,
-                core_swap(part_send), up_stay,
-            ),
-            us=US,
+        received, part_got = y_swap(dfirst_send), core_swap(part_send)
+        (mark,) = call(
+            kernels["hold"], (((8, 128), F32),), [ANY] * 3, (received, part_got, up_stay), us=US
         )
         piece = ((576, 128), BF16)
         down_kept, down_sent = call(
@@ -674,11 +664,18 @@
         )
         rest_stay, rest_leave = halve("halve_z_high", rest_stay, seq_swap(rest_leave, 2), down_own)
         down_sum = add(down_own, seq_swap(down_other, 1), rest_stay, 0.001)
+        in_grad, block_out, late = call(
+            kernels["input_grad"],
+            ((own, BF16), (own, BF16), ((8, 128), F32)),
+            [VMEM] * 9 + [ANY],
+            (t0, dfirst_own, received, dhid, exb_other, vec, hid, part, part_got, down_sum),
+            us=US,
+        )
         (up_sum,) = call(
             kernels["add_wide"],
             (((1, 592, 128), BF16),),
             [VMEM, VMEM, ANY],
-            (up_stay, seq_swap(up_leave, 4), down_sum),
+            (up_stay, seq_swap(up_leave, 4), late),
             us=STEP,
         )
         rest_sum = add(rest_stay, seq_swap(rest_leave, 4), up_sum, FILL)

time: 83.2 us -> 82.5 us (level)
  starting transfers between devices: 28.7 us -> 26.5 us
  waiting for transfers between devices: 28.2 us -> 30 us
    ppermute x33, starting transfers between devices: 28.7 us -> 26.5 us  [swap(): return lax.ppermute(x, axis, [(i, i ^ step) for i in range(size)])]
    ppermute x33, waiting for transfers between devices: 28.2 us -> 30 us  [swap(): return lax.ppermute(x, axis, [(i, i ^ step) for i in range(size)])]
    pallas_call x22 -> x23, Pallas kernels: 25.3 us -> 25 us  [call(): pl.pallas_call(kernel, out_shape=tuple((jax.ShapeDtypeStruct(s, d) for s,...]
  transfers between devices with their start and end apart: 33 -> 33, of which waited for: 16 -> 15; matrix products, arithmetic and copies ran while one was open for 0% -> 0% of each run, Pallas kernels for 24% -> 23%
where the time goes in v6:
time: 82.5 us; the launch traced here: 82.3 us
  waiting for transfers between devices  30 us (36%)
  starting transfers between devices  26.5 us (32%)
  Pallas kernels  25 us (30%)
  between operations  0.84 us (1%)
    ppermute x33, waiting for transfers between devices, swap(): return lax.ppermute(x, axis, [(i, i ^ step) for i in range(size)])  30 us
    ppermute x33, starting transfers between devices, swap(): return lax.ppermute(x, axis, [(i, i ^ step) for i in range(size)])  26.5 us
    pallas_call x23, Pallas kernels, call(): pl.pallas_call(kernel, out_shape=tuple((jax.ShapeDtypeStruct(s, d) for s,...  25 us
  transfers between devices with their start and end apart: 33, of which 15 were waited for; matrix products, arithmetic and copies ran while one was open for 0% of the time, Pallas kernels for 23%

profile of v6, /device:TPU:0, one launch (start us, length us, event | category | flops | bytes accessed | tf_op | source)
XLA Modules:
  0.0 82.3 jit_solution(13276793088474568313)
XLA Ops:
  0.6 0.5 collective-permute-start
  1.2 2.6 %collective-permute-start.1 = (bf16[2,64,768]{2,1,0:T(8,128)(2,1)}, bf16[2,64,768]{2,1,0:T(8,128)(2,1)S(1)}, u32[]{:S(2)}, u32[]{:S(2)}) collective-permute-start(bf16[2,64,768]{2,1,0:T(8,128)(2,1)} %tokens_hbm.1), channel_id=1, source_target_pairs={{0,2},{1,3},{2,0},{3,1},{4,6},{5,7},{6,4},{7,5},{8,10},{9,11},{10,... | collective-permute-start | bytes 589832 | tf_op jit(solution)/shard_map/ppermute | solution.py:530
  3.8 4.2 %near.1 = (bf16[128,2304]{1,0:T(8,128)(2,1)S(1)}, f32[256,256]{1,0:T(8,128)S(1)}, f32[8,768]{1,0:T(8,128)S(1)}, f32[1,1536]{1,0:T(1,128)S(1)}, bf16[2,64,768]{2,...) custom-call(bf16[2,64,768]{2,1,0:T(8,128)(2,1)S(1)} %collective-perm, ...), custom_call_target="tpu_custom_call" | custom-call | flops 3000000000 | bytes 300000 | tf_op jit(solution)/shard_map/near/pallas_call | solution.py:74
  8.0 1.6 %collective-permute-start.7 = (bf16[2,64,768]{2,1,0:T(8,128)(2,1)S(1)}, bf16[2,64,768]{2,1,0:T(8,128)(2,1)S(1)}, u32[]{:S(2)}, u32[]{:S(2)}) collective-permute-start(bf16[2,64,768]{2,1,0:T(8,128)(2,1)S(1)} %get-tuple-element.105.d0), channel_id=1, source_target_pairs={{0,2},{1,3},{2,0},{3,1},{4,6},{5,7},{6,4},{7,5},{8,10},{9,11},{10,... | collective-permute-start | bytes 589832 | tf_op jit(solution)/shard_map/ppermute | solution.py:530
  9.7 0.5 collective-permute-start.3
  10.2 0.8 collective-permute-done.2.t3.t3_core
  11.2 2.9 %attention.1 = (bf16[256,384]{1,0:T(8,128)(2,1)S(1)}, bf16[256,384]{1,0:T(8,128)(2,1)S(1)}, bf16[256,1152]{1,0:T(8,128)(2,1)S(1)}, f32[6,256,256]{2,1,0:T(8,128)S(1)}) custom-call(bf16[128,2304]{1,0:T(8,128)(2,1)S(1)} %get-tuple-element.93.near_in, f32[256,256]{1,0:T(8,128)S(1)} %get-tuple-element.94.mask, f32[8,768]{1,0:T(8,128)S(1)} %get-tuple-element.95.vec.params, ...), custom_call_target="tpu_custom_call" | custom-call | flops 10000000 | bytes 1000 | tf_op jit(solution)/shard_map/attention/pallas_call | solution.py:74
  14.1 0.4 collective-permute-start.4
  14.7 0.4 collective-permute-start.6
  15.2 0.4 collective-permute-done.4.othera
  15.6 0.4 collective-permute-done.5.otherb
  16.0 1.2 %residual.1 = (bf16[2,256,768]{2,1,0:T(8,128)(2,1)S(1)}, bf16[512,768]{1,0:T(8,128)(2,1)S(1)}, f32[2,256,768]{2,1,0:T(8,128)S(1)}, bf16[2,64,768]{2,1,0:T(8,128)(2,1)S(1)}) custom-call(bf16[256,384]{1,0:T(8,128)(2,1)S(1)} %get-tuple-element.100.atta, bf16[256,384]{1,0:T(8,128)(2,1)S(1)} %get-tuple-element.101.attb, ...), custom_call_target="tpu_custom_call" | custom-call | flops 10000000 | bytes 1000 | tf_op jit(solution)/shard_map/residual/pallas_call | solution.py:74
  17.2 4.3 %feed.1 = (bf16[512,1536]{1,0:T(8,128)(2,1)S(1)}, bf16[512,1536]{1,0:T(8,128)(2,1)S(1)}, bf16[256,768]{1,0:T(8,128)(2,1)S(1)}, f32[256,768]{1,0:T(8,128)S(1)}, b...) custom-call(bf16[512,768]{1,0:T(8,128)(2,1)S(1)} %get-tuple-element.103.sec_o, ...), custom_call_target="tpu_custom_call" | custom-call | flops 10000000 | bytes 1000 | tf_op jit(solution)/shard_map/feed/pallas_call | solution.py:74
  21.5 0.3 collective-permute-start.9
  21.9 1.6 %feed_weights.1 = (bf16[4,576,128]{2,1,0:T(8,128)(2,1)S(1)}, bf16[4,576,128]{2,1,0:T(8,128)(2,1)S(1)}, bf16[2,2,576,128]{3,2,1,0:T(8,128)(2,1)S(1)}, bf16[2,2,576,128]{3,2,1,0:T(8,128)(2,1)S(1)}) custom-call(bf16[384,512]{1,0:T(8,128)(2,1)S(1)} %get-tuple-element.113.chosen, bf16[512,1536]{1,0:T(8,128)(2,1)S(1)} %get-tuple-element.114.dup, ...), custom_call_target="tpu_custom_call" | custom-call | flops 20000000000 | bytes 2000000 | tf_op jit(solution)/shard_map/feed_weights/pallas_call | solution.py:74
  23.5 1.7 %collective-permute-start.14 = (bf16[2,2,576,128]{3,2,1,0:T(8,128)(2,1)S(1)}, bf16[2,2,576,128]{3,2,1,0:T(8,128)(2,1)S(1)}, u32[]{:S(2)}, u32[]{:S(2)}) collective-permute-start(bf16[2,2,576,128]{3,2,1,0:T(8,128)(2,1)S(1)} %get-tuple-element.132), channel_id=1, source_target_pairs={{0,8},{4,12},{8,0},{12,4},{16,24},{20,28},{24,16},{28,20},{1,9},{5... | collective-permute-start | bytes 1769480 | tf_op jit(solution)/shard_map/ppermute | solution.py:530
  25.2 1.5 %collective-permute-start.16 = (bf16[4,576,128]{2,1,0:T(8,128)(2,1)S(1)}, bf16[4,576,128]{2,1,0:T(8,128)(2,1)S(1)}, u32[]{:S(2)}, u32[]{:S(2)}) collective-permute-start(bf16[4,576,128]{2,1,0:T(8,128)(2,1)S(1)} %get-tuple-element.137), channel_id=1, source_target_pairs={{0,4},{4,0},{8,12},{12,8},{16,20},{20,16},{24,28},{28,24},{1,5},{5... | collective-permute-start | bytes 1769480 | tf_op jit(solution)/shard_map/ppermute | solution.py:530
  26.7 2.9 %attention_back.1 = (bf16[256,768]{1,0:T(8,128)(2,1)S(1)}, bf16[320,768]{1,0:T(8,128)(2,1)S(1)}, f32[64,768]{1,0:T(8,128)S(1)}, f32[8,768]{1,0:T(8,128)S(1)}, f32[8,384]{1,0:T(8,128)S(1)}) custom-call(f32[256,768]{1,0:T(8,128)S(1)} %get-tuple-element.108.dsec_in, bf16[256,768]{1,0:T(8,128)(2,1)S(1)} %collective-permute-done.9.got, ...), custom_call_target="tpu_custom_call" | custom-call | flops 10000000 | bytes 1000 | tf_op jit(solution)/shard_map/attention_back/pallas_call | solution.py:74
  29.7 0.5 collective-permute-start.11
  30.2 1.5 %turn.1 = (bf16[384,512]{1,0:T(8,128)(2,1)S(1)}, bf16[384,512]{1,0:T(8,128)(2,1)S(1)}, f32[2,64,768]{2,1,0:T(8,128)S(1)}, bf16[2,64,768]{2,1,0:T(8,128)(2,1)S(1)}, f32[1,1536]{1,0:T(1,128)S(1)}) custom-call(bf16[2,256,768]{2,1,0:T(8,128)(2,1)S(1)} %get-tuple-element.120.att, bf16[2,64,768]{2,1,0:T(8,128)(2,1)S(1)} %get-tuple-element.91.t0.tokens, ...), custom_call_target="tpu_custom_call" | custom-call | flops 20000000000 | bytes 2000000 | tf_op jit(solution)/shard_map/turn/pallas_call | solution.py:74
  31.7 0.4 collective-permute-done.11.otherb.other
  32.1 1.8 %attention_weights.1 = (bf16[4,592,128]{2,1,0:T(8,128)(2,1)S(1)}, bf16[4,592,128]{2,1,0:T(8,128)(2,1)S(1)}, f32[2,64,768]{2,1,0:T(8,128)S(1)}, bf16[2,64,768]{2,1,0:T(8,128)(2,1)S(1)}) custom-call(bf16[256,768]{1,0:T(8,128)(2,1)S(1)} %get-tuple-element.118.owna, bf16[320,768]{1,0:T(8,128)(2,1)S(1)} %get-tuple-element.119.ownb, ...), custom_call_target="tpu_custom_call" | custom-call | flops 10000000 | bytes 1000 | tf_op jit(solution)/shard_map/attention_weights/pallas_call | solution.py:74
  33.9 0.6 collective-permute-start.18
  34.5 1.6 %collective-permute-start.12 = (bf16[2,64,768]{2,1,0:T(8,128)(2,1)S(1)}, bf16[2,64,768]{2,1,0:T(8,128)(2,1)S(1)}, u32[]{:S(2)}, u32[]{:S(2)}) collective-permute-start(bf16[2,64,768]{2,1,0:T(8,128)(2,1)S(1)} %get-tuple-element.128), channel_id=1, source_target_pairs={{0,2},{1,3},{2,0},{3,1},{4,6},{5,7},{6,4},{7,5},{8,10},{9,11},{10,... | collective-permute-start | bytes 589832 | tf_op jit(solution)/shard_map/ppermute | solution.py:530
  36.0 3.0 %collective-permute-done.14.got = bf16[2,2,576,128]{3,2,1,0:T(8,128)(2,1)S(1)} collective-permute-done((bf16[2,2,576,128]{3,2,1,0:T(8,128)(2,1)S(1)}, bf16[2,2,576,128]{3,2,1,0:T(8,128)(2,1)S(1)}, u32[]{:S(2)}, u32[]{:S(2)}) %collective-permute-start.14) | collective-permute-done | bytes 589856 | tf_op jit(solution)/shard_map/ppermute | solution.py:530
  39.1 2.7 %collective-permute-start.15 = (bf16[1,2,576,128]{3,2,1,0:T(8,128)(2,1)S(1)}, bf16[1,2,576,128]{3,2,1,0:T(8,128)(2,1)S(1)}, u32[]{:S(2)}, u32[]{:S(2)}) collective-permute-start(bf16[1,2,576,128]{3,2,1,0:T(8,128)(2,1)S(1)} %get-tuple-element.135), channel_id=1, source_target_pairs={{0,16},{4,20},{8,24},{12,28},{16,0},{20,4},{24,8},{28,12},{1,17},{... | collective-permute-start | bytes 884744 | tf_op jit(solution)/shard_map/ppermute | solution.py:530
  42.0 1.6 %collective-permute-start.17 = (bf16[2,576,128]{2,1,0:T(8,128)(2,1)S(1)}, bf16[2,576,128]{2,1,0:T(8,128)(2,1)S(1)}, u32[]{:S(2)}, u32[]{:S(2)}) collective-permute-start(bf16[2,576,128]{2,1,0:T(8,128)(2,1)S(1)} %get-tuple-element.139), channel_id=1, source_target_pairs={{0,8},{4,12},{8,0},{12,4},{16,24},{20,28},{24,16},{28,20},{1,9},{5... | collective-permute-start | bytes 884744 | tf_op jit(solution)/shard_map/ppermute | solution.py:530
  43.7 9.7 %collective-permute-done.18.got = bf16[4,592,128]{2,1,0:T(8,128)(2,1)S(1)} collective-permute-done((bf16[4,592,128]{2,1,0:T(8,128)(2,1)S(1)}, bf16[4,592,128]{2,1,0:T(8,128)(2,1)S(1)}, u32[]{:S(2)}, u32[]{:S(2)}) %collective-permute-start.18) | collective-permute-done | bytes 606240 | tf_op jit(solution)/shard_map/ppermute | solution.py:530
  53.4 0.2 halve_z_low.3
  53.5 0.4 collective-permute-start.21
  54.0 1.3 %collective-permute-done.17.got = bf16[2,576,128]{2,1,0:T(8,128)(2,1)S(1)} collective-permute-done((bf16[2,576,128]{2,1,0:T(8,128)(2,1)S(1)}, bf16[2,576,128]{2,1,0:T(8,128)(2,1)S(1)}, u32[]{:S(2)}, u32[]{:S(2)}) %collective-permute-start.17) | collective-permute-done | bytes 294944 | tf_op jit(solution)/shard_map/ppermute | solution.py:530
  55.6 1.4 %collective-permute-start.22 = (bf16[1,576,128]{2,1,0:T(8,128)(2,1)S(1)}, bf16[1,576,128]{2,1,0:T(8,128)(2,1)S(1)}, u32[]{:S(2)}, u32[]{:S(2)}) collective-permute-start(bf16[1,576,128]{2,1,0:T(8,128)(2,1)S(1)} %get-tuple-element.151), channel_id=1, source_target_pairs={{0,16},{4,20},{8,24},{12,28},{16,0},{20,4},{24,8},{28,12},{1,17},{... | collective-permute-start | bytes 442376 | tf_op jit(solution)/shard_map/ppermute | solution.py:530
  57.0 1.6 %collective-permute-start.20 = (bf16[576,128]{1,0:T(8,128)(2,1)S(1)}, bf16[576,128]{1,0:T(8,128)(2,1)S(1)}, u32[]{:S(2)}, u32[]{:S(2)}) collective-permute-start(bf16[576,128]{1,0:T(8,128)(2,1)S(1)} %get-tuple-element.146), channel_id=1, source_target_pairs={{0,4},{4,0},{8,12},{12,8},{16,20},{20,16},{24,28},{28,24},{1,5},{5... | collective-permute-start | bytes 442376 | tf_op jit(solution)/shard_map/ppermute | solution.py:530
  58.6 6.4 %collective-permute-done.21.got = bf16[2,592,128]{2,1,0:T(8,128)(2,1)S(1)} collective-permute-done((bf16[2,592,128]{2,1,0:T(8,128)(2,1)S(1)}, bf16[2,592,128]{2,1,0:T(8,128)(2,1)S(1)}, u32[]{:S(2)}, u32[]{:S(2)}) %collective-permute-start.21) | collective-permute-done | bytes 303136 | tf_op jit(solution)/shard_map/ppermute | solution.py:530
  65.0 1.1 %collective-permute-start.25 = (bf16[1,592,128]{2,1,0:T(8,128)(2,1)S(1)}, bf16[1,592,128]{2,1,0:T(8,128)(2,1)S(1)}, u32[]{:S(2)}, u32[]{:S(2)}) collective-permute-start(bf16[1,592,128]{2,1,0:T(8,128)(2,1)S(1)} %get-tuple-element.153), channel_id=1, source_target_pairs={{0,16},{4,20},{8,24},{12,28},{16,0},{20,4},{24,8},{28,12},{1,17},{... | collective-permute-start | bytes 454664 | tf_op jit(solution)/shard_map/ppermute | solution.py:530
  66.1 1.6 %collective-permute-start.28 = (bf16[576,128]{1,0:T(8,128)(2,1)S(1)}, bf16[576,128]{1,0:T(8,128)(2,1)S(1)}, u32[]{:S(2)}, u32[]{:S(2)}) collective-permute-start(bf16[576,128]{1,0:T(8,128)(2,1)S(1)} %add.2.before.p0), channel_id=1, source_target_pairs={{0,2},{1,3},{2,0},{3,1},{4,6},{5,7},{6,4},{7,5},{8,10},{9,11},{10,... | collective-permute-start | bytes 442376 | tf_op jit(solution)/shard_map/ppermute | solution.py:530
  67.7 1.1 %input_grad.1 = (bf16[2,64,768]{2,1,0:T(8,128)(2,1)}, bf16[2,64,768]{2,1,0:T(8,128)(2,1)}, f32[8,128]{1,0:T(8,128)S(1)}) custom-call(bf16[2,64,768]{2,1,0:T(8,128)(2,1)S(1)} %get-tuple-element.91.t0.tokens, f32[2,64,768]{2,1,0:T(8,128)S(1)} %get-tuple-element.127.dfirst, bf16[2,64,768]{2,1,0:T(8,128)(2,1)S(1)} %collective-permute-done.12.received, ...), custom_call_target="tpu_custom_call" | custom-call | flops 10000000 | bytes 1000 | tf_op jit(solution)/shard_map/input_grad/pallas_call | solution.py:74
  68.9 0.6 collective-permute-start.24
  69.4 4.0 %collective-permute-done.25.b = bf16[1,592,128]{2,1,0:T(8,128)(2,1)S(1)} collective-permute-done((bf16[1,592,128]{2,1,0:T(8,128)(2,1)S(1)}, bf16[1,592,128]{2,1,0:T(8,128)(2,1)S(1)}, u32[]{:S(2)}, u32[]{:S(2)}) %collective-permute-start.25) | collective-permute-done | bytes 151584 | tf_op jit(solution)/shard_map/ppermute | solution.py:530
  73.5 1.6 %collective-permute-start.26 = (bf16[1,592,128]{2,1,0:T(8,128)(2,1)S(1)}, bf16[1,592,128]{2,1,0:T(8,128)(2,1)S(1)}, u32[]{:S(2)}, u32[]{:S(2)}) collective-permute-start(bf16[1,592,128]{2,1,0:T(8,128)(2,1)S(1)} %add.3.p0), channel_id=1, source_target_pairs={{0,2},{1,3},{2,0},{3,1},{4,6},{5,7},{6,4},{7,5},{8,10},{9,11},{10,... | collective-permute-start | bytes 454664 | tf_op jit(solution)/shard_map/ppermute | solution.py:530
  75.1 0.5 collective-permute-start.29
  75.6 0.9 %collective-permute-done.27.p1 = bf16[576,128]{1,0:T(8,128)(2,1)S(1)} collective-permute-done((bf16[576,128]{1,0:T(8,128)(2,1)S(1)}, bf16[576,128]{1,0:T(8,128)(2,1)S(1)}, u32[]{:S(2)}, u32[]{:S(2)}) %collective-permute-start.27) | collective-permute-done | bytes 147488 | tf_op jit(solution)/shard_map/ppermute | solution.py:530
  76.7 1.1 %assemble_down.1 = f32[384,768]{1,0:T(8,128)} custom-call(bf16[576,128]{1,0:T(8,128)(2,1)S(1)} %add.2.before.p0, bf16[576,128]{1,0:T(8,128)(2,1)S(1)} %collective-permute-done.27.p1, bf16[576,128]{1,0:T(8,128)(2,1)S(1)} %collective-permute-done.28.p2, bf16[576,128]{1,0:T(8,128)(2,1)S(1)} %collective-permute-done.29.p3), custom_call_target="tpu_custom_call" | custom-call | flops 10000000 | bytes 1000 | tf_op jit(solution)/shard_map/assemble_down/pallas_call | solution.py:74
  77.8 1.4 %collective-permute-done.26.p2 = bf16[1,592,128]{2,1,0:T(8,128)(2,1)S(1)} collective-permute-done((bf16[1,592,128]{2,1,0:T(8,128)(2,1)S(1)}, bf16[1,592,128]{2,1,0:T(8,128)(2,1)S(1)}, u32[]{:S(2)}, u32[]{:S(2)}) %collective-permute-start.26) | collective-permute-done | bytes 151584 | tf_op jit(solution)/shard_map/ppermute | solution.py:530
  79.2 0.5 collective-permute-start.32
  79.7 0.9 %collective-permute-done.30.a3 = bf16[1,592,128]{2,1,0:T(8,128)(2,1)S(1)} collective-permute-done((bf16[1,592,128]{2,1,0:T(8,128)(2,1)S(1)}, bf16[1,592,128]{2,1,0:T(8,128)(2,1)S(1)}, u32[]{:S(2)}, u32[]{:S(2)}) %collective-permute-start.30) | collective-permute-done | bytes 151584 | tf_op jit(solution)/shard_map/ppermute | solution.py:530
  80.6 0.2 collective-permute-done.32.p3
  80.8 1.5 %assemble_last.1 = (f32[96,3072]{1,0:T(8,128)}, f32[96,768]{1,0:T(8,128)}, f32[96,2304]{1,0:T(8,128)}, f32[96]{0:T(128)}, f32[96]{0:T(128)}, /*index=5*/f32[192]...) custom-call(bf16[1,592,128]{2,1,0:T(8,128)(2,1)S(1)} %add_wide.1.before.a0, ...), custom_call_target="tpu_custom_call" | custom-call | flops 10000000 | bytes 1000 | tf_op jit(solution)/shard_map/assemble_last/pallas_call | solution.py:74
  (41 shorter events, 1.6 us)
Async XLA Ops:
  0.6 3.1 %collective-permute-start = (bf16[2,64,768]{2,1,0:T(8,128)(2,1)}, bf16[2,64,768]{2,1,0:T(8,128)(2,1)S(1)}, u32[]{:S(2)}, u32[]{:S(2)}) collective-permute-start(bf16[2,64,768]{2,1,0:T(8,128)(2,1)} %tokens_hbm.1), channel_id=1, source_target_pairs={{0,1},{1,0},{2,3},{3,2},{4,5},{5,4},{6,7},{7,6},{8,9},{9,8},{10,11... | collective-permute-start | bytes 589832 | tf_op jit(solution)/shard_map/ppermute | solution.py:530
  1.2 8.5 %collective-permute-start.1 = (bf16[2,64,768]{2,1,0:T(8,128)(2,1)}, bf16[2,64,768]{2,1,0:T(8,128)(2,1)S(1)}, u32[]{:S(2)}, u32[]{:S(2)}) collective-permute-start(bf16[2,64,768]{2,1,0:T(8,128)(2,1)} %tokens_hbm.1), channel_id=1, source_target_pairs={{0,2},{1,3},{2,0},{3,1},{4,6},{5,7},{6,4},{7,5},{8,10},{9,11},{10,... | collective-permute-start | bytes 589832 | tf_op jit(solution)/shard_map/ppermute | solution.py:530
  8.0 7.1 %collective-permute-start.7 = (bf16[2,64,768]{2,1,0:T(8,128)(2,1)S(1)}, bf16[2,64,768]{2,1,0:T(8,128)(2,1)S(1)}, u32[]{:S(2)}, u32[]{:S(2)}) collective-permute-start(bf16[2,64,768]{2,1,0:T(8,128)(2,1)S(1)} %get-tuple-element.105.d0), channel_id=1, source_target_pairs={{0,2},{1,3},{2,0},{3,1},{4,6},{5,7},{6,4},{7,5},{8,10},{9,11},{10,... | collective-permute-start | bytes 589832 | tf_op jit(solution)/shard_map/ppermute | solution.py:530
  9.7 1.4 %collective-permute-start.2 = (bf16[64,768]{1,0:T(8,128)(2,1)S(1)}, bf16[64,768]{1,0:T(8,128)(2,1)S(1)}, u32[]{:S(2)}, u32[]{:S(2)}) collective-permute-start(bf16[64,768]{1,0:T(8,128)(2,1)S(1)} %get-tuple-element.97), channel_id=1, source_target_pairs={{0,1},{1,0},{2,3},{3,2},{4,5},{5,4},{6,7},{7,6},{8,9},{9,8},{10,11... | collective-permute-start | bytes 294920 | tf_op jit(solution)/shard_map/ppermute | solution.py:530
  9.7 1.4 %collective-permute-start.3 = (bf16[64,768]{1,0:T(8,128)(2,1)S(1)}, bf16[64,768]{1,0:T(8,128)(2,1)S(1)}, u32[]{:S(2)}, u32[]{:S(2)}) collective-permute-start(bf16[64,768]{1,0:T(8,128)(2,1)S(1)} %get-tuple-element.99), channel_id=1, source_target_pairs={{0,1},{1,0},{2,3},{3,2},{4,5},{5,4},{6,7},{7,6},{8,9},{9,8},{10,11... | collective-permute-start | bytes 294920 | tf_op jit(solution)/shard_map/ppermute | solution.py:530
  14.1 1.5 %collective-permute-start.4 = (bf16[256,384]{1,0:T(8,128)(2,1)S(1)}, bf16[256,384]{1,0:T(8,128)(2,1)S(1)}, u32[]{:S(2)}, u32[]{:S(2)}) collective-permute-start(bf16[256,384]{1,0:T(8,128)(2,1)S(1)} %get-tuple-element.100.atta), channel_id=1, source_target_pairs={{0,1},{1,0},{2,3},{3,2},{4,5},{5,4},{6,7},{7,6},{8,9},{9,8},{10,11... | collective-permute-start | bytes 589832 | tf_op jit(solution)/shard_map/ppermute | solution.py:530
  14.5 1.4 %collective-permute-start.5 = (bf16[256,384]{1,0:T(8,128)(2,1)S(1)}, bf16[256,384]{1,0:T(8,128)(2,1)S(1)}, u32[]{:S(2)}, u32[]{:S(2)}) collective-permute-start(bf16[256,384]{1,0:T(8,128)(2,1)S(1)} %get-tuple-element.101.attb), channel_id=1, source_target_pairs={{0,1},{1,0},{2,3},{3,2},{4,5},{5,4},{6,7},{7,6},{8,9},{9,8},{10,11... | collective-permute-start | bytes 589832 | tf_op jit(solution)/shard_map/ppermute | solution.py:530
  14.7 2.5 %collective-permute-start.6 = (bf16[2,64,768]{2,1,0:T(8,128)(2,1)S(1)}, bf16[2,64,768]{2,1,0:T(8,128)(2,1)S(1)}, u32[]{:S(2)}, u32[]{:S(2)}) collective-permute-start(bf16[2,64,768]{2,1,0:T(8,128)(2,1)S(1)} %get-tuple-element.105.d0), channel_id=1, source_target_pairs={{0,1},{1,0},{2,3},{3,2},{4,5},{5,4},{6,7},{7,6},{8,9},{9,8},{10,11... | collective-permute-start | bytes 589832 | tf_op jit(solution)/shard_map/ppermute | solution.py:530
  15.1 2.1 %collective-permute-start.8 = (bf16[2,64,768]{2,1,0:T(8,128)(2,1)S(1)}, bf16[2,64,768]{2,1,0:T(8,128)(2,1)S(1)}, u32[]{:S(2)}, u32[]{:S(2)}) collective-permute-start(bf16[2,64,768]{2,1,0:T(8,128)(2,1)S(1)} %collective-permute-done.7.d2), channel_id=1, source_target_pairs={{0,1},{1,0},{2,3},{3,2},{4,5},{5,4},{6,7},{7,6},{8,9},{9,8},{10,11... | collective-permute-start | bytes 589832 | tf_op jit(solution)/shard_map/ppermute | solution.py:530
  21.5 5.2 %collective-permute-start.9 = (bf16[256,768]{1,0:T(8,128)(2,1)S(1)}, bf16[256,768]{1,0:T(8,128)(2,1)S(1)}, u32[]{:S(2)}, u32[]{:S(2)}) collective-permute-start(bf16[256,768]{1,0:T(8,128)(2,1)S(1)} %get-tuple-element.109), channel_id=1, source_target_pairs={{0,1},{1,0},{2,3},{3,2},{4,5},{5,4},{6,7},{7,6},{8,9},{9,8},{10,11... | collective-permute-start | bytes 1179656 | tf_op jit(solution)/shard_map/ppermute | solution.py:530
  23.5 15.5 %collective-permute-start.14 = (bf16[2,2,576,128]{3,2,1,0:T(8,128)(2,1)S(1)}, bf16[2,2,576,128]{3,2,1,0:T(8,128)(2,1)S(1)}, u32[]{:S(2)}, u32[]{:S(2)}) collective-permute-start(bf16[2,2,576,128]{3,2,1,0:T(8,128)(2,1)S(1)} %get-tuple-element.132), channel_id=1, source_target_pairs={{0,8},{4,12},{8,0},{12,4},{16,24},{20,28},{24,16},{28,20},{1,9},{5... | collective-permute-start | bytes 1769480 | tf_op jit(solution)/shard_map/ppermute | solution.py:530
  25.2 16.7 %collective-permute-start.16 = (bf16[4,576,128]{2,1,0:T(8,128)(2,1)S(1)}, bf16[4,576,128]{2,1,0:T(8,128)(2,1)S(1)}, u32[]{:S(2)}, u32[]{:S(2)}) collective-permute-start(bf16[4,576,128]{2,1,0:T(8,128)(2,1)S(1)} %get-tuple-element.137), channel_id=1, source_target_pairs={{0,4},{4,0},{8,12},{12,8},{16,20},{20,16},{24,28},{28,24},{1,5},{5... | collective-permute-start | bytes 1769480 | tf_op jit(solution)/shard_map/ppermute | solution.py:530
  29.6 2.1 %collective-permute-start.10 = (bf16[256,768]{1,0:T(8,128)(2,1)S(1)}, bf16[256,768]{1,0:T(8,128)(2,1)S(1)}, u32[]{:S(2)}, u32[]{:S(2)}) collective-permute-start(bf16[256,768]{1,0:T(8,128)(2,1)S(1)} %get-tuple-element.118.owna), channel_id=1, source_target_pairs={{0,1},{1,0},{2,3},{3,2},{4,5},{5,4},{6,7},{7,6},{8,9},{9,8},{10,11... | collective-permute-start | bytes 1179656 | tf_op jit(solution)/shard_map/ppermute | solution.py:530
  29.7 2.4 %collective-permute-start.11 = (bf16[320,768]{1,0:T(8,128)(2,1)S(1)}, bf16[320,768]{1,0:T(8,128)(2,1)S(1)}, u32[]{:S(2)}, u32[]{:S(2)}) collective-permute-start(bf16[320,768]{1,0:T(8,128)(2,1)S(1)} %get-tuple-element.119.ownb), channel_id=1, source_target_pairs={{0,1},{1,0},{2,3},{3,2},{4,5},{5,4},{6,7},{7,6},{8,9},{9,8},{10,11... | collective-permute-start | bytes 1474568 | tf_op jit(solution)/shard_map/ppermute | solution.py:530
  33.9 19.5 %collective-permute-start.18 = (bf16[4,592,128]{2,1,0:T(8,128)(2,1)S(1)}, bf16[4,592,128]{2,1,0:T(8,128)(2,1)S(1)}, u32[]{:S(2)}, u32[]{:S(2)}) collective-permute-start(bf16[4,592,128]{2,1,0:T(8,128)(2,1)S(1)} %get-tuple-element.140), channel_id=1, source_target_pairs={{0,4},{4,0},{8,12},{12,8},{16,20},{20,16},{24,28},{28,24},{1,5},{5... | collective-permute-start | bytes 1818632 | tf_op jit(solution)/shard_map/ppermute | solution.py:530
  34.5 20.9 %collective-permute-start.13 = (bf16[2,64,768]{2,1,0:T(8,128)(2,1)S(1)}, bf16[2,64,768]{2,1,0:T(8,128)(2,1)S(1)}, u32[]{:S(2)}, u32[]{:S(2)}) collective-permute-start(bf16[2,64,768]{2,1,0:T(8,128)(2,1)S(1)} %get-tuple-element.131), channel_id=1, source_target_pairs={{0,1},{1,0},{2,3},{3,2},{4,5},{5,4},{6,7},{7,6},{8,9},{9,8},{10,11... | collective-permute-start | bytes 589832 | tf_op jit(solution)/shard_map/ppermute | solution.py:530
  34.5 20.9 %collective-permute-start.12 = (bf16[2,64,768]{2,1,0:T(8,128)(2,1)S(1)}, bf16[2,64,768]{2,1,0:T(8,128)(2,1)S(1)}, u32[]{:S(2)}, u32[]{:S(2)}) collective-permute-start(bf16[2,64,768]{2,1,0:T(8,128)(2,1)S(1)} %get-tuple-element.128), channel_id=1, source_target_pairs={{0,2},{1,3},{2,0},{3,1},{4,6},{5,7},{6,4},{7,5},{8,10},{9,11},{10,... | collective-permute-start | bytes 589832 | tf_op jit(solution)/shard_map/ppermute | solution.py:530
  39.1 16.2 %collective-permute-start.15 = (bf16[1,2,576,128]{3,2,1,0:T(8,128)(2,1)S(1)}, bf16[1,2,576,128]{3,2,1,0:T(8,128)(2,1)S(1)}, u32[]{:S(2)}, u32[]{:S(2)}) collective-permute-start(bf16[1,2,576,128]{3,2,1,0:T(8,128)(2,1)S(1)} %get-tuple-element.135), channel_id=1, source_target_pairs={{0,16},{4,20},{8,24},{12,28},{16,0},{20,4},{24,8},{28,12},{1,17},{... | collective-permute-start | bytes 884744 | tf_op jit(solution)/shard_map/ppermute | solution.py:530
  42.0 13.3 %collective-permute-start.17 = (bf16[2,576,128]{2,1,0:T(8,128)(2,1)S(1)}, bf16[2,576,128]{2,1,0:T(8,128)(2,1)S(1)}, u32[]{:S(2)}, u32[]{:S(2)}) collective-permute-start(bf16[2,576,128]{2,1,0:T(8,128)(2,1)S(1)} %get-tuple-element.139), channel_id=1, source_target_pairs={{0,8},{4,12},{8,0},{12,4},{16,24},{20,28},{24,16},{28,20},{1,9},{5... | collective-permute-start | bytes 884744 | tf_op jit(solution)/shard_map/ppermute | solution.py:530
  53.5 11.4 %collective-permute-start.21 = (bf16[2,592,128]{2,1,0:T(8,128)(2,1)S(1)}, bf16[2,592,128]{2,1,0:T(8,128)(2,1)S(1)}, u32[]{:S(2)}, u32[]{:S(2)}) collective-permute-start(bf16[2,592,128]{2,1,0:T(8,128)(2,1)S(1)} %get-tuple-element.147), channel_id=1, source_target_pairs={{0,8},{4,12},{8,0},{12,4},{16,24},{20,28},{24,16},{28,20},{1,9},{5... | collective-permute-start | bytes 909320 | tf_op jit(solution)/shard_map/ppermute | solution.py:530
  55.5 1.5 %collective-permute-start.19 = (bf16[576,128]{1,0:T(8,128)(2,1)S(1)}, bf16[576,128]{1,0:T(8,128)(2,1)S(1)}, u32[]{:S(2)}, u32[]{:S(2)}) collective-permute-start(bf16[576,128]{1,0:T(8,128)(2,1)S(1)} %get-tuple-element.144), channel_id=1, source_target_pairs={{0,1},{1,0},{2,3},{3,2},{4,5},{5,4},{6,7},{7,6},{8,9},{9,8},{10,11... | collective-permute-start | bytes 442376 | tf_op jit(solution)/shard_map/ppermute | solution.py:530
  55.6 13.3 %collective-permute-start.22 = (bf16[1,576,128]{2,1,0:T(8,128)(2,1)S(1)}, bf16[1,576,128]{2,1,0:T(8,128)(2,1)S(1)}, u32[]{:S(2)}, u32[]{:S(2)}) collective-permute-start(bf16[1,576,128]{2,1,0:T(8,128)(2,1)S(1)} %get-tuple-element.151), channel_id=1, source_target_pairs={{0,16},{4,20},{8,24},{12,28},{16,0},{20,4},{24,8},{28,12},{1,17},{... | collective-permute-start | bytes 442376 | tf_op jit(solution)/shard_map/ppermute | solution.py:530
  57.0 9.1 %collective-permute-start.20 = (bf16[576,128]{1,0:T(8,128)(2,1)S(1)}, bf16[576,128]{1,0:T(8,128)(2,1)S(1)}, u32[]{:S(2)}, u32[]{:S(2)}) collective-permute-start(bf16[576,128]{1,0:T(8,128)(2,1)S(1)} %get-tuple-element.146), channel_id=1, source_target_pairs={{0,4},{4,0},{8,12},{12,8},{16,20},{20,16},{24,28},{28,24},{1,5},{5... | collective-permute-start | bytes 442376 | tf_op jit(solution)/shard_map/ppermute | solution.py:530
  65.0 8.4 %collective-permute-start.25 = (bf16[1,592,128]{2,1,0:T(8,128)(2,1)S(1)}, bf16[1,592,128]{2,1,0:T(8,128)(2,1)S(1)}, u32[]{:S(2)}, u32[]{:S(2)}) collective-permute-start(bf16[1,592,128]{2,1,0:T(8,128)(2,1)S(1)} %get-tuple-element.153), channel_id=1, source_target_pairs={{0,16},{4,20},{8,24},{12,28},{16,0},{20,4},{24,8},{28,12},{1,17},{... | collective-permute-start | bytes 454664 | tf_op jit(solution)/shard_map/ppermute | solution.py:530
  66.1 9.0 %collective-permute-start.28 = (bf16[576,128]{1,0:T(8,128)(2,1)S(1)}, bf16[576,128]{1,0:T(8,128)(2,1)S(1)}, u32[]{:S(2)}, u32[]{:S(2)}) collective-permute-start(bf16[576,128]{1,0:T(8,128)(2,1)S(1)} %add.2.before.p0), channel_id=1, source_target_pairs={{0,2},{1,3},{2,0},{3,1},{4,6},{5,7},{6,4},{7,5},{8,10},{9,11},{10,... | collective-permute-start | bytes 442376 | tf_op jit(solution)/shard_map/ppermute | solution.py:530
  68.9 8.9 %collective-permute-start.24 = (bf16[1,592,128]{2,1,0:T(8,128)(2,1)S(1)}, bf16[1,592,128]{2,1,0:T(8,128)(2,1)S(1)}, u32[]{:S(2)}, u32[]{:S(2)}) collective-permute-start(bf16[1,592,128]{2,1,0:T(8,128)(2,1)S(1)} %add_wide.1.before.a0), channel_id=1, source_target_pairs={{0,2},{1,3},{2,0},{3,1},{4,6},{5,7},{6,4},{7,5},{8,10},{9,11},{10,... | collective-permute-start | bytes 454664 | tf_op jit(solution)/shard_map/ppermute | solution.py:530
  73.5 5.7 %collective-permute-start.26 = (bf16[1,592,128]{2,1,0:T(8,128)(2,1)S(1)}, bf16[1,592,128]{2,1,0:T(8,128)(2,1)S(1)}, u32[]{:S(2)}, u32[]{:S(2)}) collective-permute-start(bf16[1,592,128]{2,1,0:T(8,128)(2,1)S(1)} %add.3.p0), channel_id=1, source_target_pairs={{0,2},{1,3},{2,0},{3,1},{4,6},{5,7},{6,4},{7,5},{8,10},{9,11},{10,... | collective-permute-start | bytes 454664 | tf_op jit(solution)/shard_map/ppermute | solution.py:530
  75.1 1.4 %collective-permute-start.27 = (bf16[576,128]{1,0:T(8,128)(2,1)S(1)}, bf16[576,128]{1,0:T(8,128)(2,1)S(1)}, u32[]{:S(2)}, u32[]{:S(2)}) collective-permute-start(bf16[576,128]{1,0:T(8,128)(2,1)S(1)} %add.2.before.p0), channel_id=1, source_target_pairs={{0,1},{1,0},{2,3},{3,2},{4,5},{5,4},{6,7},{7,6},{8,9},{9,8},{10,11... | collective-permute-start | bytes 442376 | tf_op jit(solution)/shard_map/ppermute | solution.py:530
  75.1 1.6 %collective-permute-start.29 = (bf16[576,128]{1,0:T(8,128)(2,1)S(1)}, bf16[576,128]{1,0:T(8,128)(2,1)S(1)}, u32[]{:S(2)}, u32[]{:S(2)}) collective-permute-start(bf16[576,128]{1,0:T(8,128)(2,1)S(1)} %collective-permute-done.28.p2), channel_id=1, source_target_pairs={{0,1},{1,0},{2,3},{3,2},{4,5},{5,4},{6,7},{7,6},{8,9},{9,8},{10,11... | collective-permute-start | bytes 442376 | tf_op jit(solution)/shard_map/ppermute | solution.py:530
  75.6 4.1 %collective-permute-start.23 = (bf16[1,592,128]{2,1,0:T(8,128)(2,1)S(1)}, bf16[1,592,128]{2,1,0:T(8,128)(2,1)S(1)}, u32[]{:S(2)}, u32[]{:S(2)}) collective-permute-start(bf16[1,592,128]{2,1,0:T(8,128)(2,1)S(1)} %add_wide.1.before.a0), channel_id=1, source_target_pairs={{0,1},{1,0},{2,3},{3,2},{4,5},{5,4},{6,7},{7,6},{8,9},{9,8},{10,11... | collective-permute-start | bytes 454664 | tf_op jit(solution)/shard_map/ppermute | solution.py:530
  76.5 3.3 %collective-permute-start.31 = (bf16[1,592,128]{2,1,0:T(8,128)(2,1)S(1)}, bf16[1,592,128]{2,1,0:T(8,128)(2,1)S(1)}, u32[]{:S(2)}, u32[]{:S(2)}) collective-permute-start(bf16[1,592,128]{2,1,0:T(8,128)(2,1)S(1)} %add.3.p0), channel_id=1, source_target_pairs={{0,1},{1,0},{2,3},{3,2},{4,5},{5,4},{6,7},{7,6},{8,9},{9,8},{10,11... | collective-permute-start | bytes 454664 | tf_op jit(solution)/shard_map/ppermute | solution.py:530
  79.2 1.4 %collective-permute-start.30 = (bf16[1,592,128]{2,1,0:T(8,128)(2,1)S(1)}, bf16[1,592,128]{2,1,0:T(8,128)(2,1)S(1)}, u32[]{:S(2)}, u32[]{:S(2)}) collective-permute-start(bf16[1,592,128]{2,1,0:T(8,128)(2,1)S(1)} %collective-permute-done.24.a2), channel_id=1, source_target_pairs={{0,1},{1,0},{2,3},{3,2},{4,5},{5,4},{6,7},{7,6},{8,9},{9,8},{10,11... | collective-permute-start | bytes 454664 | tf_op jit(solution)/shard_map/ppermute | solution.py:530
  79.2 1.6 %collective-permute-start.32 = (bf16[1,592,128]{2,1,0:T(8,128)(2,1)S(1)}, bf16[1,592,128]{2,1,0:T(8,128)(2,1)S(1)}, u32[]{:S(2)}, u32[]{:S(2)}) collective-permute-start(bf16[1,592,128]{2,1,0:T(8,128)(2,1)S(1)} %collective-permute-done.26.p2), channel_id=1, source_target_pairs={{0,1},{1,0},{2,3},{3,2},{4,5},{5,4},{6,7},{7,6},{8,9},{9,8},{10,11... | collective-permute-start | bytes 454664 | tf_op jit(solution)/shard_map/ppermute | solution.py:530
